TPU v7x, 32 devices: a whole 2x2x4 slice. The times are simulated.
32 devices in a mesh: ctx: 8 (over z, y), fsdp: 4 (over x, core).
Axes of the slice: x: 2, y: 2, z: 4, core: 2. Of those that a mesh axis runs over, the one named last changes fastest.
Arguments:
- tokens: bfloat16 [4, 4096, 1024], P('fsdp', 'ctx'), may hold values from -6 to 6
- cotangent: bfloat16 [4, 4096, 1024], P('fsdp', 'ctx'), may hold values from -6 to 6
- doc_starts: int32 [4, 6], P('fsdp'), may hold values from 0 to 4095, as said below
- gain_mix: bfloat16 [1024], P('fsdp'), may hold values from 0.099609375 to 1.8984375
- w_z: bfloat16 [1024, 1536], P('fsdp'), may hold values from -0.1875 to 0.1875
- w_xbc: bfloat16 [1024, 1792], P('fsdp'), may hold values from -0.1875 to 0.1875
- w_dt: bfloat16 [1024, 24], P('fsdp'), may hold values from -0.1875 to 0.1875
- conv_w: bfloat16 [4, 1792], P(None, 'fsdp'), may hold values from -3 to 3
- conv_b: bfloat16 [1792], P('fsdp'), may hold values from -2 to 2
- dt_bias: bfloat16 [24], P('fsdp'), may hold values from -5 to -2
- a_log: bfloat16 [24], P('fsdp'), may hold values from -12 to 2
- skip_factor: bfloat16 [24], P('fsdp'), may hold values from 0.5 to 1.5
- w_mo: bfloat16 [1536, 1024], P('fsdp'), may hold values from -0.15625 to 0.15625
- w_q: bfloat16 [1024, 512], P('fsdp'), may hold values from -0.1875 to 0.1875
- key_value_weight: bfloat16 [1024, 256], P('fsdp'), may hold values from -0.1875 to 0.1875
- w_o: bfloat16 [512, 1024], P('fsdp'), may hold values from -2 to 2
- gain_ffn: bfloat16 [1024], P('fsdp'), may hold values from 0.099609375 to 1.8984375
- w_gate: bfloat16 [1024, 2048], P('fsdp'), may hold values from -0.1875 to 0.1875
- w_up: bfloat16 [1024, 2048], P('fsdp'), may hold values from -0.1875 to 0.1875
- w_down: bfloat16 [2048, 1024], P('fsdp'), may hold values from -0.125 to 0.125
Outputs:
- result: bfloat16 [4, 4096, 1024], P('fsdp', 'ctx')
- grad_tokens: float32 [4, 4096, 1024], P('fsdp', 'ctx')
- grad_gain_mix: float32 [1024], P('fsdp')
- grad_w_z: float32 [1024, 1536], P('fsdp')
- grad_w_xbc: float32 [1024, 1792], P('fsdp')
- grad_w_dt: float32 [1024, 24], P('fsdp')
- grad_conv_w: float32 [4, 1792], P(None, 'fsdp')
- grad_conv_b: float32 [1792], P('fsdp')
- grad_dt_bias: float32 [24], P('fsdp')
- grad_a_log: float32 [24], P('fsdp')
- grad_d_skip: float32 [24], P('fsdp')
- grad_w_mo: float32 [1536, 1024], P('fsdp')
- grad_w_q: float32 [1024, 512], P('fsdp')
- grad_w_kv: float32 [1024, 256], P('fsdp')
- grad_w_o: float32 [512, 1024], P('fsdp')
- grad_gain_ffn: float32 [1024], P('fsdp')
- grad_w_gate: float32 [1024, 2048], P('fsdp')
- grad_w_up: float32 [1024, 2048], P('fsdp')
- grad_w_down: float32 [2048, 1024], P('fsdp')
Inputs may be any that keep to these rules, and one draw needn't show every extreme that they name: `doc_starts`: each row is strictly increasing, begins with 0 and ends with 4095; a document runs from one start to the next start or to the end of its stream.
All inputs are finite; a program needn't handle non-finite values.
Results may differ from a plain program's by a relative error of at most 0.02.
Values may be sent and summed in bfloat16 or wider, within the bound.
No kernel may reach another device: no remote copies, remote signals or barrier semaphores. Data moves between devices by JAX's collectives and lax.ppermute only.
A program may use at most 448 MiB of HBM per device.

v0:
```python
import functools
import math

import jax
import jax.numpy as jnp
from jax import lax
from jax.sharding import PartitionSpec as P

MAMBA_HEADS = 24
MAMBA_HEAD_SIZE = 64
STATE_SIZE = 128
CONV = 4
QUERY_HEADS = 8
KEY_VALUE_HEADS = 2
HEAD_SIZE = 64
BLOCK_TOKENS = 256


EPSILON = 1e-06
ROPE_BASE = 10000.0
MASK_FILLER = -1e30
FORGET = -10000.0
HIGHEST = lax.Precision.HIGHEST


def from_behind(block, axis, distance):
    devices = range(lax.axis_size(axis))
    route = [(i - distance, i) for i in devices if i - distance in devices]
    return lax.ppermute(block, axis, route)


def entering(array, axis, join, neutral):
    place = lax.axis_index(axis)
    gathered = jax.tree.map(
        lambda a, kind: lax.all_gather(a.astype(kind), axis), array, (jnp.bfloat16, jnp.bfloat16)
    )
    state = jax.tree.map(lambda a, e: jnp.zeros_like(a) + jnp.asarray(e, a.dtype), array, neutral)

    def one(turn, state):
        return join(
            state,
            jax.tree.map(
                lambda a, own: lax.dynamic_index_in_dim(a, turn, 0, False).astype(own.dtype),
                gathered,
                array,
            ),
        )

    return lax.fori_loop(0, place, one, state)


def entering_2(array, axis, combine, identity):
    devices, index = (lax.axis_size(axis), lax.axis_index(axis))
    everything = jax.tree.map(
        lambda part, kind: lax.all_gather(part.astype(kind), axis),
        array,
        jax.tree.map(lambda a: jnp.bfloat16 if a.dtype == jnp.float32 else a.dtype, array),
    )
    start = jax.tree.map(
        lambda part, zero: jnp.broadcast_to(jnp.asarray(zero, part.dtype), part.shape),
        array,
        identity,
    )

    def turn(k, before):
        at = devices - 1 - k
        reached = at > index
        new = combine(
            before, jax.tree.map(lambda part, own: part[at].astype(own.dtype), everything, array)
        )
        return jax.tree.map(lambda a, b: jnp.where(reached, a, b), new, before)

    return lax.fori_loop(0, devices, turn, start)


def segment_of(token_positions, starts):
    counted = jnp.sum((starts[None, :] <= token_positions[:, None]).astype(jnp.int32), axis=1)
    return counted - jnp.int32(1)


def apply_rotary(value_matrix, token_positions, turn):
    half = value_matrix.shape[-1] // 2
    freqs = ROPE_BASE ** (-2.0 * jnp.arange(half, dtype=jnp.float32) / value_matrix.shape[-1])
    angles = token_positions.astype(jnp.float32)[:, None] * freqs[None, :]
    cosine = jnp.cos(angles)[:, None, :]
    sine = turn * jnp.sin(angles)[:, None, :]
    former = value_matrix[..., :half]
    latter = value_matrix[..., half:]
    return jnp.concatenate(
        [former * cosine - latter * sine, latter * cosine + former * sine], axis=-1
    )


def outer_sum(left, right):
    return lax.dot_general(
        left, right, (((0,), (0,)), ((), ())), preferred_element_type=jnp.float32
    )


def time_steps(left, right):
    return lax.dot_general(
        left, right, (((1,), (1,)), ((), ())), preferred_element_type=jnp.float32
    )


def chain_join(earlier, later):
    return (earlier[0] * later[0], later[0][:, None, None] * earlier[1] + later[1])


def chain_back(earlier, later):
    return (later[0] * earlier[0], later[1] + later[0][:, None, None] * earlier[1])


def span_step(running, slices):
    state, seg_before = running
    (
        input_weights_x,
        input_weights_b,
        input_weights_c,
        step_interval,
        decay_logarithm,
        document_segments,
    ) = slices
    cumul = jnp.cumsum(decay_logarithm, axis=0)
    order = jnp.arange(document_segments.shape[0])
    visible = (document_segments[:, None] == document_segments[None, :]) & (
        order[:, None] >= order[None, :]
    )
    spread = jnp.where(visible[:, :, None], cumul[:, None, :] - cumul[None, :, :], FORGET)
    couple = jnp.dot(input_weights_c, input_weights_b.T, precision=HIGHEST)
    mixing = couple[:, :, None] * jnp.exp(spread) * step_interval[None, :, :]
    layer_outputs = jnp.einsum("tsh,shp->thp", mixing, input_weights_x, precision=HIGHEST)
    carried = (document_segments == seg_before).astype(jnp.float32)
    layer_outputs = (
        layer_outputs
        + jnp.einsum("tn,hpn->thp", input_weights_c, state, precision=HIGHEST)
        * (jnp.exp(cumul) * carried[:, None])[:, :, None]
    )
    seg_end = document_segments[-1]
    ending = (
        jnp.exp(cumul[-1][None, :] - cumul)
        * step_interval
        * (document_segments == seg_end).astype(jnp.float32)[:, None]
    )
    keep_end = jnp.exp(cumul[-1]) * (seg_end == seg_before).astype(jnp.float32)
    fresh = jnp.einsum(
        "sh,shp,sn->hpn", ending, input_weights_x, input_weights_b, precision=HIGHEST
    )
    return ((fresh + state * keep_end[:, None, None], seg_end), layer_outputs)


def mamba_local(
    padded,
    dt_raw,
    conv_w,
    conv_b,
    dt_bias,
    a_log,
    skip_factor,
    seg_ext,
    document_segments,
    seg_before,
):
    token_count = dt_raw.shape[0]
    summed = jnp.zeros((token_count, conv_b.shape[0]), jnp.float32) + conv_b[None, :]
    for offset in range(CONV):
        agree = (seg_ext[offset : offset + token_count] == document_segments).astype(jnp.float32)
        summed = (
            summed
            + conv_w[offset][None, :] * padded[offset : offset + token_count] * agree[:, None]
        )
    activation_value = jax.nn.silu(summed)
    mamba_width = MAMBA_HEADS * MAMBA_HEAD_SIZE
    input_weights_x = activation_value[:, :mamba_width].reshape(
        token_count, MAMBA_HEADS, MAMBA_HEAD_SIZE
    )
    input_weights_b = activation_value[:, mamba_width : mamba_width + STATE_SIZE]
    input_weights_c = activation_value[:, mamba_width + STATE_SIZE :]
    step_interval = jax.nn.softplus(dt_raw + dt_bias[None, :])
    decay_logarithm = -step_interval * jnp.exp(a_log)[None, :]
    count_of_blocks = token_count // BLOCK_TOKENS
    piece_list = (
        input_weights_x.reshape(count_of_blocks, BLOCK_TOKENS, MAMBA_HEADS, MAMBA_HEAD_SIZE),
        input_weights_b.reshape(count_of_blocks, BLOCK_TOKENS, STATE_SIZE),
        input_weights_c.reshape(count_of_blocks, BLOCK_TOKENS, STATE_SIZE),
        step_interval.reshape(count_of_blocks, BLOCK_TOKENS, MAMBA_HEADS),
        decay_logarithm.reshape(count_of_blocks, BLOCK_TOKENS, MAMBA_HEADS),
        document_segments.reshape(count_of_blocks, BLOCK_TOKENS),
    )
    initial_state = jnp.zeros((MAMBA_HEADS, MAMBA_HEAD_SIZE, STATE_SIZE), jnp.float32)
    (final_state, _), layer_outputs = lax.scan(span_step, (initial_state, seg_before), piece_list)
    layer_outputs = (
        layer_outputs.reshape(token_count, MAMBA_HEADS, MAMBA_HEAD_SIZE)
        + skip_factor[None, :, None] * input_weights_x
    )
    cumul = jnp.cumsum(decay_logarithm, axis=0)
    through = jnp.exp(cumul[-1]) * (document_segments[-1] == seg_before).astype(jnp.float32)
    return (layer_outputs, final_state, through, input_weights_c, cumul)


def correction(input_weights_c, cumul, state_in, carried):
    return (
        jnp.einsum("tn,hpn->thp", input_weights_c, state_in, precision=HIGHEST)
        * (jnp.exp(cumul) * carried[:, None])[:, :, None]
    )


def fold_blocks(running, kv_piece, q_pos, q_seg, starts, visit_block):
    row_count = kv_piece.shape[0]
    block_rows = math.gcd(row_count, 512)
    count_of_blocks = row_count // block_rows
    piece_list = kv_piece.reshape(count_of_blocks, block_rows, kv_piece.shape[1])
    offsets = block_rows * jnp.arange(count_of_blocks, dtype=jnp.int32)

    def one_step(state_now, slices):
        key_block, offset = slices
        key_pos = offset + jnp.arange(block_rows, dtype=jnp.int32)
        key_seg = segment_of(key_pos, starts)
        visible = (q_seg[:, None] == key_seg[None, :]) & (q_pos[:, None] >= key_pos[None, :])
        any_visible = (offset <= q_pos[-1]) & (key_seg[-1] >= q_seg[0])
        updated = lax.cond(
            any_visible,
            lambda current: visit_block(current, key_block, visible, offset),
            lambda current: current,
            state_now,
        )
        return (updated, None)

    running, _ = lax.scan(one_step, running, (piece_list, offsets))
    return running


def attend_visit(state_now, key_block, visible, offset, query_matrix):
    row_max, summed, weighted = state_now
    block_rows = key_block.shape[0]
    heads_kv = query_matrix.shape[1]
    head_dim = query_matrix.shape[3]
    key_value_width = heads_kv * head_dim
    heads_of_keys = key_block[:, :key_value_width].reshape(block_rows, heads_kv, head_dim)
    value_matrix = key_block[:, key_value_width:].reshape(block_rows, heads_kv, head_dim)
    scores = jnp.einsum(
        "tjgd,cjd->jgtc", query_matrix, heads_of_keys, preferred_element_type=jnp.float32
    ) * (1.0 / math.sqrt(head_dim))
    scores = jnp.where(visible, scores, MASK_FILLER)
    new_max = jnp.maximum(row_max, jnp.max(scores, axis=-1))
    attn_prob = jnp.where(visible, jnp.exp(scores - new_max[..., None]), 0.0)
    fade = jnp.exp(row_max - new_max)
    summed = summed * fade + jnp.sum(attn_prob, axis=-1)
    weighted = weighted * fade[..., None] + jnp.einsum(
        "jgtc,cjd->jgtd",
        attn_prob.astype(jnp.bfloat16),
        value_matrix,
        preferred_element_type=jnp.float32,
    )
    return (new_max, summed, weighted)


def attend_piece(running, kv_piece, first_row, query_matrix, q_pos, q_seg, starts):
    visit_block = functools.partial(attend_visit, query_matrix=query_matrix)
    return fold_blocks(running, kv_piece, q_pos, q_seg, starts, visit_block)


def back_visit(
    state_now, key_block, visible, offset, query_matrix, attention_gradient, log_total, row_delta
):
    grad_q, grad_kv = state_now
    block_rows = key_block.shape[0]
    heads_kv = query_matrix.shape[1]
    head_dim = query_matrix.shape[3]
    key_value_width = heads_kv * head_dim
    scale_q = 1.0 / math.sqrt(head_dim)
    heads_of_keys = key_block[:, :key_value_width].reshape(block_rows, heads_kv, head_dim)
    value_matrix = key_block[:, key_value_width:].reshape(block_rows, heads_kv, head_dim)
    scores = (
        jnp.einsum(
            "tjgd,cjd->jgtc", query_matrix, heads_of_keys, preferred_element_type=jnp.float32
        )
        * scale_q
    )
    scores = jnp.where(visible, scores, MASK_FILLER)
    attn_prob = jnp.where(visible, jnp.exp(scores - log_total[..., None]), 0.0)
    grad_prob = jnp.einsum(
        "tjgd,cjd->jgtc", attention_gradient, value_matrix, preferred_element_type=jnp.float32
    )
    grad_scores = (attn_prob * (grad_prob - row_delta[..., None])).astype(jnp.bfloat16)
    grad_q = (
        grad_q
        + jnp.einsum(
            "jgtc,cjd->jgtd", grad_scores, heads_of_keys, preferred_element_type=jnp.float32
        )
        * scale_q
    )
    grad_keys = (
        jnp.einsum("jgtc,tjgd->cjd", grad_scores, query_matrix, preferred_element_type=jnp.float32)
        * scale_q
    )
    grad_values = jnp.einsum(
        "jgtc,tjgd->cjd",
        attn_prob.astype(jnp.bfloat16),
        attention_gradient,
        preferred_element_type=jnp.float32,
    )
    update = jnp.concatenate(
        [
            grad_keys.reshape(block_rows, key_value_width),
            grad_values.reshape(block_rows, key_value_width),
        ],
        axis=1,
    )
    current_rows = lax.dynamic_slice_in_dim(grad_kv, offset, block_rows, 0)
    grad_kv = lax.dynamic_update_slice_in_dim(grad_kv, current_rows + update, offset, 0)
    return (grad_q, grad_kv)


def attend_back(
    running,
    kv_piece,
    first_row,
    query_matrix,
    attention_gradient,
    log_total,
    row_delta,
    q_pos,
    q_seg,
    starts,
):
    visit_block = functools.partial(
        back_visit,
        query_matrix=query_matrix,
        attention_gradient=attention_gradient,
        log_total=log_total,
        row_delta=row_delta,
    )
    return fold_blocks(running, kv_piece, q_pos, q_seg, starts, visit_block)


def local(
    tokens,
    cotangent,
    doc_starts,
    gain_mix,
    w_z,
    w_xbc,
    w_dt,
    conv_w,
    conv_b,
    dt_bias,
    a_log,
    skip_factor,
    w_mo,
    w_q,
    key_value_weight,
    w_o,
    gain_ffn,
    w_gate,
    w_up,
    w_down,
):
    gathered = (
        lax.all_gather(gain_mix, "fsdp", axis=0, tiled=True),
        lax.all_gather(w_z, "fsdp", axis=0, tiled=True),
        lax.all_gather(w_xbc, "fsdp", axis=0, tiled=True),
        lax.all_gather(w_dt, "fsdp", axis=0, tiled=True),
        lax.all_gather(conv_w, "fsdp", axis=1, tiled=True),
        lax.all_gather(conv_b, "fsdp", axis=0, tiled=True),
        lax.all_gather(dt_bias, "fsdp", axis=0, tiled=True),
        lax.all_gather(a_log, "fsdp", axis=0, tiled=True),
        lax.all_gather(skip_factor, "fsdp", axis=0, tiled=True),
        lax.all_gather(w_mo, "fsdp", axis=0, tiled=True),
        lax.all_gather(w_q, "fsdp", axis=0, tiled=True),
        lax.all_gather(key_value_weight, "fsdp", axis=0, tiled=True),
        lax.all_gather(w_o, "fsdp", axis=0, tiled=True),
        lax.all_gather(gain_ffn, "fsdp", axis=0, tiled=True),
        lax.all_gather(w_gate, "fsdp", axis=0, tiled=True),
        lax.all_gather(w_up, "fsdp", axis=0, tiled=True),
        lax.all_gather(w_down, "fsdp", axis=0, tiled=True),
    )
    (
        full_gain_mix,
        full_z,
        full_xbc,
        full_dt,
        full_conv_w,
        full_conv_b,
        full_dt_bias,
        full_a_log,
        full_skip,
        full_mo,
        full_q,
        full_kv,
        full_o,
        full_gain_ffn,
        full_gate,
        full_up,
        full_down,
    ) = gathered
    ctx_count = lax.axis_size("ctx")
    ctx_rank = lax.axis_index("ctx")
    inputs = tokens[0].astype(jnp.float32)
    token_count = inputs.shape[0]
    length_all = token_count * ctx_count
    starts = doc_starts[0]
    conv_lag = CONV - 1
    ext_pos = (
        ctx_rank * token_count - conv_lag + jnp.arange(token_count + conv_lag, dtype=jnp.int32)
    )
    seg_ext = segment_of(ext_pos, starts)
    token_positions = ext_pos[conv_lag:]
    document_segments = seg_ext[conv_lag:]
    seg_before = seg_ext[conv_lag - 1]
    gain_one = full_gain_mix.astype(jnp.float32)
    scale_one = lax.rsqrt(jnp.mean(inputs * inputs, axis=-1, keepdims=True) + EPSILON)
    normed = (inputs * scale_one * gain_one[None, :]).astype(jnp.bfloat16)
    gate_z = jnp.dot(normed, full_z, preferred_element_type=jnp.float32)
    mixed_in = jnp.dot(normed, full_xbc, preferred_element_type=jnp.float32).astype(jnp.bfloat16)
    dt_raw = jnp.dot(normed, full_dt, preferred_element_type=jnp.float32)
    edge_rows = from_behind(mixed_in[token_count - conv_lag :], "ctx", 1)
    padded = jnp.concatenate([edge_rows, mixed_in], axis=0).astype(jnp.float32)
    local_fn = functools.partial(
        mamba_local, seg_ext=seg_ext, document_segments=document_segments, seg_before=seg_before
    )
    local_out, local_pull = jax.vjp(
        local_fn,
        padded,
        dt_raw,
        full_conv_w.astype(jnp.float32),
        full_conv_b.astype(jnp.float32),
        full_dt_bias.astype(jnp.float32),
        full_a_log.astype(jnp.float32),
        full_skip.astype(jnp.float32),
    )
    mamba_within_block, state_out, through, input_weights_c, cumul = local_out
    _, state_in = entering(
        (through, state_out), "ctx", chain_join, (jnp.ones_like(through), jnp.zeros_like(state_out))
    )
    carried = (document_segments == seg_before).astype(jnp.float32)
    corr_fn = functools.partial(correction, carried=carried)
    mamba_correction, corr_pull = jax.vjp(corr_fn, input_weights_c, cumul, state_in)
    mamba_output = (mamba_within_block + mamba_correction).reshape(
        token_count, MAMBA_HEADS * MAMBA_HEAD_SIZE
    )
    sig_z = jax.nn.sigmoid(gate_z)
    gate_activation = gate_z * sig_z
    gated = (mamba_output * gate_activation).astype(jnp.bfloat16)
    mamba_out = jnp.dot(gated, full_mo, preferred_element_type=jnp.float32)
    query_group = QUERY_HEADS // KEY_VALUE_HEADS
    key_value_width = KEY_VALUE_HEADS * HEAD_SIZE
    query_matrix = apply_rotary(
        jnp.dot(normed, full_q, preferred_element_type=jnp.float32).reshape(
            token_count, QUERY_HEADS, HEAD_SIZE
        ),
        token_positions,
        1.0,
    )
    query_matrix = query_matrix.astype(jnp.bfloat16).reshape(
        token_count, KEY_VALUE_HEADS, query_group, HEAD_SIZE
    )
    raw_key_value = jnp.dot(normed, full_kv, preferred_element_type=jnp.float32)
    rotated_keys = apply_rotary(
        raw_key_value[:, :key_value_width].reshape(token_count, KEY_VALUE_HEADS, HEAD_SIZE),
        token_positions,
        1.0,
    ).reshape(token_count, key_value_width)
    key_value_pairs = jnp.concatenate(
        [rotated_keys, raw_key_value[:, key_value_width:]], axis=1
    ).astype(jnp.bfloat16)
    fold_fwd = functools.partial(
        attend_piece,
        query_matrix=query_matrix,
        q_pos=token_positions,
        q_seg=document_segments,
        starts=starts,
    )
    initial_maximum = jnp.full(
        (KEY_VALUE_HEADS, query_group, token_count), MASK_FILLER, jnp.float32
    )
    initial_sum = jnp.zeros((KEY_VALUE_HEADS, query_group, token_count), jnp.float32)
    initial_accumulator = jnp.zeros(
        (KEY_VALUE_HEADS, query_group, token_count, HEAD_SIZE), jnp.float32
    )
    run_max, run_sum, run_acc = fold_fwd(
        (initial_maximum, initial_sum, initial_accumulator),
        lax.all_gather(key_value_pairs, "ctx", axis=0, tiled=True),
        jnp.int32(0),
    )
    attn_norm = run_acc / run_sum[..., None]
    log_total = run_max + jnp.log(run_sum)
    attn_vec = (
        attn_norm.transpose(2, 0, 1, 3)
        .reshape(token_count, QUERY_HEADS * HEAD_SIZE)
        .astype(jnp.bfloat16)
    )
    attn_out = jnp.dot(attn_vec, full_o, preferred_element_type=jnp.float32)
    hidden = inputs + attn_out + mamba_out
    gain_two = full_gain_ffn.astype(jnp.float32)
    scale_two = lax.rsqrt(jnp.mean(hidden * hidden, axis=-1, keepdims=True) + EPSILON)
    normed_ffn = (hidden * scale_two * gain_two[None, :]).astype(jnp.bfloat16)
    gate = jnp.dot(normed_ffn, full_gate, preferred_element_type=jnp.float32)
    upper = jnp.dot(normed_ffn, full_up, preferred_element_type=jnp.float32)
    sig_gate = jax.nn.sigmoid(gate)
    silu_gate = gate * sig_gate
    activation_value = (silu_gate * upper).astype(jnp.bfloat16)
    result = hidden + jnp.dot(activation_value, full_down, preferred_element_type=jnp.float32)
    again = (
        lax.all_gather(w_z, "fsdp", axis=0, tiled=True),
        lax.all_gather(w_xbc, "fsdp", axis=0, tiled=True),
        lax.all_gather(w_dt, "fsdp", axis=0, tiled=True),
        lax.all_gather(w_mo, "fsdp", axis=0, tiled=True),
        lax.all_gather(w_q, "fsdp", axis=0, tiled=True),
        lax.all_gather(key_value_weight, "fsdp", axis=0, tiled=True),
        lax.all_gather(w_o, "fsdp", axis=0, tiled=True),
        lax.all_gather(w_gate, "fsdp", axis=0, tiled=True),
        lax.all_gather(w_up, "fsdp", axis=0, tiled=True),
        lax.all_gather(w_down, "fsdp", axis=0, tiled=True),
    )
    (
        back_z,
        back_xbc,
        back_dt,
        back_mo,
        back_q,
        back_kv,
        output_proj_back,
        back_gate,
        back_up,
        back_down,
    ) = again
    grad_out = cotangent[0]
    grad_w_down = outer_sum(activation_value, grad_out)
    grad_act = time_steps(grad_out, back_down)
    grad_gate = (grad_act * upper * sig_gate * (1.0 + gate * (1.0 - sig_gate))).astype(jnp.bfloat16)
    grad_up = (grad_act * silu_gate).astype(jnp.bfloat16)
    grad_w_gate = outer_sum(normed_ffn, grad_gate)
    grad_w_up = outer_sum(normed_ffn, grad_up)
    grad_n2 = time_steps(grad_gate, back_gate) + time_steps(grad_up, back_up)
    grad_gain_ffn = jnp.sum(grad_n2 * hidden * scale_two, axis=0)
    scaled_two = grad_n2 * gain_two[None, :]
    grad_hidden = (
        grad_out.astype(jnp.float32)
        + scale_two * scaled_two
        - hidden * scale_two**3 * jnp.mean(scaled_two * hidden, axis=-1, keepdims=True)
    )
    hidden_block_gradient = grad_hidden.astype(jnp.bfloat16)
    grad_w_o = outer_sum(attn_vec, hidden_block_gradient)
    grad_w_mo = outer_sum(gated, hidden_block_gradient)
    attention_gradient = (
        time_steps(hidden_block_gradient, output_proj_back)
        .astype(jnp.bfloat16)
        .reshape(token_count, KEY_VALUE_HEADS, query_group, HEAD_SIZE)
    )
    gated_gradient = time_steps(hidden_block_gradient, back_mo)
    row_delta = jnp.einsum("tjgd,jgtd->jgt", attention_gradient.astype(jnp.float32), attn_norm)
    fold_back = functools.partial(
        attend_back,
        query_matrix=query_matrix,
        attention_gradient=attention_gradient,
        log_total=log_total,
        row_delta=row_delta,
        q_pos=token_positions,
        q_seg=document_segments,
        starts=starts,
    )
    grad_q_acc, grad_kv_all = fold_back(
        (
            jnp.zeros((KEY_VALUE_HEADS, query_group, token_count, HEAD_SIZE), jnp.float32),
            jnp.zeros((length_all, 2 * key_value_width), jnp.float32),
        ),
        lax.all_gather(key_value_pairs, "ctx", axis=0, tiled=True),
        jnp.int32(0),
    )
    own_key_value_gradient = lax.psum_scatter(
        grad_kv_all.astype(jnp.bfloat16), "ctx", scatter_dimension=0, tiled=True
    ).astype(jnp.float32)
    grad_keys = apply_rotary(
        own_key_value_gradient[:, :key_value_width].reshape(
            token_count, KEY_VALUE_HEADS, HEAD_SIZE
        ),
        token_positions,
        -1.0,
    ).reshape(token_count, key_value_width)
    grad_kv_b = jnp.concatenate(
        [grad_keys, own_key_value_gradient[:, key_value_width:]], axis=1
    ).astype(jnp.bfloat16)
    grad_q_b = apply_rotary(
        grad_q_acc.transpose(2, 0, 1, 3).reshape(token_count, QUERY_HEADS, HEAD_SIZE),
        token_positions,
        -1.0,
    )
    grad_q_b = grad_q_b.reshape(token_count, QUERY_HEADS * HEAD_SIZE).astype(jnp.bfloat16)
    grad_w_q = outer_sum(normed, grad_q_b)
    grad_w_kv = outer_sum(normed, grad_kv_b)
    mamba_gradient = (gated_gradient * gate_activation).reshape(
        token_count, MAMBA_HEADS, MAMBA_HEAD_SIZE
    )
    grad_z = (gated_gradient * mamba_output * sig_z * (1.0 + gate_z * (1.0 - sig_z))).astype(
        jnp.bfloat16
    )
    grad_c_corr, grad_cum_corr, grad_state_in = corr_pull(mamba_gradient)
    _, state_grad = entering_2(
        (through, grad_state_in),
        "ctx",
        chain_back,
        (jnp.ones_like(through), jnp.zeros_like(grad_state_in)),
    )
    grad_through = jnp.sum(state_grad * state_in, axis=(1, 2))
    grad_padded, grad_dt_raw, grad_conv_w, grad_conv_b, grad_dt_bias, grad_a_log, grad_skip = (
        local_pull((mamba_gradient, state_grad, grad_through, grad_c_corr, grad_cum_corr))
    )
    edge_grad = from_behind(grad_padded[:conv_lag], "ctx", -1)
    grad_mixed = (
        grad_padded[conv_lag:].at[token_count - conv_lag :].add(edge_grad).astype(jnp.bfloat16)
    )
    grad_dt_b = grad_dt_raw.astype(jnp.bfloat16)
    grad_w_z = outer_sum(normed, grad_z)
    grad_w_xbc = outer_sum(normed, grad_mixed)
    grad_w_dt = outer_sum(normed, grad_dt_b)
    grad_n1 = (
        time_steps(grad_z, back_z)
        + time_steps(grad_mixed, back_xbc)
        + time_steps(grad_dt_b, back_dt)
        + time_steps(grad_q_b, back_q)
        + time_steps(grad_kv_b, back_kv)
    )
    grad_gain_mix = jnp.sum(grad_n1 * inputs * scale_one, axis=0)
    scaled_one = grad_n1 * gain_one[None, :]
    grad_tokens = (
        grad_hidden
        + scale_one * scaled_one
        - inputs * scale_one**3 * jnp.mean(scaled_one * inputs, axis=-1, keepdims=True)
    )
    shares = (
        lax.psum_scatter(
            grad_gain_mix.astype(jnp.bfloat16), "fsdp", scatter_dimension=0, tiled=True
        ).astype(jnp.float32),
        lax.psum_scatter(
            grad_w_z.astype(jnp.bfloat16), "fsdp", scatter_dimension=0, tiled=True
        ).astype(jnp.float32),
        lax.psum_scatter(
            grad_w_xbc.astype(jnp.bfloat16), "fsdp", scatter_dimension=0, tiled=True
        ).astype(jnp.float32),
        lax.psum_scatter(
            grad_w_dt.astype(jnp.bfloat16), "fsdp", scatter_dimension=0, tiled=True
        ).astype(jnp.float32),
        lax.psum_scatter(
            grad_conv_w.astype(jnp.bfloat16), "fsdp", scatter_dimension=1, tiled=True
        ).astype(jnp.float32),
        lax.psum_scatter(
            grad_conv_b.astype(jnp.bfloat16), "fsdp", scatter_dimension=0, tiled=True
        ).astype(jnp.float32),
        lax.psum_scatter(
            grad_dt_bias.astype(jnp.bfloat16), "fsdp", scatter_dimension=0, tiled=True
        ).astype(jnp.float32),
        lax.psum_scatter(
            grad_a_log.astype(jnp.bfloat16), "fsdp", scatter_dimension=0, tiled=True
        ).astype(jnp.float32),
        lax.psum_scatter(
            grad_skip.astype(jnp.bfloat16), "fsdp", scatter_dimension=0, tiled=True
        ).astype(jnp.float32),
        lax.psum_scatter(
            grad_w_mo.astype(jnp.bfloat16), "fsdp", scatter_dimension=0, tiled=True
        ).astype(jnp.float32),
        lax.psum_scatter(
            grad_w_q.astype(jnp.bfloat16), "fsdp", scatter_dimension=0, tiled=True
        ).astype(jnp.float32),
        lax.psum_scatter(
            grad_w_kv.astype(jnp.bfloat16), "fsdp", scatter_dimension=0, tiled=True
        ).astype(jnp.float32),
        lax.psum_scatter(
            grad_w_o.astype(jnp.bfloat16), "fsdp", scatter_dimension=0, tiled=True
        ).astype(jnp.float32),
        lax.psum_scatter(
            grad_gain_ffn.astype(jnp.bfloat16), "fsdp", scatter_dimension=0, tiled=True
        ).astype(jnp.float32),
        lax.psum_scatter(
            grad_w_gate.astype(jnp.bfloat16), "fsdp", scatter_dimension=0, tiled=True
        ).astype(jnp.float32),
        lax.psum_scatter(
            grad_w_up.astype(jnp.bfloat16), "fsdp", scatter_dimension=0, tiled=True
        ).astype(jnp.float32),
        lax.psum_scatter(
            grad_w_down.astype(jnp.bfloat16), "fsdp", scatter_dimension=0, tiled=True
        ).astype(jnp.float32),
    )
    totals = (
        lax.psum(shares[0].astype(jnp.bfloat16), "ctx").astype(jnp.float32),
        lax.psum(shares[1].astype(jnp.bfloat16), "ctx").astype(jnp.float32),
        lax.psum(shares[2].astype(jnp.bfloat16), "ctx").astype(jnp.float32),
        lax.psum(shares[3].astype(jnp.bfloat16), "ctx").astype(jnp.float32),
        lax.psum(shares[4].astype(jnp.bfloat16), "ctx").astype(jnp.float32),
        lax.psum(shares[5].astype(jnp.bfloat16), "ctx").astype(jnp.float32),
        lax.psum(shares[6].astype(jnp.bfloat16), "ctx").astype(jnp.float32),
        lax.psum(shares[7].astype(jnp.bfloat16), "ctx").astype(jnp.float32),
        lax.psum(shares[8].astype(jnp.bfloat16), "ctx").astype(jnp.float32),
        lax.psum(shares[9].astype(jnp.bfloat16), "ctx").astype(jnp.float32),
        lax.psum(shares[10].astype(jnp.bfloat16), "ctx").astype(jnp.float32),
        lax.psum(shares[11].astype(jnp.bfloat16), "ctx").astype(jnp.float32),
        lax.psum(shares[12].astype(jnp.bfloat16), "ctx").astype(jnp.float32),
        lax.psum(shares[13].astype(jnp.bfloat16), "ctx").astype(jnp.float32),
        lax.psum(shares[14].astype(jnp.bfloat16), "ctx").astype(jnp.float32),
        lax.psum(shares[15].astype(jnp.bfloat16), "ctx").astype(jnp.float32),
        lax.psum(shares[16].astype(jnp.bfloat16), "ctx").astype(jnp.float32),
    )
    return (result.astype(jnp.bfloat16)[None], grad_tokens[None]) + tuple(totals)


def solution(mesh):
    in_specs = (
        P("fsdp", "ctx", None),
        P("fsdp", "ctx", None),
        P("fsdp", None),
        P("fsdp"),
        P("fsdp", None),
        P("fsdp", None),
        P("fsdp", None),
        P(None, "fsdp"),
        P("fsdp"),
        P("fsdp"),
        P("fsdp"),
        P("fsdp"),
        P("fsdp", None),
        P("fsdp", None),
        P("fsdp", None),
        P("fsdp", None),
        P("fsdp"),
        P("fsdp", None),
        P("fsdp", None),
        P("fsdp", None),
    )
    out_specs = (
        P("fsdp", "ctx", None),
        P("fsdp", "ctx", None),
        P("fsdp"),
        P("fsdp", None),
        P("fsdp", None),
        P("fsdp", None),
        P(None, "fsdp"),
        P("fsdp"),
        P("fsdp"),
        P("fsdp"),
        P("fsdp"),
        P("fsdp", None),
        P("fsdp", None),
        P("fsdp", None),
        P("fsdp", None),
        P("fsdp"),
        P("fsdp", None),
        P("fsdp", None),
        P("fsdp", None),
    )
    return jax.shard_map(local, mesh=mesh, in_specs=in_specs, out_specs=out_specs, check_vma=False)
```

profile of v0, /device:TPU:0, one launch (start us, length us, event | category | flops | bytes accessed | tf_op | source)
XLA Modules:
  0.0 1530.2 jit_solution(331543800463051916)
XLA Ops:
  11.6 6.0 all-gather.2
  17.5 10.4 all_gather.84
  44.4 7.9 all-reduce.27
  92.6 158.8 %while.141 = (s32[]{:T(128)}, f32[24,64,128]{2,1,0:T(8,128)}, s32[]{:T(128)}, f32[2,256,24,64]{1,0,3,2:T(2,128)}, pred[2,256,256,24]{2,3,1,0:T(8,128)(4,1)}, /*i...) while((s32[]{:T(128)}, f32[24,64,128]{2,1,0:T(8,128)}, ...), condition=%wide.region_12.13_spmd.clone, body=%wide.region_9.12_spmd.clone.sunk | while | flops 2532743168 | bytes 49907116 | solution.py:191
  105.0 8.4 multiply_dynamic-update-slice_fusion.2
  117.3 7.8 fusion.382
  128.0 32.4 %dynamic_update_slice.242 = f32[2,256,24,64]{1,0,3,2:T(2,128)} dynamic-update-slice(f32[2,256,24,64]{1,0,3,2:T(2,128)} %get-tuple-element.3107, f32[1,256,24,64]{1,0,3,2:T(1,128)} %copy.424, s32[]{:T(128)} %get-tuple-element.3104, s32[]{:T(128)} %constant.364.clone.1..sunk.2, s32[]{:T(128)} %constant.364.clone.1..sunk.2, s32[]{:T(128)} %constant.364.clone.1..sunk.2) | dynamic-update-slice | bytes 3145732 | tf_op jit(solution)/shard_map/jvp()/while/body/jit(dynamic_update_index_in_dim)/dynamic_update_slice | solution.py:191
  182.5 8.3 multiply_dynamic-update-slice_fusion.2
  195.9 7.8 fusion.382
  206.6 32.4 %dynamic_update_slice.242 = f32[2,256,24,64]{1,0,3,2:T(2,128)} dynamic-update-slice(f32[2,256,24,64]{1,0,3,2:T(2,128)} %get-tuple-element.3107, f32[1,256,24,64]{1,0,3,2:T(1,128)} %copy.424, s32[]{:T(128)} %get-tuple-element.3104, s32[]{:T(128)} %constant.364.clone.1..sunk.2, s32[]{:T(128)} %constant.364.clone.1..sunk.2, s32[]{:T(128)} %constant.364.clone.1..sunk.2) | dynamic-update-slice | bytes 3145732 | tf_op jit(solution)/shard_map/jvp()/while/body/jit(dynamic_update_index_in_dim)/dynamic_update_slice | solution.py:191
  261.3 20.1 %all-gather.4 = bf16[8,1,24]{2,1,0:T(2,128)(2,1)S(1)} all-gather(bf16[1,1,24]{2,1,0:T(2,128)(2,1)S(1)} %bitcast.923), channel_id=1, replica_groups=mesh['ctx'=8,'fsdp'=4] {'ctx'}, dimensions={0}, use_global_device_ids=true | all-gather | bytes 432 | tf_op jit(solution)/shard_map/all_gather | solution.py:35
  293.5 53.2 %while.137 = (s32[]{:T(128)}, f32[2,4,512]{2,1,0:T(4,128)S(1)}, f32[2,4,512]{2,1,0:T(4,128)S(1)}, f32[2,4,512,64]{2,3,1,0:T(8,128)}, s32[8]{0:T(128)S(1)}, /*ind...) while((s32[]{:T(128)}, f32[2,4,512]{2,1,0:T(4,128)S(1)}, ...), condition=%wide.region_8.9_spmd, body=%wide.region_2.8_spmd.sunk | while | flops 565463552 | bytes 38826392 | solution.py:229
  299.1 8.0 conditional.4
  348.8 5.8 reshape.722
  354.8 7.0 multiply_add_fusion.3
  365.9 7.2 multiply_convert_fusion.4
  378.5 12.7 all-gather.22.cloned.1.call-done
  395.8 31.6 %all-gather.30.cloned.1.call-done = bf16[1024,2048]{1,0:T(8,128)(2,1)} async-done(((bf16[256,2048]{1,0:T(8,128)(2,1)}), bf16[1024,2048]{1,0:T(8,128)(2,1)}) %all-gather.30.cloned.1.call-update) | async-done | bytes 4194320 | tf_op jit(solution)/shard_map/all_gather | solution.py:374
  427.3 6.8 fusion.251
  434.1 29.3 %all-gather.32.cloned.1.call-done = bf16[1024,2048]{1,0:T(8,128)(2,1)} async-done(((bf16[256,2048]{1,0:T(8,128)(2,1)}), bf16[1024,2048]{1,0:T(8,128)(2,1)}) %all-gather.32.cloned.1.call-update) | async-done | bytes 4194320 | tf_op jit(solution)/shard_map/all_gather | solution.py:375
  463.4 6.8 fusion.252
  470.2 29.1 %all-gather.34.cloned.1.call-done = bf16[2048,1024]{1,0:T(8,128)(2,1)} async-done(((bf16[512,1024]{1,0:T(8,128)(2,1)}), bf16[2048,1024]{1,0:T(8,128)(2,1)}) %all-gather.34.cloned.1.call-update) | async-done | bytes 4194320 | tf_op jit(solution)/shard_map/all_gather | solution.py:376
  499.3 10.2 multiply_convert_fusion
  522.7 69.4 %while.140 = (s32[]{:T(128)}, f32[2,4,512,64]{2,3,1,0:T(8,128)S(1)}, f32[4096,256]{0,1:T(8,128)}, s32[8]{0:T(128)S(1)}, s32[512]{0:T(512)S(1)}, /*index=5*/s32[1...) while((s32[]{:T(128)}, f32[2,4,512,64]{2,3,1,0:T(8,128)S(1)}, ...), condition=%wide.region_40.41_spmd, body=%wide.region_36.40_spmd.sunk | while | flops 1368992256 | bytes 64172464 | solution.py:229
  528.3 24.2 %conditional.5 = ((f32[2,4,512,64]{2,3,1,0:T(8,128)S(1)}, f32[4096,256]{0,1:T(8,128)})) conditional(s32[]{:T(128)} %convert_element_type.675, (f32[2,4,512,64]{2,3,1,0:T(8,128)S(1)}, f32[4096,256]{0,1:T(8,128)}) %tuple.294, (s32[512]{0:T(512)S(1)}, s32[512]{0:T(512)S(1)}, s32[512]{0:T(512)S(1)}, s32[]{:T(128)}, s32[1,512]{1,0:T(1,128)S(1)}, ...), branch_computations={%region_38.38_spmd, %region_39.39_spmd} | conditional | flops 1368982528 | bytes 64159844 | solution.py:221
  596.1 9.0 multiply_reduce_fusion.6
  619.2 214.1 %reduce-scatter.15.cloned.1.call-done = bf16[512,256]{0,1:T(8,128)(2,1)} async-done(((bf16[4096,256]{0,1:T(8,128)(2,1)}), bf16[512,256]{0,1:T(8,128)(2,1)}) %reduce-scatter.15.cloned.1.call-update) | async-done | bytes 262160 | tf_op jit(solution)/shard_map/reduce_scatter | solution.py:571
  868.2 6.3 convolution_convert_fusion
  874.6 20.2 %all-gather.38.cloned.1.call-done = bf16[192,64,128]{2,1,0:T(8,128)(2,1)} async-done(((bf16[24,64,128]{2,1,0:T(8,128)(2,1)}), bf16[192,64,128]{2,1,0:T(8,128)(2,1)}) %all-gather.38.cloned.1.call-update) | async-done | bytes 3145744 | tf_op jit(solution)/shard_map/all_gather | solution.py:55
  894.8 23.6 %while.142 = (s32[]{:T(128)}, f32[24,64,128]{2,1,0:T(8,128)}, s32[]{:T(128)}, bf16[8,24,64,128]{3,2,1,0:T(8,128)(2,1)}, bf16[8,24]{1,0:T(8,128)(2,1)}, /*index=5*/s32[]{:T(128)}, s32[]{:T(128)}, s32[]{:T(128)}, s32[]{:T(128)}) while((s32[]{:T(128)}, f32[24,64,128]{2,1,0:T(8,128)}, s32[]{:T(128)}, ...), condition=%wide.region_20.21_spmd.clone, body=%wide.region_19.20_spmd.clone.sunk | while | flops 983072 | bytes 1966487 | solution.py:73
  925.3 147.9 %while.139 = (s32[]{:T(128)}, f32[24,64,128]{2,1,0:T(8,128)}, f32[2,256,24,64]{1,3,2,0:T(8,128)}, f32[2,256,128]{2,1,0:T(8,128)}, f32[2,256,128]{2,1,0:T(8,128)}...) while((s32[]{:T(128)}, f32[24,64,128]{2,1,0:T(8,128)}, ...), condition=%wide.region_31.32_spmd, body=%wide.region_21.31_spmd.sunk | while | flops 5053673472 | bytes 163600080 | solution.py:191
  925.5 10.4 constant_dynamic-slice_fusion.16
  938.5 17.5 %fusion.370 = (f32[256,24]{0,1:T(8,128)S(1)}, f32[256,24]{0,1:T(8,128)S(1)}, f32[256,256]{1,0:T(8,128)}, f32[256,24]{0,1:T(8,128)S(1)}) fusion(f32[1,256,256,24]{2,3,1,0:T(8,128)} %get-tuple-element.2980, f32[256,24]{0,1:T(8,128)S(1)} %dynamic-slice_bitcast_fusion.14, f32[256,256]{1,0:T(8,128)S(1)} %dynamic-slice_bitcast_fusion.15, ...), kind=kOutput, calls=%fused_computation.228.clone.1 | convolution fusion | flops 1223604224 | bytes 17925120 | tf_op jit(solution)/shard_map/transpose(jvp())/while/body/eval_jaxpr/tsh,shp->thp/dot_general | solution.py:132
  988.5 5.7 bitcast_dynamic-update-slice_fusion.20
  999.3 10.4 constant_dynamic-slice_fusion.16
  1012.3 17.4 %fusion.370 = (f32[256,24]{0,1:T(8,128)S(1)}, f32[256,24]{0,1:T(8,128)S(1)}, f32[256,256]{1,0:T(8,128)}, f32[256,24]{0,1:T(8,128)S(1)}) fusion(f32[1,256,256,24]{2,3,1,0:T(8,128)} %get-tuple-element.2980, f32[256,24]{0,1:T(8,128)S(1)} %dynamic-slice_bitcast_fusion.14, f32[256,256]{1,0:T(8,128)S(1)} %dynamic-slice_bitcast_fusion.15, ...), kind=kOutput, calls=%fused_computation.228.clone.1 | convolution fusion | flops 1223604224 | bytes 17925120 | tf_op jit(solution)/shard_map/transpose(jvp())/while/body/eval_jaxpr/tsh,shp->thp/dot_general | solution.py:132
  1062.0 5.7 bitcast_dynamic-update-slice_fusion.20
  1073.2 6.0 copy.274
  1079.2 6.3 reshape.814
  1085.5 7.1 fusion.183
  1109.8 5.6 convolution_convert_fusion.4
  1128.5 19.6 %reduce-scatter.31.cloned.1.call-done = bf16[256,2048]{1,0:T(8,128)(2,1)} async-done(((bf16[1024,2048]{1,0:T(8,128)(2,1)}), bf16[256,2048]{1,0:T(8,128)(2,1)}) %reduce-scatter.31.cloned.1.call-update) | async-done | bytes 1048592 | tf_op jit(solution)/shard_map/reduce_scatter | solution.py:674
  1148.1 47.1 %reduce-scatter.35.cloned.1.call-done = bf16[512,1024]{1,0:T(8,128)(2,1)} async-done(((bf16[2048,1024]{1,0:T(8,128)(2,1)}), bf16[512,1024]{1,0:T(8,128)(2,1)}) %reduce-scatter.35.cloned.1.call-update) | async-done | bytes 1048592 | tf_op jit(solution)/shard_map/reduce_scatter | solution.py:680
  1195.2 43.8 %reduce-scatter.19.cloned.1.call-done = bf16[256,1792]{1,0:T(8,128)(2,1)} async-done(((bf16[1024,1792]{1,0:T(8,128)(2,1)}), bf16[256,1792]{1,0:T(8,128)(2,1)}) %reduce-scatter.19.cloned.1.call-update) | async-done | bytes 917520 | tf_op jit(solution)/shard_map/reduce_scatter | solution.py:638
  1255.8 6.7 all-reduce.26
  1268.0 18.4 %reduce-scatter.21.cloned.1.call-done = bf16[256,24]{0,1:T(8,128)(2,1)} async-done(((bf16[1024,24]{0,1:T(8,128)(2,1)}), bf16[256,24]{0,1:T(8,128)(2,1)}) %reduce-scatter.21.cloned.1.call-update) | async-done | bytes 12304 | tf_op jit(solution)/shard_map/reduce_scatter | solution.py:641
  1286.4 38.8 %all-reduce.24 = (bf16[256]{0:T(256)(128)(2,1)S(1)}, bf16[256,24]{0,1:T(8,128)(2,1)S(1)}, bf16[4,448]{1,0:T(4,128)(2,1)S(1)}, bf16[448]{0:T(512)(128)(2,1)S(1)},...) all-reduce(bf16[256]{0:T(256)(128)(2,1)S(1)} %dynamic-slice.13, ...), channel_id=1, replica_groups=mesh['ctx'=8,'fsdp'=4] {'ctx'}, use_global_device_ids=true, to_apply=%region_45.46 | all-reduce | flops 8914 | bytes 35656 | tf_op jit(solution)/shard_map/psum | solution.py:685
  1329.6 181.1 %all-reduce.30.cloned.1.call-done = (bf16[256,1536]{1,0:T(8,128)(2,1)}, bf16[256,1792]{1,0:T(8,128)(2,1)}, bf16[384,1024]{1,0:T(8,128)(2,1)}, bf16[256,512]{1,0:...) async-done(((bf16[256,1536]{1,0:T(8,128)(2,1)}, ...) | async-done | bytes 6291472 | tf_op jit(solution)/shard_map/psum | solution.py:686
  (965 shorter events, 475.6 us)
Async XLA Ops:
  7.2 52.5 %all-gather.24.cloned.1.call-start = ((), (), s32[]{:S(2)}) async-start(), calls=%async_computation.15 | async-start | bytes 4587520 | tf_op jit(solution)/shard_map/all_gather | solution.py:362
  7.9 278.7 %all-gather.20.cloned.1.call-start = ((), (), s32[]{:S(2)}) async-start(), calls=%async_computation.13 | async-start | bytes 1310720 | tf_op jit(solution)/shard_map/all_gather | solution.py:370
  8.7 281.9 %all-gather.18.cloned.1.call-start = ((), (), s32[]{:S(2)}) async-start(), calls=%async_computation.12 | async-start | bytes 2359296 | tf_op jit(solution)/shard_map/all_gather | solution.py:483
  10.2 27.5 %copy-start.131 = (bf16[4,448]{1,0:T(4,128)(2,1)S(1)}, bf16[4,448]{1,0:T(4,128)(2,1)}, u32[]{:S(2)}) copy-start(bf16[4,448]{1,0:T(4,128)(2,1)} %param.45) | copy-start | bytes 10756
  10.3 33.0 %copy-start.145 = (bf16[6]{0:T(256)(128)(2,1)S(1)}, bf16[6]{0:T(256)(128)(2,1)}, u32[]{:S(2)}) copy-start(bf16[6]{0:T(256)(128)(2,1)} %param.47) | copy-start | bytes 40
  10.3 33.2 %copy-start.146 = (bf16[6]{0:T(256)(128)(2,1)S(1)}, bf16[6]{0:T(256)(128)(2,1)}, u32[]{:S(2)}) copy-start(bf16[6]{0:T(256)(128)(2,1)} %param.48) | copy-start | bytes 40
  10.3 33.5 %copy-start.147 = (bf16[6]{0:T(256)(128)(2,1)S(1)}, bf16[6]{0:T(256)(128)(2,1)}, u32[]{:S(2)}) copy-start(bf16[6]{0:T(256)(128)(2,1)} %param.49) | copy-start | bytes 40
  10.3 33.7 %copy-start.138 = (bf16[448]{0:T(512)(128)(2,1)S(1)}, bf16[448]{0:T(512)(128)(2,1)}, u32[]{:S(2)}) copy-start(bf16[448]{0:T(512)(128)(2,1)} %param.46) | copy-start | bytes 2692
  10.3 42.5 %copy-start.128 = (bf16[256,24]{0,1:T(8,128)(2,1)S(1)}, bf16[256,24]{0,1:T(8,128)(2,1)}, u32[]{:S(2)}) copy-start(bf16[256,24]{0,1:T(8,128)(2,1)} %param.44) | copy-start | bytes 36868
  10.3 48.3 %copy-start.24 = (bf16[1,512,1024]{2,1,0:T(8,128)(2,1)S(1)}, bf16[1,512,1024]{2,1,0:T(8,128)(2,1)}, u32[]{:S(2)}) copy-start(bf16[1,512,1024]{2,1,0:T(8,128)(2,1)} %param.38) | copy-start | bytes 3145732
  10.9 48.8 %copy-start.120 = (f32[512]{0:T(512)}, f32[512]{0:T(512)S(1)}, u32[]{:S(2)}) copy-start(f32[512]{0:T(512)S(1)} %get-tuple-element.2403) | copy-start | bytes 6148
  17.5 42.1 %copy-start.108 = (f32[4,1,256]{2,1,0:T(1,128)}, f32[4,1,256]{2,1,0:T(1,128)S(1)}, u32[]{:S(2)}) copy-start(f32[4,1,256]{2,1,0:T(1,128)S(1)} %convert_element_type.506) | copy-start | bytes 12292
  33.7 320.9 %all-gather.36.cloned.1.call-start = ((), (), s32[]{:S(2)}) async-start(), calls=%async_computation.32 | async-start | bytes 3538944 | tf_op jit(solution)/shard_map/all_gather | solution.py:35
  37.7 32.8 %copy-start.114 = (f32[512]{0:T(512)}, f32[512]{0:T(512)S(1)}, u32[]{:S(2)}) copy-start(f32[512]{0:T(512)S(1)} %get-tuple-element.2394) | copy-start | bytes 6148
  37.7 32.8 %copy-start.116 = (f32[512]{0:T(512)}, f32[512]{0:T(512)S(1)}, u32[]{:S(2)}) copy-start(f32[512]{0:T(512)S(1)} %get-tuple-element.2395) | copy-start | bytes 6148
  37.7 32.8 %copy-start.118 = (f32[512]{0:T(512)}, f32[512]{0:T(512)S(1)}, u32[]{:S(2)}) copy-start(f32[512]{0:T(512)S(1)} %get-tuple-element.2396) | copy-start | bytes 6148
  63.9 6.3 collective-permute-start
  128.0 33.7 %copy-start.107 = (f32[24]{0:T(128)S(1)}, f32[24]{0:T(128)}, u32[]{:S(2)}) copy-start(f32[24]{0:T(128)} %copy-done.106) | copy-start | bytes 292 | tf_op jit(solution)/shard_map/jvp()/while
  206.6 33.7 %copy-start.107 = (f32[24]{0:T(128)S(1)}, f32[24]{0:T(128)}, u32[]{:S(2)}) copy-start(f32[24]{0:T(128)} %copy-done.106) | copy-start | bytes 292 | tf_op jit(solution)/shard_map/jvp()/while
  254.1 27.4 %copy-start.148 = (bf16[256]{0:T(256)(128)(2,1)S(1)}, bf16[256]{0:T(256)(128)(2,1)}, u32[]{:S(2)}) copy-start(bf16[256]{0:T(256)(128)(2,1)} %param.54) | copy-start | bytes 1540
  254.1 111.7 %all-gather.26.cloned.1.call-start = ((), (), s32[]{:S(2)}) async-start(), calls=%async_computation.16 | async-start | bytes 3932160 | tf_op jit(solution)/shard_map/all_gather | solution.py:361
  254.7 118.3 %all-gather.28.cloned.1.call-start = ((), (), s32[]{:S(2)}) async-start(), calls=%async_computation.17 | async-start | bytes 3932160 | tf_op jit(solution)/shard_map/all_gather | solution.py:369
  255.3 32.9 %copy-start.109 = (f32[4,1,256]{2,1,0:T(1,128)S(1)}, f32[4,1,256]{2,1,0:T(1,128)}, u32[]{:S(2)}) copy-start(f32[4,1,256]{2,1,0:T(1,128)} %copy-done.108) | copy-start | bytes 12292
  255.3 32.9 %copy-start.121 = (f32[512]{0:T(512)S(1)}, f32[512]{0:T(512)}, u32[]{:S(2)}) copy-start(f32[512]{0:T(512)} %copy-done.120) | copy-start | bytes 6148
  255.3 135.9 %all-gather.22.cloned.1.call-start = ((), (), s32[]{:S(2)}) async-start(), calls=%async_computation.14 | async-start | bytes 1310720 | tf_op jit(solution)/shard_map/all_gather | solution.py:372
  256.1 171.2 %all-gather.30.cloned.1.call-start = ((), (), s32[]{:S(2)}) async-start(), calls=%async_computation.18 | async-start | bytes 5242880 | tf_op jit(solution)/shard_map/all_gather | solution.py:374
  256.8 206.6 %all-gather.32.cloned.1.call-start = ((), (), s32[]{:S(2)}) async-start(), calls=%async_computation.19 | async-start | bytes 5242880 | tf_op jit(solution)/shard_map/all_gather | solution.py:375
  257.6 241.8 %all-gather.34.cloned.1.call-start = ((), (), s32[]{:S(2)}) async-start(), calls=%async_computation.20 | async-start | bytes 5242880 | tf_op jit(solution)/shard_map/all_gather | solution.py:376
  258.2 575.1 %reduce-scatter.15.cloned.1.call-start = ((), (), s32[]{:S(2)}) async-start(), calls=%async_computation.21 | async-start | bytes 2359296 | tf_op jit(solution)/shard_map/reduce_scatter | solution.py:571
  259.7 30.6 %copy-start.111 = (f32[24,4]{0,1:T(4,128)}, f32[24,4]{0,1:T(4,128)S(1)}, u32[]{:S(2)}) copy-start(f32[24,4]{0,1:T(4,128)S(1)} %slice.256) | copy-start | bytes 1156
  281.5 327.2 %copy-start.61 = (f32[512,24]{0,1:T(8,128)}, f32[512,24]{0,1:T(8,128)S(1)}, u32[]{:S(2)}) copy-start(f32[512,24]{0,1:T(8,128)S(1)} %exponential_multiply_fusion.2) | copy-start | bytes 147460
  348.8 42.4 %copy-start.41 = (bf16[2,4,512,64]{2,3,1,0:T(8,128)(2,1)}, bf16[2,4,512,64]{2,3,1,0:T(8,128)(2,1)S(1)}, u32[]{:S(2)}) copy-start(bf16[2,4,512,64]{2,3,1,0:T(8,128)(2,1)S(1)} %fusion.196) | copy-start | bytes 1572868
  394.3 122.2 %copy-start.21 = (f32[512,1024]{1,0:T(8,128)}, f32[512,1024]{1,0:T(8,128)S(1)}, u32[]{:S(2)}) copy-start(f32[512,1024]{1,0:T(8,128)S(1)} %get-tuple-element.2414) | copy-start | bytes 6291460
  596.1 298.7 %all-gather.38.cloned.1.call-start = ((), (), s32[]{:S(2)}) async-start(), calls=%async_computation.33 | async-start | bytes 3538944 | tf_op jit(solution)/shard_map/all_gather | solution.py:55
  614.0 514.3 %reduce-scatter.29.cloned.1.call-start = ((), (), s32[]{:S(2)}) async-start(), calls=%async_computation.28 | async-start | bytes 1310720 | tf_op jit(solution)/shard_map/reduce_scatter | solution.py:668
  616.9 511.5 %reduce-scatter.25.cloned.1.call-start = ((), (), s32[]{:S(2)}) async-start(), calls=%async_computation.26 | async-start | bytes 1310720 | tf_op jit(solution)/shard_map/reduce_scatter | solution.py:662
  617.2 217.2 %copy-start.42 = (bf16[512,8,64]{0,2,1:T(8,128)(2,1)}, bf16[512,8,64]{0,2,1:T(8,128)(2,1)S(1)}, u32[]{:S(2)}) copy-start(bf16[512,8,64]{0,2,1:T(8,128)(2,1)S(1)} %maximum_convert_fusion.1) | copy-start | bytes 1572868
  619.1 509.3 %reduce-scatter.27.cloned.1.call-start = ((), (), s32[]{:S(2)}) async-start(), calls=%async_computation.27 | async-start | bytes 655360 | tf_op jit(solution)/shard_map/reduce_scatter | solution.py:665
  835.8 292.6 %reduce-scatter.23.cloned.1.call-start = ((), (), s32[]{:S(2)}) async-start(), calls=%async_computation.25 | async-start | bytes 3932160 | tf_op jit(solution)/shard_map/reduce_scatter | solution.py:659
  840.8 287.7 %reduce-scatter.17.cloned.1.call-start = ((), (), s32[]{:S(2)}) async-start(), calls=%async_computation.22 | async-start | bytes 3932160 | tf_op jit(solution)/shard_map/reduce_scatter | solution.py:635
  846.0 282.4 %reduce-scatter.33.cloned.1.call-start = ((), (), s32[]{:S(2)}) async-start(), calls=%async_computation.30 | async-start | bytes 5242880 | tf_op jit(solution)/shard_map/reduce_scatter | solution.py:677
  852.3 295.8 %reduce-scatter.31.cloned.1.call-start = ((), (), s32[]{:S(2)}) async-start(), calls=%async_computation.29 | async-start | bytes 5242880 | tf_op jit(solution)/shard_map/reduce_scatter | solution.py:674
  858.4 336.8 %reduce-scatter.35.cloned.1.call-start = ((), (), s32[]{:S(2)}) async-start(), calls=%async_computation.31 | async-start | bytes 5242880 | tf_op jit(solution)/shard_map/reduce_scatter | solution.py:680
  874.5 364.5 %reduce-scatter.19.cloned.1.call-start = ((), (), s32[]{:S(2)}) async-start(), calls=%async_computation.23 | async-start | bytes 4587520 | tf_op jit(solution)/shard_map/reduce_scatter | solution.py:638
  1102.4 5.8 collective-permute-start.1
  1115.5 151.5 %reduce-scatter.37.cloned.1.call-start = ((), (), s32[]{:S(2)}) async-start(), calls=%async_computation.34 | async-start | bytes 573440
  1126.9 159.5 %reduce-scatter.21.cloned.1.call-start = ((), (), s32[]{:S(2)}) async-start(), calls=%async_computation.24 | async-start | bytes 61440 | tf_op jit(solution)/shard_map/reduce_scatter | solution.py:641
  1128.3 382.4 %all-reduce.30.cloned.1.call-start = ((), (), s32[]{:S(2)}) async-start(), calls=%async_computation.35 | async-start | bytes 12582912 | tf_op jit(solution)/shard_map/psum | solution.py:686
  (177 other events, 965.0 us)
Sparse Core Ops, SparseCore 0:
  9.6 36.2 all-gather.23
  47.5 17.5 all-gather.19
  67.7 51.0 all-gather.17
  254.3 60.0 all-gather.35
  315.7 27.1 all-gather.25
  344.4 28.5 all-gather.27
  374.5 16.7 all-gather.21
  392.8 34.4 all-gather.29
  428.9 34.4 all-gather.31
  464.8 34.4 all-gather.33
  596.2 236.9 reduce-scatter.14
  835.3 59.4 all-gather.37
  897.3 23.4 reduce-scatter.28
  923.9 24.8 reduce-scatter.24
  951.2 21.6 reduce-scatter.26
  975.4 38.0 reduce-scatter.22
  1015.9 37.9 reduce-scatter.16
  1056.4 44.5 reduce-scatter.32
  1103.5 44.5 reduce-scatter.30
  1150.6 44.4 reduce-scatter.34
  1197.7 41.2 reduce-scatter.18
  1242.2 21.5 reduce-scatter.36
  1266.9 19.4 reduce-scatter.20
  1292.1 218.5 all-reduce.29
where the time goes:
time: 1550 us; the launch traced here: 1530 us
  waiting for transfers between devices  654 us (42%)
  local copies, waits for them, and re-layouts  273 us (18%)
  matrix products  264 us (17%)
  other arithmetic  158 us (10%)
  blocking collectives  106 us (7%)
  loops' own time  48.5 us (3%)
  between operations  21.5 us (1%)
    reduce_scatter x1, waiting for transfers between devices, local(): lax.psum_scatter(grad_kv_all.astype(jnp.bfloat16), 'ctx', scatter_dimensi...  214 us
    psum x1, waiting for transfers between devices, local(): lax.psum(shares[1].astype(jnp.bfloat16), 'ctx').astype(jnp.float32)  181 us
    dynamic_update_slice x24, local copies, waits for them, and re-layouts, mamba_local(): lax.scan(span_step, (initial_state, seg_before), piece_list)  86.1 us
    dot_general x6, matrix products, span_step(): jnp.einsum('tsh,shp->thp', mixing, input_weights_x, precision=HIGHEST)  62 us
    reduce_scatter x1, waiting for transfers between devices, local(): lax.psum_scatter(grad_w_down.astype(jnp.bfloat16), 'fsdp', scatter_dimens...  47.1 us
    reduce_scatter x1, waiting for transfers between devices, local(): lax.psum_scatter(grad_w_xbc.astype(jnp.bfloat16), 'fsdp', scatter_dimensi...  43.8 us
    another operation x2, loops' own time, fold_blocks(): running, _ = lax.scan(one_step, running, (piece_list, offsets))  42.2 us
    psum x1, blocking collectives, local(): lax.psum(shares[0].astype(jnp.bfloat16), 'ctx').astype(jnp.float32)  38.8 us
  transfers between devices with their start and end apart: 26, of which 12 were waited for; matrix products, arithmetic and copies ran while one was open for 38% of the time, Pallas kernels for 0%

commit v1 on v0

v1 whole, which is shorter than its diff:
```python
import functools
import math

import jax
import jax.numpy as jnp
from jax import lax
from jax.experimental import pallas as pl
from jax.experimental.pallas import tpu as pltpu
from jax.sharding import PartitionSpec as P

MAMBA_HEADS = 24
MAMBA_HEAD_SIZE = 64
STATE_SIZE = 128
CONV = 4
QUERY_HEADS = 8
KEY_VALUE_HEADS = 2
HEAD_SIZE = 64
MAMBA_INNER = MAMBA_HEADS * MAMBA_HEAD_SIZE
CHANNELS = MAMBA_INNER + 2 * STATE_SIZE
LANES = 128
PAIRS = MAMBA_INNER // LANES
CHUNK = 128
KEY_BLOCK = 512
QUERY_TILE = 128
GROUP = QUERY_HEADS // KEY_VALUE_HEADS
MESSAGE_ROWS = STATE_SIZE + 16
VMEM_LIMIT = 56 * 1024 * 1024

EPSILON = 1e-06
ROPE_BASE = 10000.0
MASK_FILLER = -1e30
HIGHEST = lax.Precision.HIGHEST
F32 = jnp.float32
BF16 = jnp.bfloat16


def dot_nn(a, b, precision=None):
    return lax.dot_general(
        a, b, (((1,), (0,)), ((), ())), precision=precision, preferred_element_type=F32
    )


def dot_nt(a, b):
    return lax.dot_general(a, b, (((1,), (1,)), ((), ())), preferred_element_type=F32)


def dot_tn(a, b):
    return lax.dot_general(a, b, (((0,), (0,)), ((), ())), preferred_element_type=F32)


def iota(shape, dim):
    return lax.broadcasted_iota(jnp.int32, shape, dim)


def params(*semantics):
    return pltpu.CompilerParams(dimension_semantics=semantics, vmem_limit_bytes=VMEM_LIMIT)


def whole(shape):
    return pl.BlockSpec(shape, lambda *_: (0,) * len(shape))


def low_half(rows):
    return iota((rows, LANES), 1) < MAMBA_HEAD_SIZE


def spread(values, pair, low):
    a = values[:, 2 * pair : 2 * pair + 1]
    b = values[:, 2 * pair + 1 : 2 * pair + 2]
    return jnp.where(low, a, b)


def tile(i):
    return slice(i * LANES, (i + 1) * LANES)


def split_pair(x, low):
    zero = jnp.zeros_like(x)
    return jnp.concatenate([jnp.where(low, x, zero), jnp.where(low, zero, x)], axis=0)


def fill_padded(xs_ref, edge_ref, mixed_ref):
    xs_ref[0:8, :] = edge_ref[...]
    xs_ref[8:, :] = mixed_ref[...].astype(F32)


def lag_masks(positions, doc):
    return [None] + [(positions - lag >= doc).astype(F32) for lag in range(1, CONV)]


def conv_tile(xs_ref, start, i, cw_ref, masks):
    window = xs_ref[pl.ds(start, CHUNK + 8), tile(i)]
    summed = cw_ref[4:5, tile(i)] + cw_ref[3:4, tile(i)] * window[8 : 8 + CHUNK]
    for lag in range(1, CONV):
        shifted = window[8 - lag : 8 - lag + CHUNK]
        summed = summed + cw_ref[3 - lag : 4 - lag, tile(i)] * (shifted * masks[lag])
    return summed


def softplus(v):
    return jnp.maximum(v, 0.0) + jnp.log1p(jnp.exp(-jnp.abs(v)))


def decay_sums(dt_ref, hp_ref):
    raw = dt_ref[...] + hp_ref[0:1, :]
    step = softplus(raw)
    log_decay = step * hp_ref[1:2, :]
    order = iota((CHUNK, CHUNK), 0) >= iota((CHUNK, CHUNK), 1)
    cumul = dot_nn(order.astype(F32), log_decay, HIGHEST)
    return raw, step, log_decay, cumul


def mamba_forward_kernel(
    sc_ref,
    edge_ref,
    mixed_ref,
    dt_ref,
    doc_ref,
    cw_ref,
    hp_ref,
    skip_ref,
    y_ref,
    sin_ref,
    msg_ref,
    dec_ref,
    c_ref,
    xs_ref,
    xa_ref,
    state_ref,
    carry_ref,
):
    c = pl.program_id(0)
    count = pl.num_programs(0)

    @pl.when(c == 0)
    def _():
        fill_padded(xs_ref, edge_ref, mixed_ref)
        state_ref[...] = jnp.zeros_like(state_ref)
        carry_ref[...] = jnp.zeros_like(carry_ref)

    base = sc_ref[count]
    start = pl.multiple_of(c * CHUNK, CHUNK)
    first = base + start
    end_doc = sc_ref[c]
    doc = doc_ref[...]
    positions = first + iota((CHUNK, 1), 0)
    masks = lag_masks(positions, doc)
    for i in range(CHANNELS // LANES):
        summed = conv_tile(xs_ref, start, i, cw_ref, masks)
        xa_ref[:, tile(i)] = summed * jax.nn.sigmoid(summed)
    _, step, log_decay, cumul = decay_sums(dt_ref, hp_ref)
    cumul_t = cumul.T
    b_mat = xa_ref[:, tile(PAIRS)]
    c_mat = xa_ref[:, tile(PAIRS + 1)].astype(BF16)
    c_ref[...] = c_mat
    couple = dot_nt(c_mat, b_mat.astype(BF16))
    b_turned = b_mat.T.astype(BF16)
    col = first + iota((CHUNK, CHUNK), 1)
    row = first + iota((CHUNK, CHUNK), 0)
    couple = jnp.where((col <= row) & (col >= doc), couple, 0.0)
    carried = (doc < first).astype(F32)
    into = jnp.exp(cumul) * carried
    last = cumul[CHUNK - 1 : CHUNK, :]
    ending = jnp.exp(last - cumul) * (positions >= end_doc).astype(F32)
    keep = jnp.exp(last) * (end_doc < first).astype(F32)
    dec_ref[...] = jnp.where(doc < base, jnp.exp(cumul + carry_ref[0:1, :]), 0.0)
    low = low_half(CHUNK)
    low_row = low_half(1)
    for j in range(PAIRS):
        x = xa_ref[:, tile(j)]
        weighted = x * spread(step, j, low)
        mixing = []
        for h in (2 * j, 2 * j + 1):
            gap = jnp.minimum(cumul[:, h : h + 1] - cumul_t[h : h + 1, :], 0.0)
            mixing.append((couple * jnp.exp(gap)).astype(BF16))
        y = dot_nn(jnp.concatenate(mixing, axis=1), split_pair(weighted.astype(BF16), low))
        state = state_ref[:, tile(j)]
        sin_ref[0, :, tile(j)] = state
        y = y + dot_nn(c_mat, state.astype(BF16)) * spread(into, j, low)
        y_ref[:, tile(j)] = y + skip_ref[0:1, tile(j)] * x
        fresh = dot_nn(b_turned, (weighted * spread(ending, j, low)).astype(BF16))
        state_ref[:, tile(j)] = fresh + state * spread(keep, j, low_row)
    carry_ref[...] = carry_ref[...] + last

    @pl.when(c == count - 1)
    def _():
        msg_ref[0:STATE_SIZE, :] = state_ref[...].astype(BF16)
        through = jnp.exp(carry_ref[...]) * (end_doc < base).astype(F32)
        low8 = low_half(8)
        for j in range(PAIRS):
            wide = spread(through, j, low8)
            msg_ref[STATE_SIZE:, tile(j)] = jnp.concatenate([wide, wide], axis=0).astype(BF16)


def mamba_forward(scalars, edge, mixed, dt_raw, doc, conv_pack, head_pack, skip_wide):
    rows = mixed.shape[0]
    count = rows // CHUNK
    by_chunk = lambda width: pl.BlockSpec((CHUNK, width), lambda c: (c, 0))
    return pl.pallas_call(
        mamba_forward_kernel,
        grid=(count,),
        in_specs=[
            pl.BlockSpec(memory_space=pltpu.SMEM),
            whole((8, CHANNELS)),
            whole((rows, CHANNELS)),
            by_chunk(LANES),
            by_chunk(1),
            whole((8, CHANNELS)),
            whole((8, LANES)),
            whole((1, MAMBA_INNER)),
        ],
        out_specs=[
            by_chunk(MAMBA_INNER),
            pl.BlockSpec((1, STATE_SIZE, MAMBA_INNER), lambda c: (c, 0, 0)),
            whole((MESSAGE_ROWS, MAMBA_INNER)),
            by_chunk(LANES),
            by_chunk(LANES),
        ],
        out_shape=[
            jax.ShapeDtypeStruct((rows, MAMBA_INNER), F32),
            jax.ShapeDtypeStruct((count, STATE_SIZE, MAMBA_INNER), F32),
            jax.ShapeDtypeStruct((MESSAGE_ROWS, MAMBA_INNER), BF16),
            jax.ShapeDtypeStruct((rows, LANES), F32),
            jax.ShapeDtypeStruct((rows, LANES), BF16),
        ],
        scratch_shapes=[
            pltpu.VMEM((rows + 8, CHANNELS), F32),
            pltpu.VMEM((CHUNK, CHANNELS), F32),
            pltpu.VMEM((STATE_SIZE, MAMBA_INNER), F32),
            pltpu.VMEM((8, LANES), F32),
        ],
        compiler_params=params("arbitrary"),
        cost_estimate=pl.CostEstimate(
            flops=rows * MAMBA_INNER * 1024, bytes_accessed=rows * 12000, transcendentals=rows * 4096
        ),
        name="mamba_forward",
    )(scalars, edge, mixed, dt_raw, doc, conv_pack, head_pack, skip_wide)


def mamba_correct_kernel(
    y_ref, sin_ref, c_ref, dec_ref, state_ref, z_ref, total_ref, gated_ref, true_ref, edge_ref
):
    c = pl.program_id(0)

    @pl.when(c == 0)
    def _():
        edge_ref[...] = jnp.ones_like(edge_ref)

    low = low_half(CHUNK)
    low_row = low_half(1)
    decay = dec_ref[...]
    before = edge_ref[0:1, :]
    c_mat = c_ref[...]
    for j in range(PAIRS):
        state = state_ref[:, tile(j)]
        y = y_ref[:, tile(j)] + dot_nn(c_mat, state.astype(BF16)) * spread(decay, j, low)
        total_ref[:, tile(j)] = y
        z = z_ref[:, tile(j)]
        gated_ref[:, tile(j)] = (y * (z * jax.nn.sigmoid(z))).astype(BF16)
        true_ref[0, :, tile(j)] = (
            sin_ref[0, :, tile(j)] + state * spread(before, j, low_row)
        ).astype(BF16)
    edge_ref[0:1, :] = decay[CHUNK - 1 : CHUNK, :]


def mamba_correct(y, sin, c_mat, decay, state_in, gate_z):
    rows = y.shape[0]
    count = rows // CHUNK
    by_chunk = lambda width: pl.BlockSpec((CHUNK, width), lambda c: (c, 0))
    states = pl.BlockSpec((1, STATE_SIZE, MAMBA_INNER), lambda c: (c, 0, 0))
    return pl.pallas_call(
        mamba_correct_kernel,
        grid=(count,),
        in_specs=[
            by_chunk(MAMBA_INNER),
            states,
            by_chunk(LANES),
            by_chunk(LANES),
            whole((STATE_SIZE, MAMBA_INNER)),
            by_chunk(MAMBA_INNER),
        ],
        out_specs=[by_chunk(MAMBA_INNER), by_chunk(MAMBA_INNER), states],
        out_shape=[
            jax.ShapeDtypeStruct((rows, MAMBA_INNER), F32),
            jax.ShapeDtypeStruct((rows, MAMBA_INNER), BF16),
            jax.ShapeDtypeStruct((count, STATE_SIZE, MAMBA_INNER), BF16),
        ],
        scratch_shapes=[pltpu.VMEM((8, LANES), F32)],
        compiler_params=params("arbitrary"),
        cost_estimate=pl.CostEstimate(
            flops=rows * MAMBA_INNER * 256, bytes_accessed=rows * 30000, transcendentals=rows * 1536
        ),
        name="mamba_correct",
    )(y, sin, c_mat, decay, state_in, gate_z)


def mamba_gate_back_kernel(
    gg_ref, z_ref, y_ref, c_ref, dec_ref, dy_ref, gz_ref, gsi_ref, acc_ref
):
    c = pl.program_id(0)

    @pl.when(c == 0)
    def _():
        acc_ref[...] = jnp.zeros_like(acc_ref)

    low = low_half(CHUNK)
    decay = dec_ref[...]
    c_turned = c_ref[...].astype(F32).T.astype(BF16)
    for j in range(PAIRS):
        z = z_ref[:, tile(j)]
        sig = jax.nn.sigmoid(z)
        silu = z * sig
        grad = gg_ref[:, tile(j)]
        gz_ref[:, tile(j)] = (grad * y_ref[:, tile(j)] * (sig + silu * (1.0 - sig))).astype(BF16)
        dy = (grad * silu).astype(BF16)
        dy_ref[:, tile(j)] = dy
        scaled = (dy.astype(F32) * spread(decay, j, low)).astype(BF16)
        acc_ref[:, tile(j)] += dot_nn(c_turned, scaled)

    @pl.when(c == pl.num_programs(0) - 1)
    def _():
        gsi_ref[...] = acc_ref[...].astype(BF16)


def mamba_gate_back(gated_grad, gate_z, total, c_mat, decay):
    rows = total.shape[0]
    by_chunk = lambda width: pl.BlockSpec((CHUNK, width), lambda c: (c, 0))
    return pl.pallas_call(
        mamba_gate_back_kernel,
        grid=(rows // CHUNK,),
        in_specs=[
            by_chunk(MAMBA_INNER),
            by_chunk(MAMBA_INNER),
            by_chunk(MAMBA_INNER),
            by_chunk(LANES),
            by_chunk(LANES),
        ],
        out_specs=[by_chunk(MAMBA_INNER), by_chunk(MAMBA_INNER), whole((STATE_SIZE, MAMBA_INNER))],
        out_shape=[
            jax.ShapeDtypeStruct((rows, MAMBA_INNER), BF16),
            jax.ShapeDtypeStruct((rows, MAMBA_INNER), BF16),
            jax.ShapeDtypeStruct((STATE_SIZE, MAMBA_INNER), BF16),
        ],
        scratch_shapes=[pltpu.VMEM((STATE_SIZE, MAMBA_INNER), F32)],
        compiler_params=params("arbitrary"),
        cost_estimate=pl.CostEstimate(
            flops=rows * MAMBA_INNER * 256, bytes_accessed=rows * 25000, transcendentals=rows * 1536
        ),
        name="mamba_gate_back",
    )(gated_grad, gate_z, total, c_mat, decay)


def picks(pair):
    channel = iota((LANES, LANES), 0)
    head = iota((LANES, LANES), 1)
    return (head == 2 * pair + channel // MAMBA_HEAD_SIZE).astype(BF16)


def head_sums(product, select):
    high = product.astype(BF16)
    rest = (product - high.astype(F32)).astype(BF16)
    return dot_nn(high, select) + dot_nn(rest, select)


def mamba_back_kernel(
    sc_ref,
    edge_ref,
    mixed_ref,
    dt_ref,
    doc_ref,
    doc_row_ref,
    cw_ref,
    hp_ref,
    skip_ref,
    dy_ref,
    y_ref,
    sin_ref,
    ds_end_ref,
    gmix_ref,
    tail_ref,
    edge_grad_ref,
    gdt_ref,
    gconv_ref,
    ghead_ref,
    xs_ref,
    xa_ref,
    slope_ref,
    grad_ref,
    ds_ref,
    rows_ref,
):
    step_at = pl.program_id(0)
    count = pl.num_programs(0)
    c = count - 1 - step_at
    rows = count * CHUNK

    @pl.when(step_at == 0)
    def _():
        fill_padded(xs_ref, edge_ref, mixed_ref)
        ds_ref[...] = ds_end_ref[...]
        grad_ref[pl.ds(rows, 8), :] = jnp.zeros((8, CHANNELS), F32)
        gconv_ref[...] = jnp.zeros_like(gconv_ref)
        ghead_ref[...] = jnp.zeros_like(ghead_ref)
        rows_ref[...] = jnp.zeros_like(rows_ref)

    base = sc_ref[count]
    start = pl.multiple_of(c * CHUNK, CHUNK)
    first = base + start
    end_doc = sc_ref[c]
    doc_window = doc_ref[pl.ds(start, CHUNK + 8), :]
    doc = doc_window[0:CHUNK]
    positions_window = first + iota((CHUNK + 8, 1), 0)
    positions = positions_window[0:CHUNK]
    masks_window = lag_masks(positions_window, doc_window)
    masks = [None] + [m[0:CHUNK] for m in masks_window[1:]]
    for i in range(CHANNELS // LANES):
        summed = conv_tile(xs_ref, start, i, cw_ref, masks)
        sig = jax.nn.sigmoid(summed)
        act = summed * sig
        xa_ref[:, tile(i)] = act
        slope_ref[:, tile(i)] = sig + act * (1.0 - sig)
    raw, step, log_decay, cumul = decay_sums(dt_ref, hp_ref)
    cumul_t = cumul.T
    b_mat = xa_ref[:, tile(PAIRS)].astype(BF16)
    c_f32 = xa_ref[:, tile(PAIRS + 1)]
    c_mat = c_f32.astype(BF16)
    c_turned = c_f32.T.astype(BF16)
    key = first + iota((CHUNK, CHUNK), 0)
    query = first + iota((CHUNK, CHUNK), 1)
    visible = (key <= query) & (key >= doc_row_ref[0:1, :])
    couple = jnp.where(visible, dot_nt(b_mat, c_mat), 0.0)
    carried = (doc < first).astype(F32)
    into = jnp.exp(cumul) * carried
    last = cumul[CHUNK - 1 : CHUNK, :]
    ending = jnp.exp(last - cumul) * (positions >= end_doc).astype(F32)
    keep = jnp.exp(last) * (end_doc < first).astype(F32)
    low = low_half(CHUNK)
    low_row = low_half(1)
    grad_couple = jnp.zeros((CHUNK, CHUNK), F32)
    grad_b = jnp.zeros((CHUNK, STATE_SIZE), F32)
    grad_c = jnp.zeros((CHUNK, STATE_SIZE), F32)
    grad_cumul = jnp.zeros((CHUNK, LANES), F32)
    grad_step = jnp.zeros((CHUNK, LANES), F32)
    end_sums = jnp.zeros((8, LANES), F32)
    for j in range(PAIRS):
        select = picks(j)
        x = xa_ref[:, tile(j)]
        step_wide = spread(step, j, low)
        weighted = x * step_wide
        weighted_b = weighted.astype(BF16)
        dy = dy_ref[:, tile(j)]
        dy_f32 = dy.astype(F32)
        grad_mixing = dot_nt(split_pair(weighted_b, low), dy)
        mixing = []
        for side, h in enumerate((2 * j, 2 * j + 1)):
            gap = jnp.minimum(cumul_t[h : h + 1, :] - cumul[:, h : h + 1], 0.0)
            fade = jnp.exp(gap)
            mixing.append((couple * fade).astype(BF16))
            grad_couple += grad_mixing[side * CHUNK : (side + 1) * CHUNK] * fade
        grad_weighted = dot_nn(jnp.concatenate(mixing, axis=1), split_pair(dy, low))
        ending_wide = spread(ending, j, low)
        grad_state = ds_ref[:, tile(j)]
        grad_state_b = grad_state.astype(BF16)
        state = sin_ref[0, :, tile(j)]
        through_state = ending_wide * dot_nn(b_mat, grad_state_b)
        grad_weighted = grad_weighted + through_state
        dy_into = (dy_f32 * spread(into, j, low)).astype(BF16)
        grad_c += dot_nt(dy_into, state)
        grad_b += dot_nt((weighted * ending_wide).astype(BF16), grad_state_b)
        keep_wide = spread(keep, j, low_row)
        weighted_f32 = weighted_b.astype(F32)
        to_end = jnp.sum(weighted_f32 * through_state, axis=0, keepdims=True) + keep_wide * jnp.sum(
            grad_state * state.astype(F32), axis=0, keepdims=True
        )
        ds_ref[:, tile(j)] = keep_wide * grad_state + dot_nn(c_turned, dy_into)
        skip = skip_ref[0:1, tile(j)]
        grad_x = step_wide * grad_weighted + skip * dy_f32
        grad_ref[pl.ds(start, CHUNK), tile(j)] = grad_x * slope_ref[:, tile(j)]
        rows_ref[0:1, tile(j)] += jnp.sum(dy_f32 * x, axis=0, keepdims=True)
        in_out = dy_f32 * (y_ref[:, tile(j)] - skip * x) - weighted_f32 * grad_weighted
        grad_cumul += head_sums(in_out, select)
        grad_step += head_sums(grad_weighted * x, select)
        end_sums += head_sums(jnp.broadcast_to(to_end, (8, LANES)), select)
    grad_couple = jnp.where(visible, grad_couple, 0.0).astype(BF16)
    grad_b += dot_nn(grad_couple, c_mat)
    grad_c += dot_tn(grad_couple, b_mat)
    grad_ref[pl.ds(start, CHUNK), tile(PAIRS)] = grad_b * slope_ref[:, tile(PAIRS)]
    grad_ref[pl.ds(start, CHUNK), tile(PAIRS + 1)] = grad_c * slope_ref[:, tile(PAIRS + 1)]
    later = (iota((CHUNK, CHUNK), 0) <= iota((CHUNK, CHUNK), 1)).astype(F32)
    grad_log = dot_nn(later, grad_cumul, HIGHEST) + end_sums[0:1, :]
    grad_raw = (grad_step + grad_log * hp_ref[1:2, :]) * jax.nn.sigmoid(raw)
    gdt_ref[...] = grad_raw.astype(BF16)
    ghead_ref[0:1, :] += jnp.sum(grad_raw, axis=0, keepdims=True)
    ghead_ref[1:2, :] += jnp.sum(grad_log * log_decay, axis=0, keepdims=True)
    for i in range(CHANNELS // LANES):
        window = grad_ref[pl.ds(start, CHUNK + 8), tile(i)]
        own = window[0:CHUNK]
        padded = xs_ref[pl.ds(start, CHUNK + 8), tile(i)]
        total = cw_ref[3:4, tile(i)] * own
        gconv_ref[4:5, tile(i)] += jnp.sum(own, axis=0, keepdims=True)
        gconv_ref[3:4, tile(i)] += jnp.sum(own * padded[8 : 8 + CHUNK], axis=0, keepdims=True)
        for lag in range(1, CONV):
            masked = window * masks_window[lag]
            total = total + cw_ref[3 - lag : 4 - lag, tile(i)] * masked[lag : lag + CHUNK]
            gconv_ref[3 - lag : 4 - lag, tile(i)] += jnp.sum(
                masked[0:CHUNK] * padded[8 - lag : 8 - lag + CHUNK], axis=0, keepdims=True
            )
        gmix_ref[:, tile(i)] = total.astype(BF16)

        @pl.when(step_at == 0)
        def _():
            tail_ref[:, tile(i)] = total[CHUNK - 8 :]

        @pl.when(step_at == count - 1)
        def _():
            ahead = jnp.zeros((8, LANES), F32)
            for lag in range(1, CONV):
                head = jnp.concatenate(
                    [jnp.zeros((8, LANES), F32), window[0:8] * masks_window[lag][0:8]], axis=0
                )
                ahead = ahead + cw_ref[3 - lag : 4 - lag, tile(i)] * head[lag : lag + 8]
            edge_grad_ref[:, tile(i)] = ahead

    @pl.when(step_at == count - 1)
    def _():
        total = jnp.zeros((8, LANES), F32)
        for j in range(PAIRS):
            total += head_sums(rows_ref[:, tile(j)], picks(j))
        ghead_ref[2:3, :] = total[0:1, :]


def mamba_back(
    scalars, edge, mixed, dt_raw, doc, doc_row, conv_pack, head_pack, skip_wide, dy, y, sin, ds_end
):
    rows = mixed.shape[0]
    count = rows // CHUNK
    by_chunk = lambda width: pl.BlockSpec((CHUNK, width), lambda i: (count - 1 - i, 0))
    return pl.pallas_call(
        mamba_back_kernel,
        grid=(count,),
        in_specs=[
            pl.BlockSpec(memory_space=pltpu.SMEM),
            whole((8, CHANNELS)),
            whole((rows, CHANNELS)),
            by_chunk(LANES),
            whole((rows + 8, 1)),
            pl.BlockSpec((8, CHUNK), lambda i: (0, count - 1 - i)),
            whole((8, CHANNELS)),
            whole((8, LANES)),
            whole((1, MAMBA_INNER)),
            by_chunk(MAMBA_INNER),
            by_chunk(MAMBA_INNER),
            pl.BlockSpec((1, STATE_SIZE, MAMBA_INNER), lambda i: (count - 1 - i, 0, 0)),
            whole((STATE_SIZE, MAMBA_INNER)),
        ],
        out_specs=[
            by_chunk(CHANNELS),
            whole((8, CHANNELS)),
            whole((8, CHANNELS)),
            by_chunk(LANES),
            whole((8, CHANNELS)),
            whole((8, LANES)),
        ],
        out_shape=[
            jax.ShapeDtypeStruct((rows, CHANNELS), BF16),
            jax.ShapeDtypeStruct((8, CHANNELS), F32),
            jax.ShapeDtypeStruct((8, CHANNELS), F32),
            jax.ShapeDtypeStruct((rows, LANES), BF16),
            jax.ShapeDtypeStruct((8, CHANNELS), F32),
            jax.ShapeDtypeStruct((8, LANES), F32),
        ],
        scratch_shapes=[
            pltpu.VMEM((rows + 8, CHANNELS), F32),
            pltpu.VMEM((CHUNK, CHANNELS), F32),
            pltpu.VMEM((CHUNK, CHANNELS), F32),
            pltpu.VMEM((rows + 8, CHANNELS), F32),
            pltpu.VMEM((STATE_SIZE, MAMBA_INNER), F32),
            pltpu.VMEM((8, MAMBA_INNER), F32),
        ],
        compiler_params=params("arbitrary"),
        cost_estimate=pl.CostEstimate(
            flops=rows * MAMBA_INNER * 3072, bytes_accessed=rows * 20000, transcendentals=rows * 4096
        ),
        name="mamba_back",
    )(scalars, edge, mixed, dt_raw, doc, doc_row, conv_pack, head_pack, skip_wide, dy, y, sin, ds_end)


def half_roll(x):
    return pltpu.roll(x, HEAD_SIZE, 1)


def stack_low(block, rows):
    low = low_half(rows)
    parts = []
    for a in range(2):
        pair = block[:, tile(a)]
        parts.append(jnp.where(low, pair, 0.0))
        parts.append(jnp.where(low, half_roll(pair), 0.0))
    return parts


def stack_high(block, rows):
    low = low_half(rows)
    parts = []
    for a in range(2):
        pair = block[:, tile(a)]
        parts.append(jnp.where(low, 0.0, half_roll(pair)))
        parts.append(jnp.where(low, 0.0, pair))
    return parts


def tile_bounds(sc_ref, at, tiles):
    first_doc = sc_ref[at]
    last_doc = sc_ref[tiles + at]
    start = sc_ref[2 * tiles] + at * QUERY_TILE
    block_lo = first_doc // KEY_BLOCK
    block_hi = (start + QUERY_TILE - 1) // KEY_BLOCK + 1
    return start, last_doc, block_lo, block_hi


def visible_mask(block, start, doc_row):
    lanes = GROUP * QUERY_TILE
    key = block * KEY_BLOCK + iota((KEY_BLOCK, lanes), 0)
    query = start + iota((1, lanes), 1) % QUERY_TILE
    return (key <= query) & (key >= doc_row)


def attend_kernel(
    sc_ref, q_ref, kv_ref, doc_ref, vec_ref, norm_ref, lse_ref, qz_ref, max_ref, sum_ref, acc_ref
):
    at = pl.program_id(1)
    tiles = pl.num_programs(1)
    start, last_doc, block_lo, block_hi = tile_bounds(sc_ref, at, tiles)
    for g, part in enumerate(stack_low(q_ref[...].astype(F32), QUERY_TILE)):
        qz_ref[g * QUERY_TILE : (g + 1) * QUERY_TILE, :] = part.astype(BF16)
    max_ref[...] = jnp.full_like(max_ref, MASK_FILLER)
    sum_ref[...] = jnp.zeros_like(sum_ref)
    acc_ref[...] = jnp.zeros_like(acc_ref)
    doc_row = jnp.concatenate([doc_ref[0:1, :]] * GROUP, axis=1)

    def visit(block, masked):
        kv = kv_ref[pl.ds(pl.multiple_of(block * KEY_BLOCK, KEY_BLOCK), KEY_BLOCK), :]
        scores = dot_nt(kv, qz_ref[...])
        if masked:
            scores = jnp.where(visible_mask(block, start, doc_row), scores, MASK_FILLER)
        before = max_ref[0:1, :]
        top = jnp.maximum(before, jnp.max(scores, axis=0, keepdims=True))
        prob = jnp.exp(scores - top)
        fade = jnp.exp(before - top)
        max_ref[0:1, :] = top
        sum_ref[0:1, :] = sum_ref[0:1, :] * fade + jnp.sum(prob, axis=0, keepdims=True)
        acc_ref[...] = acc_ref[...] * fade + dot_tn(kv, prob.astype(BF16))

    def one(block, carry):
        full = (block * KEY_BLOCK + KEY_BLOCK - 1 <= start) & (block * KEY_BLOCK >= last_doc)

        @pl.when(full)
        def _():
            visit(block, False)

        @pl.when(jnp.logical_not(full))
        def _():
            visit(block, True)

        return carry

    lax.fori_loop(block_lo, block_hi, one, 0)
    lse_ref[0, 0] = jnp.broadcast_to(max_ref[0:1, :] + jnp.log(sum_ref[0:1, :]), lse_ref.shape[2:])
    scaled = acc_ref[...] / sum_ref[0:1, :]
    low = low_half(QUERY_TILE)
    for a in range(2):
        even = half_roll(scaled[:, (2 * a) * QUERY_TILE : (2 * a + 1) * QUERY_TILE].T)
        odd = scaled[:, (2 * a + 1) * QUERY_TILE : (2 * a + 2) * QUERY_TILE].T
        both = jnp.where(low, even, odd)
        norm_ref[:, tile(a)] = both
        vec_ref[:, tile(a)] = both.astype(BF16)


def attend(scalars, q, kv, doc_row):
    rows = q.shape[0]
    length = kv.shape[0]
    tiles = rows // QUERY_TILE
    lanes = GROUP * QUERY_TILE
    width = GROUP * HEAD_SIZE
    return pl.pallas_call(
        attend_kernel,
        grid=(KEY_VALUE_HEADS, tiles),
        in_specs=[
            pl.BlockSpec(memory_space=pltpu.SMEM),
            pl.BlockSpec((QUERY_TILE, width), lambda j, t: (t, j)),
            pl.BlockSpec((length, LANES), lambda j, t: (0, j)),
            pl.BlockSpec((8, QUERY_TILE), lambda j, t: (0, t)),
        ],
        out_specs=[
            pl.BlockSpec((QUERY_TILE, width), lambda j, t: (t, j)),
            pl.BlockSpec((QUERY_TILE, width), lambda j, t: (t, j)),
            pl.BlockSpec((1, 1, 8, lanes), lambda j, t: (j, t, 0, 0)),
        ],
        out_shape=[
            jax.ShapeDtypeStruct((rows, QUERY_HEADS * HEAD_SIZE), BF16),
            jax.ShapeDtypeStruct((rows, QUERY_HEADS * HEAD_SIZE), F32),
            jax.ShapeDtypeStruct((KEY_VALUE_HEADS, tiles, 8, lanes), F32),
        ],
        scratch_shapes=[
            pltpu.VMEM((lanes, LANES), BF16),
            pltpu.VMEM((8, lanes), F32),
            pltpu.VMEM((8, lanes), F32),
            pltpu.VMEM((LANES, lanes), F32),
        ],
        compiler_params=params("arbitrary", "arbitrary"),
        cost_estimate=pl.CostEstimate(
            flops=rows * length * 2048,
            bytes_accessed=length * 512 + rows * 6000,
            transcendentals=rows * length * 4,
        ),
        name="attend",
    )(scalars, q, kv, doc_row)


def attend_back_kernel(
    sc_ref, q_ref, do_ref, norm_ref, lse_ref, kv_ref, doc_ref, dq_ref, dkv_ref, qd_ref, dkv_acc, dq_acc
):
    at = pl.program_id(1)
    tiles = pl.num_programs(1)
    lanes = GROUP * QUERY_TILE
    start, last_doc, block_lo, block_hi = tile_bounds(sc_ref, at, tiles)

    @pl.when(at == 0)
    def _():
        dkv_acc[...] = jnp.zeros_like(dkv_acc)

    grad = do_ref[...].astype(F32)
    for g, part in enumerate(stack_low(q_ref[...].astype(F32), QUERY_TILE)):
        qd_ref[g * QUERY_TILE : (g + 1) * QUERY_TILE, :] = part.astype(BF16)
    for g, part in enumerate(stack_high(grad, QUERY_TILE)):
        qd_ref[lanes + g * QUERY_TILE : lanes + (g + 1) * QUERY_TILE, :] = part.astype(BF16)
    deltas = []
    for a in range(2):
        turned = (grad[:, tile(a)] * norm_ref[:, tile(a)]).T
        deltas.append(jnp.sum(turned[0:HEAD_SIZE], axis=0, keepdims=True))
        deltas.append(jnp.sum(turned[HEAD_SIZE:], axis=0, keepdims=True))
    delta = jnp.concatenate(deltas, axis=1)
    lse = lse_ref[0, 0, 0:1, :]
    dq_acc[...] = jnp.zeros_like(dq_acc)
    doc_row = jnp.concatenate([doc_ref[0:1, :]] * GROUP, axis=1)

    def visit(block, masked):
        at_rows = pl.ds(pl.multiple_of(block * KEY_BLOCK, KEY_BLOCK), KEY_BLOCK)
        kv = kv_ref[at_rows, :]
        scores = dot_nt(kv, qd_ref[0:lanes, :])
        prob = jnp.exp(scores - lse)
        if masked:
            prob = jnp.where(visible_mask(block, start, doc_row), prob, 0.0)
        grad_prob = dot_nt(kv, qd_ref[lanes:, :])
        grad_scores = (prob * (grad_prob - delta)).astype(BF16)
        dkv_acc[at_rows, :] += dot_nn(grad_scores, qd_ref[0:lanes, :]) + dot_nn(
            prob.astype(BF16), qd_ref[lanes:, :]
        )
        dq_acc[...] += dot_tn(kv, grad_scores)

    def one(block, carry):
        full = (block * KEY_BLOCK + KEY_BLOCK - 1 <= start) & (block * KEY_BLOCK >= last_doc)

        @pl.when(full)
        def _():
            visit(block, False)

        @pl.when(jnp.logical_not(full))
        def _():
            visit(block, True)

        return carry

    lax.fori_loop(block_lo, block_hi, one, 0)
    low = low_half(QUERY_TILE)
    scale = 1.0 / math.sqrt(HEAD_SIZE)
    for a in range(2):
        even = dq_acc[:, (2 * a) * QUERY_TILE : (2 * a + 1) * QUERY_TILE].T
        odd = half_roll(dq_acc[:, (2 * a + 1) * QUERY_TILE : (2 * a + 2) * QUERY_TILE].T)
        dq_ref[:, tile(a)] = jnp.where(low, even, odd) * scale

    @pl.when(at == tiles - 1)
    def _():
        dkv_ref[...] = dkv_acc[...].astype(BF16)


def attend_back(scalars, q, grad, norm, lse, kv, doc_row):
    rows = q.shape[0]
    length = kv.shape[0]
    tiles = rows // QUERY_TILE
    lanes = GROUP * QUERY_TILE
    width = GROUP * HEAD_SIZE
    by_tile = pl.BlockSpec((QUERY_TILE, width), lambda j, t: (t, j))
    return pl.pallas_call(
        attend_back_kernel,
        grid=(KEY_VALUE_HEADS, tiles),
        in_specs=[
            pl.BlockSpec(memory_space=pltpu.SMEM),
            by_tile,
            by_tile,
            by_tile,
            pl.BlockSpec((1, 1, 8, lanes), lambda j, t: (j, t, 0, 0)),
            pl.BlockSpec((length, LANES), lambda j, t: (0, j)),
            pl.BlockSpec((8, QUERY_TILE), lambda j, t: (0, t)),
        ],
        out_specs=[by_tile, pl.BlockSpec((length, LANES), lambda j, t: (0, j))],
        out_shape=[
            jax.ShapeDtypeStruct((rows, QUERY_HEADS * HEAD_SIZE), F32),
            jax.ShapeDtypeStruct((length, KEY_VALUE_HEADS * LANES), BF16),
        ],
        scratch_shapes=[
            pltpu.VMEM((2 * lanes, LANES), BF16),
            pltpu.VMEM((length, LANES), F32),
            pltpu.VMEM((LANES, lanes), F32),
        ],
        compiler_params=params("arbitrary", "arbitrary"),
        cost_estimate=pl.CostEstimate(
            flops=rows * length * 5120,
            bytes_accessed=length * 1024 + rows * 8000,
            transcendentals=rows * length * 4,
        ),
        name="attend_back",
    )(scalars, q, grad, norm, lse, kv, doc_row)


def turn_lanes(x, cosine, sine):
    half = HEAD_SIZE // 2
    former = iota(x.shape, 1) % HEAD_SIZE < half
    other = jnp.where(former, -pltpu.roll(x, LANES - half, 1), pltpu.roll(x, half, 1))
    return x * cosine + other * sine


def rope_kernel(q_in_ref, kv_in_ref, cos_ref, sin_ref, q_ref, kv_ref):
    cosine, sine = cos_ref[...], sin_ref[...]
    scale = 1.0 / math.sqrt(HEAD_SIZE)
    for i in range(QUERY_HEADS * HEAD_SIZE // LANES):
        turned = turn_lanes(q_in_ref[:, tile(i)], cosine, sine).astype(BF16)
        q_ref[:, tile(i)] = (turned.astype(F32) * scale).astype(BF16)
    keys = turn_lanes(kv_in_ref[:, tile(0)], cosine, sine)
    values = kv_in_ref[:, tile(1)]
    low = iota(keys.shape, 1) < HEAD_SIZE
    kv_ref[:, tile(0)] = jnp.where(low, keys, half_roll(values)).astype(BF16)
    kv_ref[:, tile(1)] = jnp.where(low, half_roll(keys), values).astype(BF16)


def rope(q_raw, kv_raw, cosine, sine):
    rows = q_raw.shape[0]
    return pl.pallas_call(
        rope_kernel,
        out_shape=[
            jax.ShapeDtypeStruct((rows, QUERY_HEADS * HEAD_SIZE), BF16),
            jax.ShapeDtypeStruct((rows, KEY_VALUE_HEADS * LANES), BF16),
        ],
        compiler_params=pltpu.CompilerParams(vmem_limit_bytes=VMEM_LIMIT),
        name="rope",
    )(q_raw, kv_raw, cosine, sine)


def rope_back_kernel(dq_ref, dkv_ref, cos_ref, sin_ref, gq_ref, gkv_ref):
    cosine, sine = cos_ref[...], -sin_ref[...]
    for i in range(QUERY_HEADS * HEAD_SIZE // LANES):
        gq_ref[:, tile(i)] = turn_lanes(dq_ref[:, tile(i)], cosine, sine).astype(BF16)
    first = dkv_ref[:, tile(0)].astype(F32)
    second = dkv_ref[:, tile(1)].astype(F32)
    low = iota(first.shape, 1) < HEAD_SIZE
    keys = jnp.where(low, first, half_roll(second))
    values = jnp.where(low, half_roll(first), second)
    gkv_ref[:, tile(0)] = turn_lanes(keys, cosine, sine).astype(BF16)
    gkv_ref[:, tile(1)] = values.astype(BF16)


def rope_back(dq, dkv, cosine, sine):
    rows = dq.shape[0]
    return pl.pallas_call(
        rope_back_kernel,
        out_shape=[
            jax.ShapeDtypeStruct((rows, QUERY_HEADS * HEAD_SIZE), BF16),
            jax.ShapeDtypeStruct((rows, KEY_VALUE_HEADS * LANES), BF16),
        ],
        compiler_params=pltpu.CompilerParams(vmem_limit_bytes=VMEM_LIMIT),
        name="rope_back",
    )(dq, dkv, cosine, sine)


def shift_along(block, axis, distance):
    devices = range(lax.axis_size(axis))
    route = [(i - distance, i) for i in devices if i - distance in devices]
    return lax.ppermute(block, axis, route)


def segment_starts(positions, starts):
    reached = starts[None, :] <= positions[:, None]
    return jnp.max(jnp.where(reached, starts[None, :], -1), axis=1)


def state_entering(message, axis):
    place = lax.axis_index(axis)
    gathered = lax.all_gather(message, axis)
    state = jnp.zeros((STATE_SIZE, MAMBA_INNER), F32)
    for i in range(lax.axis_size(axis)):
        through = gathered[i, STATE_SIZE : STATE_SIZE + 1].astype(F32)
        state = jnp.where(
            i < place, through * state + gathered[i, :STATE_SIZE].astype(F32), state
        )
    return state, gathered[:, STATE_SIZE : STATE_SIZE + 1]


def gradient_entering(grad_state, through_all, axis):
    place = lax.axis_index(axis)
    devices = lax.axis_size(axis)
    gathered = lax.all_gather(grad_state, axis)
    state = jnp.zeros((STATE_SIZE, MAMBA_INNER), F32)
    for i in reversed(range(devices)):
        through = through_all[i].astype(F32)
        state = jnp.where(i > place, through * state + gathered[i].astype(F32), state)
    return state


def outer_sum(left, right):
    return dot_tn(left, right)


def time_steps(left, right):
    return dot_nt(left, right)


def reduce_to_shard(grad, dim):
    share = lax.psum_scatter(grad.astype(BF16), "fsdp", scatter_dimension=dim, tiled=True)
    return lax.psum(share, "ctx").astype(F32)


def local(
    tokens,
    cotangent,
    doc_starts,
    gain_mix,
    w_z,
    w_xbc,
    w_dt,
    conv_w,
    conv_b,
    dt_bias,
    a_log,
    skip_factor,
    w_mo,
    w_q,
    key_value_weight,
    w_o,
    gain_ffn,
    w_gate,
    w_up,
    w_down,
):
    gather = lambda w, dim: lax.all_gather(w, "fsdp", axis=dim, tiled=True)
    full_gain_mix = gather(gain_mix, 0).astype(F32)
    full_xbc = gather(w_xbc, 0)
    full_kv = gather(key_value_weight, 0)
    full_q = gather(w_q, 0)
    full_dt = gather(w_dt, 0)
    full_z = gather(w_z, 0)
    full_conv_w = gather(conv_w, 1).astype(F32)
    full_conv_b = gather(conv_b, 0).astype(F32)
    full_dt_bias = gather(dt_bias, 0).astype(F32)
    full_a_log = gather(a_log, 0).astype(F32)
    full_skip = gather(skip_factor, 0).astype(F32)
    full_mo = gather(w_mo, 0)
    full_o = gather(w_o, 0)
    full_gain_ffn = gather(gain_ffn, 0).astype(F32)
    full_gate = gather(w_gate, 0)
    full_up = gather(w_up, 0)
    full_down = gather(w_down, 0)

    ctx_rank = lax.axis_index("ctx")
    inputs = tokens[0].astype(F32)
    rows = inputs.shape[0]
    starts = doc_starts[0]
    base = ctx_rank * rows
    positions = base + jnp.arange(rows, dtype=jnp.int32)
    doc = segment_starts(positions, starts)
    doc_col = jnp.pad(doc, (0, 8))[:, None]
    doc_row = jnp.broadcast_to(doc[None, :], (8, rows))
    scalars = jnp.concatenate([doc[CHUNK - 1 :: CHUNK], base[None]])
    attn_scalars = jnp.concatenate(
        [doc[::QUERY_TILE], doc[QUERY_TILE - 1 :: QUERY_TILE], base[None]]
    )
    half = HEAD_SIZE // 2
    freqs = ROPE_BASE ** (
        -2.0 * (jnp.arange(LANES, dtype=jnp.int32) % half).astype(F32) / HEAD_SIZE
    )
    angles = positions.astype(F32)[:, None] * freqs[None, :]
    cosine, sine = jnp.cos(angles), jnp.sin(angles)
    conv_pack = jnp.pad(
        jnp.concatenate([full_conv_w, full_conv_b[None]], axis=0), ((0, 3), (0, 0))
    )
    pad_heads = lambda v: jnp.pad(v, (0, LANES - MAMBA_HEADS))[None]
    head_pack = jnp.concatenate(
        [pad_heads(full_dt_bias), pad_heads(-jnp.exp(full_a_log)), jnp.zeros((6, LANES), F32)], axis=0
    )
    skip_wide = jnp.repeat(full_skip, MAMBA_HEAD_SIZE)[None]

    scale_one = lax.rsqrt(jnp.mean(inputs * inputs, axis=-1, keepdims=True) + EPSILON)
    normed = (inputs * scale_one * full_gain_mix[None, :]).astype(BF16)
    kv_raw = dot_nn(normed, full_kv)
    q_raw = dot_nn(normed, full_q)
    mixed_in = dot_nn(normed, full_xbc).astype(BF16)
    wide_dt = jnp.pad(full_dt, ((0, 0), (0, LANES - MAMBA_HEADS)))
    dt_raw = dot_nn(normed, wide_dt)
    gate_z = dot_nn(normed, full_z)
    query, key_value = rope(q_raw, kv_raw, cosine, sine)
    kv_all = lax.all_gather(key_value, "ctx", axis=0, tiled=True)
    edge = shift_along(mixed_in[rows - 8 :], "ctx", 1).astype(F32)

    y_local, state_local, message, decay, c_mat = mamba_forward(
        scalars, edge, mixed_in, dt_raw, doc_col[:rows], conv_pack, head_pack, skip_wide
    )
    state_in, through_all = state_entering(message, "ctx")
    attn_vec, attn_norm, lse = attend(attn_scalars, query, kv_all, doc_row)
    y_total, gated, state_true = mamba_correct(y_local, state_local, c_mat, decay, state_in, gate_z)
    hidden = inputs + dot_nn(attn_vec, full_o) + dot_nn(gated, full_mo)
    gain_two = full_gain_ffn
    scale_two = lax.rsqrt(jnp.mean(hidden * hidden, axis=-1, keepdims=True) + EPSILON)
    normed_ffn = (hidden * scale_two * gain_two[None, :]).astype(BF16)
    gate = dot_nn(normed_ffn, full_gate)
    upper = dot_nn(normed_ffn, full_up)
    sig_gate = jax.nn.sigmoid(gate)
    silu_gate = gate * sig_gate
    activ = (silu_gate * upper).astype(BF16)
    result = hidden + dot_nn(activ, full_down)

    grad_out = cotangent[0]
    grad_w_down = outer_sum(activ, grad_out)
    grad_act = time_steps(grad_out, full_down)
    grad_gate = (grad_act * upper * sig_gate * (1.0 + gate * (1.0 - sig_gate))).astype(BF16)
    grad_up = (grad_act * silu_gate).astype(BF16)
    grad_w_gate = outer_sum(normed_ffn, grad_gate)
    grad_w_up = outer_sum(normed_ffn, grad_up)
    grad_n2 = time_steps(grad_gate, full_gate) + time_steps(grad_up, full_up)
    grad_gain_ffn = jnp.sum(grad_n2 * hidden * scale_two, axis=0)
    scaled_two = grad_n2 * gain_two[None, :]
    grad_hidden = (
        grad_out.astype(F32)
        + scale_two * scaled_two
        - hidden * scale_two**3 * jnp.mean(scaled_two * hidden, axis=-1, keepdims=True)
    )
    grad_hid_b = grad_hidden.astype(BF16)
    gated_grad = time_steps(grad_hid_b, full_mo)
    grad_y, grad_z, grad_state = mamba_gate_back(gated_grad, gate_z, y_total, c_mat, decay)
    grad_attn = time_steps(grad_hid_b, full_o).astype(BF16)
    grad_w_o = outer_sum(attn_vec, grad_hid_b)
    grad_w_mo = outer_sum(gated, grad_hid_b)
    state_grad = gradient_entering(grad_state, through_all, "ctx")
    grad_q, grad_kv_all = attend_back(
        attn_scalars, query, grad_attn, attn_norm, lse, kv_all, doc_row
    )
    grad_kv = lax.psum_scatter(grad_kv_all, "ctx", scatter_dimension=0, tiled=True)
    grad_mixed, tail, edge_grad, grad_dt, grad_conv, grad_heads = mamba_back(
        scalars,
        edge,
        mixed_in,
        dt_raw,
        doc_col,
        doc_row,
        conv_pack,
        head_pack,
        skip_wide,
        grad_y,
        y_total,
        state_true,
        state_grad,
    )
    behind = shift_along(edge_grad, "ctx", -1)
    grad_mixed = grad_mixed.at[rows - 8 :].set((tail + behind).astype(BF16))
    grad_q_b, grad_kv_b = rope_back(grad_q, grad_kv, cosine, sine)
    grad_w_q = outer_sum(normed, grad_q_b)
    grad_w_kv = outer_sum(normed, grad_kv_b)
    grad_w_z = outer_sum(normed, grad_z)
    grad_w_xbc = outer_sum(normed, grad_mixed)
    grad_w_dt = outer_sum(normed, grad_dt)[:, :MAMBA_HEADS]
    grad_n1 = (
        time_steps(grad_z, full_z)
        + time_steps(grad_mixed, full_xbc)
        + time_steps(grad_dt, wide_dt)
        + time_steps(grad_q_b, full_q)
        + time_steps(grad_kv_b, full_kv)
    )
    grad_gain_mix = jnp.sum(grad_n1 * inputs * scale_one, axis=0)
    scaled_one = grad_n1 * full_gain_mix[None, :]
    grad_tokens = (
        grad_hidden
        + scale_one * scaled_one
        - inputs * scale_one**3 * jnp.mean(scaled_one * inputs, axis=-1, keepdims=True)
    )
    grads = (
        (grad_gain_mix, 0),
        (grad_w_z, 0),
        (grad_w_xbc, 0),
        (grad_w_dt, 0),
        (grad_conv[:CONV], 1),
        (grad_conv[CONV], 0),
        (grad_heads[0, :MAMBA_HEADS], 0),
        (grad_heads[1, :MAMBA_HEADS], 0),
        (grad_heads[2, :MAMBA_HEADS], 0),
        (grad_w_mo, 0),
        (grad_w_q, 0),
        (grad_w_kv, 0),
        (grad_w_o, 0),
        (grad_gain_ffn, 0),
        (grad_w_gate, 0),
        (grad_w_up, 0),
        (grad_w_down, 0),
    )
    totals = tuple(reduce_to_shard(grad, dim) for grad, dim in grads)
    return (result.astype(BF16)[None], grad_tokens[None]) + totals


def solution(mesh):
    in_specs = (
        P("fsdp", "ctx", None),
        P("fsdp", "ctx", None),
        P("fsdp", None),
        P("fsdp"),
        P("fsdp", None),
        P("fsdp", None),
        P("fsdp", None),
        P(None, "fsdp"),
        P("fsdp"),
        P("fsdp"),
        P("fsdp"),
        P("fsdp"),
        P("fsdp", None),
        P("fsdp", None),
        P("fsdp", None),
        P("fsdp", None),
        P("fsdp"),
        P("fsdp", None),
        P("fsdp", None),
        P("fsdp", None),
    )
    out_specs = (
        P("fsdp", "ctx", None),
        P("fsdp", "ctx", None),
        P("fsdp"),
        P("fsdp", None),
        P("fsdp", None),
        P("fsdp", None),
        P(None, "fsdp"),
        P("fsdp"),
        P("fsdp"),
        P("fsdp"),
        P("fsdp"),
        P("fsdp", None),
        P("fsdp", None),
        P("fsdp", None),
        P("fsdp", None),
        P("fsdp"),
        P("fsdp", None),
        P("fsdp", None),
        P("fsdp", None),
    )
    return jax.shard_map(local, mesh=mesh, in_specs=in_specs, out_specs=out_specs, check_vma=False)
```

time: 1550 us -> 1220 us (0.79)
  local copies, waits for them, and re-layouts: 273 us -> 11 us
  waiting for transfers between devices: 654 us -> 840 us
  matrix products: 264 us -> 123 us
  other arithmetic: 158 us -> 38.3 us
  Pallas kernels: 0 us -> 85 us
  loops' own time: 48.5 us -> 0 us
  blocking collectives: 106 us -> 84 us
    dot_general x64 -> x30, matrix products: 264 us -> 123 us  [the longest x10 43.5 us: dot_tn(): lax.dot_general(a, b, (((0,), (0,)), ((), ())), preferred_element_type=F32)]
    all_gather x11, waiting for transfers between devices: 123 us -> 245 us  [the longest x8 124 us: local(): gather = lambda w, dim: lax.all_gather(w, 'fsdp', axis=dim, tiled=True)]
    dynamic_update_slice x25 -> x0, local copies, waits for them, and re-layouts: 89.6 us -> none  [the longest x24 86.1 us: mamba_local(): lax.scan(span_step, (initial_state, seg_before), piece_list)]
    pallas_call x0 -> x8, Pallas kernels: none -> 85 us  [the longest x1 25.4 us: mamba_back(): pl.pallas_call(mamba_back_kernel, grid=(count,), in_specs=[pl.BlockSpec(m...]
    reduce_scatter x11, waiting for transfers between devices: 343 us -> 394 us  [the longest x10 304 us: reduce_to_shard(): lax.psum_scatter(grad.astype(BF16), 'fsdp', scatter_dimension=dim, tiled=...]
    another operation x22 -> x0, loops' own time: 48.5 us -> none  [the longest x2 42.2 us: fold_blocks(): running, _ = lax.scan(one_step, running, (piece_list, offsets))]
    dynamic_slice x28 -> x0, local copies, waits for them, and re-layouts: 43.6 us -> none  [the longest x12 34.2 us: mamba_local(): lax.scan(span_step, (initial_state, seg_before), piece_list)]
    slice x63 -> x7, local copies, waits for them, and re-layouts: 38.5 us -> 1.72 us  [the longest x1 0.86 us: local(): doc_col[:rows]]
  transfers between devices with their start and end apart: 26 -> 26, of which waited for: 12 -> 23; matrix products, arithmetic and copies ran while one was open for 38% -> 11% of each run, Pallas kernels for 0% -> 6%
where the time goes in v1:
time: 1220 us; the launch traced here: 1210 us
  waiting for transfers between devices  840 us (69%)
  matrix products  123 us (10%)
  Pallas kernels  85 us (7%)
  blocking collectives  84 us (7%)
  other arithmetic  38.3 us (3%)
  between operations  18.4 us (2%)
    reduce_scatter x10, waiting for transfers between devices, reduce_to_shard(): lax.psum_scatter(grad.astype(BF16), 'fsdp', scatter_dimension=dim, tiled=...  304 us
    psum x1, waiting for transfers between devices, reduce_to_shard(): return lax.psum(share, 'ctx').astype(F32)  181 us
    all_gather x8, waiting for transfers between devices, local(): gather = lambda w, dim: lax.all_gather(w, 'fsdp', axis=dim, tiled=True)  124 us
    reduce_scatter x1, waiting for transfers between devices, local(): lax.psum_scatter(grad_kv_all, 'ctx', scatter_dimension=0, tiled=True)  89.7 us
    all_gather x1, waiting for transfers between devices, state_entering(): gathered = lax.all_gather(message, axis)  54.8 us
    dot_general x10, matrix products, dot_tn(): lax.dot_general(a, b, (((0,), (0,)), ((), ())), preferred_element_type=F32)  43.5 us
    all_gather x1, waiting for transfers between devices, local(): kv_all = lax.all_gather(key_value, 'ctx', axis=0, tiled=True)  43.5 us
    dot_general x10, matrix products, dot_nn(): lax.dot_general(a, b, (((1,), (0,)), ((), ())), precision=precision, pref...  40.4 us
  transfers between devices with their start and end apart: 26, of which 23 were waited for; matrix products, arithmetic and copies ran while one was open for 11% of the time, Pallas kernels for 6%

profile of v1, /device:TPU:0, one launch (start us, length us, event | category | flops | bytes accessed | tf_op | source)
XLA Modules:
  0.0 1206.1 jit_solution(15530931290257684604)
XLA Ops:
  10.1 6.0 all-gather.2
  16.4 9.4 all_gather.68
  39.7 7.8 all-reduce.18
  47.5 5.2 all-gather.3
  52.9 5.4 all_gather.72
  75.9 13.2 %mamba_forward.1 = (f32[512,1536]{1,0:T(8,128)}, f32[4,128,1536]{2,1,0:T(8,128)}, bf16[144,1536]{1,0:T(8,128)(2,1)}, f32[512,128]{1,0:T(8,128)}, bf16[512,128]{1,0:T(8,128)(2,1)}) custom-call(s32[5]{0:T(128)} %pad_add_fusion.1.sc_ref, f32[8,1792]{1,0:T(8,128)} %convert_element_type.395.edge_ref, bf16[512,1792]{1,0:T(8,128)(2,1)} %copy-done.7, ...), custom_call_target="tpu_custom_call" | custom-call | flops 805306368 | bytes 6144000 | tf_op jit(solution)/shard_map/mamba_forward/pallas_call | solution.py:199
  92.6 5.4 all-gather.4
  98.6 5.4 fusion.61.z_ref
  104.0 43.5 %all-gather.19.cloned.1.call-done.kv_ref = bf16[4096,256]{1,0:T(8,128)(2,1)} async-done(((bf16[512,256]{1,0:T(8,128)(2,1)}), bf16[4096,256]{1,0:T(8,128)(2,1)}) %all-gather.19.cloned.1.call-update) | async-done | bytes 2097168 | tf_op jit(solution)/shard_map/all_gather | solution.py:1010
  148.1 10.9 attend.1
  159.0 54.8 %all-gather.35.cloned.1.call-done = bf16[1152,1536]{1,0:T(8,128)(2,1)} async-done(((bf16[144,1536]{1,0:T(8,128)(2,1)}), bf16[1152,1536]{1,0:T(8,128)(2,1)}) %all-gather.35.cloned.1.call-update) | async-done | bytes 3538960 | tf_op jit(solution)/shard_map/all_gather | solution.py:898
  218.4 8.7 mamba_correct.1
  227.1 15.3 %all-gather.27.cloned.1.call-done = bf16[1536,1024]{1,0:T(8,128)(2,1)} async-done(((bf16[384,1024]{1,0:T(8,128)(2,1)}), bf16[1536,1024]{1,0:T(8,128)(2,1)}) %all-gather.27.cloned.1.call-update) | async-done | bytes 3145744 | tf_op jit(solution)/shard_map/all_gather | solution.py:954
  242.4 5.5 fusion.71
  247.8 12.8 %all-gather.21.cloned.1.call-done = bf16[512,1024]{1,0:T(8,128)(2,1)} async-done(((bf16[128,1024]{1,0:T(8,128)(2,1)}), bf16[512,1024]{1,0:T(8,128)(2,1)}) %all-gather.21.cloned.1.call-update) | async-done | bytes 1048592 | tf_op jit(solution)/shard_map/all_gather | solution.py:954
  264.9 31.9 %all-gather.29.cloned.1.call-done = bf16[1024,2048]{1,0:T(8,128)(2,1)} async-done(((bf16[256,2048]{1,0:T(8,128)(2,1)}), bf16[1024,2048]{1,0:T(8,128)(2,1)}) %all-gather.29.cloned.1.call-update) | async-done | bytes 4194320 | tf_op jit(solution)/shard_map/all_gather | solution.py:954
  296.8 6.8 fusion.72
  303.5 29.3 %all-gather.31.cloned.1.call-done = bf16[1024,2048]{1,0:T(8,128)(2,1)} async-done(((bf16[256,2048]{1,0:T(8,128)(2,1)}), bf16[1024,2048]{1,0:T(8,128)(2,1)}) %all-gather.31.cloned.1.call-update) | async-done | bytes 4194320 | tf_op jit(solution)/shard_map/all_gather | solution.py:954
  332.9 6.8 fusion.73
  339.7 29.1 %all-gather.33.cloned.1.call-done = bf16[2048,1024]{1,0:T(8,128)(2,1)} async-done(((bf16[512,1024]{1,0:T(8,128)(2,1)}), bf16[2048,1024]{1,0:T(8,128)(2,1)}) %all-gather.33.cloned.1.call-update) | async-done | bytes 4194320 | tf_op jit(solution)/shard_map/all_gather | solution.py:954
  368.8 10.2 multiply_convert_fusion
  389.1 13.5 %attend_back.1 = (f32[512,512]{1,0:T(8,128)}, bf16[4096,256]{1,0:T(8,128)(2,1)}) custom-call(s32[9]{0:T(128)} %pad_add_fusion.sc_ref, bf16[512,512]{1,0:T(8,128)(2,1)} %get-tuple-element.57.q_ref, bf16[512,512]{1,0:T(8,128)(2,1)} %convolution_convert_fusion.10.do_ref, f32[512,512]{1,0:T(8,128)} %get-tuple-element.75.norm_ref, ...), custom_call_target="tpu_custom_call" | custom-call | flops 10737418240 | bytes 8290304 | tf_op jit(solution)/shard_map/attend_back/pallas_call | solution.py:794
  402.7 5.7 fusion.75.gg_ref
  408.4 7.4 mamba_gate_back.1
  419.0 89.7 %reduce-scatter.15.cloned.1.call-done.dkv_ref = bf16[512,256]{1,0:T(8,128)(2,1)} async-done(((bf16[4096,256]{1,0:T(8,128)(2,1)}), bf16[512,256]{1,0:T(8,128)(2,1)}) %reduce-scatter.15.cloned.1.call-update) | async-done | bytes 262160 | tf_op jit(solution)/shard_map/reduce_scatter | solution.py:1055
  514.2 5.2 convolution_convert_fusion.3
  519.6 5.1 convolution_convert_fusion.5
  527.7 6.3 convolution_convert_fusion.2
  534.1 6.3 convolution_convert_fusion.1
  540.5 6.2 convolution_convert_fusion
  548.1 22.2 %all-gather.37.cloned.1.call-done = bf16[1024,1536]{1,0:T(8,128)(2,1)} async-done(((bf16[128,1536]{1,0:T(8,128)(2,1)}), bf16[1024,1536]{1,0:T(8,128)(2,1)}) %all-gather.37.cloned.1.call-update) | async-done | bytes 3145744 | tf_op jit(solution)/shard_map/all_gather | solution.py:911
  573.8 25.4 %mamba_back.1 = (bf16[512,1792]{1,0:T(8,128)(2,1)}, f32[8,1792]{1,0:T(8,128)}, f32[8,1792]{1,0:T(8,128)}, bf16[512,128]{1,0:T(8,128)(2,1)}, f32[8,1792]{1,0:T(8,128)}, /*index=5*/f32[8,128]{1,0:T(8,128)}) custom-call(s32[5]{0:T(128)} %pad_add_fusion.1.sc_ref, f32[8,1792]{1,0:T(8,128)} %convert_element_type.395.edge_ref, bf16[512,1792]{1,0:T(8,128)(2,1)} %copy-done.7, ...), custom_call_target="tpu_custom_call" | custom-call | flops 2415919104 | bytes 10240000 | tf_op jit(solution)/shard_map/mamba_back/pallas_call | solution.py:538
  600.5 5.0 collective-permute-done.1
  606.9 5.5 convolution_convert_fusion.4
  615.7 5.4 reduce-scatter.27.cloned.1.call-done
  621.1 40.4 %reduce-scatter.23.cloned.1.call-done = bf16[384,1024]{1,0:T(8,128)(2,1)} async-done(((bf16[1536,1024]{1,0:T(8,128)(2,1)}), bf16[384,1024]{1,0:T(8,128)(2,1)}) %reduce-scatter.23.cloned.1.call-update) | async-done | bytes 786448 | tf_op jit(solution)/shard_map/reduce_scatter | solution.py:928
  661.5 40.5 %reduce-scatter.17.cloned.1.call-done = bf16[256,1536]{1,0:T(8,128)(2,1)} async-done(((bf16[1024,1536]{1,0:T(8,128)(2,1)}), bf16[256,1536]{1,0:T(8,128)(2,1)}) %reduce-scatter.17.cloned.1.call-update) | async-done | bytes 786448 | tf_op jit(solution)/shard_map/reduce_scatter | solution.py:928
  702.0 27.9 %reduce-scatter.25.cloned.1.call-done = bf16[256,512]{1,0:T(8,128)(2,1)} async-done(((bf16[1024,512]{1,0:T(8,128)(2,1)}), bf16[256,512]{1,0:T(8,128)(2,1)}) %reduce-scatter.25.cloned.1.call-update) | async-done | bytes 262160 | tf_op jit(solution)/shard_map/reduce_scatter | solution.py:928
  729.9 47.1 %reduce-scatter.31.cloned.1.call-done = bf16[256,2048]{1,0:T(8,128)(2,1)} async-done(((bf16[1024,2048]{1,0:T(8,128)(2,1)}), bf16[256,2048]{1,0:T(8,128)(2,1)}) %reduce-scatter.31.cloned.1.call-update) | async-done | bytes 1048592 | tf_op jit(solution)/shard_map/reduce_scatter | solution.py:928
  777.0 47.1 %reduce-scatter.33.cloned.1.call-done = bf16[256,2048]{1,0:T(8,128)(2,1)} async-done(((bf16[1024,2048]{1,0:T(8,128)(2,1)}), bf16[256,2048]{1,0:T(8,128)(2,1)}) %reduce-scatter.33.cloned.1.call-update) | async-done | bytes 1048592 | tf_op jit(solution)/shard_map/reduce_scatter | solution.py:928
  824.1 47.1 %reduce-scatter.35.cloned.1.call-done = bf16[512,1024]{1,0:T(8,128)(2,1)} async-done(((bf16[2048,1024]{1,0:T(8,128)(2,1)}), bf16[512,1024]{1,0:T(8,128)(2,1)}) %reduce-scatter.35.cloned.1.call-update) | async-done | bytes 1048592 | tf_op jit(solution)/shard_map/reduce_scatter | solution.py:928
  871.2 43.8 %reduce-scatter.19.cloned.1.call-done = bf16[256,1792]{1,0:T(8,128)(2,1)} async-done(((bf16[1024,1792]{1,0:T(8,128)(2,1)}), bf16[256,1792]{1,0:T(8,128)(2,1)}) %reduce-scatter.19.cloned.1.call-update) | async-done | bytes 917520 | tf_op jit(solution)/shard_map/reduce_scatter | solution.py:928
  917.0 5.6 fusion.76
  929.9 9.6 reduce-scatter.37.cloned.1.call-done
  947.3 6.0 all-reduce.17
  957.2 4.9 reduce-scatter.21.cloned.1.call-done
  962.1 38.8 %all-reduce.15 = (bf16[256]{0:T(256)(128)(2,1)S(1)}, bf16[256,24]{0,1:T(8,128)(2,1)S(1)}, bf16[4,448]{1,0:T(4,128)(2,1)S(1)}, bf16[448]{0:T(512)(128)(2,1)S(1)},...) all-reduce(bf16[256]{0:T(256)(128)(2,1)S(1)} %dynamic-slice.13, ...), channel_id=1, replica_groups=mesh['ctx'=8,'fsdp'=4] {'ctx'}, use_global_device_ids=true, to_apply=%region_8.9 | all-reduce | flops 8914 | bytes 35656 | tf_op jit(solution)/shard_map/psum | solution.py:929
  1005.3 181.3 %all-reduce.21.cloned.1.call-done = (bf16[256,1536]{1,0:T(8,128)(2,1)}, bf16[256,1792]{1,0:T(8,128)(2,1)}, bf16[384,1024]{1,0:T(8,128)(2,1)}, bf16[256,512]{1,0:...) async-done(((bf16[256,1536]{1,0:T(8,128)(2,1)}, ...) | async-done | bytes 6291472 | tf_op jit(solution)/shard_map/psum | solution.py:929
  (242 shorter events, 115.5 us)
Async XLA Ops:
  7.2 8.9 copy-start
  7.2 9.2 copy-start.22
  7.2 23.2 %all-gather.17.cloned.1.call-start = ((), (), s32[]{:S(2)}) async-start(), calls=%async_computation.12 | async-start | bytes 1310720 | tf_op jit(solution)/shard_map/all_gather | solution.py:954
  7.9 57.5 %all-gather.23.cloned.1.call-start = ((), (), s32[]{:S(2)}) async-start(), calls=%async_computation.15 | async-start | bytes 4587520 | tf_op jit(solution)/shard_map/all_gather | solution.py:954
  8.7 89.9 %all-gather.25.cloned.1.call-start = ((), (), s32[]{:S(2)}) async-start(), calls=%async_computation.16 | async-start | bytes 3932160 | tf_op jit(solution)/shard_map/all_gather | solution.py:954
  9.4 138.1 %all-gather.19.cloned.1.call-start = ((), (), s32[]{:S(2)}) async-start(), calls=%async_computation.13 | async-start | bytes 2359296 | tf_op jit(solution)/shard_map/all_gather | solution.py:1010
  33.3 3.4 copy-start.28
  33.3 5.3 copy-start.35
  33.3 5.6 copy-start.36
  33.3 5.8 copy-start.37
  33.4 6.1 copy-start.29
  33.4 14.2 %copy-start.26 = (bf16[4,448]{1,0:T(4,128)(2,1)S(1)}, bf16[4,448]{1,0:T(4,128)(2,1)}, u32[]{:S(2)}) copy-start(bf16[4,448]{1,0:T(4,128)(2,1)} %param.29) | copy-start | bytes 10756
  33.4 19.6 %copy-start.25 = (bf16[256,24]{0,1:T(8,128)(2,1)S(1)}, bf16[256,24]{0,1:T(8,128)(2,1)}, u32[]{:S(2)}) copy-start(bf16[256,24]{0,1:T(8,128)(2,1)} %param.28) | copy-start | bytes 36868
  36.5 177.3 %all-gather.35.cloned.1.call-start = ((), (), s32[]{:S(2)}) async-start(), calls=%async_computation.32 | async-start | bytes 3981312 | tf_op jit(solution)/shard_map/all_gather | solution.py:898
  69.6 6.2 copy-start.7
  69.7 5.6 collective-permute-start
  89.1 3.6 copy-start.38
  89.1 153.3 %all-gather.27.cloned.1.call-start = ((), (), s32[]{:S(2)}) async-start(), calls=%async_computation.17 | async-start | bytes 3932160 | tf_op jit(solution)/shard_map/all_gather | solution.py:954
  89.6 171.1 %all-gather.21.cloned.1.call-start = ((), (), s32[]{:S(2)}) async-start(), calls=%async_computation.14 | async-start | bytes 1310720 | tf_op jit(solution)/shard_map/all_gather | solution.py:954
  90.4 206.4 %all-gather.29.cloned.1.call-start = ((), (), s32[]{:S(2)}) async-start(), calls=%async_computation.18 | async-start | bytes 5242880 | tf_op jit(solution)/shard_map/all_gather | solution.py:954
  91.1 241.7 %all-gather.31.cloned.1.call-start = ((), (), s32[]{:S(2)}) async-start(), calls=%async_computation.19 | async-start | bytes 5242880 | tf_op jit(solution)/shard_map/all_gather | solution.py:954
  91.9 276.9 %all-gather.33.cloned.1.call-start = ((), (), s32[]{:S(2)}) async-start(), calls=%async_computation.20 | async-start | bytes 5242880 | tf_op jit(solution)/shard_map/all_gather | solution.py:954
  92.5 416.3 %reduce-scatter.15.cloned.1.call-start = ((), (), s32[]{:S(2)}) async-start(), calls=%async_computation.21 | async-start | bytes 2359296 | tf_op jit(solution)/shard_map/reduce_scatter | solution.py:1055
  368.8 10.2 copy-start.32
  379.0 3.7 copy-start.33
  402.7 167.6 %all-gather.37.cloned.1.call-start = ((), (), s32[]{:S(2)}) async-start(), calls=%async_computation.33 | async-start | bytes 3538944 | tf_op jit(solution)/shard_map/all_gather | solution.py:911
  415.8 200.0 %reduce-scatter.29.cloned.1.call-start = ((), (), s32[]{:S(2)}) async-start(), calls=%async_computation.28 | async-start | bytes 1310720 | tf_op jit(solution)/shard_map/reduce_scatter | solution.py:928
  419.0 202.1 %reduce-scatter.27.cloned.1.call-start = ((), (), s32[]{:S(2)}) async-start(), calls=%async_computation.27 | async-start | bytes 655360 | tf_op jit(solution)/shard_map/reduce_scatter | solution.py:928
  514.1 147.4 %reduce-scatter.23.cloned.1.call-start = ((), (), s32[]{:S(2)}) async-start(), calls=%async_computation.25 | async-start | bytes 3932160 | tf_op jit(solution)/shard_map/reduce_scatter | solution.py:928
  519.3 182.7 %reduce-scatter.17.cloned.1.call-start = ((), (), s32[]{:S(2)}) async-start(), calls=%async_computation.22 | async-start | bytes 3932160 | tf_op jit(solution)/shard_map/reduce_scatter | solution.py:928
  524.7 205.2 %reduce-scatter.25.cloned.1.call-start = ((), (), s32[]{:S(2)}) async-start(), calls=%async_computation.26 | async-start | bytes 1310720 | tf_op jit(solution)/shard_map/reduce_scatter | solution.py:928
  527.7 249.4 %reduce-scatter.31.cloned.1.call-start = ((), (), s32[]{:S(2)}) async-start(), calls=%async_computation.29 | async-start | bytes 5242880 | tf_op jit(solution)/shard_map/reduce_scatter | solution.py:928
  534.1 290.0 %reduce-scatter.33.cloned.1.call-start = ((), (), s32[]{:S(2)}) async-start(), calls=%async_computation.30 | async-start | bytes 5242880 | tf_op jit(solution)/shard_map/reduce_scatter | solution.py:928
  540.5 330.7 %reduce-scatter.35.cloned.1.call-start = ((), (), s32[]{:S(2)}) async-start(), calls=%async_computation.31 | async-start | bytes 5242880 | tf_op jit(solution)/shard_map/reduce_scatter | solution.py:928
  546.7 368.2 %reduce-scatter.19.cloned.1.call-start = ((), (), s32[]{:S(2)}) async-start(), calls=%async_computation.23 | async-start | bytes 4587520 | tf_op jit(solution)/shard_map/reduce_scatter | solution.py:928
  599.2 6.3 collective-permute-start.1
  612.4 327.0 %reduce-scatter.37.cloned.1.call-start = ((), (), s32[]{:S(2)}) async-start(), calls=%async_computation.34 | async-start | bytes 573440
  614.3 347.8 %reduce-scatter.21.cloned.1.call-start = ((), (), s32[]{:S(2)}) async-start(), calls=%async_computation.24 | async-start | bytes 61440 | tf_op jit(solution)/shard_map/reduce_scatter | solution.py:928
  615.5 571.1 %all-reduce.21.cloned.1.call-start = ((), (), s32[]{:S(2)}) async-start(), calls=%async_computation.35 | async-start | bytes 12582912 | tf_op jit(solution)/shard_map/psum | solution.py:929
  916.9 5.7 copy-start.31
  917.0 5.7 copy-start.41
  922.6 3.4 copy-start.5
  922.6 3.4 copy-start.20
  927.8 12.7 %copy-start.34 = (bf16[512,1792]{1,0:T(8,128)(2,1)S(1)}, bf16[512,1792]{1,0:T(8,128)(2,1)}, u32[]{:S(2)}) copy-start(bf16[512,1792]{1,0:T(8,128)(2,1)} %fusion.38) | copy-start | bytes 5505028
  940.5 4.3 copy-start.2
  940.5 4.3 copy-start.3
  940.5 4.3 copy-start.6
  944.8 8.9 copy-start.1
  (20 other events, 42.7 us)
Sparse Core Ops, SparseCore 0:
  9.6 20.7 all-gather.16
  31.9 33.4 all-gather.22
  67.0 28.5 all-gather.24
  98.1 49.2 all-gather.18
  150.1 63.7 all-gather.34
  215.3 27.0 all-gather.26
  243.9 16.7 all-gather.20
  262.3 34.4 all-gather.28
  298.3 34.4 all-gather.30
  334.3 34.4 all-gather.32
  402.8 105.9 reduce-scatter.14
  510.8 59.4 all-gather.36
  572.8 23.4 reduce-scatter.28
  599.4 21.6 reduce-scatter.26
  623.5 37.9 reduce-scatter.22
  664.1 37.9 reduce-scatter.16
  705.0 24.8 reduce-scatter.24
  732.5 44.5 reduce-scatter.30
  779.6 44.4 reduce-scatter.32
  826.6 44.4 reduce-scatter.34
  873.7 41.2 reduce-scatter.18
  918.2 21.2 reduce-scatter.36
  942.6 19.3 reduce-scatter.20
  967.7 218.8 all-reduce.20

commit v2 on v1

--- a/solution.py
+++ b/solution.py
@@ -56,6 +56,21 @@
     return pltpu.CompilerParams(dimension_semantics=semantics, vmem_limit_bytes=VMEM_LIMIT)
 
 
+def lasting(microseconds):
+    return pl.CostEstimate(flops=int(microseconds * 1.15e9), bytes_accessed=0, transcendentals=0)
+
+
+def without(kernel, at, count):
+    def body(*refs):
+        kernel(*refs[:at], *refs[at + count :])
+
+    return body
+
+
+def unread(arrays):
+    return [pl.BlockSpec(memory_space=pl.ANY)] * len(arrays)
+
+
 def whole(shape):
     return pl.BlockSpec(shape, lambda *_: (0,) * len(shape))
 
@@ -122,6 +137,7 @@
     y_ref,
     sin_ref,
     msg_ref,
+    own_ref,
     dec_ref,
     c_ref,
     xs_ref,
@@ -185,11 +201,14 @@
     @pl.when(c == count - 1)
     def _():
         msg_ref[0:STATE_SIZE, :] = state_ref[...].astype(BF16)
+        own_ref[0:STATE_SIZE, :] = state_ref[...]
         through = jnp.exp(carry_ref[...]) * (end_doc < base).astype(F32)
         low8 = low_half(8)
         for j in range(PAIRS):
             wide = spread(through, j, low8)
-            msg_ref[STATE_SIZE:, tile(j)] = jnp.concatenate([wide, wide], axis=0).astype(BF16)
+            wide = jnp.concatenate([wide, wide], axis=0)
+            msg_ref[STATE_SIZE:, tile(j)] = wide.astype(BF16)
+            own_ref[STATE_SIZE:, tile(j)] = wide
 
 
 def mamba_forward(scalars, edge, mixed, dt_raw, doc, conv_pack, head_pack, skip_wide):
@@ -213,6 +232,7 @@
             by_chunk(MAMBA_INNER),
             pl.BlockSpec((1, STATE_SIZE, MAMBA_INNER), lambda c: (c, 0, 0)),
             whole((MESSAGE_ROWS, MAMBA_INNER)),
+            whole((MESSAGE_ROWS, MAMBA_INNER)),
             by_chunk(LANES),
             by_chunk(LANES),
         ],
@@ -220,6 +240,7 @@
             jax.ShapeDtypeStruct((rows, MAMBA_INNER), F32),
             jax.ShapeDtypeStruct((count, STATE_SIZE, MAMBA_INNER), F32),
             jax.ShapeDtypeStruct((MESSAGE_ROWS, MAMBA_INNER), BF16),
+            jax.ShapeDtypeStruct((MESSAGE_ROWS, MAMBA_INNER), F32),
             jax.ShapeDtypeStruct((rows, LANES), F32),
             jax.ShapeDtypeStruct((rows, LANES), BF16),
         ],
@@ -230,15 +251,26 @@
             pltpu.VMEM((8, LANES), F32),
         ],
         compiler_params=params("arbitrary"),
-        cost_estimate=pl.CostEstimate(
-            flops=rows * MAMBA_INNER * 1024, bytes_accessed=rows * 12000, transcendentals=rows * 4096
-        ),
+        cost_estimate=lasting(13),
         name="mamba_forward",
     )(scalars, edge, mixed, dt_raw, doc, conv_pack, head_pack, skip_wide)
 
 
+QUARTERS = 4
+BLOCK_TILES = 1 + PAIRS // QUARTERS
+
+
+def attn_tile(i):
+    return tile(i * BLOCK_TILES)
+
+
+def gated_tile(j):
+    per = PAIRS // QUARTERS
+    return tile(j // per * BLOCK_TILES + 1 + j % per)
+
+
 def mamba_correct_kernel(
-    y_ref, sin_ref, c_ref, dec_ref, state_ref, z_ref, total_ref, gated_ref, true_ref, edge_ref
+    y_ref, sin_ref, c_ref, dec_ref, state_ref, z_ref, vec0_ref, vec1_ref, total_ref, both_ref, true_ref, edge_ref
 ):
     c = pl.program_id(0)
 
@@ -256,14 +288,16 @@
         y = y_ref[:, tile(j)] + dot_nn(c_mat, state.astype(BF16)) * spread(decay, j, low)
         total_ref[:, tile(j)] = y
         z = z_ref[:, tile(j)]
-        gated_ref[:, tile(j)] = (y * (z * jax.nn.sigmoid(z))).astype(BF16)
+        both_ref[:, gated_tile(j)] = (y * (z * jax.nn.sigmoid(z))).astype(BF16)
         true_ref[0, :, tile(j)] = (
             sin_ref[0, :, tile(j)] + state * spread(before, j, low_row)
         ).astype(BF16)
+    for i, vec_ref in enumerate((vec0_ref, vec0_ref, vec1_ref, vec1_ref)):
+        both_ref[:, attn_tile(i)] = vec_ref[:, tile(i % 2)]
     edge_ref[0:1, :] = decay[CHUNK - 1 : CHUNK, :]
 
 
-def mamba_correct(y, sin, c_mat, decay, state_in, gate_z):
+def mamba_correct(y, sin, c_mat, decay, state_in, gate_z, vec0, vec1):
     rows = y.shape[0]
     count = rows // CHUNK
     by_chunk = lambda width: pl.BlockSpec((CHUNK, width), lambda c: (c, 0))
@@ -278,24 +312,24 @@
             by_chunk(LANES),
             whole((STATE_SIZE, MAMBA_INNER)),
             by_chunk(MAMBA_INNER),
-        ],
-        out_specs=[by_chunk(MAMBA_INNER), by_chunk(MAMBA_INNER), states],
+            by_chunk(2 * LANES),
+            by_chunk(2 * LANES),
+        ],
+        out_specs=[by_chunk(MAMBA_INNER), by_chunk(QUARTERS * BLOCK_TILES * LANES), states],
         out_shape=[
             jax.ShapeDtypeStruct((rows, MAMBA_INNER), F32),
-            jax.ShapeDtypeStruct((rows, MAMBA_INNER), BF16),
+            jax.ShapeDtypeStruct((rows, QUARTERS * BLOCK_TILES * LANES), BF16),
             jax.ShapeDtypeStruct((count, STATE_SIZE, MAMBA_INNER), BF16),
         ],
         scratch_shapes=[pltpu.VMEM((8, LANES), F32)],
         compiler_params=params("arbitrary"),
-        cost_estimate=pl.CostEstimate(
-            flops=rows * MAMBA_INNER * 256, bytes_accessed=rows * 30000, transcendentals=rows * 1536
-        ),
+        cost_estimate=lasting(8.5),
         name="mamba_correct",
-    )(y, sin, c_mat, decay, state_in, gate_z)
+    )(y, sin, c_mat, decay, state_in, gate_z, vec0, vec1)
 
 
 def mamba_gate_back_kernel(
-    gg_ref, z_ref, y_ref, c_ref, dec_ref, dy_ref, gz_ref, gsi_ref, acc_ref
+    both_ref, z_ref, y_ref, c_ref, dec_ref, own_ref, dy_ref, gz_ref, gsi_ref, gsb_ref, gvec_ref, acc_ref
 ):
     c = pl.program_id(0)
 
@@ -310,44 +344,57 @@
         z = z_ref[:, tile(j)]
         sig = jax.nn.sigmoid(z)
         silu = z * sig
-        grad = gg_ref[:, tile(j)]
+        grad = both_ref[:, gated_tile(j)]
         gz_ref[:, tile(j)] = (grad * y_ref[:, tile(j)] * (sig + silu * (1.0 - sig))).astype(BF16)
         dy = (grad * silu).astype(BF16)
         dy_ref[:, tile(j)] = dy
         scaled = (dy.astype(F32) * spread(decay, j, low)).astype(BF16)
         acc_ref[:, tile(j)] += dot_nn(c_turned, scaled)
+    for i in range(QUARTERS):
+        gvec_ref[:, tile(i)] = both_ref[:, attn_tile(i)].astype(BF16)
 
     @pl.when(c == pl.num_programs(0) - 1)
     def _():
-        gsi_ref[...] = acc_ref[...].astype(BF16)
-
-
-def mamba_gate_back(gated_grad, gate_z, total, c_mat, decay):
+        gsi_ref[0:STATE_SIZE, :] = acc_ref[...]
+        gsb_ref[0:STATE_SIZE, :] = acc_ref[...].astype(BF16)
+        gsi_ref[STATE_SIZE:, :] = own_ref[...]
+        gsb_ref[STATE_SIZE:, :] = own_ref[...].astype(BF16)
+
+
+def mamba_gate_back(both_grad, gate_z, total, c_mat, decay, own, tokens=()):
     rows = total.shape[0]
     by_chunk = lambda width: pl.BlockSpec((CHUNK, width), lambda c: (c, 0))
     return pl.pallas_call(
-        mamba_gate_back_kernel,
+        without(mamba_gate_back_kernel, 6, len(tokens)),
         grid=(rows // CHUNK,),
         in_specs=[
-            by_chunk(MAMBA_INNER),
+            by_chunk(QUARTERS * BLOCK_TILES * LANES),
             by_chunk(MAMBA_INNER),
             by_chunk(MAMBA_INNER),
             by_chunk(LANES),
             by_chunk(LANES),
-        ],
-        out_specs=[by_chunk(MAMBA_INNER), by_chunk(MAMBA_INNER), whole((STATE_SIZE, MAMBA_INNER))],
+            pl.BlockSpec((16, MAMBA_INNER), lambda c: (STATE_SIZE // 16, 0)),
+            *unread(tokens),
+        ],
+        out_specs=[
+            by_chunk(MAMBA_INNER),
+            by_chunk(MAMBA_INNER),
+            whole((MESSAGE_ROWS, MAMBA_INNER)),
+            whole((MESSAGE_ROWS, MAMBA_INNER)),
+            by_chunk(QUARTERS * LANES),
+        ],
         out_shape=[
             jax.ShapeDtypeStruct((rows, MAMBA_INNER), BF16),
             jax.ShapeDtypeStruct((rows, MAMBA_INNER), BF16),
-            jax.ShapeDtypeStruct((STATE_SIZE, MAMBA_INNER), BF16),
+            jax.ShapeDtypeStruct((MESSAGE_ROWS, MAMBA_INNER), F32),
+            jax.ShapeDtypeStruct((MESSAGE_ROWS, MAMBA_INNER), BF16),
+            jax.ShapeDtypeStruct((rows, QUARTERS * LANES), BF16),
         ],
         scratch_shapes=[pltpu.VMEM((STATE_SIZE, MAMBA_INNER), F32)],
         compiler_params=params("arbitrary"),
-        cost_estimate=pl.CostEstimate(
-            flops=rows * MAMBA_INNER * 256, bytes_accessed=rows * 25000, transcendentals=rows * 1536
-        ),
+        cost_estimate=lasting(7.5),
         name="mamba_gate_back",
-    )(gated_grad, gate_z, total, c_mat, decay)
+    )(both_grad, gate_z, total, c_mat, decay, own, *tokens)
 
 
 def picks(pair):
@@ -530,13 +577,26 @@
 
 
 def mamba_back(
-    scalars, edge, mixed, dt_raw, doc, doc_row, conv_pack, head_pack, skip_wide, dy, y, sin, ds_end
+    scalars,
+    edge,
+    mixed,
+    dt_raw,
+    doc,
+    doc_row,
+    conv_pack,
+    head_pack,
+    skip_wide,
+    dy,
+    y,
+    sin,
+    ds_end,
+    tokens=(),
 ):
     rows = mixed.shape[0]
     count = rows // CHUNK
     by_chunk = lambda width: pl.BlockSpec((CHUNK, width), lambda i: (count - 1 - i, 0))
     return pl.pallas_call(
-        mamba_back_kernel,
+        without(mamba_back_kernel, 13, len(tokens)),
         grid=(count,),
         in_specs=[
             pl.BlockSpec(memory_space=pltpu.SMEM),
@@ -552,6 +612,7 @@
             by_chunk(MAMBA_INNER),
             pl.BlockSpec((1, STATE_SIZE, MAMBA_INNER), lambda i: (count - 1 - i, 0, 0)),
             whole((STATE_SIZE, MAMBA_INNER)),
+            *unread(tokens),
         ],
         out_specs=[
             by_chunk(CHANNELS),
@@ -578,11 +639,61 @@
             pltpu.VMEM((8, MAMBA_INNER), F32),
         ],
         compiler_params=params("arbitrary"),
-        cost_estimate=pl.CostEstimate(
-            flops=rows * MAMBA_INNER * 3072, bytes_accessed=rows * 20000, transcendentals=rows * 4096
-        ),
+        cost_estimate=lasting(25),
         name="mamba_back",
-    )(scalars, edge, mixed, dt_raw, doc, doc_row, conv_pack, head_pack, skip_wide, dy, y, sin, ds_end)
+    )(
+        scalars,
+        edge,
+        mixed,
+        dt_raw,
+        doc,
+        doc_row,
+        conv_pack,
+        head_pack,
+        skip_wide,
+        dy,
+        y,
+        sin,
+        ds_end,
+        *tokens,
+    )
+
+
+def scan_step_kernel(flag_ref, total_ref, seen_ref, got_ref, new_ref, send_ref, out_ref):
+    first = flag_ref[0] == 1
+    rows = slice(0, STATE_SIZE)
+    rest = slice(STATE_SIZE, MESSAGE_ROWS)
+    one = STATE_SIZE
+    for j in range(PAIRS):
+        total, seen = total_ref[:, tile(j)], seen_ref[:, tile(j)]
+        got = got_ref[:, tile(j)].astype(F32)
+        mine, theirs = total[one : one + 1], got[one : one + 1]
+        state = jnp.where(first, mine * got[rows] + total[rows], theirs * total[rows] + got[rows])
+        new_ref[rows, tile(j)] = state
+        send_ref[rows, tile(j)] = state.astype(BF16)
+        factor = total[rest] * got[rest]
+        new_ref[rest, tile(j)] = factor
+        send_ref[rest, tile(j)] = factor.astype(BF16)
+        passed = seen[rows] + seen[one : one + 1] * got[rows]
+        out_ref[rows, tile(j)] = jnp.where(first, passed, seen[rows])
+        out_ref[rest, tile(j)] = jnp.where(first, seen[rest] * got[rest], seen[rest])
+
+
+def scan_step(first, total, seen, got):
+    shape = (MESSAGE_ROWS, MAMBA_INNER)
+    return pl.pallas_call(
+        scan_step_kernel,
+        in_specs=[pl.BlockSpec(memory_space=pltpu.SMEM)] + [whole(shape)] * 3,
+        out_specs=[whole(shape)] * 3,
+        out_shape=[
+            jax.ShapeDtypeStruct(shape, F32),
+            jax.ShapeDtypeStruct(shape, BF16),
+            jax.ShapeDtypeStruct(shape, F32),
+        ],
+        compiler_params=pltpu.CompilerParams(vmem_limit_bytes=VMEM_LIMIT),
+        cost_estimate=lasting(2.5),
+        name="scan_step",
+    )(first.astype(jnp.int32).reshape(1), total, seen, got)
 
 
 def half_roll(x):
@@ -628,8 +739,8 @@
 def attend_kernel(
     sc_ref, q_ref, kv_ref, doc_ref, vec_ref, norm_ref, lse_ref, qz_ref, max_ref, sum_ref, acc_ref
 ):
-    at = pl.program_id(1)
-    tiles = pl.num_programs(1)
+    at = pl.program_id(0)
+    tiles = pl.num_programs(0)
     start, last_doc, block_lo, block_hi = tile_bounds(sc_ref, at, tiles)
     for g, part in enumerate(stack_low(q_ref[...].astype(F32), QUERY_TILE)):
         qz_ref[g * QUERY_TILE : (g + 1) * QUERY_TILE, :] = part.astype(BF16)
@@ -639,7 +750,8 @@
     doc_row = jnp.concatenate([doc_ref[0:1, :]] * GROUP, axis=1)
 
     def visit(block, masked):
-        kv = kv_ref[pl.ds(pl.multiple_of(block * KEY_BLOCK, KEY_BLOCK), KEY_BLOCK), :]
+        at_rows = sc_ref[2 * tiles + 1 + block] * KEY_BLOCK
+        kv = kv_ref[pl.ds(pl.multiple_of(at_rows, KEY_BLOCK), KEY_BLOCK), :]
         scores = dot_nt(kv, qz_ref[...])
         if masked:
             scores = jnp.where(visible_mask(block, start, doc_row), scores, MASK_FILLER)
@@ -665,7 +777,7 @@
         return carry
 
     lax.fori_loop(block_lo, block_hi, one, 0)
-    lse_ref[0, 0] = jnp.broadcast_to(max_ref[0:1, :] + jnp.log(sum_ref[0:1, :]), lse_ref.shape[2:])
+    lse_ref[0] = jnp.broadcast_to(max_ref[0:1, :] + jnp.log(sum_ref[0:1, :]), lse_ref.shape[1:])
     scaled = acc_ref[...] / sum_ref[0:1, :]
     low = low_half(QUERY_TILE)
     for a in range(2):
@@ -676,30 +788,28 @@
         vec_ref[:, tile(a)] = both.astype(BF16)
 
 
-def attend(scalars, q, kv, doc_row):
+def attend(scalars, q, kv, doc_row, head, tokens=()):
     rows = q.shape[0]
     length = kv.shape[0]
     tiles = rows // QUERY_TILE
     lanes = GROUP * QUERY_TILE
     width = GROUP * HEAD_SIZE
+    by_tile = pl.BlockSpec((QUERY_TILE, width), lambda t: (t, 0))
     return pl.pallas_call(
-        attend_kernel,
-        grid=(KEY_VALUE_HEADS, tiles),
+        without(attend_kernel, 4, len(tokens)),
+        grid=(tiles,),
         in_specs=[
             pl.BlockSpec(memory_space=pltpu.SMEM),
-            pl.BlockSpec((QUERY_TILE, width), lambda j, t: (t, j)),
-            pl.BlockSpec((length, LANES), lambda j, t: (0, j)),
-            pl.BlockSpec((8, QUERY_TILE), lambda j, t: (0, t)),
-        ],
-        out_specs=[
-            pl.BlockSpec((QUERY_TILE, width), lambda j, t: (t, j)),
-            pl.BlockSpec((QUERY_TILE, width), lambda j, t: (t, j)),
-            pl.BlockSpec((1, 1, 8, lanes), lambda j, t: (j, t, 0, 0)),
-        ],
+            pl.BlockSpec((QUERY_TILE, width), lambda t: (t, head)),
+            whole((length, LANES)),
+            pl.BlockSpec((8, QUERY_TILE), lambda t: (0, t)),
+            *unread(tokens),
+        ],
+        out_specs=[by_tile, by_tile, pl.BlockSpec((1, 8, lanes), lambda t: (t, 0, 0))],
         out_shape=[
-            jax.ShapeDtypeStruct((rows, QUERY_HEADS * HEAD_SIZE), BF16),
-            jax.ShapeDtypeStruct((rows, QUERY_HEADS * HEAD_SIZE), F32),
-            jax.ShapeDtypeStruct((KEY_VALUE_HEADS, tiles, 8, lanes), F32),
+            jax.ShapeDtypeStruct((rows, width), BF16),
+            jax.ShapeDtypeStruct((rows, width), F32),
+            jax.ShapeDtypeStruct((tiles, 8, lanes), F32),
         ],
         scratch_shapes=[
             pltpu.VMEM((lanes, LANES), BF16),
@@ -707,21 +817,17 @@
             pltpu.VMEM((8, lanes), F32),
             pltpu.VMEM((LANES, lanes), F32),
         ],
-        compiler_params=params("arbitrary", "arbitrary"),
-        cost_estimate=pl.CostEstimate(
-            flops=rows * length * 2048,
-            bytes_accessed=length * 512 + rows * 6000,
-            transcendentals=rows * length * 4,
-        ),
+        compiler_params=params("arbitrary"),
+        cost_estimate=lasting(22),
         name="attend",
-    )(scalars, q, kv, doc_row)
+    )(scalars, q, kv, doc_row, *tokens)
 
 
 def attend_back_kernel(
     sc_ref, q_ref, do_ref, norm_ref, lse_ref, kv_ref, doc_ref, dq_ref, dkv_ref, qd_ref, dkv_acc, dq_acc
 ):
-    at = pl.program_id(1)
-    tiles = pl.num_programs(1)
+    at = pl.program_id(0)
+    tiles = pl.num_programs(0)
     lanes = GROUP * QUERY_TILE
     start, last_doc, block_lo, block_hi = tile_bounds(sc_ref, at, tiles)
 
@@ -740,12 +846,13 @@
         deltas.append(jnp.sum(turned[0:HEAD_SIZE], axis=0, keepdims=True))
         deltas.append(jnp.sum(turned[HEAD_SIZE:], axis=0, keepdims=True))
     delta = jnp.concatenate(deltas, axis=1)
-    lse = lse_ref[0, 0, 0:1, :]
+    lse = lse_ref[0, 0:1, :]
     dq_acc[...] = jnp.zeros_like(dq_acc)
     doc_row = jnp.concatenate([doc_ref[0:1, :]] * GROUP, axis=1)
 
     def visit(block, masked):
-        at_rows = pl.ds(pl.multiple_of(block * KEY_BLOCK, KEY_BLOCK), KEY_BLOCK)
+        first_row = sc_ref[2 * tiles + 1 + block] * KEY_BLOCK
+        at_rows = pl.ds(pl.multiple_of(first_row, KEY_BLOCK), KEY_BLOCK)
         kv = kv_ref[at_rows, :]
         scores = dot_nt(kv, qd_ref[0:lanes, :])
         prob = jnp.exp(scores - lse)
@@ -784,43 +891,41 @@
         dkv_ref[...] = dkv_acc[...].astype(BF16)
 
 
-def attend_back(scalars, q, grad, norm, lse, kv, doc_row):
+def attend_back(scalars, q, grad, norm, lse, kv, doc_row, head, tokens=()):
     rows = q.shape[0]
     length = kv.shape[0]
     tiles = rows // QUERY_TILE
     lanes = GROUP * QUERY_TILE
     width = GROUP * HEAD_SIZE
-    by_tile = pl.BlockSpec((QUERY_TILE, width), lambda j, t: (t, j))
+    by_tile = pl.BlockSpec((QUERY_TILE, width), lambda t: (t, 0))
+    by_head = pl.BlockSpec((QUERY_TILE, width), lambda t: (t, head))
     return pl.pallas_call(
-        attend_back_kernel,
-        grid=(KEY_VALUE_HEADS, tiles),
+        without(attend_back_kernel, 7, len(tokens)),
+        grid=(tiles,),
         in_specs=[
             pl.BlockSpec(memory_space=pltpu.SMEM),
+            by_head,
+            by_head,
             by_tile,
-            by_tile,
-            by_tile,
-            pl.BlockSpec((1, 1, 8, lanes), lambda j, t: (j, t, 0, 0)),
-            pl.BlockSpec((length, LANES), lambda j, t: (0, j)),
-            pl.BlockSpec((8, QUERY_TILE), lambda j, t: (0, t)),
-        ],
-        out_specs=[by_tile, pl.BlockSpec((length, LANES), lambda j, t: (0, j))],
+            pl.BlockSpec((1, 8, lanes), lambda t: (t, 0, 0)),
+            whole((length, LANES)),
+            pl.BlockSpec((8, QUERY_TILE), lambda t: (0, t)),
+            *unread(tokens),
+        ],
+        out_specs=[by_tile, whole((length, LANES))],
         out_shape=[
-            jax.ShapeDtypeStruct((rows, QUERY_HEADS * HEAD_SIZE), F32),
-            jax.ShapeDtypeStruct((length, KEY_VALUE_HEADS * LANES), BF16),
+            jax.ShapeDtypeStruct((rows, width), F32),
+            jax.ShapeDtypeStruct((length, LANES), BF16),
         ],
         scratch_shapes=[
             pltpu.VMEM((2 * lanes, LANES), BF16),
             pltpu.VMEM((length, LANES), F32),
             pltpu.VMEM((LANES, lanes), F32),
         ],
-        compiler_params=params("arbitrary", "arbitrary"),
-        cost_estimate=pl.CostEstimate(
-            flops=rows * length * 5120,
-            bytes_accessed=length * 1024 + rows * 8000,
-            transcendentals=rows * length * 4,
-        ),
+        compiler_params=params("arbitrary"),
+        cost_estimate=lasting(26),
         name="attend_back",
-    )(scalars, q, grad, norm, lse, kv, doc_row)
+    )(scalars, q, grad, norm, lse, kv, doc_row, *tokens)
 
 
 def turn_lanes(x, cosine, sine):
@@ -830,7 +935,7 @@
     return x * cosine + other * sine
 
 
-def rope_kernel(q_in_ref, kv_in_ref, cos_ref, sin_ref, q_ref, kv_ref):
+def rope_kernel(q_in_ref, kv_in_ref, cos_ref, sin_ref, q_ref, kv0_ref, kv1_ref):
     cosine, sine = cos_ref[...], sin_ref[...]
     scale = 1.0 / math.sqrt(HEAD_SIZE)
     for i in range(QUERY_HEADS * HEAD_SIZE // LANES):
@@ -839,8 +944,8 @@
     keys = turn_lanes(kv_in_ref[:, tile(0)], cosine, sine)
     values = kv_in_ref[:, tile(1)]
     low = iota(keys.shape, 1) < HEAD_SIZE
-    kv_ref[:, tile(0)] = jnp.where(low, keys, half_roll(values)).astype(BF16)
-    kv_ref[:, tile(1)] = jnp.where(low, half_roll(keys), values).astype(BF16)
+    kv0_ref[...] = jnp.where(low, keys, half_roll(values)).astype(BF16)
+    kv1_ref[...] = jnp.where(low, half_roll(keys), values).astype(BF16)
 
 
 def rope(q_raw, kv_raw, cosine, sine):
@@ -849,37 +954,402 @@
         rope_kernel,
         out_shape=[
             jax.ShapeDtypeStruct((rows, QUERY_HEADS * HEAD_SIZE), BF16),
-            jax.ShapeDtypeStruct((rows, KEY_VALUE_HEADS * LANES), BF16),
+            jax.ShapeDtypeStruct((rows, LANES), BF16),
+            jax.ShapeDtypeStruct((rows, LANES), BF16),
         ],
         compiler_params=pltpu.CompilerParams(vmem_limit_bytes=VMEM_LIMIT),
+        cost_estimate=lasting(3),
         name="rope",
     )(q_raw, kv_raw, cosine, sine)
 
 
-def rope_back_kernel(dq_ref, dkv_ref, cos_ref, sin_ref, gq_ref, gkv_ref):
+def rope_back_kernel(dq0_ref, dq1_ref, dkv0_ref, dkv1_ref, cos_ref, sin_ref, grad_ref):
     cosine, sine = cos_ref[...], -sin_ref[...]
-    for i in range(QUERY_HEADS * HEAD_SIZE // LANES):
-        gq_ref[:, tile(i)] = turn_lanes(dq_ref[:, tile(i)], cosine, sine).astype(BF16)
-    first = dkv_ref[:, tile(0)].astype(F32)
-    second = dkv_ref[:, tile(1)].astype(F32)
+    for head, dq_ref in enumerate((dq0_ref, dq1_ref)):
+        for i in range(2):
+            turned = turn_lanes(dq_ref[:, tile(i)], cosine, sine)
+            grad_ref[:, tile(2 * head + i)] = turned.astype(BF16)
+    first = dkv0_ref[...].astype(F32)
+    second = dkv1_ref[...].astype(F32)
     low = iota(first.shape, 1) < HEAD_SIZE
     keys = jnp.where(low, first, half_roll(second))
     values = jnp.where(low, half_roll(first), second)
-    gkv_ref[:, tile(0)] = turn_lanes(keys, cosine, sine).astype(BF16)
-    gkv_ref[:, tile(1)] = values.astype(BF16)
-
-
-def rope_back(dq, dkv, cosine, sine):
-    rows = dq.shape[0]
+    grad_ref[:, tile(4)] = turn_lanes(keys, cosine, sine).astype(BF16)
+    grad_ref[:, tile(5)] = values.astype(BF16)
+
+
+def rope_back(dq0, dq1, dkv0, dkv1, cosine, sine):
+    rows = dq0.shape[0]
     return pl.pallas_call(
         rope_back_kernel,
-        out_shape=[
-            jax.ShapeDtypeStruct((rows, QUERY_HEADS * HEAD_SIZE), BF16),
-            jax.ShapeDtypeStruct((rows, KEY_VALUE_HEADS * LANES), BF16),
-        ],
+        out_shape=jax.ShapeDtypeStruct(
+            (rows, QUERY_HEADS * HEAD_SIZE + KEY_VALUE_HEADS * LANES), BF16
+        ),
         compiler_params=pltpu.CompilerParams(vmem_limit_bytes=VMEM_LIMIT),
+        cost_estimate=lasting(3),
         name="rope_back",
-    )(dq, dkv, cosine, sine)
+    )(dq0, dq1, dkv0, dkv1, cosine, sine)
+
+
+DEVICES = ("ctx", "fsdp")
+
+
+def swap(block, axis, bit):
+    count, width = lax.axis_size("ctx"), lax.axis_size("fsdp")
+    partner = lambda c, f: (c ^ bit) * width + f if axis == "ctx" else c * width + (f ^ bit)
+    route = [(c * width + f, partner(c, f)) for c in range(count) for f in range(width)]
+    return lax.ppermute(block, DEVICES, route)
+
+
+def take_rows(block, index, rows):
+    return lax.dynamic_slice_in_dim(block, index * rows, rows, 0)
+
+
+def after_kernel(*refs):
+    pass
+
+
+def after(block, *others):
+    return pl.pallas_call(
+        after_kernel,
+        in_specs=[pl.BlockSpec(memory_space=pl.ANY)] * (1 + len(others)),
+        out_specs=pl.BlockSpec(memory_space=pl.ANY),
+        out_shape=jax.ShapeDtypeStruct(block.shape, block.dtype),
+        input_output_aliases={0: 0},
+        name="after",
+    )(block, *others)
+
+
+def place_kernel(parts, tokens, at_ref, *refs):
+    count = 1 + max(part[0] for part in parts)
+    outs = 1 + max(part[5] for part in parts)
+    pieces, refs = refs[:count], refs[count + tokens :]
+    out_refs, held = refs[:outs], refs[outs:-1]
+    sems = refs[-1]
+    come = [pltpu.make_async_copy(pieces[i], held[i], sems.at[i]) for i in range(count)]
+    for copy in come:
+        copy.start()
+    leave = []
+    for i in range(count):
+        come[i].wait()
+        for k, (piece, row, rows, col, cols, out) in enumerate(parts):
+            if piece == i:
+                here = held[i].at[pl.ds(row, rows), pl.ds(col, cols)]
+                to = out_refs[out].at[pl.ds(pl.multiple_of(at_ref[k], 16), rows), :]
+                leave.append(pltpu.make_async_copy(here, to, sems.at[count + k]))
+                leave[-1].start()
+    for copy in leave:
+        copy.wait()
+
+
+def place(pieces, parts, offsets, shapes, tokens=()):
+    size = sum(math.prod(piece.shape) for piece in pieces) * 4
+    return pl.pallas_call(
+        functools.partial(place_kernel, tuple(parts), len(tokens)),
+        in_specs=[pl.BlockSpec(memory_space=pltpu.SMEM)]
+        + [pl.BlockSpec(memory_space=pl.ANY)] * (len(pieces) + len(tokens)),
+        out_specs=[pl.BlockSpec(memory_space=pl.ANY)] * len(shapes),
+        out_shape=[jax.ShapeDtypeStruct(shape, BF16) for shape in shapes],
+        scratch_shapes=[pltpu.VMEM(piece.shape, BF16) for piece in pieces]
+        + [pltpu.SemaphoreType.DMA((len(pieces) + len(parts),))],
+        compiler_params=pltpu.CompilerParams(vmem_limit_bytes=VMEM_LIMIT),
+        cost_estimate=lasting(1 + size / 3e6),
+        name="place",
+    )(jnp.stack(offsets).astype(jnp.int32), *pieces, *tokens)
+
+
+def move(block, axis, bit, start=(), arrive=()):
+    sent = after(block, *start) if start else block
+    got = swap(sent, axis, bit)
+    return sent, after(got, *arrive) if arrive else got
+
+
+def send_x(shard, extra=0):
+    side = lax.axis_index("ctx") % 2
+    rows = shard.shape[0] - extra
+    sent = take_rows(shard[:rows], side, rows // 2)
+    return jnp.concatenate([sent, shard[rows:]], axis=0) if extra else sent
+
+
+def collect(shard, near, extra=0, arrive=()):
+    rank, ranks = lax.axis_index("fsdp"), lax.axis_size("fsdp")
+    side = lax.axis_index("ctx") % 2
+    rows, width = shard.shape[0] - extra, shard.shape[1]
+    half = rows // 2
+    _, far = move(near[:half] if extra else near, "ctx", 1, (), arrive)
+    _, near_other = move(near, "fsdp", 1, (), arrive)
+    pieces = [shard, swap(shard, "fsdp", 1), near, near_other, far, swap(far, "fsdp", 1)]
+    whose = [rank, rank ^ 1, rank ^ 2, rank ^ 3, rank ^ 2, rank ^ 3]
+    parts, offsets = [], []
+    for k in range(6):
+        size = rows if k < 2 else half
+        parts.append((k, 0, size, 0, width, 0))
+        offsets.append(whose[k] * rows + (0, 0, side, side, 1 - side, 1 - side)[k] * half)
+        if extra and k < 4:
+            parts.append((k, size, extra, 0, width, 1))
+            offsets.append(whose[k] * extra)
+    shapes = [(ranks * rows, width)] + ([(ranks * extra, width)] if extra else [])
+    return place(pieces, parts, offsets, shapes)
+
+
+def collect_whole(shard, other, near, columns, tokens=(), arrive=()):
+    rank, ranks = lax.axis_index("fsdp"), lax.axis_size("fsdp")
+    rows = shard.shape[0]
+    pieces = [shard, other, near, move(near, "fsdp", 1, (), arrive)[1]]
+    parts, offsets, shapes = [], [], {}
+    for k, piece in enumerate((0, 1, 2, 3)):
+        at = 0
+        for width, out, shard_rows, first in columns:
+            parts.append((piece, 0, rows, at, width, out))
+            offsets.append((rank ^ k) * shard_rows + first)
+            shapes[out] = (ranks * shard_rows, width)
+            at += width
+    return place(pieces, parts, offsets, [shapes[out] for out in sorted(shapes)], tokens)
+
+
+def own_order(block):
+    rank = lax.axis_index("fsdp")
+    width = block.shape[1] // 4
+    return [lax.dynamic_slice_in_dim(block, (rank ^ k) * width, width, 1) for k in (0, 2, 1, 3)]
+
+
+class Reduction:
+    def __init__(self, left, grad, more=None):
+        self.left, self.grad, self.more = left, grad, more
+        _, _, by_core, by_both = left
+        sent = dot_tn(jnp.concatenate([by_core, by_both], axis=1), grad)
+        if more:
+            sent = sent + jnp.concatenate(more[2:], axis=0)
+        self.sent, self.got = move(sent.astype(BF16), "fsdp", 1)
+
+    def over_x(self, start=(), arrive=()):
+        own, by_x, _, _ = self.left
+        rows = own.shape[1]
+        self.near = self.got[:rows]
+        sent = dot_tn(by_x, self.grad) + self.got[rows:].astype(F32)
+        if self.more:
+            sent = sent + self.more[1]
+        sent = sent.astype(BF16)
+        self.sent, self.got = move(sent, "fsdp", 2, start, arrive)
+
+    def halve(self, bit, start, arrive):
+        side = (lax.axis_index("ctx") // bit) % 2
+        half = self.own.shape[0] // 2
+        self.kept = take_rows(self.own, side, half)
+        sent = take_rows(self.own, 1 - side, half).astype(BF16)
+        self.sent, self.got = move(sent, "ctx", bit, start, arrive)
+
+    def add_x(self):
+        self.own = dot_tn(self.left[0], self.grad) + self.near.astype(F32) + self.got.astype(F32)
+        if self.more:
+            self.own = self.own + self.more[0]
+
+    def over_y(self, start=(), arrive=()):
+        self.add_x()
+        self.halve(1, start, arrive)
+
+    def over_z(self, start=(), arrive=()):
+        self.own = self.kept + self.got.astype(F32)
+        self.halve(2, start, arrive)
+
+    def rest(self, start=(), arrive=()):
+        self.own = (self.kept + self.got.astype(F32)).astype(BF16)
+        bit = 4
+        while bit < lax.axis_size("ctx"):
+            self.sent, self.got = move(self.own, "ctx", bit, start, arrive)
+            self.own = (self.own.astype(F32) + self.got.astype(F32)).astype(BF16)
+            bit *= 2
+
+    def join(self, bit, start=()):
+        side = (lax.axis_index("ctx") // bit) % 2
+        self.sent, other = move(self.own, "ctx", bit, start)
+        self.own = jnp.concatenate(
+            [jnp.where(side == 0, self.own, other), jnp.where(side == 0, other, self.own)], axis=0
+        )
+
+    def result(self, z_start=(), y_start=()):
+        self.join(2, z_start)
+        self.join(1, y_start)
+        return self.own.astype(F32)
+
+
+def ctx_bits():
+    bits = [1]
+    while 2 * bits[-1] < lax.axis_size("ctx"):
+        bits.append(2 * bits[-1])
+    return bits
+
+
+def spread_order():
+    apart = jnp.arange(lax.axis_size("ctx"), dtype=jnp.int32) ^ lax.axis_index("ctx")
+    where = jnp.zeros_like(apart)
+    for k, bit in enumerate(reversed(ctx_bits())):
+        where += ((apart // bit) % 2) << k
+    return where
+
+
+class Spread:
+    def __init__(self, block):
+        self.block, self.bits = block, ctx_bits()
+
+    def step(self, arrive=()):
+        _, got = move(self.block, "ctx", self.bits.pop(), (), arrive)
+        self.block = jnp.concatenate([self.block, got], axis=0)
+
+    def finish(self, arrive=()):
+        while self.bits:
+            self.step(arrive)
+        return self.block
+
+
+class BlockSums:
+    def __init__(self, blocks):
+        self.blocks, self.bits = blocks, ctx_bits()
+
+    def step(self, start=(), arrive=()):
+        half = self.blocks.shape[0] // 2
+        bit = self.bits.pop(0)
+        self.sent, got = move(self.blocks[half:], "ctx", bit, start, arrive)
+        self.blocks = (self.blocks[:half].astype(F32) + got.astype(F32)).astype(BF16)
+
+    def finish(self, start=()):
+        while self.bits:
+            self.step(start)
+        return self.blocks
+
+
+def stretches_of(shapes, rows):
+    found, at = [], 0
+    for index, (height, width) in enumerate(shapes):
+        for first in range(0, height, rows):
+            found.append((index, first, at))
+            at += width
+    return found, at
+
+
+def split_kernel(count, side_ref, *refs):
+    owns, (kept_ref, sent_ref) = refs[:count], refs[count:]
+    half = kept_ref.shape[0]
+    found, _ = stretches_of([own.shape for own in owns], 2 * half)
+    mine = pl.multiple_of(side_ref[0] * half, half)
+    theirs = pl.multiple_of((1 - side_ref[0]) * half, half)
+    for index, first, at in found:
+        own = owns[index]
+        columns = slice(at, at + own.shape[1])
+        kept_ref[:, columns] = own[pl.ds(first + mine, half), :]
+        sent_ref[:, columns] = own[pl.ds(first + theirs, half), :]
+
+
+def split_pack(side, owns):
+    rows = min(own.shape[0] for own in owns)
+    _, width = stretches_of([own.shape for own in owns], rows)
+    shape = (rows // 2, width)
+    return pl.pallas_call(
+        functools.partial(split_kernel, len(owns)),
+        in_specs=[pl.BlockSpec(memory_space=pltpu.SMEM)] + [whole(own.shape) for own in owns],
+        out_specs=[whole(shape)] * 2,
+        out_shape=[jax.ShapeDtypeStruct(shape, BF16)] * 2,
+        compiler_params=pltpu.CompilerParams(vmem_limit_bytes=VMEM_LIMIT),
+        cost_estimate=lasting(3),
+        name="split",
+    )(side.reshape(1), *owns)
+
+
+def fold_kernel(side_ref, kept_ref, got_ref, new_ref, sent_ref):
+    half = new_ref.shape[0]
+    mine = pl.ds(pl.multiple_of(side_ref[0] * half, half), half)
+    theirs = pl.ds(pl.multiple_of((1 - side_ref[0]) * half, half), half)
+    new_ref[...] = (kept_ref[mine, :].astype(F32) + got_ref[mine, :].astype(F32)).astype(BF16)
+    sent_ref[...] = (kept_ref[theirs, :].astype(F32) + got_ref[theirs, :].astype(F32)).astype(BF16)
+
+
+def fold_pack(side, kept, got):
+    shape = (kept.shape[0] // 2, kept.shape[1])
+    return pl.pallas_call(
+        fold_kernel,
+        in_specs=[pl.BlockSpec(memory_space=pltpu.SMEM)] + [whole(kept.shape)] * 2,
+        out_specs=[whole(shape)] * 2,
+        out_shape=[jax.ShapeDtypeStruct(shape, BF16)] * 2,
+        compiler_params=pltpu.CompilerParams(vmem_limit_bytes=VMEM_LIMIT),
+        cost_estimate=lasting(2),
+        name="fold",
+    )(side.reshape(1), kept, got)
+
+
+def join_kernel(side_ref, own_ref, got_ref, out_ref):
+    half = own_ref.shape[0]
+    out_ref[pl.ds(pl.multiple_of(side_ref[0] * half, half), half), :] = own_ref[...]
+    out_ref[pl.ds(pl.multiple_of((1 - side_ref[0]) * half, half), half), :] = got_ref[...]
+
+
+def join_pack(side, own, got):
+    shape = (2 * own.shape[0], own.shape[1])
+    return pl.pallas_call(
+        join_kernel,
+        in_specs=[pl.BlockSpec(memory_space=pltpu.SMEM)] + [whole(own.shape)] * 2,
+        out_specs=whole(shape),
+        out_shape=jax.ShapeDtypeStruct(shape, BF16),
+        compiler_params=pltpu.CompilerParams(vmem_limit_bytes=VMEM_LIMIT),
+        cost_estimate=lasting(2),
+        name="join",
+    )(side.reshape(1), own, got)
+
+
+def unpack_kernel(parts, side_ref, own_ref, got_ref, *out_refs):
+    half = own_ref.shape[0]
+    mine = pl.multiple_of(side_ref[0] * half, half)
+    theirs = pl.multiple_of((1 - side_ref[0]) * half, half)
+    for out, first, at, skip, width in parts:
+        columns = slice(at, at + width)
+        to = slice(skip, skip + width)
+        out_refs[out][pl.ds(first + mine, half), to] = own_ref[:, columns].astype(F32)
+        out_refs[out][pl.ds(first + theirs, half), to] = got_ref[:, columns].astype(F32)
+
+
+def unpack(side, own, got, shapes):
+    rows = 2 * own.shape[0]
+    found, _ = stretches_of(shapes, rows)
+    parts = [(index, first, at, 0, shapes[index][1]) for index, first, at in found]
+    return pl.pallas_call(
+        functools.partial(unpack_kernel, parts),
+        in_specs=[pl.BlockSpec(memory_space=pltpu.SMEM)] + [whole(own.shape)] * 2,
+        out_specs=[whole(shape) for shape in shapes],
+        out_shape=[jax.ShapeDtypeStruct(shape, F32) for shape in shapes],
+        compiler_params=pltpu.CompilerParams(vmem_limit_bytes=VMEM_LIMIT),
+        cost_estimate=lasting(4),
+        name="unpack",
+    )(side.reshape(1), own, got)
+
+
+class Pack:
+    def __init__(self, owns):
+        self.shapes = [own.shape for own in owns]
+        self.owns = owns
+
+    def side(self, bit):
+        return (lax.axis_index("ctx") // bit) % 2
+
+    def over_y(self, start=(), arrive=()):
+        self.kept, sent = split_pack(self.side(1), self.owns)
+        self.sent, self.got = move(sent, "ctx", 1, start, arrive)
+
+    def over_z(self, start=(), arrive=()):
+        self.kept, sent = fold_pack(self.side(2), self.kept, self.got)
+        self.sent, self.got = move(sent, "ctx", 2, start, arrive)
+
+    def rest(self, start=(), arrive=()):
+        self.own = (self.kept.astype(F32) + self.got.astype(F32)).astype(BF16)
+        for bit in ctx_bits()[2:]:
+            self.sent, self.got = move(self.own, "ctx", bit, start, arrive)
+            self.own = (self.own.astype(F32) + self.got.astype(F32)).astype(BF16)
+
+    def back_z(self, start=(), arrive=()):
+        self.sent, got = move(self.own, "ctx", 2, start, arrive)
+        self.own = join_pack(self.side(2), self.own, got)
+
+    def back_y(self, start=(), arrive=()):
+        self.sent, got = move(self.own, "ctx", 1, start, arrive)
+        return unpack(self.side(1), self.own, got, self.shapes)
 
 
 def shift_along(block, axis, distance):
@@ -893,27 +1363,26 @@
     return jnp.max(jnp.where(reached, starts[None, :], -1), axis=1)
 
 
-def state_entering(message, axis):
-    place = lax.axis_index(axis)
-    gathered = lax.all_gather(message, axis)
-    state = jnp.zeros((STATE_SIZE, MAMBA_INNER), F32)
-    for i in range(lax.axis_size(axis)):
-        through = gathered[i, STATE_SIZE : STATE_SIZE + 1].astype(F32)
-        state = jnp.where(
-            i < place, through * state + gathered[i, :STATE_SIZE].astype(F32), state
-        )
-    return state, gathered[:, STATE_SIZE : STATE_SIZE + 1]
-
-
-def gradient_entering(grad_state, through_all, axis):
-    place = lax.axis_index(axis)
-    devices = lax.axis_size(axis)
-    gathered = lax.all_gather(grad_state, axis)
-    state = jnp.zeros((STATE_SIZE, MAMBA_INNER), F32)
-    for i in reversed(range(devices)):
-        through = through_all[i].astype(F32)
-        state = jnp.where(i > place, through * state + gathered[i].astype(F32), state)
-    return state
+class Scan:
+    def __init__(self, own, send, upwards):
+        shape = (MESSAGE_ROWS, MAMBA_INNER)
+        self.own, self.send, self.upwards = own, send, upwards
+        factor_row = lax.broadcasted_iota(jnp.int32, shape, 0) >= STATE_SIZE
+        self.seen = factor_row.astype(F32)
+        self.bits = ctx_bits()
+
+    def step(self, arrive=()):
+        bit = self.bits.pop(0)
+        above = (lax.axis_index("ctx") // bit) % 2 == 1
+        _, got = move(self.send, "ctx", bit, (), arrive)
+        first = above if self.upwards else jnp.logical_not(above)
+        self.own, self.send, self.seen = scan_step(first, self.own, self.seen, got)
+        return self.send
+
+    def finish(self, arrive=()):
+        while self.bits:
+            self.step(arrive)
+        return self.seen
 
 
 def outer_sum(left, right):
@@ -922,11 +1391,6 @@
 
 def time_steps(left, right):
     return dot_nt(left, right)
-
-
-def reduce_to_shard(grad, dim):
-    share = lax.psum_scatter(grad.astype(BF16), "fsdp", scatter_dimension=dim, tiled=True)
-    return lax.psum(share, "ctx").astype(F32)
 
 
 def local(
@@ -951,25 +1415,53 @@
     w_up,
     w_down,
 ):
-    gather = lambda w, dim: lax.all_gather(w, "fsdp", axis=dim, tiled=True)
-    full_gain_mix = gather(gain_mix, 0).astype(F32)
-    full_xbc = gather(w_xbc, 0)
-    full_kv = gather(key_value_weight, 0)
-    full_q = gather(w_q, 0)
-    full_dt = gather(w_dt, 0)
-    full_z = gather(w_z, 0)
-    full_conv_w = gather(conv_w, 1).astype(F32)
-    full_conv_b = gather(conv_b, 0).astype(F32)
-    full_dt_bias = gather(dt_bias, 0).astype(F32)
-    full_a_log = gather(a_log, 0).astype(F32)
-    full_skip = gather(skip_factor, 0).astype(F32)
-    full_mo = gather(w_mo, 0)
-    full_o = gather(w_o, 0)
-    full_gain_ffn = gather(gain_ffn, 0).astype(F32)
-    full_gate = gather(w_gate, 0)
-    full_up = gather(w_up, 0)
-    full_down = gather(w_down, 0)
-
+    xbc_dt = jnp.pad(
+        jnp.concatenate([w_xbc, w_dt], axis=1), ((0, 0), (0, LANES - MAMBA_HEADS))
+    )
+    small = jnp.concatenate(
+        [v.reshape(-1) for v in (gain_mix, conv_w, conv_b, dt_bias, a_log, skip_factor, gain_ffn)]
+    )
+    wide = w_q.shape[1] + key_value_weight.shape[1]
+    small_rows = 16
+    small = jnp.pad(small, (0, small_rows * wide - small.shape[0])).reshape(small_rows, wide)
+    shard_qkv = jnp.concatenate([jnp.concatenate([w_q, key_value_weight], axis=1), small], axis=0)
+    near_qkv = swap(send_x(shard_qkv, small_rows), "fsdp", 2)
+    near_xbc = swap(send_x(xbc_dt), "fsdp", 2)
+    side_by_side = lambda w, rows: [w[i : i + rows] for i in range(0, w.shape[0], rows)]
+    rows_in = w_z.shape[0]
+    shard_omo = jnp.concatenate([w_o, w_mo], axis=0)
+    shard_zo = jnp.concatenate([w_z] + side_by_side(shard_omo, rows_in), axis=1)
+    shard_gate_up = jnp.concatenate([w_gate, w_up], axis=1)
+    sent_zo = after(shard_zo, near_qkv)
+    near_zo = swap(sent_zo, "fsdp", 2)
+    sent_gate_up = after(shard_gate_up, near_xbc)
+    near_gate_up = swap(sent_gate_up, "fsdp", 2)
+    sent_down = after(w_down, near_zo)
+    near_down = swap(sent_down, "fsdp", 2)
+    full_qkv, small_all = collect(shard_qkv, near_qkv, small_rows)
+    model = w_down.shape[1]
+
+    def stretches(out, shard_rows):
+        return [(model, out, shard_rows, first) for first in range(0, shard_rows, rows_in)]
+
+    ranks = lax.axis_size("fsdp")
+    small_all = small_all.reshape(ranks, -1).astype(F32)
+    at = [0]
+
+    def unpack(rows, width):
+        part = small_all[:, at[0] : at[0] + rows * width].reshape(-1, rows, width)
+        at[0] += rows * width
+        return part.transpose(1, 0, 2).reshape(rows, -1)
+
+    full_gain_mix = unpack(1, gain_mix.shape[0])[0]
+    full_conv_w = unpack(CONV, conv_b.shape[0])
+    full_conv_b = unpack(1, conv_b.shape[0])[0]
+    full_dt_bias = unpack(1, dt_bias.shape[0])[0]
+    full_a_log = unpack(1, dt_bias.shape[0])[0]
+    full_skip = unpack(1, dt_bias.shape[0])[0]
+    full_gain_ffn = unpack(1, gain_ffn.shape[0])[0]
+    o_rows = w_o.shape[0]
+    wide_in = xbc_dt.shape[1]
     ctx_rank = lax.axis_index("ctx")
     inputs = tokens[0].astype(F32)
     rows = inputs.shape[0]
@@ -981,7 +1473,7 @@
     doc_row = jnp.broadcast_to(doc[None, :], (8, rows))
     scalars = jnp.concatenate([doc[CHUNK - 1 :: CHUNK], base[None]])
     attn_scalars = jnp.concatenate(
-        [doc[::QUERY_TILE], doc[QUERY_TILE - 1 :: QUERY_TILE], base[None]]
+        [doc[::QUERY_TILE], doc[QUERY_TILE - 1 :: QUERY_TILE], base[None], spread_order()]
     )
     half = HEAD_SIZE // 2
     freqs = ROPE_BASE ** (
@@ -1000,42 +1492,82 @@
 
     scale_one = lax.rsqrt(jnp.mean(inputs * inputs, axis=-1, keepdims=True) + EPSILON)
     normed = (inputs * scale_one * full_gain_mix[None, :]).astype(BF16)
-    kv_raw = dot_nn(normed, full_kv)
-    q_raw = dot_nn(normed, full_q)
-    mixed_in = dot_nn(normed, full_xbc).astype(BF16)
-    wide_dt = jnp.pad(full_dt, ((0, 0), (0, LANES - MAMBA_HEADS)))
-    dt_raw = dot_nn(normed, wide_dt)
+    q_width = QUERY_HEADS * HEAD_SIZE
+    qkv_raw = dot_nn(normed, full_qkv)
+    query, kv_first, kv_second = rope(
+        qkv_raw[:, :q_width], qkv_raw[:, q_width:], cosine, sine
+    )
+    spreads = [Spread(kv) for kv in (kv_first, kv_second)]
+    full_xbc = collect(xbc_dt, near_xbc, 0, [query])[0]
+    for spread_kv in spreads:
+        spread_kv.step()
+        spread_kv.step([full_xbc])
+    mixed_in = dot_nn(normed, full_xbc[:, :CHANNELS]).astype(BF16)
+    dt_raw = dot_nn(normed, full_xbc[:, CHANNELS:])
+    edge = shift_along(mixed_in[rows - 8 :], "ctx", 1).astype(F32)
+    y_local, state_local, message, own_state, decay, c_mat = mamba_forward(
+        scalars, edge, mixed_in, dt_raw, doc_col[:rows], conv_pack, head_pack, skip_wide
+    )
+    kv_all = [spread_kv.finish([message]) for spread_kv in spreads]
+    scan = Scan(own_state, message, True)
+    tokens = [message, sent_gate_up, sent_down]
+    attended = [attend(attn_scalars, query, kv_all[0], doc_row, 0, tokens)]
+    first_done = attended[0][0]
+    other_zo, other_gate_up, other_down = [
+        move(shard, "fsdp", 1, (), [first_done])[1] for shard in (shard_zo, shard_gate_up, w_down)
+    ]
+    tokens = [scan.step([first_done]), first_done, other_zo, other_gate_up, other_down]
+    attended.append(attend(attn_scalars, query, kv_all[1], doc_row, 1, tokens))
+    second_done = attended[1][0]
+    scan.step([second_done])
+    full_z, full_omo = collect_whole(
+        shard_zo,
+        other_zo,
+        near_zo,
+        [(w_z.shape[1], 0, rows_in, 0)] + stretches(1, shard_omo.shape[0]),
+        [second_done],
+        [first_done],
+    )
     gate_z = dot_nn(normed, full_z)
-    query, key_value = rope(q_raw, kv_raw, cosine, sine)
-    kv_all = lax.all_gather(key_value, "ctx", axis=0, tiled=True)
-    edge = shift_along(mixed_in[rows - 8 :], "ctx", 1).astype(F32)
-
-    y_local, state_local, message, decay, c_mat = mamba_forward(
-        scalars, edge, mixed_in, dt_raw, doc_col[:rows], conv_pack, head_pack, skip_wide
-    )
-    state_in, through_all = state_entering(message, "ctx")
-    attn_vec, attn_norm, lse = attend(attn_scalars, query, kv_all, doc_row)
-    y_total, gated, state_true = mamba_correct(y_local, state_local, c_mat, decay, state_in, gate_z)
-    hidden = inputs + dot_nn(attn_vec, full_o) + dot_nn(gated, full_mo)
+    full_gate_up = collect_whole(
+        shard_gate_up,
+        other_gate_up,
+        after(near_gate_up, second_done),
+        [(2 * w_gate.shape[1], 0, rows_in, 0)],
+        [second_done],
+        [second_done],
+    )[0]
+    state_in = scan.finish([gate_z, full_gate_up])
+    full_down = collect_whole(
+        w_down,
+        other_down,
+        after(near_down, second_done),
+        [(model, 0, w_down.shape[0], 0)],
+    )[0]
+    y_total, both, state_true = mamba_correct(
+        y_local, state_local, c_mat, decay, state_in, gate_z, attended[0][0], attended[1][0]
+    )
+    hidden = inputs + dot_nn(both, full_omo)
     gain_two = full_gain_ffn
     scale_two = lax.rsqrt(jnp.mean(hidden * hidden, axis=-1, keepdims=True) + EPSILON)
     normed_ffn = (hidden * scale_two * gain_two[None, :]).astype(BF16)
-    gate = dot_nn(normed_ffn, full_gate)
-    upper = dot_nn(normed_ffn, full_up)
+    gate_up = dot_nn(normed_ffn, full_gate_up)
+    ff = gate_up.shape[1] // 2
+    gate, upper = gate_up[:, :ff], gate_up[:, ff:]
     sig_gate = jax.nn.sigmoid(gate)
     silu_gate = gate * sig_gate
     activ = (silu_gate * upper).astype(BF16)
     result = hidden + dot_nn(activ, full_down)
 
     grad_out = cotangent[0]
-    grad_w_down = outer_sum(activ, grad_out)
+    down = Reduction(own_order(activ), grad_out)
     grad_act = time_steps(grad_out, full_down)
     grad_gate = (grad_act * upper * sig_gate * (1.0 + gate * (1.0 - sig_gate))).astype(BF16)
     grad_up = (grad_act * silu_gate).astype(BF16)
-    grad_w_gate = outer_sum(normed_ffn, grad_gate)
-    grad_w_up = outer_sum(normed_ffn, grad_up)
-    grad_n2 = time_steps(grad_gate, full_gate) + time_steps(grad_up, full_up)
-    grad_gain_ffn = jnp.sum(grad_n2 * hidden * scale_two, axis=0)
+    grad_gate_up = jnp.concatenate([grad_gate, grad_up], axis=1)
+    gate_up_sum = Reduction(own_order(normed_ffn), grad_gate_up)
+    down.over_x()
+    grad_n2 = time_steps(grad_gate_up, full_gate_up)
     scaled_two = grad_n2 * gain_two[None, :]
     grad_hidden = (
         grad_out.astype(F32)
@@ -1043,16 +1575,58 @@
         - hidden * scale_two**3 * jnp.mean(scaled_two * hidden, axis=-1, keepdims=True)
     )
     grad_hid_b = grad_hidden.astype(BF16)
-    gated_grad = time_steps(grad_hid_b, full_mo)
-    grad_y, grad_z, grad_state = mamba_gate_back(gated_grad, gate_z, y_total, c_mat, decay)
-    grad_attn = time_steps(grad_hid_b, full_o).astype(BF16)
-    grad_w_o = outer_sum(attn_vec, grad_hid_b)
-    grad_w_mo = outer_sum(gated, grad_hid_b)
-    state_grad = gradient_entering(grad_state, through_all, "ctx")
-    grad_q, grad_kv_all = attend_back(
-        attn_scalars, query, grad_attn, attn_norm, lse, kv_all, doc_row
-    )
-    grad_kv = lax.psum_scatter(grad_kv_all, "ctx", scatter_dimension=0, tiled=True)
+    gate_up_sum.over_x()
+    both_grad = time_steps(grad_hid_b, full_omo)
+    grad_y, grad_z, own_grad, grad_message, grad_attn = mamba_gate_back(
+        both_grad, gate_z, y_total, c_mat, decay, own_state, [down.sent, gate_up_sum.sent]
+    )
+    omo = Reduction(own_order(both), grad_hid_b)
+    left_mix = own_order(normed)
+    z_sum = Reduction(left_mix, grad_z)
+    scan = Scan(own_grad, grad_message, False)
+    backs = []
+
+    def back(j, tokens):
+        backs.append(
+            attend_back(
+                attn_scalars,
+                query,
+                grad_attn,
+                attended[j][1],
+                attended[j][2],
+                kv_all[j],
+                doc_row,
+                j,
+                tokens,
+            )
+        )
+
+    grad_n1_z = time_steps(grad_z, full_z)
+    first_send = scan.step()
+    back(0, [first_send, omo.sent, z_sum.sent, grad_n1_z])
+    first_done = backs[0][0]
+    for part in (down, gate_up_sum, omo, z_sum):
+        part.got = after(part.got, first_done)
+    second_send = scan.step([first_done])
+    down.add_x()
+    gate_up_sum.add_x()
+    ffn = Pack([gate_up_sum.own.astype(BF16), down.own.astype(BF16)])
+    ffn.over_y()
+    omo.over_x()
+    z_sum.over_x()
+    kv_sums = [BlockSums(backs[0][1])]
+    back(1, [second_send, ffn.sent, omo.sent, z_sum.sent, first_done])
+    second_done = backs[1][0]
+    for part in (ffn, omo, z_sum):
+        part.got = after(part.got, second_done)
+    kv_sums[0].step((), [second_done])
+    state_grad = scan.finish([second_done])
+    ffn.over_z()
+    omo.add_x()
+    z_sum.add_x()
+    mixer = Pack([z_sum.own.astype(BF16), omo.own.astype(BF16)])
+    mixer.over_y()
+    kv_sums.append(BlockSums(backs[1][1]))
     grad_mixed, tail, edge_grad, grad_dt, grad_conv, grad_heads = mamba_back(
         scalars,
         edge,
@@ -1067,49 +1641,97 @@
         y_total,
         state_true,
         state_grad,
+        [ffn.sent, mixer.sent, kv_sums[0].blocks],
     )
     behind = shift_along(edge_grad, "ctx", -1)
     grad_mixed = grad_mixed.at[rows - 8 :].set((tail + behind).astype(BF16))
-    grad_q_b, grad_kv_b = rope_back(grad_q, grad_kv, cosine, sine)
-    grad_w_q = outer_sum(normed, grad_q_b)
-    grad_w_kv = outer_sum(normed, grad_kv_b)
-    grad_w_z = outer_sum(normed, grad_z)
-    grad_w_xbc = outer_sum(normed, grad_mixed)
-    grad_w_dt = outer_sum(normed, grad_dt)[:, :MAMBA_HEADS]
+    third_done = grad_dt
+    for part in (ffn, mixer):
+        part.got = after(part.got, third_done)
+    kv_sums[1].step((), [third_done])
+    kv_both = BlockSums(jnp.concatenate([part.blocks for part in kv_sums], axis=1))
+    kv_both.bits = kv_sums[0].bits
+    grad_xbc = jnp.concatenate([grad_mixed, grad_dt], axis=1)
+    fsdp_rank = lax.axis_index("fsdp")
+    conv_width, heads_width = conv_b.shape[0], dt_bias.shape[0]
+    small_width = -(-(conv_width * (CONV + 1) + heads_width * 3) // rows_in)
+    small_at = CHANNELS + MAMBA_HEADS
+    blocks = [
+        g.reshape(g.shape[0], ranks, -1).transpose(1, 0, 2).reshape(ranks, -1)
+        for g in (grad_conv[: CONV + 1], grad_heads[:3, :MAMBA_HEADS])
+    ]
+    small_grad = jnp.concatenate(blocks, axis=1)
+    small_count = small_grad.shape[1]
+    small_grad = jnp.pad(small_grad, ((0, 0), (0, small_width * rows_in - small_count)))
+    small_grad = jnp.pad(
+        small_grad.reshape(ranks, rows_in, small_width),
+        ((0, 0), (0, 0), (small_at, wide_in - small_at - small_width)),
+    )
+    more = [lax.dynamic_index_in_dim(small_grad, fsdp_rank ^ k, 0, False) for k in (0, 2, 1, 3)]
+    xbc_sum = Reduction(left_mix, grad_xbc, more)
+    xbc_sum.over_x()
+    x_left = [xbc_sum.sent]
+    kv_both.step((), x_left)
+    ffn.rest((), x_left)
+    grad_kv = kv_both.finish()
+    grad_qkv = rope_back(
+        backs[0][0], backs[1][0], grad_kv[:, :LANES], grad_kv[:, LANES:], cosine, sine
+    )
+    qkv_sum = Reduction(left_mix, grad_qkv)
+    qkv_sum.over_x()
+    xbc_sum.add_x()
+    qkv_sum.add_x()
+    last_own = jnp.concatenate([xbc_sum.own, qkv_sum.own], axis=1).astype(BF16)
+    ffn.back_z()
+    mixer.over_z(x_left)
+    mixer.rest()
+    mixer.back_z()
+    grad_w_gate_up, grad_w_down = ffn.back_y()
+    grad_w_z, grad_w_omo = mixer.back_y()
+    last_total = lax.psum(last_own, "ctx").astype(F32)
+    grad_w_xbc, grad_w_qkv = last_total[:, :wide_in], last_total[:, wide_in:]
+    small_own = grad_w_xbc[:, small_at : small_at + small_width].reshape(-1)[:small_count]
+    conv_own = small_own[: conv_width * (CONV + 1)].reshape(CONV + 1, conv_width)
+    heads_own = small_own[conv_width * (CONV + 1) :].reshape(3, heads_width)
     grad_n1 = (
-        time_steps(grad_z, full_z)
-        + time_steps(grad_mixed, full_xbc)
-        + time_steps(grad_dt, wide_dt)
-        + time_steps(grad_q_b, full_q)
-        + time_steps(grad_kv_b, full_kv)
-    )
-    grad_gain_mix = jnp.sum(grad_n1 * inputs * scale_one, axis=0)
+        grad_n1_z
+        + time_steps(grad_xbc, full_xbc)
+        + time_steps(grad_qkv, full_qkv)
+    )
     scaled_one = grad_n1 * full_gain_mix[None, :]
     grad_tokens = (
         grad_hidden
         + scale_one * scaled_one
         - inputs * scale_one**3 * jnp.mean(scaled_one * inputs, axis=-1, keepdims=True)
     )
-    grads = (
-        (grad_gain_mix, 0),
-        (grad_w_z, 0),
-        (grad_w_xbc, 0),
-        (grad_w_dt, 0),
-        (grad_conv[:CONV], 1),
-        (grad_conv[CONV], 0),
-        (grad_heads[0, :MAMBA_HEADS], 0),
-        (grad_heads[1, :MAMBA_HEADS], 0),
-        (grad_heads[2, :MAMBA_HEADS], 0),
-        (grad_w_mo, 0),
-        (grad_w_q, 0),
-        (grad_w_kv, 0),
-        (grad_w_o, 0),
-        (grad_gain_ffn, 0),
-        (grad_w_gate, 0),
-        (grad_w_up, 0),
-        (grad_w_down, 0),
-    )
-    totals = tuple(reduce_to_shard(grad, dim) for grad, dim in grads)
+    row_sums = lambda grad, weight: jnp.sum(grad * weight.astype(F32), axis=1)
+    grad_gain_ffn = row_sums(
+        grad_w_gate_up, jnp.concatenate([w_gate, w_up], axis=1)
+    ) / gain_ffn.astype(F32)
+    grad_gain_mix = (
+        row_sums(grad_w_z, w_z)
+        + row_sums(grad_w_xbc, xbc_dt)
+        + row_sums(grad_w_qkv, jnp.concatenate([w_q, key_value_weight], axis=1))
+    ) / gain_mix.astype(F32)
+    totals = (
+        grad_gain_mix,
+        grad_w_z,
+        grad_w_xbc[:, :CHANNELS],
+        grad_w_xbc[:, CHANNELS : CHANNELS + MAMBA_HEADS],
+        conv_own[:CONV],
+        conv_own[CONV],
+        heads_own[0],
+        heads_own[1],
+        heads_own[2],
+        grad_w_omo[o_rows:],
+        grad_w_qkv[:, :q_width],
+        grad_w_qkv[:, q_width:],
+        grad_w_omo[:o_rows],
+        grad_gain_ffn,
+        grad_w_gate_up[:, :ff],
+        grad_w_gate_up[:, ff:],
+        grad_w_down,
+    )
     return (result.astype(BF16)[None], grad_tokens[None]) + totals
 
 

time: 1220 us -> 675 us (0.55)
  waiting for transfers between devices: 840 us -> 167 us
  starting transfers between devices: 6.43 us -> 94.6 us
  blocking collectives: 84 us -> 0 us
  Pallas kernels: 85 us -> 161 us
  local copies, waits for them, and re-layouts: 11 us -> 63.7 us
  other arithmetic: 38.3 us -> 63.6 us
  matrix products: 123 us -> 101 us
    reduce_scatter x11 -> x0, waiting for transfers between devices: 394 us -> none  [the longest x10 304 us: reduce_to_shard(): lax.psum_scatter(grad.astype(BF16), 'fsdp', scatter_dimension=dim, tiled=...]
    all_gather x11 -> x0, waiting for transfers between devices: 245 us -> none  [the longest x8 124 us: local(): gather = lambda w, dim: lax.all_gather(w, 'fsdp', axis=dim, tiled=True)]
    psum x1, waiting for transfers between devices: 181 us -> 20.1 us  [local(): last_total = lax.psum(last_own, 'ctx').astype(F32)]
    ppermute x0 -> x57, waiting for transfers between devices: none -> 147 us  [swap(): return lax.ppermute(block, DEVICES, route)]
    ppermute x0 -> x57, starting transfers between devices: none -> 89.3 us  [swap(): return lax.ppermute(block, DEVICES, route)]
    pallas_call x5 -> x61, Pallas kernels: 60.1 us -> 136 us  [the longest x1 25.4 us: mamba_back(): pl.pallas_call(without(mamba_back_kernel, 13, len(tokens)), grid=(count,)...]
    psum x1 -> x0, blocking collectives: 38.8 us -> none  [reduce_to_shard(): return lax.psum(share, 'ctx').astype(F32)]
    all_gather x5 -> x0, blocking collectives: 31.5 us -> none  [local(): gather = lambda w, dim: lax.all_gather(w, 'fsdp', axis=dim, tiled=True)]
  transfers between devices with their start and end apart: 26 -> 60, of which waited for: 23 -> 17; matrix products, arithmetic and copies ran while one was open for 11% -> 27% of each run, Pallas kernels for 6% -> 22%
where the time goes in v2:
time: 675 us; the launch traced here: 667 us
  waiting for transfers between devices  167 us (25%)
  Pallas kernels  161 us (24%)
  matrix products  101 us (15%)
  starting transfers between devices  94.6 us (14%)
  local copies, waits for them, and re-layouts  63.7 us (9%)
  other arithmetic  63.6 us (9%)
  between operations  15.8 us (2%)
    ppermute x57, waiting for transfers between devices, swap(): return lax.ppermute(block, DEVICES, route)  147 us
    ppermute x57, starting transfers between devices, swap(): return lax.ppermute(block, DEVICES, route)  89.3 us
    dot_general x18, matrix products, dot_tn(): lax.dot_general(a, b, (((0,), (0,)), ((), ())), preferred_element_type=F32)  44.6 us
    dot_general x6, matrix products, dot_nt(): lax.dot_general(a, b, (((1,), (1,)), ((), ())), preferred_element_type=F32)  31.2 us
    pallas_call x1, Pallas kernels, mamba_back(): pl.pallas_call(without(mamba_back_kernel, 13, len(tokens)), grid=(count,)...  25.4 us
    pallas_call x5, Pallas kernels, place(): pl.pallas_call(functools.partial(place_kernel, tuple(parts), len(tokens))...  25.3 us
    dot_general x7, matrix products, dot_nn(): lax.dot_general(a, b, (((1,), (0,)), ((), ())), precision=precision, pref...  24.9 us
    psum x1, waiting for transfers between devices, local(): last_total = lax.psum(last_own, 'ctx').astype(F32)  20.1 us
  transfers between devices with their start and end apart: 60, of which 17 were waited for; matrix products, arithmetic and copies ran while one was open for 27% of the time, Pallas kernels for 22%

profile of v2, /device:TPU:0, one launch (start us, length us, event | category | flops | bytes accessed | tf_op | source)
XLA Modules:
  0.0 666.7 jit_solution(4045541773814418702)
XLA Ops:
  8.1 4.1 concatenate.97
  64.5 5.5 collective-permute-done.12
  76.6 4.0 place.6.refs_1_
  80.6 4.1 fusion.8.mixed_ref.refs_2_
  86.5 3.8 collective-permute-start.10
  99.9 13.5 %mamba_forward.1 = (f32[512,1536]{1,0:T(8,128)}, f32[4,128,1536]{2,1,0:T(8,128)}, bf16[144,1536]{1,0:T(8,128)(2,1)}, f32[144,1536]{1,0:T(8,128)}, f32[512,128]{1,0:T(8,128)}, /*index=5*/bf16[512,128]{1,0:T(8,128)(2,1)}) custom-call(s32[5]{0:T(128)} %pad_add_fusion.sc_ref.refs_0_, f32[8,1792]{1,0:T(8,128)} %convert_element_type.288.edge_ref.refs_1_, ...), custom_call_target="tpu_custom_call" | custom-call | flops 14949999616 | tf_op jit(solution)/shard_map/mamba_forward/pallas_call | solution.py:218
  113.4 5.7 collective-permute-done.19.refs_0_
  125.2 6.3 attend.2
  140.1 4.9 collective-permute-start.16
  145.1 6.4 attend.3
  151.4 16.6 %collective-permute-done.25.refs_0_ = bf16[256,4096]{1,0:T(8,128)(2,1)} collective-permute-done((bf16[256,4096]{1,0:T(8,128)(2,1)}, bf16[256,4096]{1,0:T(8,128)(2,1)}, u32[]{:S(2)}, u32[]{:S(2)}) %collective-permute-start.25) | collective-permute-done | bytes 2097184 | tf_op jit(solution)/shard_map/ppermute | solution.py:1001
  173.2 6.7 %collective-permute-start.23 = (bf16[144,1536]{1,0:T(8,128)(2,1)}, bf16[144,1536]{1,0:T(8,128)(2,1)S(1)}, u32[]{:S(2)}, u32[]{:S(2)}) collective-permute-start(bf16[144,1536]{1,0:T(8,128)(2,1)} %get-tuple-element.112), channel_id=1, source_target_pairs={{0,16},{1,17},{2,18},{3,19},{4,20},{5,21},{6,22},{7,23},{8,24},{9,... | collective-permute-start | bytes 1327112 | tf_op jit(solution)/shard_map/ppermute | solution.py:1001
  179.9 7.8 %collective-permute-done.27.refs_0_ = bf16[512,1024]{1,0:T(8,128)(2,1)} collective-permute-done((bf16[512,1024]{1,0:T(8,128)(2,1)}, bf16[512,1024]{1,0:T(8,128)(2,1)}, u32[]{:S(2)}, u32[]{:S(2)}) %collective-permute-start.27) | collective-permute-done | bytes 1048608 | tf_op jit(solution)/shard_map/ppermute | solution.py:1001
  187.7 6.8 %place.7 = (bf16[1024,1536]{1,0:T(8,128)(2,1)}, bf16[2048,1024]{1,0:T(8,128)(2,1)}) custom-call(s32[12]{0:T(128)} %stack.113.at_ref, bf16[256,3584]{1,0:T(8,128)(2,1)} %fusion.30.refs_0_, bf16[256,3584]{1,0:T(8,128)(2,1)} %after.45.refs_6_.refs_1_, bf16[256,3584]{1,0:T(8,128)(2,1)} %collective-permute-done.15.refs_1_.refs_2_, ...), custom_call_target="tpu_custom_call" | custom-call | flops 6777357824 | tf_op jit(solution)/shard_map/place/pallas_call | solution.py:1047
  194.5 5.3 fusion.126.refs_1_.z_ref
  199.9 3.9 place.9
  203.8 7.6 %place.8.refs_2_ = bf16[1024,4096]{1,0:T(8,128)(2,1)} custom-call(s32[4]{0:T(128)} %pad_add_fusion.2.at_ref, bf16[256,4096]{1,0:T(8,128)(2,1)} %copy-done.4, bf16[256,4096]{1,0:T(8,128)(2,1)} %after.46.refs_7_.refs_1_, bf16[256,4096]{1,0:T(8,128)(2,1)} %after.50.refs_2_, bf16[256,4096]{1,0:T(8,128)(2,1)} %after.51.refs_3_, ...), custom_call_target="tpu_custom_call" | custom-call | flops 7581265920 | tf_op jit(solution)/shard_map/place/pallas_call | solution.py:1047
  215.4 8.8 %mamba_correct.1 = (f32[512,1536]{1,0:T(8,128)}, bf16[512,2048]{1,0:T(8,128)(2,1)}, bf16[4,128,1536]{2,1,0:T(8,128)(2,1)}) custom-call(f32[512,1536]{1,0:T(8,128)} %get-tuple-element.97.y_ref, f32[4,128,1536]{2,1,0:T(8,128)} %get-tuple-element.98.sin_ref, bf16[512,128]{1,0:T(8,128)(2,1)} %get-tuple-element.99.c_ref.refs_3_, ...), custom_call_target="tpu_custom_call" | custom-call | flops 9774999552 | tf_op jit(solution)/shard_map/mamba_correct/pallas_call | solution.py:305
  224.2 4.2 multiply_reduce_fusion.2
  228.7 4.6 fusion.127
  233.4 7.5 %fusion.2 = (bf16[512,2048]{1,0:T(8,128)(2,1)S(1)}, bf16[512,2048]{1,0:T(8,128)(2,1)S(1)}, bf16[512,2048]{1,0:T(8,128)(2,1)}) fusion(f32[512,4096]{1,0:T(8,128)S(1)} %fusion.127, bf16[2048,1024]{1,0:T(8,128)(2,1)} %place.9, bf16[1,512,1024]{2,1,0:T(8,128)(2,1)S(1)} %copy-done.18), kind=kOutput, calls=%fused_computation.10 | convolution fusion | flops 2163212288 | bytes 19922944 | tf_op jit(solution)/shard_map/dot_general | solution.py:44
  240.9 4.5 convolution_convert_fusion
  246.0 6.9 %multiply_reduce_fusion.1 = (f32[512]{0:T(512)S(1)}, f32[512,1024]{1,0:T(8,128)S(1)}) fusion(f32[512,1024]{1,0:T(8,128)S(1)} %get-tuple-element.248, f32[1024]{0:T(1024)S(1)} %bitcast.140, bf16[1024,4096]{1,0:T(8,128)(2,1)S(1)} %bitcast.133, bf16[512,2048]{1,0:T(8,128)(2,1)} %copy-done.87, bf16[512,2048]{1,0:T(8,128)(2,1)} %copy-done.85), kind=kOutput, calls=%fused_computation.42 | convolution fusion | flops 4304928256 | bytes 16783360 | tf_op jit(solution)/shard_map/dot_general | solution.py:44
  268.8 4.4 fusion.128.refs_0_
  278.7 4.7 add_convert_fusion.1.refs_7_
  285.1 8.6 %mamba_gate_back.1 = (bf16[512,1536]{1,0:T(8,128)(2,1)}, bf16[512,1536]{1,0:T(8,128)(2,1)}, f32[144,1536]{1,0:T(8,128)}, bf16[144,1536]{1,0:T(8,128)(2,1)}, bf16[512,512]{1,0:T(8,128)(2,1)}) custom-call(f32[512,2048]{1,0:T(8,128)} %fusion.128.refs_0_, f32[512,1536]{1,0:T(8,128)} %fusion.126.refs_1_.z_ref, f32[512,1536]{1,0:T(8,128)} %get-tuple-element.117.refs_2_.refs_10_, ...), custom_call_target="tpu_custom_call" | custom-call | flops 8625000448 | tf_op jit(solution)/shard_map/mamba_gate_back/pallas_call | solution.py:367
  311.5 7.9 %attend_back.2 = (f32[512,256]{1,0:T(8,128)}, bf16[4096,128]{1,0:T(8,128)(2,1)}) custom-call(s32[17]{0:T(128)} %pad_add_fusion.1.refs_0_, bf16[512,512]{1,0:T(8,128)(2,1)} %get-tuple-element.96.refs_1_, bf16[512,512]{1,0:T(8,128)(2,1)} %get-tuple-element.126.refs_2_, f32[512,256]{1,0:T(8,128)} %get-tuple-element.127.refs_3_, ...), custom_call_target="tpu_custom_call" | custom-call | flops 29899999232 | tf_op jit(solution)/shard_map/attend_back/pallas_call | solution.py:902
  319.4 3.5 add_convert_fusion.3.refs_9_
  324.1 4.9 collective-permute-start.41
  329.1 3.7 add_convert_fusion.4.refs_1_
  335.9 13.9 %collective-permute-start.33 = (bf16[144,1536]{1,0:T(8,128)(2,1)}, bf16[144,1536]{1,0:T(8,128)(2,1)}, u32[]{:S(2)}, u32[]{:S(2)}) collective-permute-start(bf16[144,1536]{1,0:T(8,128)(2,1)} %get-tuple-element.132.refs_7_), channel_id=1, source_target_pairs={{0,16},{1,17},{2,18},{3,19},{4,20},{5,21},{6,22},{7,23},{8,24},{9,... | collective-permute-start | bytes 1327112 | tf_op jit(solution)/shard_map/ppermute | solution.py:1001
  354.4 5.8 add_convert_fusion.refs_0_
  360.2 3.7 split.2
  363.9 8.0 %attend_back.3 = (f32[512,256]{1,0:T(8,128)}, bf16[4096,128]{1,0:T(8,128)(2,1)}) custom-call(s32[17]{0:T(128)} %pad_add_fusion.1.refs_0_, bf16[512,512]{1,0:T(8,128)(2,1)} %get-tuple-element.96.refs_1_, bf16[512,512]{1,0:T(8,128)(2,1)} %get-tuple-element.126.refs_2_, f32[512,256]{1,0:T(8,128)} %get-tuple-element.133.refs_3_, ...), custom_call_target="tpu_custom_call" | custom-call | flops 29899999232 | tf_op jit(solution)/shard_map/attend_back/pallas_call | solution.py:902
  373.9 5.5 collective-permute-start.43
  394.4 7.2 %collective-permute-done.38.refs_0_ = bf16[128,6144]{1,0:T(8,128)(2,1)} collective-permute-done((bf16[128,6144]{1,0:T(8,128)(2,1)}, bf16[128,6144]{1,0:T(8,128)(2,1)}, u32[]{:S(2)}, u32[]{:S(2)}) %collective-permute-start.38) | collective-permute-done | bytes 1572896 | tf_op jit(solution)/shard_map/ppermute | solution.py:1001
  404.9 3.6 collective-permute-start.55
  408.5 25.4 %mamba_back.1 = (bf16[512,1792]{1,0:T(8,128)(2,1)}, f32[8,1792]{1,0:T(8,128)}, f32[8,1792]{1,0:T(8,128)}, bf16[512,128]{1,0:T(8,128)(2,1)}, f32[8,1792]{1,0:T(8,128)}, /*index=5*/f32[8,128]{1,0:T(8,128)}) custom-call(s32[5]{0:T(128)} %pad_add_fusion.sc_ref.refs_0_, f32[8,1792]{1,0:T(8,128)} %convert_element_type.288.edge_ref.refs_1_, ...), custom_call_target="tpu_custom_call" | custom-call | flops 28750000128 | tf_op jit(solution)/shard_map/mamba_back/pallas_call | solution.py:598
  444.3 4.1 fusion.5
  451.7 10.2 %collective-permute-start.56 = (bf16[64,6144]{1,0:T(8,128)(2,1)}, bf16[64,6144]{1,0:T(8,128)(2,1)}, u32[]{:S(2)}, u32[]{:S(2)}) collective-permute-start(bf16[64,6144]{1,0:T(8,128)(2,1)} %add_convert_fusion.8), channel_id=1, source_target_pairs={{0,16},{1,17},{2,18},{3,19},{4,20},{5,21},{6,22},{7,23},{8,24},{9,... | collective-permute-start | bytes 2359304 | tf_op jit(solution)/shard_map/ppermute | solution.py:1001
  462.0 5.8 fusion.118
  474.8 3.6 collective-permute-start.48
  478.4 24.9 %collective-permute-done.56.refs_0_ = bf16[64,6144]{1,0:T(8,128)(2,1)} collective-permute-done((bf16[64,6144]{1,0:T(8,128)(2,1)}, bf16[64,6144]{1,0:T(8,128)(2,1)}, u32[]{:S(2)}, u32[]{:S(2)}) %collective-permute-start.56) | collective-permute-done | bytes 786464 | tf_op jit(solution)/shard_map/ppermute | solution.py:1001
  521.6 19.9 %collective-permute-done.49 = bf16[64,3584]{1,0:T(8,128)(2,1)S(1)} collective-permute-done((bf16[64,3584]{1,0:T(8,128)(2,1)S(1)}, bf16[64,3584]{1,0:T(8,128)(2,1)S(1)}, u32[]{:S(2)}, u32[]{:S(2)}) %collective-permute-start.49) | collective-permute-done | bytes 458784 | tf_op jit(solution)/shard_map/ppermute | solution.py:1001
  554.9 5.0 collective-permute-start.51
  563.1 46.7 %collective-permute-done.51.got_ref = bf16[128,3584]{1,0:T(8,128)(2,1)S(1)} collective-permute-done((bf16[128,3584]{1,0:T(8,128)(2,1)}, bf16[128,3584]{1,0:T(8,128)(2,1)S(1)}, u32[]{:S(2)}, u32[]{:S(2)}) %collective-permute-start.51) | collective-permute-done | bytes 917536 | tf_op jit(solution)/shard_map/ppermute | solution.py:1001
  619.2 5.1 unpack.3
  630.1 20.1 %all-reduce.10.cloned.1.call-done = bf16[256,2688]{1,0:T(8,128)(2,1)} async-done(((bf16[256,2688]{1,0:T(8,128)(2,1)}), bf16[256,2688]{1,0:T(8,128)(2,1)}) %all-reduce.10.cloned.1.call-update) | async-done | bytes 1376272 | tf_op jit(solution)/shard_map/psum | solution.py:1691
  (496 shorter events, 245.2 us)
Async XLA Ops:
  7.2 643.0 %all-reduce.10.cloned.1.call-start = ((), (), s32[]{:S(2)}) async-start(), calls=%async_computation | async-start | bytes 2752512 | tf_op jit(solution)/shard_map/psum | solution.py:1691
  15.0 27.5 %collective-permute-start = (bf16[272,768]{1,0:T(8,128)(2,1)}, bf16[272,768]{1,0:T(8,128)(2,1)}, u32[]{:S(2)}, u32[]{:S(2)}) collective-permute-start(bf16[272,768]{1,0:T(8,128)(2,1)} %pad_maximum_fusion.10.refs_0_), channel_id=1, source_target_pairs={{0,1},{1,0},{2,3},{3,2},{4,5},{5,4},{6,7},{7,6},{8,9},{9,8},{10,11... | collective-permute-start | bytes 1253384 | tf_op jit(solution)/shard_map/ppermute | solution.py:1001
  19.8 54.7 %collective-permute-start.5 = (bf16[256,1920]{1,0:T(8,128)(2,1)}, bf16[256,1920]{1,0:T(8,128)(2,1)}, u32[]{:S(2)}, u32[]{:S(2)}) collective-permute-start(bf16[256,1920]{1,0:T(8,128)(2,1)} %fusion.47.refs_0_), channel_id=1, source_target_pairs={{0,1},{1,0},{2,3},{3,2},{4,5},{5,4},{6,7},{7,6},{8,9},{9,8},{10,11... | collective-permute-start | bytes 2949128 | tf_op jit(solution)/shard_map/ppermute | solution.py:1001
  21.9 20.5 %collective-permute-start.6 = (bf16[128,1920]{1,0:T(8,128)(2,1)}, bf16[128,1920]{1,0:T(8,128)(2,1)}, u32[]{:S(2)}, u32[]{:S(2)}) collective-permute-start(bf16[128,1920]{1,0:T(8,128)(2,1)} %constant_dynamic-slice_fusion.8), channel_id=1, source_target_pairs={{0,2},{1,3},{2,0},{3,1},{4,6},{5,7},{6,4},{7,5},{8,10},{9,11},{10,... | collective-permute-start | bytes 1474568 | tf_op jit(solution)/shard_map/ppermute | solution.py:1001
  42.4 30.5 %collective-permute-start.7 = (bf16[128,1920]{1,0:T(8,128)(2,1)}, bf16[128,1920]{1,0:T(8,128)(2,1)}, u32[]{:S(2)}, u32[]{:S(2)}) collective-permute-start(bf16[128,1920]{1,0:T(8,128)(2,1)} %collective-permute-done.6.refs_2_.refs_1_), channel_id=1, source_target_pairs={{0,1},{1,0},{2,3},{3,2},{4,5},{5,4},{6,7},{7,6},{8,9},{9,8},{10,11... | collective-permute-start | bytes 1474568 | tf_op jit(solution)/shard_map/ppermute | solution.py:1001
  42.5 18.0 %collective-permute-start.8 = (bf16[128,1920]{1,0:T(8,128)(2,1)}, bf16[128,1920]{1,0:T(8,128)(2,1)}, u32[]{:S(2)}, u32[]{:S(2)}) collective-permute-start(bf16[128,1920]{1,0:T(8,128)(2,1)} %collective-permute-done.6.refs_2_.refs_1_), channel_id=1, source_target_pairs={{0,4},{1,5},{2,6},{3,7},{4,0},{5,1},{6,2},{7,3},{8,12},{9,13},{10,... | collective-permute-start | bytes 1474568 | tf_op jit(solution)/shard_map/ppermute | solution.py:1001
  57.0 13.1 %collective-permute-start.12 = (bf16[512,128]{1,0:T(8,128)(2,1)}, bf16[512,128]{1,0:T(8,128)(2,1)S(1)}, u32[]{:S(2)}, u32[]{:S(2)}) collective-permute-start(bf16[512,128]{1,0:T(8,128)(2,1)} %get-tuple-element.103), channel_id=1, source_target_pairs={{0,16},{1,17},{2,18},{3,19},{4,20},{5,21},{6,22},{7,23},{8,24},{9,... | collective-permute-start | bytes 393224 | tf_op jit(solution)/shard_map/ppermute | solution.py:1001
  59.6 12.5 %collective-permute-start.17 = (bf16[512,128]{1,0:T(8,128)(2,1)}, bf16[512,128]{1,0:T(8,128)(2,1)S(1)}, u32[]{:S(2)}, u32[]{:S(2)}) collective-permute-start(bf16[512,128]{1,0:T(8,128)(2,1)} %get-tuple-element.108), channel_id=1, source_target_pairs={{0,16},{1,17},{2,18},{3,19},{4,20},{5,21},{6,22},{7,23},{8,24},{9,... | collective-permute-start | bytes 393224 | tf_op jit(solution)/shard_map/ppermute | solution.py:1001
  60.6 14.6 %collective-permute-start.9 = (bf16[128,1920]{1,0:T(8,128)(2,1)}, bf16[128,1920]{1,0:T(8,128)(2,1)}, u32[]{:S(2)}, u32[]{:S(2)}) collective-permute-start(bf16[128,1920]{1,0:T(8,128)(2,1)} %after.36.refs_4_), channel_id=1, source_target_pairs={{0,1},{1,0},{2,3},{3,2},{4,5},{5,4},{6,7},{7,6},{8,9},{9,8},{10,11... | collective-permute-start | bytes 1474568 | tf_op jit(solution)/shard_map/ppermute | solution.py:1001
  70.0 70.0 %collective-permute-start.20 = (bf16[256,3584]{1,0:T(8,128)(2,1)}, bf16[256,3584]{1,0:T(8,128)(2,1)}, u32[]{:S(2)}, u32[]{:S(2)}) collective-permute-start(bf16[256,3584]{1,0:T(8,128)(2,1)} %fusion.30.refs_0_), channel_id=1, source_target_pairs={{0,1},{1,0},{2,3},{3,2},{4,5},{5,4},{6,7},{7,6},{8,9},{9,8},{10,11... | collective-permute-start | bytes 5505032 | tf_op jit(solution)/shard_map/ppermute | solution.py:1001
  72.1 72.9 %collective-permute-start.21 = (bf16[256,4096]{1,0:T(8,128)(2,1)S(1)}, bf16[256,4096]{1,0:T(8,128)(2,1)}, u32[]{:S(2)}, u32[]{:S(2)}) collective-permute-start(bf16[256,4096]{1,0:T(8,128)(2,1)S(1)} %constant_dynamic-update-slice_fusion.2.refs_0_), channel_id=1, source_target_pairs={{0,1},{1,0},{2,3},{3,2},{4,5},{5,4},{6,7},{7,6},{8,9},{9,8},{10,11... | collective-permute-start | bytes 6291464 | tf_op jit(solution)/shard_map/ppermute | solution.py:1001
  73.0 51.0 %collective-permute-start.15 = (bf16[256,3584]{1,0:T(8,128)(2,1)}, bf16[256,3584]{1,0:T(8,128)(2,1)}, u32[]{:S(2)}, u32[]{:S(2)}) collective-permute-start(bf16[256,3584]{1,0:T(8,128)(2,1)} %after.40), channel_id=1, source_target_pairs={{0,2},{1,3},{2,0},{3,1},{4,6},{5,7},{6,4},{7,5},{8,10},{9,11},{10,... | collective-permute-start | bytes 5505032 | tf_op jit(solution)/shard_map/ppermute | solution.py:1001
  75.2 19.4 %collective-permute-start.18 = (bf16[1024,128]{1,0:T(8,128)(2,1)}, bf16[1024,128]{1,0:T(8,128)(2,1)S(1)}, u32[]{:S(2)}, u32[]{:S(2)}) collective-permute-start(bf16[1024,128]{1,0:T(8,128)(2,1)} %pad_maximum_fusion.12), channel_id=1, source_target_pairs={{0,8},{1,9},{2,10},{3,11},{4,12},{5,13},{6,14},{7,15},{8,0},{9,1},... | collective-permute-start | bytes 786440 | tf_op jit(solution)/shard_map/ppermute | solution.py:1001
  94.6 18.7 %collective-permute-start.14 = (bf16[2048,128]{1,0:T(8,128)(2,1)}, bf16[2048,128]{1,0:T(8,128)(2,1)}, u32[]{:S(2)}, u32[]{:S(2)}) collective-permute-start(bf16[2048,128]{1,0:T(8,128)(2,1)} %pad_maximum_fusion.7), channel_id=1, source_target_pairs={{0,4},{1,5},{2,6},{3,7},{4,0},{5,1},{6,2},{7,3},{8,12},{9,13},{10,... | collective-permute-start | bytes 1572872 | tf_op jit(solution)/shard_map/ppermute | solution.py:1001
  97.1 22.0 %collective-permute-start.19 = (bf16[2048,128]{1,0:T(8,128)(2,1)}, bf16[2048,128]{1,0:T(8,128)(2,1)}, u32[]{:S(2)}, u32[]{:S(2)}) collective-permute-start(bf16[2048,128]{1,0:T(8,128)(2,1)} %pad_maximum_fusion.8), channel_id=1, source_target_pairs={{0,4},{1,5},{2,6},{3,7},{4,0},{5,1},{6,2},{7,3},{8,12},{9,13},{10,... | collective-permute-start | bytes 1572872 | tf_op jit(solution)/shard_map/ppermute | solution.py:1001
  113.3 31.7 %collective-permute-start.22 = (bf16[512,1024]{1,0:T(8,128)(2,1)}, bf16[512,1024]{1,0:T(8,128)(2,1)}, u32[]{:S(2)}, u32[]{:S(2)}) collective-permute-start(bf16[512,1024]{1,0:T(8,128)(2,1)} %refs_0_.2), channel_id=1, source_target_pairs={{0,1},{1,0},{2,3},{3,2},{4,5},{5,4},{6,7},{7,6},{8,9},{9,8},{10,11... | collective-permute-start | bytes 3145736 | tf_op jit(solution)/shard_map/ppermute | solution.py:1001
  119.2 48.9 %collective-permute-start.25 = (bf16[256,4096]{1,0:T(8,128)(2,1)}, bf16[256,4096]{1,0:T(8,128)(2,1)}, u32[]{:S(2)}, u32[]{:S(2)}) collective-permute-start(bf16[256,4096]{1,0:T(8,128)(2,1)} %after.39.refs_5_), channel_id=1, source_target_pairs={{0,2},{1,3},{2,0},{3,1},{4,6},{5,7},{6,4},{7,5},{8,10},{9,11},{10,... | collective-permute-start | bytes 6291464 | tf_op jit(solution)/shard_map/ppermute | solution.py:1001
  134.4 53.4 %collective-permute-start.27 = (bf16[512,1024]{1,0:T(8,128)(2,1)}, bf16[512,1024]{1,0:T(8,128)(2,1)}, u32[]{:S(2)}, u32[]{:S(2)}) collective-permute-start(bf16[512,1024]{1,0:T(8,128)(2,1)} %after.41.refs_6_), channel_id=1, source_target_pairs={{0,2},{1,3},{2,0},{3,1},{4,6},{5,7},{6,4},{7,5},{8,10},{9,11},{10,... | collective-permute-start | bytes 3145736 | tf_op jit(solution)/shard_map/ppermute | solution.py:1001
  140.1 29.9 %collective-permute-start.16 = (bf16[144,1536]{1,0:T(8,128)(2,1)}, bf16[144,1536]{1,0:T(8,128)(2,1)}, u32[]{:S(2)}, u32[]{:S(2)}) collective-permute-start(bf16[144,1536]{1,0:T(8,128)(2,1)} %get-tuple-element.107.refs_4_), channel_id=1, source_target_pairs={{0,8},{1,9},{2,10},{3,11},{4,12},{5,13},{6,14},{7,15},{8,0},{9,1},... | collective-permute-start | bytes 1327112 | tf_op jit(solution)/shard_map/ppermute | solution.py:1001
  145.0 42.7 %collective-permute-start.24 = (bf16[256,3584]{1,0:T(8,128)(2,1)}, bf16[256,3584]{1,0:T(8,128)(2,1)}, u32[]{:S(2)}, u32[]{:S(2)}) collective-permute-start(bf16[256,3584]{1,0:T(8,128)(2,1)} %collective-permute-done.15.refs_1_.refs_2_), channel_id=1, source_target_pairs={{0,1},{1,0},{2,3},{3,2},{4,5},{5,4},{6,7},{7,6},{8,9},{9,8},{10,11... | collective-permute-start | bytes 5505032 | tf_op jit(solution)/shard_map/ppermute | solution.py:1001
  168.0 35.8 %collective-permute-start.26 = (bf16[256,4096]{1,0:T(8,128)(2,1)}, bf16[256,4096]{1,0:T(8,128)(2,1)}, u32[]{:S(2)}, u32[]{:S(2)}) collective-permute-start(bf16[256,4096]{1,0:T(8,128)(2,1)} %after.50.refs_2_), channel_id=1, source_target_pairs={{0,1},{1,0},{2,3},{3,2},{4,5},{5,4},{6,7},{7,6},{8,9},{9,8},{10,11... | collective-permute-start | bytes 6291464 | tf_op jit(solution)/shard_map/ppermute | solution.py:1001
  173.2 38.3 %collective-permute-start.23 = (bf16[144,1536]{1,0:T(8,128)(2,1)}, bf16[144,1536]{1,0:T(8,128)(2,1)S(1)}, u32[]{:S(2)}, u32[]{:S(2)}) collective-permute-start(bf16[144,1536]{1,0:T(8,128)(2,1)} %get-tuple-element.112), channel_id=1, source_target_pairs={{0,16},{1,17},{2,18},{3,19},{4,20},{5,21},{6,22},{7,23},{8,24},{9,... | collective-permute-start | bytes 1327112 | tf_op jit(solution)/shard_map/ppermute | solution.py:1001
  245.4 33.4 %collective-permute-start.30 = (bf16[512,4096]{1,0:T(8,128)(2,1)}, bf16[512,4096]{1,0:T(8,128)(2,1)}, u32[]{:S(2)}, u32[]{:S(2)}) collective-permute-start(bf16[512,4096]{1,0:T(8,128)(2,1)} %convolution_convert_fusion), channel_id=1, source_target_pairs={{0,1},{1,0},{2,3},{3,2},{4,5},{5,4},{6,7},{7,6},{8,9},{9,8},{10,11... | collective-permute-start | bytes 12582920 | tf_op jit(solution)/shard_map/ppermute | solution.py:1001
  255.5 21.2 %collective-permute-start.29 = (bf16[1024,1024]{1,0:T(8,128)(2,1)S(1)}, bf16[1024,1024]{1,0:T(8,128)(2,1)S(1)}, u32[]{:S(2)}, u32[]{:S(2)}) collective-permute-start(bf16[1024,1024]{1,0:T(8,128)(2,1)S(1)} %convolution_convert_fusion.3), channel_id=1, source_target_pairs={{0,1},{1,0},{2,3},{3,2},{4,5},{5,4},{6,7},{7,6},{8,9},{9,8},{10,11... | collective-permute-start | bytes 6291464 | tf_op jit(solution)/shard_map/ppermute | solution.py:1001
  260.5 58.9 %collective-permute-start.36 = (bf16[1024,1024]{1,0:T(8,128)(2,1)}, bf16[1024,1024]{1,0:T(8,128)(2,1)}, u32[]{:S(2)}, u32[]{:S(2)}) collective-permute-start(bf16[1024,1024]{1,0:T(8,128)(2,1)} %convolution_convert_fusion.2.refs_8_), channel_id=1, source_target_pairs={{0,1},{1,0},{2,3},{3,2},{4,5},{5,4},{6,7},{7,6},{8,9},{9,8},{10,11... | collective-permute-start | bytes 6291464 | tf_op jit(solution)/shard_map/ppermute | solution.py:1001
  278.3 45.8 %collective-permute-start.35 = (bf16[512,1024]{1,0:T(8,128)(2,1)}, bf16[512,1024]{1,0:T(8,128)(2,1)}, u32[]{:S(2)}, u32[]{:S(2)}) collective-permute-start(bf16[512,1024]{1,0:T(8,128)(2,1)} %add_convert_fusion.5.refs_6_), channel_id=1, source_target_pairs={{0,2},{1,3},{2,0},{3,1},{4,6},{5,7},{6,4},{7,5},{8,10},{9,11},{10,... | collective-permute-start | bytes 3145736 | tf_op jit(solution)/shard_map/ppermute | solution.py:1001
  283.4 71.0 %collective-permute-start.34 = (bf16[256,4096]{1,0:T(8,128)(2,1)}, bf16[256,4096]{1,0:T(8,128)(2,1)}, u32[]{:S(2)}, u32[]{:S(2)}) collective-permute-start(bf16[256,4096]{1,0:T(8,128)(2,1)} %add_convert_fusion.1.refs_7_), channel_id=1, source_target_pairs={{0,2},{1,3},{2,0},{3,1},{4,6},{5,7},{6,4},{7,5},{8,10},{9,11},{10,... | collective-permute-start | bytes 6291464 | tf_op jit(solution)/shard_map/ppermute | solution.py:1001
  299.8 49.9 %collective-permute-start.37 = (bf16[512,1536]{1,0:T(8,128)(2,1)}, bf16[512,1536]{1,0:T(8,128)(2,1)}, u32[]{:S(2)}, u32[]{:S(2)}) collective-permute-start(bf16[512,1536]{1,0:T(8,128)(2,1)} %convolution_convert_fusion.1.refs_9_), channel_id=1, source_target_pairs={{0,1},{1,0},{2,3},{3,2},{4,5},{5,4},{6,7},{7,6},{8,9},{9,8},{10,11... | collective-permute-start | bytes 4718600 | tf_op jit(solution)/shard_map/ppermute | solution.py:1001
  309.7 23.0 %collective-permute-start.32 = (bf16[144,1536]{1,0:T(8,128)(2,1)}, bf16[144,1536]{1,0:T(8,128)(2,1)}, u32[]{:S(2)}, u32[]{:S(2)}) collective-permute-start(bf16[144,1536]{1,0:T(8,128)(2,1)} %get-tuple-element.125.refs_7_), channel_id=1, source_target_pairs={{0,8},{1,9},{2,10},{3,11},{4,12},{5,13},{6,14},{7,15},{8,0},{9,1},... | collective-permute-start | bytes 1327112 | tf_op jit(solution)/shard_map/ppermute | solution.py:1001
  322.9 50.9 %collective-permute-start.40 = (bf16[512,1024]{1,0:T(8,128)(2,1)}, bf16[512,1024]{1,0:T(8,128)(2,1)}, u32[]{:S(2)}, u32[]{:S(2)}) collective-permute-start(bf16[512,1024]{1,0:T(8,128)(2,1)} %add_convert_fusion.3.refs_9_), channel_id=1, source_target_pairs={{0,2},{1,3},{2,0},{3,1},{4,6},{5,7},{6,4},{7,5},{8,10},{9,11},{10,... | collective-permute-start | bytes 3145736 | tf_op jit(solution)/shard_map/ppermute | solution.py:1001
  324.1 58.2 %collective-permute-start.41 = (bf16[2048,128]{1,0:T(8,128)(2,1)}, bf16[2048,128]{1,0:T(8,128)(2,1)}, u32[]{:S(2)}, u32[]{:S(2)}) collective-permute-start(bf16[2048,128]{1,0:T(8,128)(2,1)} %slice.252), channel_id=1, source_target_pairs={{0,4},{1,5},{2,6},{3,7},{4,0},{5,1},{6,2},{7,3},{8,12},{9,13},{10,... | collective-permute-start | bytes 1572872 | tf_op jit(solution)/shard_map/ppermute | solution.py:1001
  335.9 46.5 %collective-permute-start.33 = (bf16[144,1536]{1,0:T(8,128)(2,1)}, bf16[144,1536]{1,0:T(8,128)(2,1)}, u32[]{:S(2)}, u32[]{:S(2)}) collective-permute-start(bf16[144,1536]{1,0:T(8,128)(2,1)} %get-tuple-element.132.refs_7_), channel_id=1, source_target_pairs={{0,16},{1,17},{2,18},{3,19},{4,20},{5,21},{6,22},{7,23},{8,24},{9,... | collective-permute-start | bytes 1327112 | tf_op jit(solution)/shard_map/ppermute | solution.py:1001
  352.8 35.5 %collective-permute-start.39 = (bf16[256,1536]{1,0:T(8,128)(2,1)}, bf16[256,1536]{1,0:T(8,128)(2,1)}, u32[]{:S(2)}, u32[]{:S(2)}) collective-permute-start(bf16[256,1536]{1,0:T(8,128)(2,1)} %add_convert_fusion.10.refs_10_), channel_id=1, source_target_pairs={{0,2},{1,3},{2,0},{3,1},{4,6},{5,7},{6,4},{7,5},{8,10},{9,11},{10,... | collective-permute-start | bytes 2359304 | tf_op jit(solution)/shard_map/ppermute | solution.py:1001
  363.9 37.6 %collective-permute-start.38 = (bf16[128,6144]{1,0:T(8,128)(2,1)}, bf16[128,6144]{1,0:T(8,128)(2,1)}, u32[]{:S(2)}, u32[]{:S(2)}) collective-permute-start(bf16[128,6144]{1,0:T(8,128)(2,1)} %get-tuple-element.135.refs_8_), channel_id=1, source_target_pairs={{0,4},{1,5},{2,6},{3,7},{4,0},{5,1},{6,2},{7,3},{8,12},{9,13},{10,... | collective-permute-start | bytes 4718600 | tf_op jit(solution)/shard_map/ppermute | solution.py:1001
  373.9 60.1 %collective-permute-start.43 = (bf16[2048,128]{1,0:T(8,128)(2,1)}, bf16[2048,128]{1,0:T(8,128)(2,1)}, u32[]{:S(2)}, u32[]{:S(2)}) collective-permute-start(bf16[2048,128]{1,0:T(8,128)(2,1)} %slice.254), channel_id=1, source_target_pairs={{0,4},{1,5},{2,6},{3,7},{4,0},{5,1},{6,2},{7,3},{8,12},{9,13},{10,... | collective-permute-start | bytes 1572872 | tf_op jit(solution)/shard_map/ppermute | solution.py:1001
  393.7 47.2 %collective-permute-start.47 = (bf16[128,3584]{1,0:T(8,128)(2,1)}, bf16[128,3584]{1,0:T(8,128)(2,1)}, u32[]{:S(2)}, u32[]{:S(2)}) collective-permute-start(bf16[128,3584]{1,0:T(8,128)(2,1)} %get-tuple-element.140.refs_14_), channel_id=1, source_target_pairs={{0,4},{1,5},{2,6},{3,7},{4,0},{5,1},{6,2},{7,3},{8,12},{9,13},{10,... | collective-permute-start | bytes 2752520 | tf_op jit(solution)/shard_map/ppermute | solution.py:1001
  404.9 43.5 %collective-permute-start.55 = (bf16[64,6144]{1,0:T(8,128)(2,1)}, bf16[64,6144]{1,0:T(8,128)(2,1)}, u32[]{:S(2)}, u32[]{:S(2)}) collective-permute-start(bf16[64,6144]{1,0:T(8,128)(2,1)} %get-tuple-element.139.refs_13_), channel_id=1, source_target_pairs={{0,8},{1,9},{2,10},{3,11},{4,12},{5,13},{6,14},{7,15},{8,0},{9,1},... | collective-permute-start | bytes 2359304 | tf_op jit(solution)/shard_map/ppermute | solution.py:1001
  436.3 36.0 %collective-permute-start.44 = (bf16[1024,256]{1,0:T(8,128)(2,1)}, bf16[1024,256]{1,0:T(8,128)(2,1)}, u32[]{:S(2)}, u32[]{:S(2)}) collective-permute-start(bf16[1024,256]{1,0:T(8,128)(2,1)} %pad_maximum_fusion.6), channel_id=1, source_target_pairs={{0,8},{1,9},{2,10},{3,11},{4,12},{5,13},{6,14},{7,15},{8,0},{9,1},... | collective-permute-start | bytes 1572872 | tf_op jit(solution)/shard_map/ppermute | solution.py:1001
  448.4 21.4 %collective-permute-start.45 = (bf16[512,1920]{1,0:T(8,128)(2,1)}, bf16[512,1920]{1,0:T(8,128)(2,1)}, u32[]{:S(2)}, u32[]{:S(2)}) collective-permute-start(bf16[512,1920]{1,0:T(8,128)(2,1)} %fusion.5), channel_id=1, source_target_pairs={{0,1},{1,0},{2,3},{3,2},{4,5},{5,4},{6,7},{7,6},{8,9},{9,8},{10,11... | collective-permute-start | bytes 5898248 | tf_op jit(solution)/shard_map/ppermute | solution.py:1001
  451.7 51.5 %collective-permute-start.56 = (bf16[64,6144]{1,0:T(8,128)(2,1)}, bf16[64,6144]{1,0:T(8,128)(2,1)}, u32[]{:S(2)}, u32[]{:S(2)}) collective-permute-start(bf16[64,6144]{1,0:T(8,128)(2,1)} %add_convert_fusion.8), channel_id=1, source_target_pairs={{0,16},{1,17},{2,18},{3,19},{4,20},{5,21},{6,22},{7,23},{8,24},{9,... | collective-permute-start | bytes 2359304 | tf_op jit(solution)/shard_map/ppermute | solution.py:1001
  471.8 88.1 %collective-permute-start.52 = (bf16[256,1920]{1,0:T(8,128)(2,1)S(1)}, bf16[256,1920]{1,0:T(8,128)(2,1)}, u32[]{:S(2)}, u32[]{:S(2)}) collective-permute-start(bf16[256,1920]{1,0:T(8,128)(2,1)S(1)} %fusion.22.refs_1_), channel_id=1, source_target_pairs={{0,2},{1,3},{2,0},{3,1},{4,6},{5,7},{6,4},{7,5},{8,10},{9,11},{10,... | collective-permute-start | bytes 2949128 | tf_op jit(solution)/shard_map/ppermute | solution.py:1001
  474.7 32.9 %collective-permute-start.46 = (bf16[512,256]{1,0:T(8,128)(2,1)S(1)}, bf16[512,256]{1,0:T(8,128)(2,1)S(1)}, u32[]{:S(2)}, u32[]{:S(2)}) collective-permute-start(bf16[512,256]{1,0:T(8,128)(2,1)S(1)} %slice.311), channel_id=1, source_target_pairs={{0,16},{1,17},{2,18},{3,19},{4,20},{5,21},{6,22},{7,23},{8,24},{9,... | collective-permute-start | bytes 786440 | tf_op jit(solution)/shard_map/ppermute | solution.py:1001
  474.8 43.4 %collective-permute-start.48 = (bf16[64,3584]{1,0:T(8,128)(2,1)}, bf16[64,3584]{1,0:T(8,128)(2,1)}, u32[]{:S(2)}, u32[]{:S(2)}) collective-permute-start(bf16[64,3584]{1,0:T(8,128)(2,1)} %after.67), channel_id=1, source_target_pairs={{0,8},{1,9},{2,10},{3,11},{4,12},{5,13},{6,14},{7,15},{8,0},{9,1},... | collective-permute-start | bytes 1376264 | tf_op jit(solution)/shard_map/ppermute | solution.py:1001
  504.8 37.5 %collective-permute-start.57 = (bf16[64,6144]{1,0:T(8,128)(2,1)S(1)}, bf16[64,6144]{1,0:T(8,128)(2,1)}, u32[]{:S(2)}, u32[]{:S(2)}) collective-permute-start(bf16[64,6144]{1,0:T(8,128)(2,1)S(1)} %add_convert_fusion.7.own_ref), channel_id=1, source_target_pairs={{0,8},{1,9},{2,10},{3,11},{4,12},{5,13},{6,14},{7,15},{8,0},{9,1},... | collective-permute-start | bytes 2359304 | tf_op jit(solution)/shard_map/ppermute | solution.py:1001
  519.4 22.1 %collective-permute-start.49 = (bf16[64,3584]{1,0:T(8,128)(2,1)S(1)}, bf16[64,3584]{1,0:T(8,128)(2,1)S(1)}, u32[]{:S(2)}, u32[]{:S(2)}) collective-permute-start(bf16[64,3584]{1,0:T(8,128)(2,1)S(1)} %add_convert_fusion.15), channel_id=1, source_target_pairs={{0,16},{1,17},{2,18},{3,19},{4,20},{5,21},{6,22},{7,23},{8,24},{9,... | collective-permute-start | bytes 1376264 | tf_op jit(solution)/shard_map/ppermute | solution.py:1001
  519.8 28.5 %collective-permute-start.53 = (bf16[512,768]{1,0:T(8,128)(2,1)}, bf16[512,768]{1,0:T(8,128)(2,1)S(1)}, u32[]{:S(2)}, u32[]{:S(2)}) collective-permute-start(bf16[512,768]{1,0:T(8,128)(2,1)} %convolution_convert_fusion.4), channel_id=1, source_target_pairs={{0,1},{1,0},{2,3},{3,2},{4,5},{5,4},{6,7},{7,6},{8,9},{9,8},{10,11... | collective-permute-start | bytes 2359304 | tf_op jit(solution)/shard_map/ppermute | solution.py:1001
  544.9 74.3 %collective-permute-start.58 = (bf16[128,6144]{1,0:T(8,128)(2,1)}, bf16[128,6144]{1,0:T(8,128)(2,1)}, u32[]{:S(2)}, u32[]{:S(2)}) collective-permute-start(bf16[128,6144]{1,0:T(8,128)(2,1)} %join.3.own_ref), channel_id=1, source_target_pairs={{0,4},{1,5},{2,6},{3,7},{4,0},{5,1},{6,2},{7,3},{8,12},{9,13},{10,... | collective-permute-start | bytes 4718600 | tf_op jit(solution)/shard_map/ppermute | solution.py:1001
  554.9 54.8 %collective-permute-start.51 = (bf16[128,3584]{1,0:T(8,128)(2,1)}, bf16[128,3584]{1,0:T(8,128)(2,1)S(1)}, u32[]{:S(2)}, u32[]{:S(2)}) collective-permute-start(bf16[128,3584]{1,0:T(8,128)(2,1)} %join.2.own_ref), channel_id=1, source_target_pairs={{0,4},{1,5},{2,6},{3,7},{4,0},{5,1},{6,2},{7,3},{8,12},{9,13},{10,... | collective-permute-start | bytes 2752520 | tf_op jit(solution)/shard_map/ppermute | solution.py:1001
  (108 other events, 664.1 us)
Sparse Core Ops, SparseCore 0:
  563.2 86.9 all-reduce.9

commit v3 on v2

--- a/solution.py
+++ b/solution.py
@@ -21,7 +21,7 @@
 PAIRS = MAMBA_INNER // LANES
 CHUNK = 128
 KEY_BLOCK = 512
-QUERY_TILE = 128
+QUERY_TILE = 256
 GROUP = QUERY_HEADS // KEY_VALUE_HEADS
 MESSAGE_ROWS = STATE_SIZE + 16
 VMEM_LIMIT = 56 * 1024 * 1024
@@ -659,41 +659,53 @@
     )
 
 
-def scan_step_kernel(flag_ref, total_ref, seen_ref, got_ref, new_ref, send_ref, out_ref):
+def scan_step_kernel(begins, ends, flag_ref, *refs):
+    total_ref, refs = refs[0], refs[1:]
+    seen_ref, refs = (None, refs) if begins else (refs[0], refs[1:])
+    got_ref, out_ref = refs[0], refs[-1]
     first = flag_ref[0] == 1
     rows = slice(0, STATE_SIZE)
     rest = slice(STATE_SIZE, MESSAGE_ROWS)
     one = STATE_SIZE
     for j in range(PAIRS):
-        total, seen = total_ref[:, tile(j)], seen_ref[:, tile(j)]
         got = got_ref[:, tile(j)].astype(F32)
-        mine, theirs = total[one : one + 1], got[one : one + 1]
-        state = jnp.where(first, mine * got[rows] + total[rows], theirs * total[rows] + got[rows])
-        new_ref[rows, tile(j)] = state
-        send_ref[rows, tile(j)] = state.astype(BF16)
-        factor = total[rest] * got[rest]
-        new_ref[rest, tile(j)] = factor
-        send_ref[rest, tile(j)] = factor.astype(BF16)
-        passed = seen[rows] + seen[one : one + 1] * got[rows]
-        out_ref[rows, tile(j)] = jnp.where(first, passed, seen[rows])
-        out_ref[rest, tile(j)] = jnp.where(first, seen[rest] * got[rest], seen[rest])
-
-
-def scan_step(first, total, seen, got):
+        if begins:
+            out_ref[rows, tile(j)] = jnp.where(first, got[rows], 0.0)
+            out_ref[rest, tile(j)] = jnp.where(first, got[rest], 1.0)
+        else:
+            seen = seen_ref[:, tile(j)]
+            passed = seen[rows] + seen[one : one + 1] * got[rows]
+            out_ref[rows, tile(j)] = jnp.where(first, passed, seen[rows])
+            out_ref[rest, tile(j)] = jnp.where(first, seen[rest] * got[rest], seen[rest])
+        if not ends:
+            new_ref, send_ref = refs[1:3]
+            total = total_ref[:, tile(j)]
+            mine, theirs = total[one : one + 1], got[one : one + 1]
+            state = jnp.where(first, mine * got[rows] + total[rows], theirs * total[rows] + got[rows])
+            new_ref[rows, tile(j)] = state
+            send_ref[rows, tile(j)] = state.astype(BF16)
+            factor = total[rest] * got[rest]
+            new_ref[rest, tile(j)] = factor
+            send_ref[rest, tile(j)] = factor.astype(BF16)
+
+
+def scan_step(first, total, seen, got, ends):
     shape = (MESSAGE_ROWS, MAMBA_INNER)
-    return pl.pallas_call(
-        scan_step_kernel,
-        in_specs=[pl.BlockSpec(memory_space=pltpu.SMEM)] + [whole(shape)] * 3,
-        out_specs=[whole(shape)] * 3,
-        out_shape=[
-            jax.ShapeDtypeStruct(shape, F32),
-            jax.ShapeDtypeStruct(shape, BF16),
-            jax.ShapeDtypeStruct(shape, F32),
-        ],
+    ins = [total, got] if seen is None else [total, seen, got]
+    outs = [F32] if ends else [F32, BF16, F32]
+    specs = [whole(shape)] * len(ins)
+    if ends:
+        specs[0] = pl.BlockSpec(memory_space=pl.ANY)
+    found = pl.pallas_call(
+        functools.partial(scan_step_kernel, seen is None, ends),
+        in_specs=[pl.BlockSpec(memory_space=pltpu.SMEM)] + specs,
+        out_specs=[whole(shape)] * len(outs),
+        out_shape=[jax.ShapeDtypeStruct(shape, kind) for kind in outs],
         compiler_params=pltpu.CompilerParams(vmem_limit_bytes=VMEM_LIMIT),
         cost_estimate=lasting(2.5),
         name="scan_step",
-    )(first.astype(jnp.int32).reshape(1), total, seen, got)
+    )(first.astype(jnp.int32).reshape(1), *ins)
+    return (None, None, found[0]) if ends else found
 
 
 def half_roll(x):
@@ -737,7 +749,7 @@
 
 
 def attend_kernel(
-    sc_ref, q_ref, kv_ref, doc_ref, vec_ref, norm_ref, lse_ref, qz_ref, max_ref, sum_ref, acc_ref
+    sc_ref, q_ref, kv_ref, doc_ref, vec_ref, norm_ref, lse_ref, qz_ref, max_ref, acc_ref
 ):
     at = pl.program_id(0)
     tiles = pl.num_programs(0)
@@ -745,13 +757,13 @@
     for g, part in enumerate(stack_low(q_ref[...].astype(F32), QUERY_TILE)):
         qz_ref[g * QUERY_TILE : (g + 1) * QUERY_TILE, :] = part.astype(BF16)
     max_ref[...] = jnp.full_like(max_ref, MASK_FILLER)
-    sum_ref[...] = jnp.zeros_like(sum_ref)
     acc_ref[...] = jnp.zeros_like(acc_ref)
     doc_row = jnp.concatenate([doc_ref[0:1, :]] * GROUP, axis=1)
 
     def visit(block, masked):
         at_rows = sc_ref[2 * tiles + 1 + block] * KEY_BLOCK
         kv = kv_ref[pl.ds(pl.multiple_of(at_rows, KEY_BLOCK), KEY_BLOCK), :]
+        values = jnp.where(low_half(KEY_BLOCK), jnp.ones_like(kv), kv)
         scores = dot_nt(kv, qz_ref[...])
         if masked:
             scores = jnp.where(visible_mask(block, start, doc_row), scores, MASK_FILLER)
@@ -760,8 +772,7 @@
         prob = jnp.exp(scores - top)
         fade = jnp.exp(before - top)
         max_ref[0:1, :] = top
-        sum_ref[0:1, :] = sum_ref[0:1, :] * fade + jnp.sum(prob, axis=0, keepdims=True)
-        acc_ref[...] = acc_ref[...] * fade + dot_tn(kv, prob.astype(BF16))
+        acc_ref[...] = acc_ref[...] * fade + dot_tn(values, prob.astype(BF16))
 
     def one(block, carry):
         full = (block * KEY_BLOCK + KEY_BLOCK - 1 <= start) & (block * KEY_BLOCK >= last_doc)
@@ -777,8 +788,9 @@
         return carry
 
     lax.fori_loop(block_lo, block_hi, one, 0)
-    lse_ref[0] = jnp.broadcast_to(max_ref[0:1, :] + jnp.log(sum_ref[0:1, :]), lse_ref.shape[1:])
-    scaled = acc_ref[...] / sum_ref[0:1, :]
+    total = acc_ref[0:1, :]
+    lse_ref[0] = jnp.broadcast_to(max_ref[0:1, :] + jnp.log(total), lse_ref.shape[1:])
+    scaled = acc_ref[...] / total
     low = low_half(QUERY_TILE)
     for a in range(2):
         even = half_roll(scaled[:, (2 * a) * QUERY_TILE : (2 * a + 1) * QUERY_TILE].T)
@@ -788,39 +800,98 @@
         vec_ref[:, tile(a)] = both.astype(BF16)
 
 
-def attend(scalars, q, kv, doc_row, head, tokens=()):
+def carrying(kernel, ins, outs, parts, pieces):
+    def body(*refs):
+        own_ins, refs = refs[:ins], refs[ins:]
+        at_ref, piece_refs, refs = refs[0], refs[1 : 1 + pieces], refs[1 + pieces :]
+        own_outs, refs = refs[:outs], refs[outs:]
+        places = 1 + max(part[5] for part in parts)
+        place_refs, refs = refs[:places], refs[places:]
+        own_scratch, held, sems = refs[: -pieces - 1], refs[-pieces - 1 : -1], refs[-1]
+        step, last = pl.program_id(0), pl.num_programs(0) - 1
+        come, leave = place_copies(parts, at_ref, piece_refs, place_refs, held, sems)
+
+        @pl.when(step == 0)
+        def _():
+            for copy in come:
+                copy.start()
+
+        kernel(*own_ins, *own_outs, *own_scratch)
+
+        @pl.when(step == 0)
+        def _():
+            for copy in come:
+                copy.wait()
+            for _, copy in leave:
+                copy.start()
+
+        @pl.when(step == last)
+        def _():
+            for _, copy in leave:
+                copy.wait()
+
+    return body
+
+
+def place_copies(parts, at_ref, pieces, out_refs, held, sems):
+    come = [
+        pltpu.make_async_copy(piece, here, sems.at[i])
+        for i, (piece, here) in enumerate(zip(pieces, held))
+    ]
+    leave = []
+    for k, (piece, row, rows, col, cols, out) in enumerate(parts):
+        here = held[piece].at[pl.ds(row, rows), pl.ds(col, cols)]
+        to = out_refs[out].at[pl.ds(pl.multiple_of(at_ref[k], 16), rows), :]
+        leave.append((piece, pltpu.make_async_copy(here, to, sems.at[len(pieces) + k])))
+    return come, leave
+
+
+def attend(scalars, q, kv, doc_row, head, tokens=(), carried=None):
     rows = q.shape[0]
     length = kv.shape[0]
     tiles = rows // QUERY_TILE
     lanes = GROUP * QUERY_TILE
     width = GROUP * HEAD_SIZE
     by_tile = pl.BlockSpec((QUERY_TILE, width), lambda t: (t, 0))
+    kernel = attend_kernel
+    more_in, more_out, more_shape, more_scratch, more = [], [], [], [], []
+    if carried:
+        pieces, parts, offsets, shapes = carried
+        kernel = carrying(kernel, 4, 3, parts, len(pieces))
+        more_in = [pl.BlockSpec(memory_space=pltpu.SMEM)] + unread(pieces)
+        more_out = unread(shapes)
+        more_shape = [jax.ShapeDtypeStruct(shape, BF16) for shape in shapes]
+        more_scratch = [pltpu.VMEM(piece.shape, BF16) for piece in pieces]
+        more_scratch.append(pltpu.SemaphoreType.DMA((len(pieces) + len(parts),)))
+        more = [jnp.stack(offsets).astype(jnp.int32), *pieces]
     return pl.pallas_call(
-        without(attend_kernel, 4, len(tokens)),
+        without(kernel, 4 + len(more_in), len(tokens)),
         grid=(tiles,),
         in_specs=[
             pl.BlockSpec(memory_space=pltpu.SMEM),
             pl.BlockSpec((QUERY_TILE, width), lambda t: (t, head)),
             whole((length, LANES)),
             pl.BlockSpec((8, QUERY_TILE), lambda t: (0, t)),
+            *more_in,
             *unread(tokens),
         ],
-        out_specs=[by_tile, by_tile, pl.BlockSpec((1, 8, lanes), lambda t: (t, 0, 0))],
+        out_specs=[by_tile, by_tile, pl.BlockSpec((1, 8, lanes), lambda t: (t, 0, 0)), *more_out],
         out_shape=[
             jax.ShapeDtypeStruct((rows, width), BF16),
             jax.ShapeDtypeStruct((rows, width), F32),
             jax.ShapeDtypeStruct((tiles, 8, lanes), F32),
+            *more_shape,
         ],
         scratch_shapes=[
             pltpu.VMEM((lanes, LANES), BF16),
             pltpu.VMEM((8, lanes), F32),
-            pltpu.VMEM((8, lanes), F32),
             pltpu.VMEM((LANES, lanes), F32),
+            *more_scratch,
         ],
         compiler_params=params("arbitrary"),
-        cost_estimate=lasting(22),
+        cost_estimate=lasting(18),
         name="attend",
-    )(scalars, q, kv, doc_row, *tokens)
+    )(scalars, q, kv, doc_row, *more, *tokens)
 
 
 def attend_back_kernel(
@@ -1024,21 +1095,16 @@
     count = 1 + max(part[0] for part in parts)
     outs = 1 + max(part[5] for part in parts)
     pieces, refs = refs[:count], refs[count + tokens :]
-    out_refs, held = refs[:outs], refs[outs:-1]
-    sems = refs[-1]
-    come = [pltpu.make_async_copy(pieces[i], held[i], sems.at[i]) for i in range(count)]
+    out_refs, held, sems = refs[:outs], refs[outs:-1], refs[-1]
+    come, leave = place_copies(parts, at_ref, pieces, out_refs, held, sems)
     for copy in come:
         copy.start()
-    leave = []
     for i in range(count):
         come[i].wait()
-        for k, (piece, row, rows, col, cols, out) in enumerate(parts):
+        for piece, copy in leave:
             if piece == i:
-                here = held[i].at[pl.ds(row, rows), pl.ds(col, cols)]
-                to = out_refs[out].at[pl.ds(pl.multiple_of(at_ref[k], 16), rows), :]
-                leave.append(pltpu.make_async_copy(here, to, sems.at[count + k]))
-                leave[-1].start()
-    for copy in leave:
+                copy.start()
+    for _, copy in leave:
         copy.wait()
 
 
@@ -1064,113 +1130,126 @@
     return sent, after(got, *arrive) if arrive else got
 
 
-def send_x(shard, extra=0):
-    side = lax.axis_index("ctx") % 2
+def whole_parts(shard, other, near, columns, arrive=(), extra=0):
+    rank, ranks = lax.axis_index("fsdp"), lax.axis_size("fsdp")
     rows = shard.shape[0] - extra
-    sent = take_rows(shard[:rows], side, rows // 2)
-    return jnp.concatenate([sent, shard[rows:]], axis=0) if extra else sent
-
-
-def collect(shard, near, extra=0, arrive=()):
-    rank, ranks = lax.axis_index("fsdp"), lax.axis_size("fsdp")
-    side = lax.axis_index("ctx") % 2
-    rows, width = shard.shape[0] - extra, shard.shape[1]
-    half = rows // 2
-    _, far = move(near[:half] if extra else near, "ctx", 1, (), arrive)
-    _, near_other = move(near, "fsdp", 1, (), arrive)
-    pieces = [shard, swap(shard, "fsdp", 1), near, near_other, far, swap(far, "fsdp", 1)]
-    whose = [rank, rank ^ 1, rank ^ 2, rank ^ 3, rank ^ 2, rank ^ 3]
-    parts, offsets = [], []
-    for k in range(6):
-        size = rows if k < 2 else half
-        parts.append((k, 0, size, 0, width, 0))
-        offsets.append(whose[k] * rows + (0, 0, side, side, 1 - side, 1 - side)[k] * half)
-        if extra and k < 4:
-            parts.append((k, size, extra, 0, width, 1))
-            offsets.append(whose[k] * extra)
-    shapes = [(ranks * rows, width)] + ([(ranks * extra, width)] if extra else [])
-    return place(pieces, parts, offsets, shapes)
-
-
-def collect_whole(shard, other, near, columns, tokens=(), arrive=()):
-    rank, ranks = lax.axis_index("fsdp"), lax.axis_size("fsdp")
-    rows = shard.shape[0]
     pieces = [shard, other, near, move(near, "fsdp", 1, (), arrive)[1]]
     parts, offsets, shapes = [], [], {}
-    for k, piece in enumerate((0, 1, 2, 3)):
+    for k in range(4):
         at = 0
         for width, out, shard_rows, first in columns:
-            parts.append((piece, 0, rows, at, width, out))
+            parts.append((k, 0, rows, at, width, out))
             offsets.append((rank ^ k) * shard_rows + first)
             shapes[out] = (ranks * shard_rows, width)
             at += width
-    return place(pieces, parts, offsets, [shapes[out] for out in sorted(shapes)], tokens)
-
-
-def own_order(block):
-    rank = lax.axis_index("fsdp")
-    width = block.shape[1] // 4
-    return [lax.dynamic_slice_in_dim(block, (rank ^ k) * width, width, 1) for k in (0, 2, 1, 3)]
+        if extra:
+            out = 1 + max(column[1] for column in columns)
+            parts.append((k, rows, extra, 0, at, out))
+            offsets.append((rank ^ k) * extra)
+            shapes[out] = (ranks * extra, at)
+    return pieces, parts, offsets, [shapes[out] for out in sorted(shapes)]
+
+
+def product_kernel(blocks, adds, halves, at_ref, *refs):
+    left_refs, refs = refs[:blocks], refs[blocks:]
+    grad_ref, refs = refs[0], refs[1:]
+    add_refs, refs = refs[:adds], refs[adds:]
+    rows = left_refs[0].shape[1]
+    turned_ref = refs[-2]
+
+    @pl.when(pl.program_id(0) == 0)
+    def _():
+        for i, left_ref in enumerate(left_refs):
+            turned = left_ref[...].astype(F32).T.astype(BF16)
+            turned_ref[i * rows : (i + 1) * rows, :] = turned
+
+    total = dot_nn(turned_ref[...], grad_ref[...])
+    for add_ref in add_refs:
+        total = total + add_ref[...].astype(F32)
+    if not halves:
+        refs[0][...] = total.astype(BF16)
+        return
+    kept_ref, sent_ref, total_ref = refs[0], refs[1], refs[-1]
+    total_ref[...] = total
+    half = rows // 2
+    side = at_ref[blocks]
+    for i in range(blocks):
+        to = slice(i * half, (i + 1) * half)
+        mine = pl.multiple_of(i * rows + side * half, half)
+        theirs = pl.multiple_of(i * rows + (1 - side) * half, half)
+        kept_ref[to, :] = total_ref[pl.ds(mine, half), :].astype(BF16)
+        sent_ref[to, :] = total_ref[pl.ds(theirs, half), :].astype(BF16)
+
+
+def product(left, which, grad, adds=(), halves=False, tokens=()):
+    tokens_count = len(tokens)
+    depth, width = grad.shape
+    rows = left.shape[1] // lax.axis_size("fsdp")
+    height = rows * len(which)
+    span = max(w for w in range(LANES, min(width, 2049), LANES) if width % w == 0)
+    span = span if 5 * span >= 2 * width else width
+    rank, side = lax.axis_index("fsdp"), lax.axis_index("ctx") % 2
+    at = jnp.stack([rank ^ k for k in which] + [side]).astype(jnp.int32)
+    block_of = lambda i: pl.BlockSpec((depth, rows), lambda t, at: (0, at[i]))
+    add_of = lambda block: pl.BlockSpec((height, span), lambda t, at: (block, t))
+    outs = 2 if halves else 1
+    shape = (height // outs, width)
+    found = pl.pallas_call(
+        without(
+            functools.partial(product_kernel, len(which), len(adds), halves),
+            2 + len(which) + len(adds),
+            tokens_count,
+        ),
+        grid_spec=pltpu.PrefetchScalarGridSpec(
+            num_scalar_prefetch=1,
+            grid=(width // span,),
+            in_specs=[block_of(i) for i in range(len(which))]
+            + [pl.BlockSpec((depth, span), lambda t, at: (0, t))]
+            + [add_of(block) for _, block in adds]
+            + unread(tokens),
+            out_specs=[pl.BlockSpec((height // outs, span), lambda t, at: (0, t))] * outs,
+            scratch_shapes=[
+                pltpu.VMEM((height, depth), BF16),
+                pltpu.VMEM((height, span), F32),
+            ],
+        ),
+        out_shape=[jax.ShapeDtypeStruct(shape, BF16)] * outs,
+        compiler_params=params("arbitrary"),
+        cost_estimate=lasting(1 + height * width * 3e-6),
+        name="product",
+    )(at, *([left] * len(which)), grad, *[array for array, _ in adds], *tokens)
+    return found if halves else found[0]
 
 
 class Reduction:
     def __init__(self, left, grad, more=None):
-        self.left, self.grad, self.more = left, grad, more
-        _, _, by_core, by_both = left
-        sent = dot_tn(jnp.concatenate([by_core, by_both], axis=1), grad)
-        if more:
-            sent = sent + jnp.concatenate(more[2:], axis=0)
-        self.sent, self.got = move(sent.astype(BF16), "fsdp", 1)
-
-    def over_x(self, start=(), arrive=()):
-        own, by_x, _, _ = self.left
-        rows = own.shape[1]
-        self.near = self.got[:rows]
-        sent = dot_tn(by_x, self.grad) + self.got[rows:].astype(F32)
-        if self.more:
-            sent = sent + self.more[1]
-        sent = sent.astype(BF16)
+        self.left, self.grad = left, grad
+        self.more = more or [[], [], []]
+        sent = product(left, (1, 3), grad, self.more[2])
+        self.sent, self.got = move(sent, "fsdp", 1)
+
+    def hold(self, *tokens):
+        self.got = after(self.got, *tokens)
+
+    def over_x(self, start=(), arrive=(), tokens=()):
+        self.near = self.got
+        sent = product(self.left, (2,), self.grad, [(self.got, 1)] + self.more[1], False, tokens)
         self.sent, self.got = move(sent, "fsdp", 2, start, arrive)
 
-    def halve(self, bit, start, arrive):
-        side = (lax.axis_index("ctx") // bit) % 2
-        half = self.own.shape[0] // 2
-        self.kept = take_rows(self.own, side, half)
-        sent = take_rows(self.own, 1 - side, half).astype(BF16)
-        self.sent, self.got = move(sent, "ctx", bit, start, arrive)
-
-    def add_x(self):
-        self.own = dot_tn(self.left[0], self.grad) + self.near.astype(F32) + self.got.astype(F32)
-        if self.more:
-            self.own = self.own + self.more[0]
-
-    def over_y(self, start=(), arrive=()):
-        self.add_x()
-        self.halve(1, start, arrive)
-
-    def over_z(self, start=(), arrive=()):
-        self.own = self.kept + self.got.astype(F32)
-        self.halve(2, start, arrive)
-
-    def rest(self, start=(), arrive=()):
-        self.own = (self.kept + self.got.astype(F32)).astype(BF16)
-        bit = 4
-        while bit < lax.axis_size("ctx"):
-            self.sent, self.got = move(self.own, "ctx", bit, start, arrive)
-            self.own = (self.own.astype(F32) + self.got.astype(F32)).astype(BF16)
-            bit *= 2
-
-    def join(self, bit, start=()):
-        side = (lax.axis_index("ctx") // bit) % 2
-        self.sent, other = move(self.own, "ctx", bit, start)
-        self.own = jnp.concatenate(
-            [jnp.where(side == 0, self.own, other), jnp.where(side == 0, other, self.own)], axis=0
-        )
-
-    def result(self, z_start=(), y_start=()):
-        self.join(2, z_start)
-        self.join(1, y_start)
-        return self.own.astype(F32)
+    def then_over_y(self, start=(), arrive=(), tokens=()):
+        adds = [(self.near, 0), (self.got, 0)] + self.more[0]
+        self.kept, sent = product(self.left, (0,), self.grad, adds, True, tokens)
+        self.sent, self.got = move(sent, "ctx", 1, start, arrive)
+
+    def first_over_y(self, start=(), arrive=(), tokens=()):
+        self.kept, sent = product(self.left, (0, 2), self.grad, [(self.got, 0)], True, tokens)
+        self.sent, self.got = move(sent, "ctx", 1, start, arrive)
+
+    def then_over_x(self, start=(), arrive=()):
+        total = (self.kept.astype(F32) + self.got.astype(F32)).astype(BF16)
+        half = total.shape[0] // 2
+        self.kept = total[:half]
+        self.sent, self.got = move(total[half:], "fsdp", 2, start, arrive)
 
 
 def ctx_bits():
@@ -1227,53 +1306,38 @@
     return found, at
 
 
-def split_kernel(count, side_ref, *refs):
-    owns, (kept_ref, sent_ref) = refs[:count], refs[count:]
-    half = kept_ref.shape[0]
-    found, _ = stretches_of([own.shape for own in owns], 2 * half)
+def fold_kernel(count, side_ref, *refs):
+    new_ref, sent_ref = refs[2 * count :]
+    half = new_ref.shape[0]
     mine = pl.multiple_of(side_ref[0] * half, half)
     theirs = pl.multiple_of((1 - side_ref[0]) * half, half)
-    for index, first, at in found:
-        own = owns[index]
-        columns = slice(at, at + own.shape[1])
-        kept_ref[:, columns] = own[pl.ds(first + mine, half), :]
-        sent_ref[:, columns] = own[pl.ds(first + theirs, half), :]
-
-
-def split_pack(side, owns):
-    rows = min(own.shape[0] for own in owns)
-    _, width = stretches_of([own.shape for own in owns], rows)
+    at = 0
+    for i in range(count):
+        kept_ref, got_ref = refs[2 * i], refs[2 * i + 1]
+        height, width = kept_ref.shape
+        for first in range(0, height, 2 * half):
+            columns = slice(at, at + width)
+            for row, out_ref in ((mine, new_ref), (theirs, sent_ref)):
+                rows = pl.ds(first + row, half)
+                total = kept_ref[rows, :].astype(F32) + got_ref[rows, :].astype(F32)
+                out_ref[:, columns] = total.astype(BF16)
+            at += width
+
+
+def fold_pack(side, pairs):
+    arrays = [array for pair in pairs for array in pair]
+    rows = min(array.shape[0] for array in arrays)
+    _, width = stretches_of([kept.shape for kept, _ in pairs], rows)
     shape = (rows // 2, width)
     return pl.pallas_call(
-        functools.partial(split_kernel, len(owns)),
-        in_specs=[pl.BlockSpec(memory_space=pltpu.SMEM)] + [whole(own.shape) for own in owns],
-        out_specs=[whole(shape)] * 2,
-        out_shape=[jax.ShapeDtypeStruct(shape, BF16)] * 2,
-        compiler_params=pltpu.CompilerParams(vmem_limit_bytes=VMEM_LIMIT),
-        cost_estimate=lasting(3),
-        name="split",
-    )(side.reshape(1), *owns)
-
-
-def fold_kernel(side_ref, kept_ref, got_ref, new_ref, sent_ref):
-    half = new_ref.shape[0]
-    mine = pl.ds(pl.multiple_of(side_ref[0] * half, half), half)
-    theirs = pl.ds(pl.multiple_of((1 - side_ref[0]) * half, half), half)
-    new_ref[...] = (kept_ref[mine, :].astype(F32) + got_ref[mine, :].astype(F32)).astype(BF16)
-    sent_ref[...] = (kept_ref[theirs, :].astype(F32) + got_ref[theirs, :].astype(F32)).astype(BF16)
-
-
-def fold_pack(side, kept, got):
-    shape = (kept.shape[0] // 2, kept.shape[1])
-    return pl.pallas_call(
-        fold_kernel,
-        in_specs=[pl.BlockSpec(memory_space=pltpu.SMEM)] + [whole(kept.shape)] * 2,
+        functools.partial(fold_kernel, len(pairs)),
+        in_specs=[pl.BlockSpec(memory_space=pltpu.SMEM)] + [whole(array.shape) for array in arrays],
         out_specs=[whole(shape)] * 2,
         out_shape=[jax.ShapeDtypeStruct(shape, BF16)] * 2,
         compiler_params=pltpu.CompilerParams(vmem_limit_bytes=VMEM_LIMIT),
         cost_estimate=lasting(2),
         name="fold",
-    )(side.reshape(1), kept, got)
+    )(side.reshape(1), *arrays)
 
 
 def join_kernel(side_ref, own_ref, got_ref, out_ref):
@@ -1295,26 +1359,30 @@
     )(side.reshape(1), own, got)
 
 
-def unpack_kernel(parts, side_ref, own_ref, got_ref, *out_refs):
-    half = own_ref.shape[0]
-    mine = pl.multiple_of(side_ref[0] * half, half)
-    theirs = pl.multiple_of((1 - side_ref[0]) * half, half)
-    for out, first, at, skip, width in parts:
-        columns = slice(at, at + width)
-        to = slice(skip, skip + width)
-        out_refs[out][pl.ds(first + mine, half), to] = own_ref[:, columns].astype(F32)
-        out_refs[out][pl.ds(first + theirs, half), to] = got_ref[:, columns].astype(F32)
-
-
-def unpack(side, own, got, shapes):
-    rows = 2 * own.shape[0]
-    found, _ = stretches_of(shapes, rows)
-    parts = [(index, first, at, 0, shapes[index][1]) for index, first, at in found]
+def unpack_kernel(parts, outs, side_ref, own_ref, got_ref, *out_refs):
+    rows = own_ref.shape[0]
+    for side in range(2):
+
+        @pl.when(side_ref[0] == side)
+        def _():
+            for array, height, first, at in parts:
+                for half, ref in ((side, own_ref), (1 - side, got_ref)):
+                    row = half * (height // 2) + first
+                    for out_ref, (source, top, end, left, right) in zip(out_refs, outs):
+                        if source == array and top <= row < end:
+                            to = slice(row - top, row - top + rows)
+                            out_ref[to, :] = ref[:, at + left : at + right].astype(F32)
+
+
+def unpack(side, own, got, shapes, outs):
+    found, _ = stretches_of([(height // 2, width) for height, width in shapes], own.shape[0])
+    parts = [(index, shapes[index][0], first, at) for index, first, at in found]
+    out_shapes = [(end - top, right - left) for _, top, end, left, right in outs]
     return pl.pallas_call(
-        functools.partial(unpack_kernel, parts),
+        functools.partial(unpack_kernel, parts, outs),
         in_specs=[pl.BlockSpec(memory_space=pltpu.SMEM)] + [whole(own.shape)] * 2,
-        out_specs=[whole(shape) for shape in shapes],
-        out_shape=[jax.ShapeDtypeStruct(shape, F32) for shape in shapes],
+        out_specs=[whole(shape) for shape in out_shapes],
+        out_shape=[jax.ShapeDtypeStruct(shape, F32) for shape in out_shapes],
         compiler_params=pltpu.CompilerParams(vmem_limit_bytes=VMEM_LIMIT),
         cost_estimate=lasting(4),
         name="unpack",
@@ -1322,34 +1390,41 @@
 
 
 class Pack:
-    def __init__(self, owns):
-        self.shapes = [own.shape for own in owns]
-        self.owns = owns
+    def __init__(self, pairs):
+        self.pairs = pairs
+        self.shapes = [(2 * kept.shape[0], kept.shape[1]) for kept, _ in pairs]
+
+    def hold(self, *tokens):
+        self.got = after(self.got, *tokens)
 
     def side(self, bit):
         return (lax.axis_index("ctx") // bit) % 2
 
-    def over_y(self, start=(), arrive=()):
-        self.kept, sent = split_pack(self.side(1), self.owns)
-        self.sent, self.got = move(sent, "ctx", 1, start, arrive)
-
     def over_z(self, start=(), arrive=()):
-        self.kept, sent = fold_pack(self.side(2), self.kept, self.got)
+        self.kept, sent = fold_pack(self.side(2), self.pairs)
         self.sent, self.got = move(sent, "ctx", 2, start, arrive)
 
     def rest(self, start=(), arrive=()):
         self.own = (self.kept.astype(F32) + self.got.astype(F32)).astype(BF16)
+        self.kept = None
         for bit in ctx_bits()[2:]:
+            self.total()
             self.sent, self.got = move(self.own, "ctx", bit, start, arrive)
-            self.own = (self.own.astype(F32) + self.got.astype(F32)).astype(BF16)
+            self.kept = self.own
+
+    def total(self):
+        if self.kept is not None:
+            self.own = (self.kept.astype(F32) + self.got.astype(F32)).astype(BF16)
+            self.kept = None
 
     def back_z(self, start=(), arrive=()):
+        self.total()
         self.sent, got = move(self.own, "ctx", 2, start, arrive)
         self.own = join_pack(self.side(2), self.own, got)
 
-    def back_y(self, start=(), arrive=()):
+    def back_y(self, outs, start=(), arrive=()):
         self.sent, got = move(self.own, "ctx", 1, start, arrive)
-        return unpack(self.side(1), self.own, got, self.shapes)
+        return unpack(self.side(1), self.own, got, self.shapes, outs)
 
 
 def shift_along(block, axis, distance):
@@ -1365,10 +1440,8 @@
 
 class Scan:
     def __init__(self, own, send, upwards):
-        shape = (MESSAGE_ROWS, MAMBA_INNER)
         self.own, self.send, self.upwards = own, send, upwards
-        factor_row = lax.broadcasted_iota(jnp.int32, shape, 0) >= STATE_SIZE
-        self.seen = factor_row.astype(F32)
+        self.seen = None
         self.bits = ctx_bits()
 
     def step(self, arrive=()):
@@ -1376,7 +1449,9 @@
         above = (lax.axis_index("ctx") // bit) % 2 == 1
         _, got = move(self.send, "ctx", bit, (), arrive)
         first = above if self.upwards else jnp.logical_not(above)
-        self.own, self.send, self.seen = scan_step(first, self.own, self.seen, got)
+        self.own, self.send, self.seen = scan_step(
+            first, self.own, self.seen, got, not self.bits
+        )
         return self.send
 
     def finish(self, arrive=()):
@@ -1425,20 +1500,30 @@
     small_rows = 16
     small = jnp.pad(small, (0, small_rows * wide - small.shape[0])).reshape(small_rows, wide)
     shard_qkv = jnp.concatenate([jnp.concatenate([w_q, key_value_weight], axis=1), small], axis=0)
-    near_qkv = swap(send_x(shard_qkv, small_rows), "fsdp", 2)
-    near_xbc = swap(send_x(xbc_dt), "fsdp", 2)
+    near_qkv = swap(shard_qkv, "fsdp", 2)
+    near_xbc = swap(xbc_dt, "fsdp", 2)
     side_by_side = lambda w, rows: [w[i : i + rows] for i in range(0, w.shape[0], rows)]
     rows_in = w_z.shape[0]
     shard_omo = jnp.concatenate([w_o, w_mo], axis=0)
     shard_zo = jnp.concatenate([w_z] + side_by_side(shard_omo, rows_in), axis=1)
-    shard_gate_up = jnp.concatenate([w_gate, w_up], axis=1)
-    sent_zo = after(shard_zo, near_qkv)
-    near_zo = swap(sent_zo, "fsdp", 2)
-    sent_gate_up = after(shard_gate_up, near_xbc)
-    near_gate_up = swap(sent_gate_up, "fsdp", 2)
-    sent_down = after(w_down, near_zo)
-    near_down = swap(sent_down, "fsdp", 2)
-    full_qkv, small_all = collect(shard_qkv, near_qkv, small_rows)
+    shard_ffn = jnp.concatenate([w_gate, w_up] + side_by_side(w_down, rows_in), axis=1)
+    shard_zo = after(shard_zo, near_qkv)
+    near_zo = swap(shard_zo, "fsdp", 2)
+    shard_ffn = after(shard_ffn, near_qkv)
+    near_ffn = swap(shard_ffn, "fsdp", 2)
+    other_xbc, other_zo, other_ffn = [
+        swap(shard, "fsdp", 1) for shard in (xbc_dt, shard_zo, shard_ffn)
+    ]
+    full_qkv, small_all = place(
+        *whole_parts(
+            shard_qkv,
+            swap(shard_qkv, "fsdp", 1),
+            near_qkv,
+            [(shard_qkv.shape[1], 0, rows_in, 0)],
+            (),
+            small_rows,
+        )
+    )
     model = w_down.shape[1]
 
     def stretches(out, shard_rows):
@@ -1498,52 +1583,54 @@
         qkv_raw[:, :q_width], qkv_raw[:, q_width:], cosine, sine
     )
     spreads = [Spread(kv) for kv in (kv_first, kv_second)]
-    full_xbc = collect(xbc_dt, near_xbc, 0, [query])[0]
+    full_xbc = place(
+        *whole_parts(
+            xbc_dt,
+            other_xbc,
+            after(near_xbc, query),
+            [(xbc_dt.shape[1], 0, rows_in, 0)],
+        ),
+        [other_zo, other_ffn],
+    )[0]
     for spread_kv in spreads:
         spread_kv.step()
-        spread_kv.step([full_xbc])
+        spread_kv.block = after(spread_kv.block, full_xbc)
+        spread_kv.step()
     mixed_in = dot_nn(normed, full_xbc[:, :CHANNELS]).astype(BF16)
     dt_raw = dot_nn(normed, full_xbc[:, CHANNELS:])
     edge = shift_along(mixed_in[rows - 8 :], "ctx", 1).astype(F32)
     y_local, state_local, message, own_state, decay, c_mat = mamba_forward(
         scalars, edge, mixed_in, dt_raw, doc_col[:rows], conv_pack, head_pack, skip_wide
     )
-    kv_all = [spread_kv.finish([message]) for spread_kv in spreads]
+    kv_all = [spreads[0].finish([message])]
     scan = Scan(own_state, message, True)
-    tokens = [message, sent_gate_up, sent_down]
+    tokens = [message]
     attended = [attend(attn_scalars, query, kv_all[0], doc_row, 0, tokens)]
     first_done = attended[0][0]
-    other_zo, other_gate_up, other_down = [
-        move(shard, "fsdp", 1, (), [first_done])[1] for shard in (shard_zo, shard_gate_up, w_down)
-    ]
-    tokens = [scan.step([first_done]), first_done, other_zo, other_gate_up, other_down]
-    attended.append(attend(attn_scalars, query, kv_all[1], doc_row, 1, tokens))
+    kv_all.append(spreads[1].finish([first_done]))
+    carried = whole_parts(
+        shard_zo,
+        other_zo,
+        after(near_zo, message),
+        [(w_z.shape[1], 0, rows_in, 0)] + stretches(1, shard_omo.shape[0]),
+    )
+    tokens = [scan.step([first_done]), first_done]
+    *second, full_z, full_omo = attend(
+        attn_scalars, query, kv_all[1], doc_row, 1, tokens, carried
+    )
+    attended.append(second)
     second_done = attended[1][0]
     scan.step([second_done])
-    full_z, full_omo = collect_whole(
-        shard_zo,
-        other_zo,
-        near_zo,
-        [(w_z.shape[1], 0, rows_in, 0)] + stretches(1, shard_omo.shape[0]),
-        [second_done],
-        [first_done],
-    )
     gate_z = dot_nn(normed, full_z)
-    full_gate_up = collect_whole(
-        shard_gate_up,
-        other_gate_up,
-        after(near_gate_up, second_done),
-        [(2 * w_gate.shape[1], 0, rows_in, 0)],
-        [second_done],
-        [second_done],
-    )[0]
-    state_in = scan.finish([gate_z, full_gate_up])
-    full_down = collect_whole(
-        w_down,
-        other_down,
-        after(near_down, second_done),
-        [(model, 0, w_down.shape[0], 0)],
-    )[0]
+    state_in = scan.finish([gate_z])
+    full_gate_up, full_down = place(
+        *whole_parts(
+            shard_ffn,
+            other_ffn,
+            after(near_ffn, state_in),
+            [(2 * w_gate.shape[1], 0, rows_in, 0)] + stretches(1, w_down.shape[0]),
+        )
+    )
     y_total, both, state_true = mamba_correct(
         y_local, state_local, c_mat, decay, state_in, gate_z, attended[0][0], attended[1][0]
     )
@@ -1560,13 +1647,12 @@
     result = hidden + dot_nn(activ, full_down)
 
     grad_out = cotangent[0]
-    down = Reduction(own_order(activ), grad_out)
+    down = Reduction(activ, grad_out)
     grad_act = time_steps(grad_out, full_down)
     grad_gate = (grad_act * upper * sig_gate * (1.0 + gate * (1.0 - sig_gate))).astype(BF16)
     grad_up = (grad_act * silu_gate).astype(BF16)
     grad_gate_up = jnp.concatenate([grad_gate, grad_up], axis=1)
-    gate_up_sum = Reduction(own_order(normed_ffn), grad_gate_up)
-    down.over_x()
+    gate_up_sum = Reduction(normed_ffn, grad_gate_up)
     grad_n2 = time_steps(grad_gate_up, full_gate_up)
     scaled_two = grad_n2 * gain_two[None, :]
     grad_hidden = (
@@ -1574,15 +1660,15 @@
         + scale_two * scaled_two
         - hidden * scale_two**3 * jnp.mean(scaled_two * hidden, axis=-1, keepdims=True)
     )
-    grad_hid_b = grad_hidden.astype(BF16)
     gate_up_sum.over_x()
+    down.first_over_y(tokens=[gate_up_sum.sent])
+    grad_hid_b = after(grad_hidden.astype(BF16), gate_up_sum.sent, down.sent)
     both_grad = time_steps(grad_hid_b, full_omo)
     grad_y, grad_z, own_grad, grad_message, grad_attn = mamba_gate_back(
-        both_grad, gate_z, y_total, c_mat, decay, own_state, [down.sent, gate_up_sum.sent]
-    )
-    omo = Reduction(own_order(both), grad_hid_b)
-    left_mix = own_order(normed)
-    z_sum = Reduction(left_mix, grad_z)
+        both_grad, gate_z, y_total, c_mat, decay, own_state
+    )
+    omo = Reduction(both, grad_hid_b)
+    z_sum = Reduction(normed, grad_z)
     scan = Scan(own_grad, grad_message, False)
     backs = []
 
@@ -1601,32 +1687,46 @@
             )
         )
 
+    down.hold(grad_attn)
+    down.then_over_x()
+    backs = []
+
+    def back(j, tokens):
+        backs.append(
+            attend_back(
+                attn_scalars,
+                query,
+                grad_attn,
+                attended[j][1],
+                attended[j][2],
+                kv_all[j],
+                doc_row,
+                j,
+                tokens,
+            )
+        )
+
+    scan.step()
+    gate_up_sum.hold(scan.send)
+    gate_up_sum.then_over_y()
+    omo.first_over_y(tokens=[gate_up_sum.sent])
+    z_sum.over_x()
     grad_n1_z = time_steps(grad_z, full_z)
-    first_send = scan.step()
-    back(0, [first_send, omo.sent, z_sum.sent, grad_n1_z])
+    scan.step([gate_up_sum.sent])
+    gate_up_sum.hold(scan.send)
+    down.hold(scan.send)
+    ffn = Pack([(gate_up_sum.kept, gate_up_sum.got), (down.kept, down.got)])
+    ffn.over_z()
+    back(0, [scan.send, ffn.sent, omo.sent, z_sum.sent, grad_n1_z])
     first_done = backs[0][0]
-    for part in (down, gate_up_sum, omo, z_sum):
-        part.got = after(part.got, first_done)
-    second_send = scan.step([first_done])
-    down.add_x()
-    gate_up_sum.add_x()
-    ffn = Pack([gate_up_sum.own.astype(BF16), down.own.astype(BF16)])
-    ffn.over_y()
-    omo.over_x()
-    z_sum.over_x()
-    kv_sums = [BlockSums(backs[0][1])]
-    back(1, [second_send, ffn.sent, omo.sent, z_sum.sent, first_done])
-    second_done = backs[1][0]
     for part in (ffn, omo, z_sum):
-        part.got = after(part.got, second_done)
-    kv_sums[0].step((), [second_done])
-    state_grad = scan.finish([second_done])
-    ffn.over_z()
-    omo.add_x()
-    z_sum.add_x()
-    mixer = Pack([z_sum.own.astype(BF16), omo.own.astype(BF16)])
-    mixer.over_y()
-    kv_sums.append(BlockSums(backs[1][1]))
+        part.hold(first_done)
+    state_grad = scan.finish([first_done])
+    ffn.rest()
+    omo.then_over_x()
+    z_sum.then_over_y()
+    first_kv = BlockSums(backs[0][1])
+    first_kv.sent = first_kv.blocks[first_kv.blocks.shape[0] // 2 :]
     grad_mixed, tail, edge_grad, grad_dt, grad_conv, grad_heads = mamba_back(
         scalars,
         edge,
@@ -1641,16 +1741,16 @@
         y_total,
         state_true,
         state_grad,
-        [ffn.sent, mixer.sent, kv_sums[0].blocks],
-    )
+        [ffn.sent, z_sum.sent, omo.sent, first_kv.sent, first_done],
+    )
+    third_done = grad_dt
+    for part in (ffn, omo, z_sum):
+        part.hold(third_done)
+    first_kv.step((), [third_done])
+    mixer = Pack([(z_sum.kept, z_sum.got), (omo.kept, omo.got)])
+    mixer.over_z()
     behind = shift_along(edge_grad, "ctx", -1)
     grad_mixed = grad_mixed.at[rows - 8 :].set((tail + behind).astype(BF16))
-    third_done = grad_dt
-    for part in (ffn, mixer):
-        part.got = after(part.got, third_done)
-    kv_sums[1].step((), [third_done])
-    kv_both = BlockSums(jnp.concatenate([part.blocks for part in kv_sums], axis=1))
-    kv_both.bits = kv_sums[0].bits
     grad_xbc = jnp.concatenate([grad_mixed, grad_dt], axis=1)
     fsdp_rank = lax.axis_index("fsdp")
     conv_width, heads_width = conv_b.shape[0], dt_bias.shape[0]
@@ -1667,36 +1767,79 @@
         small_grad.reshape(ranks, rows_in, small_width),
         ((0, 0), (0, 0), (small_at, wide_in - small_at - small_width)),
     )
-    more = [lax.dynamic_index_in_dim(small_grad, fsdp_rank ^ k, 0, False) for k in (0, 2, 1, 3)]
-    xbc_sum = Reduction(left_mix, grad_xbc, more)
+    block_of = lambda k: lax.dynamic_index_in_dim(small_grad, fsdp_rank ^ k, 0, False)
+    more = [
+        [(block_of(0), 0)],
+        [(block_of(2), 0)],
+        [(jnp.concatenate([block_of(1), block_of(3)], axis=0), 0)],
+    ]
+    xbc_sum = Reduction(normed, grad_xbc, more)
+    grad_n1_xbc = time_steps(grad_xbc, full_xbc)
     xbc_sum.over_x()
-    x_left = [xbc_sum.sent]
-    kv_both.step((), x_left)
-    ffn.rest((), x_left)
-    grad_kv = kv_both.finish()
-    grad_qkv = rope_back(
-        backs[0][0], backs[1][0], grad_kv[:, :LANES], grad_kv[:, LANES:], cosine, sine
-    )
-    qkv_sum = Reduction(left_mix, grad_qkv)
+    ffn.back_z((), [xbc_sum.sent])
+    back(1, [xbc_sum.sent, mixer.sent, ffn.own, first_kv.blocks, grad_n1_xbc, third_done])
+    second_done = backs[1][0]
+    ff = w_gate.shape[1]
+    grad_w_gate, grad_w_up, grad_w_down = ffn.back_y(
+        [
+            (0, 0, rows_in, 0, ff),
+            (0, 0, rows_in, ff, 2 * ff),
+            (1, 0, w_down.shape[0], 0, model),
+        ],
+        (),
+        [second_done],
+    )
+    xbc_sum.hold(second_done)
+    mixer.hold(second_done)
+    first_kv.step((), [second_done])
+    second_kv = BlockSums(backs[1][1])
+    second_kv.step((), [grad_w_down])
+    y_in = [second_kv.blocks]
+    xbc_sum.then_over_y()
+    y_left = [xbc_sum.sent]
+    xbc = Pack([(xbc_sum.kept, after(xbc_sum.got, *y_in))])
+    second_kv.step(y_left)
+    z_in = [second_kv.blocks]
+    first_kv.step((), y_in)
+    grad_kv0, grad_kv1 = first_kv.finish(), second_kv.finish()
+    grad_qkv = rope_back(backs[0][0], backs[1][0], grad_kv0, grad_kv1, cosine, sine)
+    qkv_sum = Reduction(normed, grad_qkv)
+    core_left = [qkv_sum.sent]
+    xbc.over_z((), core_left)
+    mixer.rest((), core_left)
     qkv_sum.over_x()
-    xbc_sum.add_x()
-    qkv_sum.add_x()
-    last_own = jnp.concatenate([xbc_sum.own, qkv_sum.own], axis=1).astype(BF16)
-    ffn.back_z()
-    mixer.over_z(x_left)
-    mixer.rest()
-    mixer.back_z()
-    grad_w_gate_up, grad_w_down = ffn.back_y()
-    grad_w_z, grad_w_omo = mixer.back_y()
-    last_total = lax.psum(last_own, "ctx").astype(F32)
-    grad_w_xbc, grad_w_qkv = last_total[:, :wide_in], last_total[:, wide_in:]
-    small_own = grad_w_xbc[:, small_at : small_at + small_width].reshape(-1)[:small_count]
+    x_left = [qkv_sum.sent]
+    qkv_sum.then_over_y()
+    y_left = [qkv_sum.sent]
+    xbc.rest((), y_left)
+    mixer.back_z((), y_left)
+    qkv = Pack([(qkv_sum.kept, after(qkv_sum.got, mixer.own))])
+    qkv.over_z()
+    z_left = [qkv.sent]
+    xbc.back_z((), z_left)
+    omo_rows = shard_omo.shape[0]
+    mixer_outs = [
+        (0, 0, rows_in, 0, w_z.shape[1]),
+        (1, 0, o_rows, 0, model),
+        (1, o_rows, omo_rows, 0, model),
+    ]
+    qkv.rest()
+    qkv.back_z()
+    join_left = [qkv.own]
+    grad_w_q, grad_w_kv = qkv.back_y(
+        [(0, 0, rows_in, 0, q_width), (0, 0, rows_in, q_width, qkv_raw.shape[1])]
+    )
+    grad_w_z, grad_w_o, grad_w_mo = mixer.back_y(mixer_outs, (), join_left)
+    grad_w_xbc, grad_w_dt = xbc.back_y(
+        [(0, 0, rows_in, 0, CHANNELS), (0, 0, rows_in, CHANNELS, wide_in)], (), join_left
+    )
+    small_own = grad_w_dt[:, small_at - CHANNELS : small_at - CHANNELS + small_width].reshape(-1)[:small_count]
     conv_own = small_own[: conv_width * (CONV + 1)].reshape(CONV + 1, conv_width)
     heads_own = small_own[conv_width * (CONV + 1) :].reshape(3, heads_width)
     grad_n1 = (
         grad_n1_z
-        + time_steps(grad_xbc, full_xbc)
-        + time_steps(grad_qkv, full_qkv)
+        + grad_n1_xbc
+        + time_steps(after(grad_qkv, *x_left), full_qkv)
     )
     scaled_one = grad_n1 * full_gain_mix[None, :]
     grad_tokens = (
@@ -1705,31 +1848,33 @@
         - inputs * scale_one**3 * jnp.mean(scaled_one * inputs, axis=-1, keepdims=True)
     )
     row_sums = lambda grad, weight: jnp.sum(grad * weight.astype(F32), axis=1)
-    grad_gain_ffn = row_sums(
-        grad_w_gate_up, jnp.concatenate([w_gate, w_up], axis=1)
+    grad_gain_ffn = (
+        row_sums(grad_w_gate, w_gate) + row_sums(grad_w_up, w_up)
     ) / gain_ffn.astype(F32)
     grad_gain_mix = (
         row_sums(grad_w_z, w_z)
-        + row_sums(grad_w_xbc, xbc_dt)
-        + row_sums(grad_w_qkv, jnp.concatenate([w_q, key_value_weight], axis=1))
+        + row_sums(grad_w_xbc, w_xbc)
+        + row_sums(grad_w_dt[:, :MAMBA_HEADS], w_dt)
+        + row_sums(grad_w_q, w_q)
+        + row_sums(grad_w_kv, key_value_weight)
     ) / gain_mix.astype(F32)
     totals = (
         grad_gain_mix,
         grad_w_z,
-        grad_w_xbc[:, :CHANNELS],
-        grad_w_xbc[:, CHANNELS : CHANNELS + MAMBA_HEADS],
+        grad_w_xbc,
+        grad_w_dt[:, :MAMBA_HEADS],
         conv_own[:CONV],
         conv_own[CONV],
         heads_own[0],
         heads_own[1],
         heads_own[2],
-        grad_w_omo[o_rows:],
-        grad_w_qkv[:, :q_width],
-        grad_w_qkv[:, q_width:],
-        grad_w_omo[:o_rows],
+        grad_w_mo,
+        grad_w_q,
+        grad_w_kv,
+        grad_w_o,
         grad_gain_ffn,
-        grad_w_gate_up[:, :ff],
-        grad_w_gate_up[:, ff:],
+        grad_w_gate,
+        grad_w_up,
         grad_w_down,
     )
     return (result.astype(BF16)[None], grad_tokens[None]) + totals

time: 675 us -> 635 us (0.941)
  waiting for transfers between devices: 167 us -> 94.4 us
  Pallas kernels: 161 us -> 232 us
  matrix products: 101 us -> 60.7 us
  starting transfers between devices: 94.6 us -> 118 us
  between operations: 15.8 us -> 2.23 us
    pallas_call x14 -> x32, Pallas kernels: 52.8 us -> 131 us  [the longest x16 78.1 us: product(): pl.pallas_call(without(functools.partial(product_kernel, len(which), len(...]
    ppermute x57 -> x64, waiting for transfers between devices: 147 us -> 94.4 us  [swap(): return lax.ppermute(block, DEVICES, route)]
    dot_general x18 -> x0, matrix products: 44.6 us -> none  [dot_tn(): lax.dot_general(a, b, (((0,), (0,)), ((), ())), preferred_element_type=F32)]
    ppermute x57 -> x64, starting transfers between devices: 89.3 us -> 113 us  [swap(): return lax.ppermute(block, DEVICES, route)]
    psum x1 -> x0, waiting for transfers between devices: 20.1 us -> none  [local(): last_total = lax.psum(last_own, 'ctx').astype(F32)]
    unnamed x200 -> x193, local copies, waits for them, and re-layouts: 18.4 us -> 30 us
    convert_element_type x9 -> x7, other arithmetic: 20.7 us -> 10.4 us  [the longest x4 4.47 us: total(): self.own = (self.kept.astype(F32) + self.got.astype(F32)).astype(BF16)]
    pallas_call x5 -> x3, Pallas kernels: 25.3 us -> 16.2 us  [place(): pl.pallas_call(functools.partial(place_kernel, tuple(parts), len(tokens))...]
  transfers between devices with their start and end apart: 60 -> 66, of which waited for: 17 -> 23; matrix products, arithmetic and copies ran while one was open for 27% -> 20% of each run, Pallas kernels for 22% -> 34%
where the time goes in v3:
time: 635 us; the launch traced here: 627 us
  Pallas kernels  232 us (37%)
  starting transfers between devices  118 us (19%)
  waiting for transfers between devices  94.4 us (15%)
  other arithmetic  61.5 us (10%)
  matrix products  60.7 us (10%)
  local copies, waits for them, and re-layouts  57.3 us (9%)
    ppermute x64, starting transfers between devices, swap(): return lax.ppermute(block, DEVICES, route)  113 us
    ppermute x64, waiting for transfers between devices, swap(): return lax.ppermute(block, DEVICES, route)  94.4 us
    pallas_call x16, Pallas kernels, product(): pl.pallas_call(without(functools.partial(product_kernel, len(which), len(...  78.1 us
    dot_general x6, matrix products, dot_nt(): lax.dot_general(a, b, (((1,), (1,)), ((), ())), preferred_element_type=F32)  34.1 us
    unnamed x193, local copies, waits for them, and re-layouts  30 us
    dot_general x7, matrix products, dot_nn(): lax.dot_general(a, b, (((1,), (0,)), ((), ())), precision=precision, pref...  26.6 us
    pallas_call x1, Pallas kernels, mamba_back(): pl.pallas_call(without(mamba_back_kernel, 13, len(tokens)), grid=(count,)...  25.6 us
    pallas_call x6, Pallas kernels, scan_step(): pl.pallas_call(functools.partial(scan_step_kernel, seen is None, ends), i...  16.8 us
  transfers between devices with their start and end apart: 66, of which 23 were waited for; matrix products, arithmetic and copies ran while one was open for 20% of the time, Pallas kernels for 34%

profile of v3, /device:TPU:0, one launch (start us, length us, event | category | flops | bytes accessed | tf_op | source)
XLA Modules:
  0.0 626.8 jit_solution(2557542170000536546)
XLA Ops:
  1.5 4.1 concatenate.69
  43.0 5.6 collective-permute-done.10
  50.9 6.5 %collective-permute-done.14 = bf16[512,128]{1,0:T(8,128)(2,1)S(1)} collective-permute-done((bf16[512,128]{1,0:T(8,128)(2,1)S(1)}, bf16[512,128]{1,0:T(8,128)(2,1)S(1)}, u32[]{:S(2)}, u32[]{:S(2)}) %collective-permute-start.14) | collective-permute-done | bytes 131104 | tf_op jit(solution)/shard_map/ppermute | solution.py:1072
  64.0 4.1 fusion.7.mixed_ref.refs_2_
  83.0 13.5 %mamba_forward.1 = (f32[512,1536]{1,0:T(8,128)}, f32[4,128,1536]{2,1,0:T(8,128)}, bf16[144,1536]{1,0:T(8,128)(2,1)}, f32[144,1536]{1,0:T(8,128)}, f32[512,128]{1,0:T(8,128)}, /*index=5*/bf16[512,128]{1,0:T(8,128)(2,1)}) custom-call(s32[5]{0:T(128)} %pad_add_fusion.sc_ref.refs_0_, f32[8,1792]{1,0:T(8,128)} %convert_element_type.257.edge_ref.refs_1_, ...), custom_call_target="tpu_custom_call" | custom-call | flops 14949999616 | tf_op jit(solution)/shard_map/mamba_forward/pallas_call | solution.py:218
  105.7 4.9 attend.2
  119.8 8.4 %attend.3 = (bf16[512,256]{1,0:T(8,128)(2,1)}, f32[512,256]{1,0:T(8,128)}, f32[2,8,1024]{2,1,0:T(8,128)}, bf16[1024,1536]{1,0:T(8,128)(2,1)}, bf16[2048,1024]{1,0:T(8,128)(2,1)}) custom-call(s32[13]{0:T(128)} %pad_add_fusion.2.refs_0_, bf16[512,512]{1,0:T(8,128)(2,1)} %get-tuple-element.114.refs_1_, bf16[4096,128]{1,0:T(8,128)(2,1)} %pad_maximum_fusion.6.refs_2_.refs_5_, ...), custom_call_target="tpu_custom_call" | custom-call | flops 20700000256 | tf_op jit(solution)/shard_map/attend/pallas_call | solution.py:867
  132.2 15.9 %collective-permute-start.19 = (bf16[144,1536]{1,0:T(8,128)(2,1)}, bf16[144,1536]{1,0:T(8,128)(2,1)S(1)}, u32[]{:S(2)}, u32[]{:S(2)}) collective-permute-start(bf16[144,1536]{1,0:T(8,128)(2,1)} %get-tuple-element.130), channel_id=1, source_target_pairs={{0,16},{1,17},{2,18},{3,19},{4,20},{5,21},{6,22},{7,23},{8,24},{9,... | collective-permute-start | bytes 1327112 | tf_op jit(solution)/shard_map/ppermute | solution.py:1072
  151.5 16.5 %collective-permute-done.19.refs_0_ = bf16[144,1536]{1,0:T(8,128)(2,1)S(1)} collective-permute-done((bf16[144,1536]{1,0:T(8,128)(2,1)}, bf16[144,1536]{1,0:T(8,128)(2,1)S(1)}, u32[]{:S(2)}, u32[]{:S(2)}) %collective-permute-start.19) | collective-permute-done | bytes 442400 | tf_op jit(solution)/shard_map/ppermute | solution.py:1072
  171.7 8.6 %mamba_correct.1 = (f32[512,1536]{1,0:T(8,128)}, bf16[512,2048]{1,0:T(8,128)(2,1)}, bf16[4,128,1536]{2,1,0:T(8,128)(2,1)}) custom-call(f32[512,1536]{1,0:T(8,128)} %get-tuple-element.115.y_ref, f32[4,128,1536]{2,1,0:T(8,128)} %get-tuple-element.116.sin_ref, bf16[512,128]{1,0:T(8,128)(2,1)} %get-tuple-element.117.c_ref.refs_3_, ...), custom_call_target="tpu_custom_call" | custom-call | flops 9774999552 | tf_op jit(solution)/shard_map/mamba_correct/pallas_call | solution.py:305
  180.3 5.3 multiply_reduce_fusion.3
  187.6 9.5 %place.5 = (bf16[1024,4096]{1,0:T(8,128)(2,1)}, bf16[2048,1024]{1,0:T(8,128)(2,1)}) custom-call(s32[12]{0:T(128)} %stack.74.refs_4_.at_ref, bf16[256,6144]{1,0:T(8,128)(2,1)} %after.46.refs_0_, bf16[256,6144]{1,0:T(8,128)(2,1)} %collective-permute-done.7.refs_5_.refs_1_, bf16[256,6144]{1,0:T(8,128)(2,1)} %after.55.refs_2_, bf16[256,6144]{1,0:T(8,128)(2,1)} %copy-done.84), custom_call_target="tpu_custom_call" | custom-call | flops 10796899328 | tf_op jit(solution)/shard_map/place/pallas_call | solution.py:1113
  197.1 7.0 %fusion.55 = f32[512,4096]{1,0:T(8,128)S(1)} fusion(bf16[512,1024]{1,0:T(8,128)(2,1)S(1)} %multiply_convert_fusion.1.refs_1_.refs_2_, bf16[1024,4096]{1,0:T(8,128)(2,1)} %get-tuple-element.134), kind=kOutput, calls=%fused_computation.155 | convolution fusion | flops 4294967296 | bytes 17825792 | tf_op jit(solution)/shard_map/dot_general | solution.py:38
  204.2 5.1 fusion.2
  213.8 6.6 %product.16 = bf16[512,4096]{1,0:T(8,128)(2,1)} custom-call(s32[3]{0:T(128)} %add_add_fusion.refs_0_, bf16[512,1024]{1,0:T(8,128)(2,1)} %copy-done.46, bf16[512,1024]{1,0:T(8,128)(2,1)} %copy-done.46, bf16[512,4096]{1,0:T(8,128)(2,1)} %pad_maximum_fusion.refs_3_.refs_2_), custom_call_target="tpu_custom_call" | custom-call | flops 8385174528 | tf_op jit(solution)/shard_map/product/pallas_call | solution.py:1197
  224.2 5.4 product.18
  229.6 7.6 %multiply_reduce_fusion.2 = (f32[512]{0:T(512)S(1)}, f32[512,1024]{1,0:T(8,128)S(1)}) fusion(f32[512,1024]{1,0:T(8,128)S(1)} %get-tuple-element.301, f32[1024]{0:T(1024)S(1)} %bitcast.115, bf16[1024,4096]{1,0:T(8,128)(2,1)} %get-tuple-element.134, bf16[512,2048]{1,0:T(8,128)(2,1)S(1)} %copy-done.36, bf16[512,2048]{1,0:T(8,128)(2,1)S(1)} %copy-done.34), kind=kOutput, calls=%fused_computation.37 | convolution fusion | flops 4304928256 | bytes 16783360 | tf_op jit(solution)/shard_map/dot_general | solution.py:44
  244.6 5.2 product.17.refs_5_.refs_1_
  251.4 5.3 product.19
  256.7 6.9 %fusion.56.refs_0_ = f32[512,2048]{1,0:T(8,128)} fusion(bf16[512,1024]{1,0:T(8,128)(2,1)} %after.56.refs_3_, bf16[2048,1024]{1,0:T(8,128)(2,1)} %get-tuple-element.133), kind=kOutput, calls=%fused_computation.156 | convolution fusion | flops 2147483648 | bytes 9437184 | tf_op jit(solution)/shard_map/dot_general | solution.py:44
  263.7 8.3 %mamba_gate_back.1 = (bf16[512,1536]{1,0:T(8,128)(2,1)}, bf16[512,1536]{1,0:T(8,128)(2,1)}, f32[144,1536]{1,0:T(8,128)}, bf16[144,1536]{1,0:T(8,128)(2,1)}, bf16[512,512]{1,0:T(8,128)(2,1)}) custom-call(f32[512,2048]{1,0:T(8,128)} %fusion.56.refs_0_, f32[512,1536]{1,0:T(8,128)} %fusion.54.refs_1_.z_ref, f32[512,1536]{1,0:T(8,128)} %get-tuple-element.137.refs_2_.refs_10_, ...), custom_call_target="tpu_custom_call" | custom-call | flops 8625000448 | tf_op jit(solution)/shard_map/mamba_gate_back/pallas_call | solution.py:367
  274.0 4.8 product.21
  278.8 4.5 product.23
  283.9 4.6 fusion.57.refs_11_
  300.3 6.0 product.20
  320.0 5.3 product.22
  327.8 4.8 collective-permute-done.28.refs_0_
  338.1 7.1 %attend_back.2 = (f32[512,256]{1,0:T(8,128)}, bf16[4096,128]{1,0:T(8,128)(2,1)}) custom-call(s32[13]{0:T(128)} %pad_add_fusion.2.refs_0_, bf16[512,512]{1,0:T(8,128)(2,1)} %get-tuple-element.114.refs_1_, bf16[512,512]{1,0:T(8,128)(2,1)} %get-tuple-element.150.refs_1_.refs_2_, f32[512,256]{1,0:T(8,128)} %get-tuple-element.151.refs_3_, ...), custom_call_target="tpu_custom_call" | custom-call | flops 29899999232 | tf_op jit(solution)/shard_map/attend_back/pallas_call | solution.py:973
  347.2 4.0 product.25
  365.4 13.9 %collective-permute-start.40 = (bf16[64,6144]{1,0:T(8,128)(2,1)}, bf16[64,6144]{1,0:T(8,128)(2,1)S(1)}, u32[]{:S(2)}, u32[]{:S(2)}) collective-permute-start(bf16[64,6144]{1,0:T(8,128)(2,1)} %add_convert_fusion.4.refs_13_), channel_id=1, source_target_pairs={{0,16},{1,17},{2,18},{3,19},{4,20},{5,21},{6,22},{7,23},{8,24},{9,... | collective-permute-start | bytes 2359304 | tf_op jit(solution)/shard_map/ppermute | solution.py:1072
  379.3 25.6 %mamba_back.1 = (bf16[512,1792]{1,0:T(8,128)(2,1)}, f32[8,1792]{1,0:T(8,128)}, f32[8,1792]{1,0:T(8,128)}, bf16[512,128]{1,0:T(8,128)(2,1)}, f32[8,1792]{1,0:T(8,128)}, /*index=5*/f32[8,128]{1,0:T(8,128)}) custom-call(s32[5]{0:T(128)} %pad_add_fusion.sc_ref.refs_0_, f32[8,1792]{1,0:T(8,128)} %convert_element_type.257.edge_ref.refs_1_, ...), custom_call_target="tpu_custom_call" | custom-call | flops 28750000128 | tf_op jit(solution)/shard_map/mamba_back/pallas_call | solution.py:598
  411.5 6.2 collective-permute-start.43
  426.5 6.2 product.26
  437.2 5.8 fusion.44.refs_11_
  443.0 4.9 product.27.refs_1_.refs_7_
  449.5 6.1 collective-permute-done.41.refs_0_
  460.2 7.4 %attend_back.3 = (f32[512,256]{1,0:T(8,128)}, bf16[4096,128]{1,0:T(8,128)(2,1)}) custom-call(s32[13]{0:T(128)} %pad_add_fusion.2.refs_0_, bf16[512,512]{1,0:T(8,128)(2,1)} %get-tuple-element.114.refs_1_, bf16[512,512]{1,0:T(8,128)(2,1)} %get-tuple-element.150.refs_1_.refs_2_, f32[512,256]{1,0:T(8,128)} %get-tuple-element.166.refs_3_, ...), custom_call_target="tpu_custom_call" | custom-call | flops 29899999232 | tf_op jit(solution)/shard_map/attend_back/pallas_call | solution.py:973
  469.4 12.9 %collective-permute-start.44 = (bf16[512,128]{1,0:T(8,128)(2,1)}, bf16[512,128]{1,0:T(8,128)(2,1)S(1)}, u32[]{:S(2)}, u32[]{:S(2)}) collective-permute-start(bf16[512,128]{1,0:T(8,128)(2,1)} %slice.249), channel_id=1, source_target_pairs={{0,16},{1,17},{2,18},{3,19},{4,20},{5,21},{6,22},{7,23},{8,24},{9,... | collective-permute-start | bytes 393224 | tf_op jit(solution)/shard_map/ppermute | solution.py:1072
  482.4 5.0 collective-permute-start.45
  489.3 5.3 product.28
  495.7 5.0 unpack.4
  500.7 6.1 collective-permute-done.45.refs_0_
  524.7 4.4 collective-permute-done.49
  532.8 4.0 product.29.refs_1_
  550.1 8.1 %collective-permute-done.54.refs_4_ = bf16[256,768]{1,0:T(8,128)(2,1)S(1)} collective-permute-done((bf16[256,768]{1,0:T(8,128)(2,1)}, bf16[256,768]{1,0:T(8,128)(2,1)S(1)}, u32[]{:S(2)}, u32[]{:S(2)}) %collective-permute-start.54) | collective-permute-done | bytes 393248 | tf_op jit(solution)/shard_map/ppermute | solution.py:1072
  563.6 4.2 fusion.16
  585.4 4.4 collective-permute-done.58
  600.2 4.1 collective-permute-done.65.got_ref
  (504 shorter events, 283.7 us)
Async XLA Ops:
  7.5 17.5 %collective-permute-start = (bf16[272,768]{1,0:T(8,128)(2,1)}, bf16[272,768]{1,0:T(8,128)(2,1)}, u32[]{:S(2)}, u32[]{:S(2)}) collective-permute-start(bf16[272,768]{1,0:T(8,128)(2,1)} %pad_maximum_fusion.9.refs_0_), channel_id=1, source_target_pairs={{0,1},{1,0},{2,3},{3,2},{4,5},{5,4},{6,7},{7,6},{8,9},{9,8},{10,11... | collective-permute-start | bytes 1253384 | tf_op jit(solution)/shard_map/ppermute | solution.py:1072
  13.5 46.0 %collective-permute-start.3 = (bf16[256,1920]{1,0:T(8,128)(2,1)}, bf16[256,1920]{1,0:T(8,128)(2,1)}, u32[]{:S(2)}, u32[]{:S(2)}) collective-permute-start(bf16[256,1920]{1,0:T(8,128)(2,1)} %fusion.26.refs_0_), channel_id=1, source_target_pairs={{0,1},{1,0},{2,3},{3,2},{4,5},{5,4},{6,7},{7,6},{8,9},{9,8},{10,11... | collective-permute-start | bytes 2949128 | tf_op jit(solution)/shard_map/ppermute | solution.py:1072
  13.7 28.4 %collective-permute-start.4 = (bf16[256,1920]{1,0:T(8,128)(2,1)}, bf16[256,1920]{1,0:T(8,128)(2,1)}, u32[]{:S(2)}, u32[]{:S(2)}) collective-permute-start(bf16[256,1920]{1,0:T(8,128)(2,1)} %fusion.26.refs_0_), channel_id=1, source_target_pairs={{0,2},{1,3},{2,0},{3,1},{4,6},{5,7},{6,4},{7,5},{8,10},{9,11},{10,... | collective-permute-start | bytes 2949128 | tf_op jit(solution)/shard_map/ppermute | solution.py:1072
  21.3 38.8 %collective-permute-start.7 = (bf16[256,6144]{1,0:T(8,128)(2,1)}, bf16[256,6144]{1,0:T(8,128)(2,1)}, u32[]{:S(2)}, u32[]{:S(2)}) collective-permute-start(bf16[256,6144]{1,0:T(8,128)(2,1)} %after.46.refs_0_), channel_id=1, source_target_pairs={{0,1},{1,0},{2,3},{3,2},{4,5},{5,4},{6,7},{7,6},{8,9},{9,8},{10,11... | collective-permute-start | bytes 9437192 | tf_op jit(solution)/shard_map/ppermute | solution.py:1072
  25.0 35.1 %collective-permute-start.6 = (bf16[256,3584]{1,0:T(8,128)(2,1)}, bf16[256,3584]{1,0:T(8,128)(2,1)}, u32[]{:S(2)}, u32[]{:S(2)}) collective-permute-start(bf16[256,3584]{1,0:T(8,128)(2,1)} %after.45.refs_5_), channel_id=1, source_target_pairs={{0,1},{1,0},{2,3},{3,2},{4,5},{5,4},{6,7},{7,6},{8,9},{9,8},{10,11... | collective-permute-start | bytes 5505032 | tf_op jit(solution)/shard_map/ppermute | solution.py:1072
  42.2 18.0 %collective-permute-start.5 = (bf16[256,1920]{1,0:T(8,128)(2,1)}, bf16[256,1920]{1,0:T(8,128)(2,1)}, u32[]{:S(2)}, u32[]{:S(2)}) collective-permute-start(bf16[256,1920]{1,0:T(8,128)(2,1)} %after.44.refs_2_), channel_id=1, source_target_pairs={{0,1},{1,0},{2,3},{3,2},{4,5},{5,4},{6,7},{7,6},{8,9},{9,8},{10,11... | collective-permute-start | bytes 2949128 | tf_op jit(solution)/shard_map/ppermute | solution.py:1072
  57.4 43.1 %collective-permute-start.17 = (bf16[256,3584]{1,0:T(8,128)(2,1)S(1)}, bf16[256,3584]{1,0:T(8,128)(2,1)}, u32[]{:S(2)}, u32[]{:S(2)}) collective-permute-start(bf16[256,3584]{1,0:T(8,128)(2,1)S(1)} %copy-done.5), channel_id=1, source_target_pairs={{0,2},{1,3},{2,0},{3,1},{4,6},{5,7},{6,4},{7,5},{8,10},{9,11},{10,... | collective-permute-start | bytes 5505032 | tf_op jit(solution)/shard_map/ppermute | solution.py:1072
  59.5 111.6 %collective-permute-start.20 = (bf16[256,6144]{1,0:T(8,128)(2,1)}, bf16[256,6144]{1,0:T(8,128)(2,1)}, u32[]{:S(2)}, u32[]{:S(2)}) collective-permute-start(bf16[256,6144]{1,0:T(8,128)(2,1)} %after.46.refs_0_), channel_id=1, source_target_pairs={{0,2},{1,3},{2,0},{3,1},{4,6},{5,7},{6,4},{7,5},{8,10},{9,11},{10,... | collective-permute-start | bytes 9437192 | tf_op jit(solution)/shard_map/ppermute | solution.py:1072
  75.3 25.1 %collective-permute-start.15 = (bf16[1024,128]{1,0:T(8,128)(2,1)}, bf16[1024,128]{1,0:T(8,128)(2,1)}, u32[]{:S(2)}, u32[]{:S(2)}) collective-permute-start(bf16[1024,128]{1,0:T(8,128)(2,1)} %after.50), channel_id=1, source_target_pairs={{0,8},{1,9},{2,10},{3,11},{4,12},{5,13},{6,14},{7,15},{8,0},{9,1},... | collective-permute-start | bytes 786440 | tf_op jit(solution)/shard_map/ppermute | solution.py:1072
  82.3 20.7 %collective-permute-start.12 = (bf16[2048,128]{1,0:T(8,128)(2,1)}, bf16[2048,128]{1,0:T(8,128)(2,1)}, u32[]{:S(2)}, u32[]{:S(2)}) collective-permute-start(bf16[2048,128]{1,0:T(8,128)(2,1)} %pad_maximum_fusion.7), channel_id=1, source_target_pairs={{0,4},{1,5},{2,6},{3,7},{4,0},{5,1},{6,2},{7,3},{8,12},{9,13},{10,... | collective-permute-start | bytes 1572872 | tf_op jit(solution)/shard_map/ppermute | solution.py:1072
  96.5 14.2 %collective-permute-start.9 = (bf16[144,1536]{1,0:T(8,128)(2,1)}, bf16[144,1536]{1,0:T(8,128)(2,1)}, u32[]{:S(2)}, u32[]{:S(2)}) collective-permute-start(bf16[144,1536]{1,0:T(8,128)(2,1)} %get-tuple-element.120.refs_1_.refs_4_), channel_id=1, source_target_pairs={{0,4},{1,5},{2,6},{3,7},{4,0},{5,1},{6,2},{7,3},{8,12},{9,13},{10,... | collective-permute-start | bytes 1327112 | tf_op jit(solution)/shard_map/ppermute | solution.py:1072
  100.4 19.4 %collective-permute-start.18 = (bf16[256,3584]{1,0:T(8,128)(2,1)}, bf16[256,3584]{1,0:T(8,128)(2,1)}, u32[]{:S(2)}, u32[]{:S(2)}) collective-permute-start(bf16[256,3584]{1,0:T(8,128)(2,1)} %after.52.refs_7_), channel_id=1, source_target_pairs={{0,1},{1,0},{2,3},{3,2},{4,5},{5,4},{6,7},{7,6},{8,9},{9,8},{10,11... | collective-permute-start | bytes 5505032 | tf_op jit(solution)/shard_map/ppermute | solution.py:1072
  101.5 15.4 %collective-permute-start.16 = (bf16[2048,128]{1,0:T(8,128)(2,1)S(1)}, bf16[2048,128]{1,0:T(8,128)(2,1)S(1)}, u32[]{:S(2)}, u32[]{:S(2)}) collective-permute-start(bf16[2048,128]{1,0:T(8,128)(2,1)S(1)} %pad_maximum_fusion.8), channel_id=1, source_target_pairs={{0,4},{1,5},{2,6},{3,7},{4,0},{5,1},{6,2},{7,3},{8,12},{9,13},{10,... | collective-permute-start | bytes 1572872 | tf_op jit(solution)/shard_map/ppermute | solution.py:1072
  113.5 14.7 %collective-permute-start.13 = (bf16[144,1536]{1,0:T(8,128)(2,1)}, bf16[144,1536]{1,0:T(8,128)(2,1)S(1)}, u32[]{:S(2)}, u32[]{:S(2)}) collective-permute-start(bf16[144,1536]{1,0:T(8,128)(2,1)} %get-tuple-element.125.refs_9_), channel_id=1, source_target_pairs={{0,8},{1,9},{2,10},{3,11},{4,12},{5,13},{6,14},{7,15},{8,0},{9,1},... | collective-permute-start | bytes 1327112 | tf_op jit(solution)/shard_map/ppermute | solution.py:1072
  132.2 35.8 %collective-permute-start.19 = (bf16[144,1536]{1,0:T(8,128)(2,1)}, bf16[144,1536]{1,0:T(8,128)(2,1)S(1)}, u32[]{:S(2)}, u32[]{:S(2)}) collective-permute-start(bf16[144,1536]{1,0:T(8,128)(2,1)} %get-tuple-element.130), channel_id=1, source_target_pairs={{0,16},{1,17},{2,18},{3,19},{4,20},{5,21},{6,22},{7,23},{8,24},{9,... | collective-permute-start | bytes 1327112 | tf_op jit(solution)/shard_map/ppermute | solution.py:1072
  171.1 14.7 %collective-permute-start.21 = (bf16[256,6144]{1,0:T(8,128)(2,1)}, bf16[256,6144]{1,0:T(8,128)(2,1)S(1)}, u32[]{:S(2)}, u32[]{:S(2)}) collective-permute-start(bf16[256,6144]{1,0:T(8,128)(2,1)} %after.55.refs_2_), channel_id=1, source_target_pairs={{0,1},{1,0},{2,3},{3,2},{4,5},{5,4},{6,7},{7,6},{8,9},{9,8},{10,11... | collective-permute-start | bytes 9437192 | tf_op jit(solution)/shard_map/ppermute | solution.py:1072
  220.4 24.2 %collective-permute-start.22 = (bf16[512,4096]{1,0:T(8,128)(2,1)}, bf16[512,4096]{1,0:T(8,128)(2,1)}, u32[]{:S(2)}, u32[]{:S(2)}) collective-permute-start(bf16[512,4096]{1,0:T(8,128)(2,1)} %product.16), channel_id=1, source_target_pairs={{0,1},{1,0},{2,3},{3,2},{4,5},{5,4},{6,7},{7,6},{8,9},{9,8},{10,11... | collective-permute-start | bytes 12582920 | tf_op jit(solution)/shard_map/ppermute | solution.py:1072
  229.6 21.8 %collective-permute-start.23 = (bf16[1024,1024]{1,0:T(8,128)(2,1)}, bf16[1024,1024]{1,0:T(8,128)(2,1)}, u32[]{:S(2)}, u32[]{:S(2)}) collective-permute-start(bf16[1024,1024]{1,0:T(8,128)(2,1)} %product.18), channel_id=1, source_target_pairs={{0,1},{1,0},{2,3},{3,2},{4,5},{5,4},{6,7},{7,6},{8,9},{9,8},{10,11... | collective-permute-start | bytes 6291464 | tf_op jit(solution)/shard_map/ppermute | solution.py:1072
  249.9 49.1 %collective-permute-start.26 = (bf16[256,4096]{1,0:T(8,128)(2,1)}, bf16[256,4096]{1,0:T(8,128)(2,1)S(1)}, u32[]{:S(2)}, u32[]{:S(2)}) collective-permute-start(bf16[256,4096]{1,0:T(8,128)(2,1)} %product.17.refs_5_.refs_1_), channel_id=1, source_target_pairs={{0,2},{1,3},{2,0},{3,1},{4,6},{5,7},{6,4},{7,5},{8,10},{9,11},{10,... | collective-permute-start | bytes 6291464 | tf_op jit(solution)/shard_map/ppermute | solution.py:1072
  256.7 39.4 %collective-permute-start.29 = (bf16[512,1024]{1,0:T(8,128)(2,1)}, bf16[512,1024]{1,0:T(8,128)(2,1)S(1)}, u32[]{:S(2)}, u32[]{:S(2)}) collective-permute-start(bf16[512,1024]{1,0:T(8,128)(2,1)} %get-tuple-element.136.refs_2_), channel_id=1, source_target_pairs={{0,4},{1,5},{2,6},{3,7},{4,0},{5,1},{6,2},{7,3},{8,12},{9,13},{10,... | collective-permute-start | bytes 3145736 | tf_op jit(solution)/shard_map/ppermute | solution.py:1072
  272.0 19.6 %collective-permute-start.24 = (bf16[144,1536]{1,0:T(8,128)(2,1)}, bf16[144,1536]{1,0:T(8,128)(2,1)S(1)}, u32[]{:S(2)}, u32[]{:S(2)}) collective-permute-start(bf16[144,1536]{1,0:T(8,128)(2,1)} %get-tuple-element.142), channel_id=1, source_target_pairs={{0,4},{1,5},{2,6},{3,7},{4,0},{5,1},{6,2},{7,3},{8,12},{9,13},{10,... | collective-permute-start | bytes 1327112 | tf_op jit(solution)/shard_map/ppermute | solution.py:1072
  278.8 41.2 %collective-permute-start.31 = (bf16[1024,1024]{1,0:T(8,128)(2,1)}, bf16[1024,1024]{1,0:T(8,128)(2,1)}, u32[]{:S(2)}, u32[]{:S(2)}) collective-permute-start(bf16[1024,1024]{1,0:T(8,128)(2,1)} %product.21), channel_id=1, source_target_pairs={{0,1},{1,0},{2,3},{3,2},{4,5},{5,4},{6,7},{7,6},{8,9},{9,8},{10,11... | collective-permute-start | bytes 6291464 | tf_op jit(solution)/shard_map/ppermute | solution.py:1072
  283.4 24.8 %collective-permute-start.32 = (bf16[512,1536]{1,0:T(8,128)(2,1)}, bf16[512,1536]{1,0:T(8,128)(2,1)}, u32[]{:S(2)}, u32[]{:S(2)}) collective-permute-start(bf16[512,1536]{1,0:T(8,128)(2,1)} %product.23), channel_id=1, source_target_pairs={{0,1},{1,0},{2,3},{3,2},{4,5},{5,4},{6,7},{7,6},{8,9},{9,8},{10,11... | collective-permute-start | bytes 4718600 | tf_op jit(solution)/shard_map/ppermute | solution.py:1072
  295.2 18.4 %collective-permute-start.25 = (bf16[144,1536]{1,0:T(8,128)(2,1)}, bf16[144,1536]{1,0:T(8,128)(2,1)}, u32[]{:S(2)}, u32[]{:S(2)}) collective-permute-start(bf16[144,1536]{1,0:T(8,128)(2,1)} %get-tuple-element.145.refs_1_), channel_id=1, source_target_pairs={{0,8},{1,9},{2,10},{3,11},{4,12},{5,13},{6,14},{7,15},{8,0},{9,1},... | collective-permute-start | bytes 1327112 | tf_op jit(solution)/shard_map/ppermute | solution.py:1072
  306.3 26.3 %collective-permute-start.28 = (bf16[128,4096]{1,0:T(8,128)(2,1)}, bf16[128,4096]{1,0:T(8,128)(2,1)S(1)}, u32[]{:S(2)}, u32[]{:S(2)}) collective-permute-start(bf16[128,4096]{1,0:T(8,128)(2,1)} %get-tuple-element.146.refs_1_.refs_5_), channel_id=1, source_target_pairs={{0,4},{1,5},{2,6},{3,7},{4,0},{5,1},{6,2},{7,3},{8,12},{9,13},{10,... | collective-permute-start | bytes 3145736 | tf_op jit(solution)/shard_map/ppermute | solution.py:1072
  307.7 19.4 %collective-permute-start.30 = (bf16[256,1024]{1,0:T(8,128)(2,1)}, bf16[256,1024]{1,0:T(8,128)(2,1)S(1)}, u32[]{:S(2)}, u32[]{:S(2)}) collective-permute-start(bf16[256,1024]{1,0:T(8,128)(2,1)} %get-tuple-element.276), channel_id=1, source_target_pairs={{0,2},{1,3},{2,0},{3,1},{4,6},{5,7},{6,4},{7,5},{8,10},{9,11},{10,... | collective-permute-start | bytes 1572872 | tf_op jit(solution)/shard_map/ppermute | solution.py:1072
  312.1 34.2 %collective-permute-start.34 = (bf16[256,1536]{1,0:T(8,128)(2,1)}, bf16[256,1536]{1,0:T(8,128)(2,1)S(1)}, u32[]{:S(2)}, u32[]{:S(2)}) collective-permute-start(bf16[256,1536]{1,0:T(8,128)(2,1)} %product.24.refs_10_), channel_id=1, source_target_pairs={{0,2},{1,3},{2,0},{3,1},{4,6},{5,7},{6,4},{7,5},{8,10},{9,11},{10,... | collective-permute-start | bytes 2359304 | tf_op jit(solution)/shard_map/ppermute | solution.py:1072
  316.7 42.7 %collective-permute-start.27 = (bf16[144,1536]{1,0:T(8,128)(2,1)}, bf16[144,1536]{1,0:T(8,128)(2,1)}, u32[]{:S(2)}, u32[]{:S(2)}) collective-permute-start(bf16[144,1536]{1,0:T(8,128)(2,1)} %get-tuple-element.149.refs_1_.refs_7_), channel_id=1, source_target_pairs={{0,16},{1,17},{2,18},{3,19},{4,20},{5,21},{6,22},{7,23},{8,24},{9,... | collective-permute-start | bytes 1327112 | tf_op jit(solution)/shard_map/ppermute | solution.py:1072
  325.3 29.3 %collective-permute-start.35 = (bf16[512,1024]{1,0:T(8,128)(2,1)}, bf16[512,1024]{1,0:T(8,128)(2,1)S(1)}, u32[]{:S(2)}, u32[]{:S(2)}) collective-permute-start(bf16[512,1024]{1,0:T(8,128)(2,1)} %get-tuple-element.156.refs_9_), channel_id=1, source_target_pairs={{0,4},{1,5},{2,6},{3,7},{4,0},{5,1},{6,2},{7,3},{8,12},{9,13},{10,... | collective-permute-start | bytes 3145736 | tf_op jit(solution)/shard_map/ppermute | solution.py:1072
  336.9 24.9 %collective-permute-start.33 = (bf16[64,6144]{1,0:T(8,128)(2,1)}, bf16[64,6144]{1,0:T(8,128)(2,1)S(1)}, u32[]{:S(2)}, u32[]{:S(2)}) collective-permute-start(bf16[64,6144]{1,0:T(8,128)(2,1)} %get-tuple-element.155.refs_8_), channel_id=1, source_target_pairs={{0,8},{1,9},{2,10},{3,11},{4,12},{5,13},{6,14},{7,15},{8,0},{9,1},... | collective-permute-start | bytes 2359304 | tf_op jit(solution)/shard_map/ppermute | solution.py:1072
  351.2 66.5 %collective-permute-start.38 = (bf16[128,1536]{1,0:T(8,128)(2,1)}, bf16[128,1536]{1,0:T(8,128)(2,1)}, u32[]{:S(2)}, u32[]{:S(2)}) collective-permute-start(bf16[128,1536]{1,0:T(8,128)(2,1)} %get-tuple-element.159.refs_14_), channel_id=1, source_target_pairs={{0,4},{1,5},{2,6},{3,7},{4,0},{5,1},{6,2},{7,3},{8,12},{9,13},{10,... | collective-permute-start | bytes 1179656 | tf_op jit(solution)/shard_map/ppermute | solution.py:1072
  358.3 59.4 %collective-permute-start.39 = (bf16[256,1024]{1,0:T(8,128)(2,1)}, bf16[256,1024]{1,0:T(8,128)(2,1)}, u32[]{:S(2)}, u32[]{:S(2)}) collective-permute-start(bf16[256,1024]{1,0:T(8,128)(2,1)} %get-tuple-element.275.refs_15_), channel_id=1, source_target_pairs={{0,2},{1,3},{2,0},{3,1},{4,6},{5,7},{6,4},{7,5},{8,10},{9,11},{10,... | collective-permute-start | bytes 1572872 | tf_op jit(solution)/shard_map/ppermute | solution.py:1072
  358.9 49.7 %collective-permute-start.42 = (bf16[2048,128]{1,0:T(8,128)(2,1)S(1)}, bf16[2048,128]{1,0:T(8,128)(2,1)S(1)}, u32[]{:S(2)}, u32[]{:S(2)}) collective-permute-start(bf16[2048,128]{1,0:T(8,128)(2,1)S(1)} %slice.205.refs_16_), channel_id=1, source_target_pairs={{0,4},{1,5},{2,6},{3,7},{4,0},{5,1},{6,2},{7,3},{8,12},{9,13},{10,... | collective-permute-start | bytes 1572872 | tf_op jit(solution)/shard_map/ppermute | solution.py:1072
  365.4 67.3 %collective-permute-start.40 = (bf16[64,6144]{1,0:T(8,128)(2,1)}, bf16[64,6144]{1,0:T(8,128)(2,1)S(1)}, u32[]{:S(2)}, u32[]{:S(2)}) collective-permute-start(bf16[64,6144]{1,0:T(8,128)(2,1)} %add_convert_fusion.4.refs_13_), channel_id=1, source_target_pairs={{0,16},{1,17},{2,18},{3,19},{4,20},{5,21},{6,22},{7,23},{8,24},{9,... | collective-permute-start | bytes 2359304 | tf_op jit(solution)/shard_map/ppermute | solution.py:1072
  404.9 20.1 %collective-permute-start.36 = (f32[8,1792]{1,0:T(8,128)}, f32[8,1792]{1,0:T(8,128)S(1)}, u32[]{:S(2)}, u32[]{:S(2)}) collective-permute-start(f32[8,1792]{1,0:T(8,128)} %get-tuple-element.164), channel_id=1, source_target_pairs={{4,0},{8,4},{12,8},{16,12},{20,16},{24,20},{28,24},{5,1},{9,5},{13... | collective-permute-start | bytes 172040 | tf_op jit(solution)/shard_map/ppermute | solution.py:1433
  411.5 56.1 %collective-permute-start.43 = (bf16[1024,128]{1,0:T(8,128)(2,1)}, bf16[1024,128]{1,0:T(8,128)(2,1)}, u32[]{:S(2)}, u32[]{:S(2)}) collective-permute-start(bf16[1024,128]{1,0:T(8,128)(2,1)} %slice.247), channel_id=1, source_target_pairs={{0,8},{1,9},{2,10},{3,11},{4,12},{5,13},{6,14},{7,15},{8,0},{9,1},... | collective-permute-start | bytes 786440 | tf_op jit(solution)/shard_map/ppermute | solution.py:1072
  420.3 67.1 %collective-permute-start.51 = (bf16[64,3584]{1,0:T(8,128)(2,1)}, bf16[64,3584]{1,0:T(8,128)(2,1)S(1)}, u32[]{:S(2)}, u32[]{:S(2)}) collective-permute-start(bf16[64,3584]{1,0:T(8,128)(2,1)} %get-tuple-element.171.refs_8_), channel_id=1, source_target_pairs={{0,8},{1,9},{2,10},{3,11},{4,12},{5,13},{6,14},{7,15},{8,0},{9,1},... | collective-permute-start | bytes 1376264 | tf_op jit(solution)/shard_map/ppermute | solution.py:1072
  435.1 20.4 %collective-permute-start.41 = (bf16[64,6144]{1,0:T(8,128)(2,1)S(1)}, bf16[64,6144]{1,0:T(8,128)(2,1)}, u32[]{:S(2)}, u32[]{:S(2)}) collective-permute-start(bf16[64,6144]{1,0:T(8,128)(2,1)S(1)} %add_convert_fusion.3.own_ref), channel_id=1, source_target_pairs={{0,8},{1,9},{2,10},{3,11},{4,12},{5,13},{6,14},{7,15},{8,0},{9,1},... | collective-permute-start | bytes 2359304 | tf_op jit(solution)/shard_map/ppermute | solution.py:1072
  448.0 41.3 %collective-permute-start.47 = (bf16[256,1920]{1,0:T(8,128)(2,1)}, bf16[256,1920]{1,0:T(8,128)(2,1)}, u32[]{:S(2)}, u32[]{:S(2)}) collective-permute-start(bf16[256,1920]{1,0:T(8,128)(2,1)} %product.27.refs_1_.refs_7_), channel_id=1, source_target_pairs={{0,2},{1,3},{2,0},{3,1},{4,6},{5,7},{6,4},{7,5},{8,10},{9,11},{10,... | collective-permute-start | bytes 2949128 | tf_op jit(solution)/shard_map/ppermute | solution.py:1072
  458.2 37.5 %collective-permute-start.46 = (bf16[128,6144]{1,0:T(8,128)(2,1)}, bf16[128,6144]{1,0:T(8,128)(2,1)}, u32[]{:S(2)}, u32[]{:S(2)}) collective-permute-start(bf16[128,6144]{1,0:T(8,128)(2,1)} %join.4.refs_9_.own_ref), channel_id=1, source_target_pairs={{0,4},{1,5},{2,6},{3,7},{4,0},{5,1},{6,2},{7,3},{8,12},{9,13},{10,... | collective-permute-start | bytes 4718600 | tf_op jit(solution)/shard_map/ppermute | solution.py:1072
  469.4 42.0 %collective-permute-start.44 = (bf16[512,128]{1,0:T(8,128)(2,1)}, bf16[512,128]{1,0:T(8,128)(2,1)S(1)}, u32[]{:S(2)}, u32[]{:S(2)}) collective-permute-start(bf16[512,128]{1,0:T(8,128)(2,1)} %slice.249), channel_id=1, source_target_pairs={{0,16},{1,17},{2,18},{3,19},{4,20},{5,21},{6,22},{7,23},{8,24},{9,... | collective-permute-start | bytes 393224 | tf_op jit(solution)/shard_map/ppermute | solution.py:1072
  482.4 24.5 %collective-permute-start.45 = (bf16[2048,128]{1,0:T(8,128)(2,1)S(1)}, bf16[2048,128]{1,0:T(8,128)(2,1)S(1)}, u32[]{:S(2)}, u32[]{:S(2)}) collective-permute-start(bf16[2048,128]{1,0:T(8,128)(2,1)S(1)} %slice.215), channel_id=1, source_target_pairs={{0,4},{1,5},{2,6},{3,7},{4,0},{5,1},{6,2},{7,3},{8,12},{9,13},{10,... | collective-permute-start | bytes 1572872 | tf_op jit(solution)/shard_map/ppermute | solution.py:1072
  489.2 47.6 %collective-permute-start.52 = (bf16[64,3584]{1,0:T(8,128)(2,1)S(1)}, bf16[64,3584]{1,0:T(8,128)(2,1)S(1)}, u32[]{:S(2)}, u32[]{:S(2)}) collective-permute-start(bf16[64,3584]{1,0:T(8,128)(2,1)S(1)} %add_convert_fusion.8), channel_id=1, source_target_pairs={{0,16},{1,17},{2,18},{3,19},{4,20},{5,21},{6,22},{7,23},{8,24},{9,... | collective-permute-start | bytes 1376264 | tf_op jit(solution)/shard_map/ppermute | solution.py:1072
  494.7 22.1 %collective-permute-start.60 = (bf16[128,1920]{1,0:T(8,128)(2,1)}, bf16[128,1920]{1,0:T(8,128)(2,1)}, u32[]{:S(2)}, u32[]{:S(2)}) collective-permute-start(bf16[128,1920]{1,0:T(8,128)(2,1)} %get-tuple-element.175.refs_1_), channel_id=1, source_target_pairs={{0,4},{1,5},{2,6},{3,7},{4,0},{5,1},{6,2},{7,3},{8,12},{9,13},{10,... | collective-permute-start | bytes 1474568 | tf_op jit(solution)/shard_map/ppermute | solution.py:1072
  518.9 22.9 %collective-permute-start.61 = (bf16[64,1920]{1,0:T(8,128)(2,1)}, bf16[64,1920]{1,0:T(8,128)(2,1)S(1)}, u32[]{:S(2)}, u32[]{:S(2)}) collective-permute-start(bf16[64,1920]{1,0:T(8,128)(2,1)} %get-tuple-element.184), channel_id=1, source_target_pairs={{0,8},{1,9},{2,10},{3,11},{4,12},{5,13},{6,14},{7,15},{8,0},{9,1},... | collective-permute-start | bytes 737288 | tf_op jit(solution)/shard_map/ppermute | solution.py:1072
  539.5 29.1 %collective-permute-start.53 = (bf16[64,3584]{1,0:T(8,128)(2,1)}, bf16[64,3584]{1,0:T(8,128)(2,1)}, u32[]{:S(2)}, u32[]{:S(2)}) collective-permute-start(bf16[64,3584]{1,0:T(8,128)(2,1)} %add_convert_fusion.7.own_ref), channel_id=1, source_target_pairs={{0,8},{1,9},{2,10},{3,11},{4,12},{5,13},{6,14},{7,15},{8,0},{9,1},... | collective-permute-start | bytes 1376264 | tf_op jit(solution)/shard_map/ppermute | solution.py:1072
  548.3 23.7 %collective-permute-start.62 = (bf16[64,1920]{1,0:T(8,128)(2,1)S(1)}, bf16[64,1920]{1,0:T(8,128)(2,1)}, u32[]{:S(2)}, u32[]{:S(2)}) collective-permute-start(bf16[64,1920]{1,0:T(8,128)(2,1)S(1)} %add_convert_fusion.12), channel_id=1, source_target_pairs={{0,16},{1,17},{2,18},{3,19},{4,20},{5,21},{6,22},{7,23},{8,24},{9,... | collective-permute-start | bytes 737288 | tf_op jit(solution)/shard_map/ppermute | solution.py:1072
  570.7 49.8 %collective-permute-start.55 = (bf16[128,3584]{1,0:T(8,128)(2,1)}, bf16[128,3584]{1,0:T(8,128)(2,1)}, u32[]{:S(2)}, u32[]{:S(2)}) collective-permute-start(bf16[128,3584]{1,0:T(8,128)(2,1)} %join.5.refs_1_.own_ref), channel_id=1, source_target_pairs={{0,4},{1,5},{2,6},{3,7},{4,0},{5,1},{6,2},{7,3},{8,12},{9,13},{10,... | collective-permute-start | bytes 2752520 | tf_op jit(solution)/shard_map/ppermute | solution.py:1072
  (113 other events, 641.4 us)

commit v4 on v3

--- a/solution.py
+++ b/solution.py
@@ -211,12 +211,14 @@
             own_ref[STATE_SIZE:, tile(j)] = wide
 
 
-def mamba_forward(scalars, edge, mixed, dt_raw, doc, conv_pack, head_pack, skip_wide):
+def mamba_forward(
+    scalars, edge, mixed, dt_raw, doc, conv_pack, head_pack, skip_wide, tokens=()
+):
     rows = mixed.shape[0]
     count = rows // CHUNK
     by_chunk = lambda width: pl.BlockSpec((CHUNK, width), lambda c: (c, 0))
     return pl.pallas_call(
-        mamba_forward_kernel,
+        without(mamba_forward_kernel, 8, len(tokens)),
         grid=(count,),
         in_specs=[
             pl.BlockSpec(memory_space=pltpu.SMEM),
@@ -227,6 +229,7 @@
             whole((8, CHANNELS)),
             whole((8, LANES)),
             whole((1, MAMBA_INNER)),
+            *unread(tokens),
         ],
         out_specs=[
             by_chunk(MAMBA_INNER),
@@ -253,7 +256,7 @@
         compiler_params=params("arbitrary"),
         cost_estimate=lasting(13),
         name="mamba_forward",
-    )(scalars, edge, mixed, dt_raw, doc, conv_pack, head_pack, skip_wide)
+    )(scalars, edge, mixed, dt_raw, doc, conv_pack, head_pack, skip_wide, *tokens)
 
 
 QUARTERS = 4
@@ -344,14 +347,14 @@
         z = z_ref[:, tile(j)]
         sig = jax.nn.sigmoid(z)
         silu = z * sig
-        grad = both_ref[:, gated_tile(j)]
+        grad = both_ref[:, gated_tile(j)].astype(F32)
         gz_ref[:, tile(j)] = (grad * y_ref[:, tile(j)] * (sig + silu * (1.0 - sig))).astype(BF16)
         dy = (grad * silu).astype(BF16)
         dy_ref[:, tile(j)] = dy
         scaled = (dy.astype(F32) * spread(decay, j, low)).astype(BF16)
         acc_ref[:, tile(j)] += dot_nn(c_turned, scaled)
     for i in range(QUARTERS):
-        gvec_ref[:, tile(i)] = both_ref[:, attn_tile(i)].astype(BF16)
+        gvec_ref[:, tile(i)] = both_ref[:, attn_tile(i)]
 
     @pl.when(c == pl.num_programs(0) - 1)
     def _():
@@ -426,7 +429,6 @@
     gmix_ref,
     tail_ref,
     edge_grad_ref,
-    gdt_ref,
     gconv_ref,
     ghead_ref,
     xs_ref,
@@ -536,7 +538,7 @@
     later = (iota((CHUNK, CHUNK), 0) <= iota((CHUNK, CHUNK), 1)).astype(F32)
     grad_log = dot_nn(later, grad_cumul, HIGHEST) + end_sums[0:1, :]
     grad_raw = (grad_step + grad_log * hp_ref[1:2, :]) * jax.nn.sigmoid(raw)
-    gdt_ref[...] = grad_raw.astype(BF16)
+    gmix_ref[:, tile(CHANNELS // LANES)] = grad_raw.astype(BF16)
     ghead_ref[0:1, :] += jnp.sum(grad_raw, axis=0, keepdims=True)
     ghead_ref[1:2, :] += jnp.sum(grad_log * log_decay, axis=0, keepdims=True)
     for i in range(CHANNELS // LANES):
@@ -615,18 +617,16 @@
             *unread(tokens),
         ],
         out_specs=[
-            by_chunk(CHANNELS),
+            by_chunk(CHANNELS + LANES),
             whole((8, CHANNELS)),
             whole((8, CHANNELS)),
-            by_chunk(LANES),
             whole((8, CHANNELS)),
             whole((8, LANES)),
         ],
         out_shape=[
-            jax.ShapeDtypeStruct((rows, CHANNELS), BF16),
+            jax.ShapeDtypeStruct((rows, CHANNELS + LANES), BF16),
             jax.ShapeDtypeStruct((8, CHANNELS), F32),
             jax.ShapeDtypeStruct((8, CHANNELS), F32),
-            jax.ShapeDtypeStruct((rows, LANES), BF16),
             jax.ShapeDtypeStruct((8, CHANNELS), F32),
             jax.ShapeDtypeStruct((8, LANES), F32),
         ],
@@ -1150,12 +1150,13 @@
     return pieces, parts, offsets, [shapes[out] for out in sorted(shapes)]
 
 
-def product_kernel(blocks, adds, halves, at_ref, *refs):
+def product_kernel(blocks, adds, tail, halves, at_ref, *refs):
     left_refs, refs = refs[:blocks], refs[blocks:]
     grad_ref, refs = refs[0], refs[1:]
     add_refs, refs = refs[:adds], refs[adds:]
+    tail_ref, refs = (refs[0], refs[1:]) if tail else (None, refs)
     rows = left_refs[0].shape[1]
-    turned_ref = refs[-2]
+    turned_ref, total_ref = refs[-2], refs[-1]
 
     @pl.when(pl.program_id(0) == 0)
     def _():
@@ -1166,11 +1167,19 @@
     total = dot_nn(turned_ref[...], grad_ref[...])
     for add_ref in add_refs:
         total = total + add_ref[...].astype(F32)
+    if tail or halves:
+        total_ref[...] = total
+    if tail:
+
+        @pl.when(pl.program_id(0) == pl.num_programs(0) - 1)
+        def _():
+            total_ref[:, total_ref.shape[1] - LANES :] += tail_ref[...]
+
+        total = total_ref[...]
     if not halves:
         refs[0][...] = total.astype(BF16)
         return
-    kept_ref, sent_ref, total_ref = refs[0], refs[1], refs[-1]
-    total_ref[...] = total
+    kept_ref, sent_ref = refs[0], refs[1]
     half = rows // 2
     side = at_ref[blocks]
     for i in range(blocks):
@@ -1181,8 +1190,9 @@
         sent_ref[to, :] = total_ref[pl.ds(theirs, half), :].astype(BF16)
 
 
-def product(left, which, grad, adds=(), halves=False, tokens=()):
+def product(left, which, grad, adds=(), halves=False, tokens=(), tail=None):
     tokens_count = len(tokens)
+    tails = [] if tail is None else [tail]
     depth, width = grad.shape
     rows = left.shape[1] // lax.axis_size("fsdp")
     height = rows * len(which)
@@ -1196,8 +1206,8 @@
     shape = (height // outs, width)
     found = pl.pallas_call(
         without(
-            functools.partial(product_kernel, len(which), len(adds), halves),
-            2 + len(which) + len(adds),
+            functools.partial(product_kernel, len(which), len(adds), tail is not None, halves),
+            2 + len(which) + len(adds) + len(tails),
             tokens_count,
         ),
         grid_spec=pltpu.PrefetchScalarGridSpec(
@@ -1206,6 +1216,7 @@
             in_specs=[block_of(i) for i in range(len(which))]
             + [pl.BlockSpec((depth, span), lambda t, at: (0, t))]
             + [add_of(block) for _, block in adds]
+            + [whole((height, LANES)) for _ in tails]
             + unread(tokens),
             out_specs=[pl.BlockSpec((height // outs, span), lambda t, at: (0, t))] * outs,
             scratch_shapes=[
@@ -1217,15 +1228,14 @@
         compiler_params=params("arbitrary"),
         cost_estimate=lasting(1 + height * width * 3e-6),
         name="product",
-    )(at, *([left] * len(which)), grad, *[array for array, _ in adds], *tokens)
+    )(at, *([left] * len(which)), grad, *[array for array, _ in adds], *tails, *tokens)
     return found if halves else found[0]
 
 
 class Reduction:
-    def __init__(self, left, grad, more=None):
-        self.left, self.grad = left, grad
-        self.more = more or [[], [], []]
-        sent = product(left, (1, 3), grad, self.more[2])
+    def __init__(self, left, grad, more=(None, None, None), tokens=()):
+        self.left, self.grad, self.more = left, grad, more
+        sent = product(left, (1, 3), grad, (), False, tokens, more[2])
         self.sent, self.got = move(sent, "fsdp", 1)
 
     def hold(self, *tokens):
@@ -1233,12 +1243,14 @@
 
     def over_x(self, start=(), arrive=(), tokens=()):
         self.near = self.got
-        sent = product(self.left, (2,), self.grad, [(self.got, 1)] + self.more[1], False, tokens)
+        sent = product(
+            self.left, (2,), self.grad, [(self.got, 1)], False, tokens, self.more[1]
+        )
         self.sent, self.got = move(sent, "fsdp", 2, start, arrive)
 
     def then_over_y(self, start=(), arrive=(), tokens=()):
-        adds = [(self.near, 0), (self.got, 0)] + self.more[0]
-        self.kept, sent = product(self.left, (0,), self.grad, adds, True, tokens)
+        adds = [(self.near, 0), (self.got, 0)]
+        self.kept, sent = product(self.left, (0,), self.grad, adds, True, tokens, self.more[0])
         self.sent, self.got = move(sent, "ctx", 1, start, arrive)
 
     def first_over_y(self, start=(), arrive=(), tokens=()):
@@ -1600,18 +1612,27 @@
     dt_raw = dot_nn(normed, full_xbc[:, CHANNELS:])
     edge = shift_along(mixed_in[rows - 8 :], "ctx", 1).astype(F32)
     y_local, state_local, message, own_state, decay, c_mat = mamba_forward(
-        scalars, edge, mixed_in, dt_raw, doc_col[:rows], conv_pack, head_pack, skip_wide
+        scalars,
+        edge,
+        mixed_in,
+        dt_raw,
+        doc_col[:rows],
+        conv_pack,
+        head_pack,
+        skip_wide,
+        [spreads[0].block],
     )
     kv_all = [spreads[0].finish([message])]
     scan = Scan(own_state, message, True)
-    tokens = [message]
+    first_send = scan.step([kv_all[0]])
+    tokens = [first_send]
     attended = [attend(attn_scalars, query, kv_all[0], doc_row, 0, tokens)]
     first_done = attended[0][0]
     kv_all.append(spreads[1].finish([first_done]))
     carried = whole_parts(
         shard_zo,
         other_zo,
-        after(near_zo, message),
+        after(near_zo, first_send),
         [(w_z.shape[1], 0, rows_in, 0)] + stretches(1, shard_omo.shape[0]),
     )
     tokens = [scan.step([first_done]), first_done]
@@ -1620,19 +1641,18 @@
     )
     attended.append(second)
     second_done = attended[1][0]
-    scan.step([second_done])
     gate_z = dot_nn(normed, full_z)
-    state_in = scan.finish([gate_z])
+    state_in = scan.finish([second_done])
+    y_total, both, state_true = mamba_correct(
+        y_local, state_local, c_mat, decay, state_in, gate_z, attended[0][0], attended[1][0]
+    )
     full_gate_up, full_down = place(
         *whole_parts(
             shard_ffn,
             other_ffn,
-            after(near_ffn, state_in),
+            after(near_ffn, y_total),
             [(2 * w_gate.shape[1], 0, rows_in, 0)] + stretches(1, w_down.shape[0]),
         )
-    )
-    y_total, both, state_true = mamba_correct(
-        y_local, state_local, c_mat, decay, state_in, gate_z, attended[0][0], attended[1][0]
     )
     hidden = inputs + dot_nn(both, full_omo)
     gain_two = full_gain_ffn
@@ -1663,7 +1683,7 @@
     gate_up_sum.over_x()
     down.first_over_y(tokens=[gate_up_sum.sent])
     grad_hid_b = after(grad_hidden.astype(BF16), gate_up_sum.sent, down.sent)
-    both_grad = time_steps(grad_hid_b, full_omo)
+    both_grad = time_steps(grad_hid_b, full_omo).astype(BF16)
     grad_y, grad_z, own_grad, grad_message, grad_attn = mamba_gate_back(
         both_grad, gate_z, y_total, c_mat, decay, own_state
     )
@@ -1711,13 +1731,12 @@
     gate_up_sum.then_over_y()
     omo.first_over_y(tokens=[gate_up_sum.sent])
     z_sum.over_x()
-    grad_n1_z = time_steps(grad_z, full_z)
     scan.step([gate_up_sum.sent])
     gate_up_sum.hold(scan.send)
     down.hold(scan.send)
     ffn = Pack([(gate_up_sum.kept, gate_up_sum.got), (down.kept, down.got)])
     ffn.over_z()
-    back(0, [scan.send, ffn.sent, omo.sent, z_sum.sent, grad_n1_z])
+    back(0, [scan.send, ffn.sent, omo.sent, z_sum.sent])
     first_done = backs[0][0]
     for part in (ffn, omo, z_sum):
         part.hold(first_done)
@@ -1727,7 +1746,7 @@
     z_sum.then_over_y()
     first_kv = BlockSums(backs[0][1])
     first_kv.sent = first_kv.blocks[first_kv.blocks.shape[0] // 2 :]
-    grad_mixed, tail, edge_grad, grad_dt, grad_conv, grad_heads = mamba_back(
+    grad_xbc, tail, edge_grad, grad_conv, grad_heads = mamba_back(
         scalars,
         edge,
         mixed_in,
@@ -1743,15 +1762,14 @@
         state_grad,
         [ffn.sent, z_sum.sent, omo.sent, first_kv.sent, first_done],
     )
-    third_done = grad_dt
+    third_done = grad_heads
     for part in (ffn, omo, z_sum):
         part.hold(third_done)
     first_kv.step((), [third_done])
     mixer = Pack([(z_sum.kept, z_sum.got), (omo.kept, omo.got)])
     mixer.over_z()
     behind = shift_along(edge_grad, "ctx", -1)
-    grad_mixed = grad_mixed.at[rows - 8 :].set((tail + behind).astype(BF16))
-    grad_xbc = jnp.concatenate([grad_mixed, grad_dt], axis=1)
+    grad_xbc = lax.dynamic_update_slice(grad_xbc, (tail + behind).astype(BF16), (rows - 8, 0))
     fsdp_rank = lax.axis_index("fsdp")
     conv_width, heads_width = conv_b.shape[0], dt_bias.shape[0]
     small_width = -(-(conv_width * (CONV + 1) + heads_width * 3) // rows_in)
@@ -1765,35 +1783,24 @@
     small_grad = jnp.pad(small_grad, ((0, 0), (0, small_width * rows_in - small_count)))
     small_grad = jnp.pad(
         small_grad.reshape(ranks, rows_in, small_width),
-        ((0, 0), (0, 0), (small_at, wide_in - small_at - small_width)),
+        ((0, 0), (0, 0), (MAMBA_HEADS, LANES - MAMBA_HEADS - small_width)),
     )
     block_of = lambda k: lax.dynamic_index_in_dim(small_grad, fsdp_rank ^ k, 0, False)
-    more = [
-        [(block_of(0), 0)],
-        [(block_of(2), 0)],
-        [(jnp.concatenate([block_of(1), block_of(3)], axis=0), 0)],
-    ]
-    xbc_sum = Reduction(normed, grad_xbc, more)
-    grad_n1_xbc = time_steps(grad_xbc, full_xbc)
+    more = [block_of(0), block_of(2), jnp.concatenate([block_of(1), block_of(3)], axis=0)]
+    ffn.total()
+    xbc_sum = Reduction(
+        normed, grad_xbc, more, [ffn.own, z_sum.got, omo.got, first_kv.blocks]
+    )
     xbc_sum.over_x()
     ffn.back_z((), [xbc_sum.sent])
-    back(1, [xbc_sum.sent, mixer.sent, ffn.own, first_kv.blocks, grad_n1_xbc, third_done])
+    back(1, [xbc_sum.sent, mixer.sent, ffn.own, first_kv.blocks, third_done])
     second_done = backs[1][0]
-    ff = w_gate.shape[1]
-    grad_w_gate, grad_w_up, grad_w_down = ffn.back_y(
-        [
-            (0, 0, rows_in, 0, ff),
-            (0, 0, rows_in, ff, 2 * ff),
-            (1, 0, w_down.shape[0], 0, model),
-        ],
-        (),
-        [second_done],
-    )
     xbc_sum.hold(second_done)
     mixer.hold(second_done)
     first_kv.step((), [second_done])
     second_kv = BlockSums(backs[1][1])
-    second_kv.step((), [grad_w_down])
+    second_kv.step()
+    kv_left = second_kv.sent
     y_in = [second_kv.blocks]
     xbc_sum.then_over_y()
     y_left = [xbc_sum.sent]
@@ -1805,10 +1812,21 @@
     grad_qkv = rope_back(backs[0][0], backs[1][0], grad_kv0, grad_kv1, cosine, sine)
     qkv_sum = Reduction(normed, grad_qkv)
     core_left = [qkv_sum.sent]
-    xbc.over_z((), core_left)
     mixer.rest((), core_left)
     qkv_sum.over_x()
     x_left = [qkv_sum.sent]
+    xbc.pairs = [(xbc_sum.kept, after(xbc_sum.got, *x_left))]
+    xbc.over_z()
+    ff = w_gate.shape[1]
+    grad_w_gate, grad_w_up, grad_w_down = ffn.back_y(
+        [
+            (0, 0, rows_in, 0, ff),
+            (0, 0, rows_in, ff, 2 * ff),
+            (1, 0, w_down.shape[0], 0, model),
+        ],
+        [kv_left],
+        x_left,
+    )
     qkv_sum.then_over_y()
     y_left = [qkv_sum.sent]
     xbc.rest((), y_left)
@@ -1826,20 +1844,22 @@
     qkv.rest()
     qkv.back_z()
     join_left = [qkv.own]
+    last_left = [qkv.sent]
+    grad_w_z, grad_w_o, grad_w_mo = mixer.back_y(mixer_outs, (), last_left)
     grad_w_q, grad_w_kv = qkv.back_y(
-        [(0, 0, rows_in, 0, q_width), (0, 0, rows_in, q_width, qkv_raw.shape[1])]
-    )
-    grad_w_z, grad_w_o, grad_w_mo = mixer.back_y(mixer_outs, (), join_left)
+        [(0, 0, rows_in, 0, q_width), (0, 0, rows_in, q_width, qkv_raw.shape[1])],
+        [grad_w_z],
+    )
     grad_w_xbc, grad_w_dt = xbc.back_y(
-        [(0, 0, rows_in, 0, CHANNELS), (0, 0, rows_in, CHANNELS, wide_in)], (), join_left
+        [(0, 0, rows_in, 0, CHANNELS), (0, 0, rows_in, CHANNELS, wide_in)], (), [qkv.sent]
     )
     small_own = grad_w_dt[:, small_at - CHANNELS : small_at - CHANNELS + small_width].reshape(-1)[:small_count]
     conv_own = small_own[: conv_width * (CONV + 1)].reshape(CONV + 1, conv_width)
     heads_own = small_own[conv_width * (CONV + 1) :].reshape(3, heads_width)
     grad_n1 = (
-        grad_n1_z
-        + grad_n1_xbc
-        + time_steps(after(grad_qkv, *x_left), full_qkv)
+        time_steps(after(grad_z, *y_in), full_z)
+        + time_steps(after(grad_xbc, *y_left), full_xbc)
+        + time_steps(after(grad_qkv, *z_left), full_qkv)
     )
     scaled_one = grad_n1 * full_gain_mix[None, :]
     grad_tokens = (

time: 635 us -> 602 us (0.948)
  waiting for transfers between devices: 94.4 us -> 83.2 us
  local copies, waits for them, and re-layouts: 57.3 us -> 48.8 us
  starting transfers between devices: 118 us -> 110 us
    ppermute x64, waiting for transfers between devices: 94.4 us -> 83.2 us  [swap(): return lax.ppermute(block, DEVICES, route)]
    unnamed x193 -> x159, local copies, waits for them, and re-layouts: 30 us -> 21 us
    ppermute x64, starting transfers between devices: 113 us -> 105 us  [swap(): return lax.ppermute(block, DEVICES, route)]
  transfers between devices with their start and end apart: 66 -> 66, of which waited for: 23 -> 21; matrix products, arithmetic and copies ran while one was open for 20% -> 21% of each run, Pallas kernels for 34% -> 35%
where the time goes in v4:
time: 602 us; the launch traced here: 594 us
  Pallas kernels  229 us (38%)
  starting transfers between devices  110 us (18%)
  waiting for transfers between devices  83.2 us (14%)
  matrix products  62 us (10%)
  other arithmetic  59 us (10%)
  local copies, waits for them, and re-layouts  48.8 us (8%)
    ppermute x64, starting transfers between devices, swap(): return lax.ppermute(block, DEVICES, route)  105 us
    ppermute x64, waiting for transfers between devices, swap(): return lax.ppermute(block, DEVICES, route)  83.2 us
    pallas_call x16, Pallas kernels, product(): pl.pallas_call(without(functools.partial(product_kernel, len(which), len(...  75.2 us
    dot_general x6, matrix products, dot_nt(): lax.dot_general(a, b, (((1,), (1,)), ((), ())), preferred_element_type=F32)  32.7 us
    dot_general x7, matrix products, dot_nn(): lax.dot_general(a, b, (((1,), (0,)), ((), ())), precision=precision, pref...  29.3 us
    pallas_call x1, Pallas kernels, mamba_back(): pl.pallas_call(without(mamba_back_kernel, 13, len(tokens)), grid=(count,)...  25.4 us
    unnamed x159, local copies, waits for them, and re-layouts  21 us
    pallas_call x6, Pallas kernels, scan_step(): pl.pallas_call(functools.partial(scan_step_kernel, seen is None, ends), i...  16.8 us
  transfers between devices with their start and end apart: 66, of which 21 were waited for; matrix products, arithmetic and copies ran while one was open for 21% of the time, Pallas kernels for 35%

profile of v4, /device:TPU:0, one launch (start us, length us, event | category | flops | bytes accessed | tf_op | source)
XLA Modules:
  0.0 593.6 jit_solution(17931585053454717197)
XLA Ops:
  1.5 4.1 concatenate.64
  43.0 5.6 collective-permute-done.9
  50.9 6.5 %collective-permute-done.15 = bf16[512,128]{1,0:T(8,128)(2,1)S(1)} collective-permute-done((bf16[512,128]{1,0:T(8,128)(2,1)S(1)}, bf16[512,128]{1,0:T(8,128)(2,1)S(1)}, u32[]{:S(2)}, u32[]{:S(2)}) %collective-permute-start.15) | collective-permute-done | bytes 131104 | tf_op jit(solution)/shard_map/ppermute | solution.py:1072
  60.2 3.8 place.4.refs_1_
  64.0 4.1 fusion.7.refs_2_
  83.1 13.5 %mamba_forward.1 = (f32[512,1536]{1,0:T(8,128)}, f32[4,128,1536]{2,1,0:T(8,128)}, bf16[144,1536]{1,0:T(8,128)(2,1)}, f32[144,1536]{1,0:T(8,128)}, f32[512,128]{1,0:T(8,128)}, /*index=5*/bf16[512,128]{1,0:T(8,128)(2,1)}) custom-call(s32[5]{0:T(128)} %pad_add_fusion.refs_0_, f32[8,1792]{1,0:T(8,128)} %convert_element_type.260.refs_1_, ...), custom_call_target="tpu_custom_call" | custom-call | flops 14949999616 | tf_op jit(solution)/shard_map/mamba_forward/pallas_call | solution.py:220
  102.4 6.5 %collective-permute-done.11.refs_0_ = bf16[144,1536]{1,0:T(8,128)(2,1)} collective-permute-done((bf16[144,1536]{1,0:T(8,128)(2,1)}, bf16[144,1536]{1,0:T(8,128)(2,1)}, u32[]{:S(2)}, u32[]{:S(2)}) %collective-permute-start.11) | collective-permute-done | bytes 442400 | tf_op jit(solution)/shard_map/ppermute | solution.py:1072
  113.4 5.0 attend.2
  123.6 10.7 %collective-permute-start.14 = (bf16[144,1536]{1,0:T(8,128)(2,1)}, bf16[144,1536]{1,0:T(8,128)(2,1)S(1)}, u32[]{:S(2)}, u32[]{:S(2)}) collective-permute-start(bf16[144,1536]{1,0:T(8,128)(2,1)} %get-tuple-element.115.refs_9_), channel_id=1, source_target_pairs={{0,16},{1,17},{2,18},{3,19},{4,20},{5,21},{6,22},{7,23},{8,24},{9,... | collective-permute-start | bytes 1327112 | tf_op jit(solution)/shard_map/ppermute | solution.py:1072
  134.3 8.5 %attend.3 = (bf16[512,256]{1,0:T(8,128)(2,1)}, f32[512,256]{1,0:T(8,128)}, f32[2,8,1024]{2,1,0:T(8,128)}, bf16[1024,1536]{1,0:T(8,128)(2,1)}, bf16[2048,1024]{1,0:T(8,128)(2,1)}) custom-call(s32[13]{0:T(128)} %pad_add_fusion.2.refs_0_, bf16[512,512]{1,0:T(8,128)(2,1)} %get-tuple-element.101.refs_1_, bf16[4096,128]{1,0:T(8,128)(2,1)} %pad_maximum_fusion.4.refs_2_.refs_5_, ...), custom_call_target="tpu_custom_call" | custom-call | flops 20700000256 | tf_op jit(solution)/shard_map/attend/pallas_call | solution.py:867
  142.8 12.0 %collective-permute-done.14.refs_0_ = bf16[144,1536]{1,0:T(8,128)(2,1)S(1)} collective-permute-done((bf16[144,1536]{1,0:T(8,128)(2,1)}, bf16[144,1536]{1,0:T(8,128)(2,1)S(1)}, u32[]{:S(2)}, u32[]{:S(2)}) %collective-permute-start.14) | collective-permute-done | bytes 442400 | tf_op jit(solution)/shard_map/ppermute | solution.py:1072
  161.9 8.8 %mamba_correct.1 = (f32[512,1536]{1,0:T(8,128)}, bf16[512,2048]{1,0:T(8,128)(2,1)}, bf16[4,128,1536]{2,1,0:T(8,128)(2,1)}) custom-call(f32[512,1536]{1,0:T(8,128)} %get-tuple-element.103.y_ref, f32[4,128,1536]{2,1,0:T(8,128)} %get-tuple-element.104.sin_ref, bf16[512,128]{1,0:T(8,128)(2,1)} %get-tuple-element.105.c_ref.refs_3_, ...), custom_call_target="tpu_custom_call" | custom-call | flops 9774999552 | tf_op jit(solution)/shard_map/mamba_correct/pallas_call | solution.py:308
  171.3 5.3 multiply_reduce_fusion.3
  178.5 9.4 %place.5 = (bf16[1024,4096]{1,0:T(8,128)(2,1)}, bf16[2048,1024]{1,0:T(8,128)(2,1)}) custom-call(s32[12]{0:T(128)} %stack.74.refs_4_.at_ref, bf16[256,6144]{1,0:T(8,128)(2,1)} %after.48.refs_0_, bf16[256,6144]{1,0:T(8,128)(2,1)} %collective-permute-done.7.refs_5_.refs_1_, bf16[256,6144]{1,0:T(8,128)(2,1)} %after.57.refs_2_, bf16[256,6144]{1,0:T(8,128)(2,1)} %copy-done.72), custom_call_target="tpu_custom_call" | custom-call | flops 10796899328 | tf_op jit(solution)/shard_map/place/pallas_call | solution.py:1113
  187.9 7.0 %fusion.54 = f32[512,4096]{1,0:T(8,128)S(1)} fusion(bf16[512,1024]{1,0:T(8,128)(2,1)S(1)} %multiply_convert_fusion.1.refs_1_.refs_2_, bf16[1024,4096]{1,0:T(8,128)(2,1)} %get-tuple-element.122), kind=kOutput, calls=%fused_computation.154 | convolution fusion | flops 4294967296 | bytes 17825792 | tf_op jit(solution)/shard_map/dot_general | solution.py:38
  195.0 5.2 fusion.2
  202.7 6.4 %product.16 = bf16[512,4096]{1,0:T(8,128)(2,1)} custom-call(s32[3]{0:T(128)} %add_add_fusion.refs_0_, bf16[512,1024]{1,0:T(8,128)(2,1)} %copy-done.33, bf16[512,1024]{1,0:T(8,128)(2,1)} %copy-done.33, bf16[512,4096]{1,0:T(8,128)(2,1)} %pad_maximum_fusion.refs_3_.refs_2_), custom_call_target="tpu_custom_call" | custom-call | flops 8385174528 | tf_op jit(solution)/shard_map/product/pallas_call | solution.py:1207
  210.8 4.9 product.18
  215.7 7.2 %multiply_reduce_fusion.2 = (f32[512]{0:T(512)S(1)}, f32[512,1024]{1,0:T(8,128)S(1)}) fusion(f32[512,1024]{1,0:T(8,128)S(1)} %get-tuple-element.287, f32[1024]{0:T(1024)S(1)} %bitcast.116, bf16[1024,4096]{1,0:T(8,128)(2,1)} %get-tuple-element.122, bf16[512,2048]{1,0:T(8,128)(2,1)S(1)} %get-tuple-element.258, bf16[512,2048]{1,0:T(8,128)(2,1)S(1)} %get-tuple-element.257), kind=kOutput, calls=%fused_computation.33 | convolution fusion | flops 4304928256 | bytes 16783360 | tf_op jit(solution)/shard_map/dot_general | solution.py:44
  225.2 5.2 product.17.refs_5_.refs_1_
  231.6 5.6 product.19
  237.4 6.3 %convolution_convert_fusion.refs_0_ = bf16[512,2048]{1,0:T(8,128)(2,1)} fusion(bf16[512,1024]{1,0:T(8,128)(2,1)} %after.58.refs_3_, bf16[2048,1024]{1,0:T(8,128)(2,1)} %get-tuple-element.120), kind=kOutput, calls=%fused_computation.19 | convolution fusion | flops 2148532224 | bytes 7340032 | tf_op jit(solution)/shard_map/dot_general | solution.py:44
  243.7 7.9 %mamba_gate_back.1 = (bf16[512,1536]{1,0:T(8,128)(2,1)}, bf16[512,1536]{1,0:T(8,128)(2,1)}, f32[144,1536]{1,0:T(8,128)}, bf16[144,1536]{1,0:T(8,128)(2,1)}, bf16[512,512]{1,0:T(8,128)(2,1)}) custom-call(bf16[512,2048]{1,0:T(8,128)(2,1)} %convolution_convert_fusion.refs_0_, f32[512,1536]{1,0:T(8,128)} %fusion.53.z_ref.refs_1_, ...), custom_call_target="tpu_custom_call" | custom-call | flops 8625000448 | tf_op jit(solution)/shard_map/mamba_gate_back/pallas_call | solution.py:370
  251.6 4.9 product.21
  258.3 4.4 product.23
  264.7 7.4 %collective-permute-done.24.refs_1_ = bf16[144,1536]{1,0:T(8,128)(2,1)} collective-permute-done((bf16[144,1536]{1,0:T(8,128)(2,1)}, bf16[144,1536]{1,0:T(8,128)(2,1)}, u32[]{:S(2)}, u32[]{:S(2)}) %collective-permute-start.24) | collective-permute-done | bytes 442400 | tf_op jit(solution)/shard_map/ppermute | solution.py:1072
  278.8 6.0 %product.20 = (bf16[128,4096]{1,0:T(8,128)(2,1)}, bf16[128,4096]{1,0:T(8,128)(2,1)}) custom-call(s32[2]{0:T(128)} %pad_add_fusion.4.refs_0_, bf16[512,1024]{1,0:T(8,128)(2,1)} %copy-done.33, bf16[512,4096]{1,0:T(8,128)(2,1)} %pad_maximum_fusion.refs_3_.refs_2_, bf16[512,4096]{1,0:T(8,128)(2,1)} %collective-permute-done.22.refs_3_, ...), custom_call_target="tpu_custom_call" | custom-call | flops 4767587328 | tf_op jit(solution)/shard_map/product/pallas_call | solution.py:1207
  287.1 3.7 product.24.refs_10_
  298.3 5.4 product.22
  305.4 5.8 collective-permute-done.28.refs_0_
  315.8 7.5 %attend_back.2 = (f32[512,256]{1,0:T(8,128)}, bf16[4096,128]{1,0:T(8,128)(2,1)}) custom-call(s32[13]{0:T(128)} %pad_add_fusion.2.refs_0_, bf16[512,512]{1,0:T(8,128)(2,1)} %get-tuple-element.101.refs_1_, bf16[512,512]{1,0:T(8,128)(2,1)} %get-tuple-element.126.refs_1_.refs_2_, f32[512,256]{1,0:T(8,128)} %get-tuple-element.140.refs_3_, ...), custom_call_target="tpu_custom_call" | custom-call | flops 29899999232 | tf_op jit(solution)/shard_map/attend_back/pallas_call | solution.py:973
  325.2 4.0 product.25
  344.3 13.0 %collective-permute-start.37 = (bf16[64,6144]{1,0:T(8,128)(2,1)}, bf16[64,6144]{1,0:T(8,128)(2,1)S(1)}, u32[]{:S(2)}, u32[]{:S(2)}) collective-permute-start(bf16[64,6144]{1,0:T(8,128)(2,1)} %add_convert_fusion.4.refs_13_), channel_id=1, source_target_pairs={{0,16},{1,17},{2,18},{3,19},{4,20},{5,21},{6,22},{7,23},{8,24},{9,... | collective-permute-start | bytes 2359304 | tf_op jit(solution)/shard_map/ppermute | solution.py:1072
  357.3 25.4 %mamba_back.1 = (bf16[512,1920]{1,0:T(8,128)(2,1)}, f32[8,1792]{1,0:T(8,128)}, f32[8,1792]{1,0:T(8,128)}, f32[8,1792]{1,0:T(8,128)}, f32[8,128]{1,0:T(8,128)}) custom-call(s32[5]{0:T(128)} %pad_add_fusion.refs_0_, f32[8,1792]{1,0:T(8,128)} %convert_element_type.260.refs_1_, bf16[512,1792]{1,0:T(8,128)(2,1)} %copy-done.71, f32[512,128]{1,0:T(8,128)} %fusion.23.refs_3_, ...), custom_call_target="tpu_custom_call" | custom-call | flops 28750000128 | tf_op jit(solution)/shard_map/mamba_back/pallas_call | solution.py:600
  397.7 5.1 product.26
  403.0 6.7 %collective-permute-start.42 = (bf16[64,6144]{1,0:T(8,128)(2,1)}, bf16[64,6144]{1,0:T(8,128)(2,1)}, u32[]{:S(2)}, u32[]{:S(2)}) collective-permute-start(bf16[64,6144]{1,0:T(8,128)(2,1)} %add_convert_fusion.3.refs_5_.own_ref), channel_id=1, source_target_pairs={{0,8},{1,9},{2,10},{3,11},{4,12},{5,13},{6,14},{7,15},{8,0},{9,1},... | collective-permute-start | bytes 2359304 | tf_op jit(solution)/shard_map/ppermute | solution.py:1072
  409.6 6.1 %fusion.21 = bf16[1,512,1024]{2,1,0:T(8,128)(2,1)} fusion(f32[512,1024]{1,0:T(8,128)S(1)} %get-tuple-element.287, bf16[512,2048]{1,0:T(8,128)(2,1)} %get-tuple-element.259.refs_1_.refs_2_, bf16[2048,1024]{1,0:T(8,128)(2,1)} %get-tuple-element.123), kind=kOutput, calls=%fused_computation.47 | convolution fusion | flops 2148532224 | bytes 9437184 | tf_op jit(solution)/shard_map/dot_general | solution.py:38
  420.4 4.3 product.27.refs_1_.refs_7_
  431.0 7.2 %attend_back.3 = (f32[512,256]{1,0:T(8,128)}, bf16[4096,128]{1,0:T(8,128)(2,1)}) custom-call(s32[13]{0:T(128)} %pad_add_fusion.2.refs_0_, bf16[512,512]{1,0:T(8,128)(2,1)} %get-tuple-element.101.refs_1_, bf16[512,512]{1,0:T(8,128)(2,1)} %get-tuple-element.126.refs_1_.refs_2_, f32[512,256]{1,0:T(8,128)} %get-tuple-element.127.refs_3_, ...), custom_call_target="tpu_custom_call" | custom-call | flops 29899999232 | tf_op jit(solution)/shard_map/attend_back/pallas_call | solution.py:973
  441.8 14.5 %collective-permute-start.45 = (bf16[512,128]{1,0:T(8,128)(2,1)}, bf16[512,128]{1,0:T(8,128)(2,1)S(1)}, u32[]{:S(2)}, u32[]{:S(2)}) collective-permute-start(bf16[512,128]{1,0:T(8,128)(2,1)} %slice.232), channel_id=1, source_target_pairs={{0,16},{1,17},{2,18},{3,19},{4,20},{5,21},{6,22},{7,23},{8,24},{9,... | collective-permute-start | bytes 393224 | tf_op jit(solution)/shard_map/ppermute | solution.py:1072
  461.2 10.6 %collective-permute-done.43 = bf16[2048,128]{1,0:T(8,128)(2,1)S(1)} collective-permute-done((bf16[2048,128]{1,0:T(8,128)(2,1)S(1)}, bf16[2048,128]{1,0:T(8,128)(2,1)S(1)}, u32[]{:S(2)}, u32[]{:S(2)}) %collective-permute-start.43) | collective-permute-done | bytes 524320 | tf_op jit(solution)/shard_map/ppermute | solution.py:1072
  473.6 4.6 product.28
  478.2 5.3 collective-permute-start.47
  483.5 4.2 fusion.55
  492.1 7.4 %collective-permute-done.48 = bf16[512,128]{1,0:T(8,128)(2,1)S(1)} collective-permute-done((bf16[512,128]{1,0:T(8,128)(2,1)S(1)}, bf16[512,128]{1,0:T(8,128)(2,1)S(1)}, u32[]{:S(2)}, u32[]{:S(2)}) %collective-permute-start.48) | collective-permute-done | bytes 131104 | tf_op jit(solution)/shard_map/ppermute | solution.py:1072
  517.0 4.9 collective-permute-start.59
  521.9 5.1 unpack.7
  534.8 6.4 %fusion.56 = f32[512,1024]{1,0:T(8,128)} fusion(bf16[512,1920]{1,0:T(8,128)(2,1)} %after.78, bf16[1024,1920]{1,0:T(8,128)(2,1)} %place.4.refs_1_), kind=kOutput, calls=%fused_computation.156 | convolution fusion | flops 2013265920 | bytes 7995392 | tf_op jit(solution)/shard_map/dot_general | solution.py:44
  (471 shorter events, 252.3 us)
Async XLA Ops:
  7.5 17.5 %collective-permute-start = (bf16[272,768]{1,0:T(8,128)(2,1)}, bf16[272,768]{1,0:T(8,128)(2,1)}, u32[]{:S(2)}, u32[]{:S(2)}) collective-permute-start(bf16[272,768]{1,0:T(8,128)(2,1)} %pad_maximum_fusion.7.refs_0_), channel_id=1, source_target_pairs={{0,1},{1,0},{2,3},{3,2},{4,5},{5,4},{6,7},{7,6},{8,9},{9,8},{10,11... | collective-permute-start | bytes 1253384 | tf_op jit(solution)/shard_map/ppermute | solution.py:1072
  13.5 46.0 %collective-permute-start.3 = (bf16[256,1920]{1,0:T(8,128)(2,1)}, bf16[256,1920]{1,0:T(8,128)(2,1)}, u32[]{:S(2)}, u32[]{:S(2)}) collective-permute-start(bf16[256,1920]{1,0:T(8,128)(2,1)} %fusion.22.refs_0_), channel_id=1, source_target_pairs={{0,1},{1,0},{2,3},{3,2},{4,5},{5,4},{6,7},{7,6},{8,9},{9,8},{10,11... | collective-permute-start | bytes 2949128 | tf_op jit(solution)/shard_map/ppermute | solution.py:1072
  13.7 28.4 %collective-permute-start.4 = (bf16[256,1920]{1,0:T(8,128)(2,1)}, bf16[256,1920]{1,0:T(8,128)(2,1)}, u32[]{:S(2)}, u32[]{:S(2)}) collective-permute-start(bf16[256,1920]{1,0:T(8,128)(2,1)} %fusion.22.refs_0_), channel_id=1, source_target_pairs={{0,2},{1,3},{2,0},{3,1},{4,6},{5,7},{6,4},{7,5},{8,10},{9,11},{10,... | collective-permute-start | bytes 2949128 | tf_op jit(solution)/shard_map/ppermute | solution.py:1072
  21.3 38.8 %collective-permute-start.7 = (bf16[256,6144]{1,0:T(8,128)(2,1)}, bf16[256,6144]{1,0:T(8,128)(2,1)}, u32[]{:S(2)}, u32[]{:S(2)}) collective-permute-start(bf16[256,6144]{1,0:T(8,128)(2,1)} %after.48.refs_0_), channel_id=1, source_target_pairs={{0,1},{1,0},{2,3},{3,2},{4,5},{5,4},{6,7},{7,6},{8,9},{9,8},{10,11... | collective-permute-start | bytes 9437192 | tf_op jit(solution)/shard_map/ppermute | solution.py:1072
  25.0 35.1 %collective-permute-start.6 = (bf16[256,3584]{1,0:T(8,128)(2,1)}, bf16[256,3584]{1,0:T(8,128)(2,1)}, u32[]{:S(2)}, u32[]{:S(2)}) collective-permute-start(bf16[256,3584]{1,0:T(8,128)(2,1)} %after.47.refs_5_), channel_id=1, source_target_pairs={{0,1},{1,0},{2,3},{3,2},{4,5},{5,4},{6,7},{7,6},{8,9},{9,8},{10,11... | collective-permute-start | bytes 5505032 | tf_op jit(solution)/shard_map/ppermute | solution.py:1072
  42.2 18.0 %collective-permute-start.5 = (bf16[256,1920]{1,0:T(8,128)(2,1)}, bf16[256,1920]{1,0:T(8,128)(2,1)}, u32[]{:S(2)}, u32[]{:S(2)}) collective-permute-start(bf16[256,1920]{1,0:T(8,128)(2,1)} %after.46.refs_2_), channel_id=1, source_target_pairs={{0,1},{1,0},{2,3},{3,2},{4,5},{5,4},{6,7},{7,6},{8,9},{9,8},{10,11... | collective-permute-start | bytes 2949128 | tf_op jit(solution)/shard_map/ppermute | solution.py:1072
  57.4 55.4 %collective-permute-start.18 = (bf16[256,3584]{1,0:T(8,128)(2,1)S(1)}, bf16[256,3584]{1,0:T(8,128)(2,1)}, u32[]{:S(2)}, u32[]{:S(2)}) collective-permute-start(bf16[256,3584]{1,0:T(8,128)(2,1)S(1)} %copy-done.5), channel_id=1, source_target_pairs={{0,2},{1,3},{2,0},{3,1},{4,6},{5,7},{6,4},{7,5},{8,10},{9,11},{10,... | collective-permute-start | bytes 5505032 | tf_op jit(solution)/shard_map/ppermute | solution.py:1072
  59.5 111.1 %collective-permute-start.20 = (bf16[256,6144]{1,0:T(8,128)(2,1)}, bf16[256,6144]{1,0:T(8,128)(2,1)}, u32[]{:S(2)}, u32[]{:S(2)}) collective-permute-start(bf16[256,6144]{1,0:T(8,128)(2,1)} %after.48.refs_0_), channel_id=1, source_target_pairs={{0,2},{1,3},{2,0},{3,1},{4,6},{5,7},{6,4},{7,5},{8,10},{9,11},{10,... | collective-permute-start | bytes 9437192 | tf_op jit(solution)/shard_map/ppermute | solution.py:1072
  75.4 22.6 %collective-permute-start.16 = (bf16[1024,128]{1,0:T(8,128)(2,1)}, bf16[1024,128]{1,0:T(8,128)(2,1)S(1)}, u32[]{:S(2)}, u32[]{:S(2)}) collective-permute-start(bf16[1024,128]{1,0:T(8,128)(2,1)} %after.53), channel_id=1, source_target_pairs={{0,8},{1,9},{2,10},{3,11},{4,12},{5,13},{6,14},{7,15},{8,0},{9,1},... | collective-permute-start | bytes 786440 | tf_op jit(solution)/shard_map/ppermute | solution.py:1072
  82.3 17.9 %collective-permute-start.12 = (bf16[2048,128]{1,0:T(8,128)(2,1)S(1)}, bf16[2048,128]{1,0:T(8,128)(2,1)}, u32[]{:S(2)}, u32[]{:S(2)}) collective-permute-start(bf16[2048,128]{1,0:T(8,128)(2,1)S(1)} %pad_maximum_fusion.5.refs_8_), channel_id=1, source_target_pairs={{0,4},{1,5},{2,6},{3,7},{4,0},{5,1},{6,2},{7,3},{8,12},{9,13},{10,... | collective-permute-start | bytes 1572872 | tf_op jit(solution)/shard_map/ppermute | solution.py:1072
  99.5 18.9 %collective-permute-start.17 = (bf16[2048,128]{1,0:T(8,128)(2,1)}, bf16[2048,128]{1,0:T(8,128)(2,1)}, u32[]{:S(2)}, u32[]{:S(2)}) collective-permute-start(bf16[2048,128]{1,0:T(8,128)(2,1)} %pad_maximum_fusion.6), channel_id=1, source_target_pairs={{0,4},{1,5},{2,6},{3,7},{4,0},{5,1},{6,2},{7,3},{8,12},{9,13},{10,... | collective-permute-start | bytes 1572872 | tf_op jit(solution)/shard_map/ppermute | solution.py:1072
  112.8 21.6 %collective-permute-start.19 = (bf16[256,3584]{1,0:T(8,128)(2,1)}, bf16[256,3584]{1,0:T(8,128)(2,1)}, u32[]{:S(2)}, u32[]{:S(2)}) collective-permute-start(bf16[256,3584]{1,0:T(8,128)(2,1)} %after.55.refs_7_), channel_id=1, source_target_pairs={{0,1},{1,0},{2,3},{3,2},{4,5},{5,4},{6,7},{7,6},{8,9},{9,8},{10,11... | collective-permute-start | bytes 5505032 | tf_op jit(solution)/shard_map/ppermute | solution.py:1072
  123.6 31.3 %collective-permute-start.14 = (bf16[144,1536]{1,0:T(8,128)(2,1)}, bf16[144,1536]{1,0:T(8,128)(2,1)S(1)}, u32[]{:S(2)}, u32[]{:S(2)}) collective-permute-start(bf16[144,1536]{1,0:T(8,128)(2,1)} %get-tuple-element.115.refs_9_), channel_id=1, source_target_pairs={{0,16},{1,17},{2,18},{3,19},{4,20},{5,21},{6,22},{7,23},{8,24},{9,... | collective-permute-start | bytes 1327112 | tf_op jit(solution)/shard_map/ppermute | solution.py:1072
  209.1 16.2 %collective-permute-start.22 = (bf16[512,4096]{1,0:T(8,128)(2,1)}, bf16[512,4096]{1,0:T(8,128)(2,1)}, u32[]{:S(2)}, u32[]{:S(2)}) collective-permute-start(bf16[512,4096]{1,0:T(8,128)(2,1)} %product.16), channel_id=1, source_target_pairs={{0,1},{1,0},{2,3},{3,2},{4,5},{5,4},{6,7},{7,6},{8,9},{9,8},{10,11... | collective-permute-start | bytes 12582920 | tf_op jit(solution)/shard_map/ppermute | solution.py:1072
  215.7 15.9 %collective-permute-start.23 = (bf16[1024,1024]{1,0:T(8,128)(2,1)}, bf16[1024,1024]{1,0:T(8,128)(2,1)}, u32[]{:S(2)}, u32[]{:S(2)}) collective-permute-start(bf16[1024,1024]{1,0:T(8,128)(2,1)} %product.18), channel_id=1, source_target_pairs={{0,1},{1,0},{2,3},{3,2},{4,5},{5,4},{6,7},{7,6},{8,9},{9,8},{10,11... | collective-permute-start | bytes 6291464 | tf_op jit(solution)/shard_map/ppermute | solution.py:1072
  230.5 48.3 %collective-permute-start.26 = (bf16[256,4096]{1,0:T(8,128)(2,1)}, bf16[256,4096]{1,0:T(8,128)(2,1)}, u32[]{:S(2)}, u32[]{:S(2)}) collective-permute-start(bf16[256,4096]{1,0:T(8,128)(2,1)} %product.17.refs_5_.refs_1_), channel_id=1, source_target_pairs={{0,2},{1,3},{2,0},{3,1},{4,6},{5,7},{6,4},{7,5},{8,10},{9,11},{10,... | collective-permute-start | bytes 6291464 | tf_op jit(solution)/shard_map/ppermute | solution.py:1072
  237.2 38.7 %collective-permute-start.29 = (bf16[512,1024]{1,0:T(8,128)(2,1)}, bf16[512,1024]{1,0:T(8,128)(2,1)S(1)}, u32[]{:S(2)}, u32[]{:S(2)}) collective-permute-start(bf16[512,1024]{1,0:T(8,128)(2,1)} %get-tuple-element.124.refs_2_), channel_id=1, source_target_pairs={{0,4},{1,5},{2,6},{3,7},{4,0},{5,1},{6,2},{7,3},{8,12},{9,13},{10,... | collective-permute-start | bytes 3145736 | tf_op jit(solution)/shard_map/ppermute | solution.py:1072
  256.5 15.6 %collective-permute-start.24 = (bf16[144,1536]{1,0:T(8,128)(2,1)}, bf16[144,1536]{1,0:T(8,128)(2,1)}, u32[]{:S(2)}, u32[]{:S(2)}) collective-permute-start(bf16[144,1536]{1,0:T(8,128)(2,1)} %get-tuple-element.132), channel_id=1, source_target_pairs={{0,4},{1,5},{2,6},{3,7},{4,0},{5,1},{6,2},{7,3},{8,12},{9,13},{10,... | collective-permute-start | bytes 1327112 | tf_op jit(solution)/shard_map/ppermute | solution.py:1072
  258.3 40.0 %collective-permute-start.31 = (bf16[1024,1024]{1,0:T(8,128)(2,1)}, bf16[1024,1024]{1,0:T(8,128)(2,1)}, u32[]{:S(2)}, u32[]{:S(2)}) collective-permute-start(bf16[1024,1024]{1,0:T(8,128)(2,1)} %product.21), channel_id=1, source_target_pairs={{0,1},{1,0},{2,3},{3,2},{4,5},{5,4},{6,7},{7,6},{8,9},{9,8},{10,11... | collective-permute-start | bytes 6291464 | tf_op jit(solution)/shard_map/ppermute | solution.py:1072
  262.8 24.3 %collective-permute-start.32 = (bf16[512,1536]{1,0:T(8,128)(2,1)}, bf16[512,1536]{1,0:T(8,128)(2,1)}, u32[]{:S(2)}, u32[]{:S(2)}) collective-permute-start(bf16[512,1536]{1,0:T(8,128)(2,1)} %product.23), channel_id=1, source_target_pairs={{0,1},{1,0},{2,3},{3,2},{4,5},{5,4},{6,7},{7,6},{8,9},{9,8},{10,11... | collective-permute-start | bytes 4718600 | tf_op jit(solution)/shard_map/ppermute | solution.py:1072
  275.0 16.9 %collective-permute-start.25 = (bf16[144,1536]{1,0:T(8,128)(2,1)}, bf16[144,1536]{1,0:T(8,128)(2,1)}, u32[]{:S(2)}, u32[]{:S(2)}) collective-permute-start(bf16[144,1536]{1,0:T(8,128)(2,1)} %get-tuple-element.135.refs_1_), channel_id=1, source_target_pairs={{0,8},{1,9},{2,10},{3,11},{4,12},{5,13},{6,14},{7,15},{8,0},{9,1},... | collective-permute-start | bytes 1327112 | tf_op jit(solution)/shard_map/ppermute | solution.py:1072
  284.8 26.4 %collective-permute-start.28 = (bf16[128,4096]{1,0:T(8,128)(2,1)}, bf16[128,4096]{1,0:T(8,128)(2,1)}, u32[]{:S(2)}, u32[]{:S(2)}) collective-permute-start(bf16[128,4096]{1,0:T(8,128)(2,1)} %get-tuple-element.136.refs_1_.refs_5_), channel_id=1, source_target_pairs={{0,4},{1,5},{2,6},{3,7},{4,0},{5,1},{6,2},{7,3},{8,12},{9,13},{10,... | collective-permute-start | bytes 3145736 | tf_op jit(solution)/shard_map/ppermute | solution.py:1072
  286.2 19.3 %collective-permute-start.30 = (bf16[256,1024]{1,0:T(8,128)(2,1)}, bf16[256,1024]{1,0:T(8,128)(2,1)}, u32[]{:S(2)}, u32[]{:S(2)}) collective-permute-start(bf16[256,1024]{1,0:T(8,128)(2,1)} %get-tuple-element.262), channel_id=1, source_target_pairs={{0,2},{1,3},{2,0},{3,1},{4,6},{5,7},{6,4},{7,5},{8,10},{9,11},{10,... | collective-permute-start | bytes 1572872 | tf_op jit(solution)/shard_map/ppermute | solution.py:1072
  290.8 34.3 %collective-permute-start.34 = (bf16[256,1536]{1,0:T(8,128)(2,1)}, bf16[256,1536]{1,0:T(8,128)(2,1)}, u32[]{:S(2)}, u32[]{:S(2)}) collective-permute-start(bf16[256,1536]{1,0:T(8,128)(2,1)} %product.24.refs_10_), channel_id=1, source_target_pairs={{0,2},{1,3},{2,0},{3,1},{4,6},{5,7},{6,4},{7,5},{8,10},{9,11},{10,... | collective-permute-start | bytes 2359304 | tf_op jit(solution)/shard_map/ppermute | solution.py:1072
  295.0 43.6 %collective-permute-start.27 = (bf16[144,1536]{1,0:T(8,128)(2,1)}, bf16[144,1536]{1,0:T(8,128)(2,1)}, u32[]{:S(2)}, u32[]{:S(2)}) collective-permute-start(bf16[144,1536]{1,0:T(8,128)(2,1)} %get-tuple-element.139.refs_1_.refs_7_), channel_id=1, source_target_pairs={{0,16},{1,17},{2,18},{3,19},{4,20},{5,21},{6,22},{7,23},{8,24},{9,... | collective-permute-start | bytes 1327112 | tf_op jit(solution)/shard_map/ppermute | solution.py:1072
  303.7 29.9 %collective-permute-start.35 = (bf16[512,1024]{1,0:T(8,128)(2,1)}, bf16[512,1024]{1,0:T(8,128)(2,1)S(1)}, u32[]{:S(2)}, u32[]{:S(2)}) collective-permute-start(bf16[512,1024]{1,0:T(8,128)(2,1)} %get-tuple-element.145.refs_9_), channel_id=1, source_target_pairs={{0,4},{1,5},{2,6},{3,7},{4,0},{5,1},{6,2},{7,3},{8,12},{9,13},{10,... | collective-permute-start | bytes 3145736 | tf_op jit(solution)/shard_map/ppermute | solution.py:1072
  314.6 26.4 %collective-permute-start.33 = (bf16[64,6144]{1,0:T(8,128)(2,1)}, bf16[64,6144]{1,0:T(8,128)(2,1)}, u32[]{:S(2)}, u32[]{:S(2)}) collective-permute-start(bf16[64,6144]{1,0:T(8,128)(2,1)} %get-tuple-element.144.refs_8_), channel_id=1, source_target_pairs={{0,8},{1,9},{2,10},{3,11},{4,12},{5,13},{6,14},{7,15},{8,0},{9,1},... | collective-permute-start | bytes 2359304 | tf_op jit(solution)/shard_map/ppermute | solution.py:1072
  329.2 63.0 %collective-permute-start.38 = (bf16[128,1536]{1,0:T(8,128)(2,1)}, bf16[128,1536]{1,0:T(8,128)(2,1)S(1)}, u32[]{:S(2)}, u32[]{:S(2)}) collective-permute-start(bf16[128,1536]{1,0:T(8,128)(2,1)} %get-tuple-element.148.refs_14_), channel_id=1, source_target_pairs={{0,4},{1,5},{2,6},{3,7},{4,0},{5,1},{6,2},{7,3},{8,12},{9,13},{10,... | collective-permute-start | bytes 1179656 | tf_op jit(solution)/shard_map/ppermute | solution.py:1072
  337.6 55.4 %collective-permute-start.39 = (bf16[256,1024]{1,0:T(8,128)(2,1)}, bf16[256,1024]{1,0:T(8,128)(2,1)}, u32[]{:S(2)}, u32[]{:S(2)}) collective-permute-start(bf16[256,1024]{1,0:T(8,128)(2,1)} %get-tuple-element.261.refs_15_), channel_id=1, source_target_pairs={{0,2},{1,3},{2,0},{3,1},{4,6},{5,7},{6,4},{7,5},{8,10},{9,11},{10,... | collective-permute-start | bytes 1572872 | tf_op jit(solution)/shard_map/ppermute | solution.py:1072
  338.6 47.4 %collective-permute-start.40 = (bf16[2048,128]{1,0:T(8,128)(2,1)}, bf16[2048,128]{1,0:T(8,128)(2,1)}, u32[]{:S(2)}, u32[]{:S(2)}) collective-permute-start(bf16[2048,128]{1,0:T(8,128)(2,1)} %slice.188.refs_16_), channel_id=1, source_target_pairs={{0,4},{1,5},{2,6},{3,7},{4,0},{5,1},{6,2},{7,3},{8,12},{9,13},{10,... | collective-permute-start | bytes 1572872 | tf_op jit(solution)/shard_map/ppermute | solution.py:1072
  344.3 50.1 %collective-permute-start.37 = (bf16[64,6144]{1,0:T(8,128)(2,1)}, bf16[64,6144]{1,0:T(8,128)(2,1)S(1)}, u32[]{:S(2)}, u32[]{:S(2)}) collective-permute-start(bf16[64,6144]{1,0:T(8,128)(2,1)} %add_convert_fusion.4.refs_13_), channel_id=1, source_target_pairs={{0,16},{1,17},{2,18},{3,19},{4,20},{5,21},{6,22},{7,23},{8,24},{9,... | collective-permute-start | bytes 2359304 | tf_op jit(solution)/shard_map/ppermute | solution.py:1072
  402.8 17.6 %collective-permute-start.41 = (bf16[512,1920]{1,0:T(8,128)(2,1)}, bf16[512,1920]{1,0:T(8,128)(2,1)}, u32[]{:S(2)}, u32[]{:S(2)}) collective-permute-start(bf16[512,1920]{1,0:T(8,128)(2,1)} %product.26), channel_id=1, source_target_pairs={{0,1},{1,0},{2,3},{3,2},{4,5},{5,4},{6,7},{7,6},{8,9},{9,8},{10,11... | collective-permute-start | bytes 5898248 | tf_op jit(solution)/shard_map/ppermute | solution.py:1072
  403.0 25.4 %collective-permute-start.42 = (bf16[64,6144]{1,0:T(8,128)(2,1)}, bf16[64,6144]{1,0:T(8,128)(2,1)}, u32[]{:S(2)}, u32[]{:S(2)}) collective-permute-start(bf16[64,6144]{1,0:T(8,128)(2,1)} %add_convert_fusion.3.refs_5_.own_ref), channel_id=1, source_target_pairs={{0,8},{1,9},{2,10},{3,11},{4,12},{5,13},{6,14},{7,15},{8,0},{9,1},... | collective-permute-start | bytes 2359304 | tf_op jit(solution)/shard_map/ppermute | solution.py:1072
  415.8 23.6 %collective-permute-start.44 = (bf16[1024,128]{1,0:T(8,128)(2,1)S(1)}, bf16[1024,128]{1,0:T(8,128)(2,1)S(1)}, u32[]{:S(2)}, u32[]{:S(2)}) collective-permute-start(bf16[1024,128]{1,0:T(8,128)(2,1)S(1)} %slice.230), channel_id=1, source_target_pairs={{0,8},{1,9},{2,10},{3,11},{4,12},{5,13},{6,14},{7,15},{8,0},{9,1},... | collective-permute-start | bytes 786440 | tf_op jit(solution)/shard_map/ppermute | solution.py:1072
  418.5 40.6 %collective-permute-start.52 = (bf16[64,3584]{1,0:T(8,128)(2,1)}, bf16[64,3584]{1,0:T(8,128)(2,1)S(1)}, u32[]{:S(2)}, u32[]{:S(2)}) collective-permute-start(bf16[64,3584]{1,0:T(8,128)(2,1)} %get-tuple-element.157.refs_8_), channel_id=1, source_target_pairs={{0,8},{1,9},{2,10},{3,11},{4,12},{5,13},{6,14},{7,15},{8,0},{9,1},... | collective-permute-start | bytes 1376264 | tf_op jit(solution)/shard_map/ppermute | solution.py:1072
  424.7 48.9 %collective-permute-start.46 = (bf16[256,1920]{1,0:T(8,128)(2,1)}, bf16[256,1920]{1,0:T(8,128)(2,1)}, u32[]{:S(2)}, u32[]{:S(2)}) collective-permute-start(bf16[256,1920]{1,0:T(8,128)(2,1)} %product.27.refs_1_.refs_7_), channel_id=1, source_target_pairs={{0,2},{1,3},{2,0},{3,1},{4,6},{5,7},{6,4},{7,5},{8,10},{9,11},{10,... | collective-permute-start | bytes 2949128 | tf_op jit(solution)/shard_map/ppermute | solution.py:1072
  441.8 31.1 %collective-permute-start.45 = (bf16[512,128]{1,0:T(8,128)(2,1)}, bf16[512,128]{1,0:T(8,128)(2,1)S(1)}, u32[]{:S(2)}, u32[]{:S(2)}) collective-permute-start(bf16[512,128]{1,0:T(8,128)(2,1)} %slice.232), channel_id=1, source_target_pairs={{0,16},{1,17},{2,18},{3,19},{4,20},{5,21},{6,22},{7,23},{8,24},{9,... | collective-permute-start | bytes 393224 | tf_op jit(solution)/shard_map/ppermute | solution.py:1072
  456.4 15.5 %collective-permute-start.43 = (bf16[2048,128]{1,0:T(8,128)(2,1)S(1)}, bf16[2048,128]{1,0:T(8,128)(2,1)S(1)}, u32[]{:S(2)}, u32[]{:S(2)}) collective-permute-start(bf16[2048,128]{1,0:T(8,128)(2,1)S(1)} %slice.194.refs_1_), channel_id=1, source_target_pairs={{0,4},{1,5},{2,6},{3,7},{4,0},{5,1},{6,2},{7,3},{8,12},{9,13},{10,... | collective-permute-start | bytes 1572872 | tf_op jit(solution)/shard_map/ppermute | solution.py:1072
  461.0 46.0 %collective-permute-start.53 = (bf16[64,3584]{1,0:T(8,128)(2,1)S(1)}, bf16[64,3584]{1,0:T(8,128)(2,1)}, u32[]{:S(2)}, u32[]{:S(2)}) collective-permute-start(bf16[64,3584]{1,0:T(8,128)(2,1)S(1)} %add_convert_fusion.8), channel_id=1, source_target_pairs={{0,16},{1,17},{2,18},{3,19},{4,20},{5,21},{6,22},{7,23},{8,24},{9,... | collective-permute-start | bytes 1376264 | tf_op jit(solution)/shard_map/ppermute | solution.py:1072
  461.1 60.8 %collective-permute-start.65 = (bf16[128,6144]{1,0:T(8,128)(2,1)}, bf16[128,6144]{1,0:T(8,128)(2,1)}, u32[]{:S(2)}, u32[]{:S(2)}) collective-permute-start(bf16[128,6144]{1,0:T(8,128)(2,1)} %after.90), channel_id=1, source_target_pairs={{0,4},{1,5},{2,6},{3,7},{4,0},{5,1},{6,2},{7,3},{8,12},{9,13},{10,... | collective-permute-start | bytes 4718600 | tf_op jit(solution)/shard_map/ppermute | solution.py:1072
  492.1 22.9 %collective-permute-start.58 = (bf16[128,1920]{1,0:T(8,128)(2,1)S(1)}, bf16[128,1920]{1,0:T(8,128)(2,1)}, u32[]{:S(2)}, u32[]{:S(2)}) collective-permute-start(bf16[128,1920]{1,0:T(8,128)(2,1)S(1)} %copy-done.47), channel_id=1, source_target_pairs={{0,4},{1,5},{2,6},{3,7},{4,0},{5,1},{6,2},{7,3},{8,12},{9,13},{10,... | collective-permute-start | bytes 1474568 | tf_op jit(solution)/shard_map/ppermute | solution.py:1072
  508.9 32.3 %collective-permute-start.54 = (bf16[64,3584]{1,0:T(8,128)(2,1)}, bf16[64,3584]{1,0:T(8,128)(2,1)S(1)}, u32[]{:S(2)}, u32[]{:S(2)}) collective-permute-start(bf16[64,3584]{1,0:T(8,128)(2,1)} %add_convert_fusion.7.own_ref), channel_id=1, source_target_pairs={{0,8},{1,9},{2,10},{3,11},{4,12},{5,13},{6,14},{7,15},{8,0},{9,1},... | collective-permute-start | bytes 1376264 | tf_op jit(solution)/shard_map/ppermute | solution.py:1072
  512.9 18.0 %collective-permute-start.50 = (bf16[256,768]{1,0:T(8,128)(2,1)}, bf16[256,768]{1,0:T(8,128)(2,1)}, u32[]{:S(2)}, u32[]{:S(2)}) collective-permute-start(bf16[256,768]{1,0:T(8,128)(2,1)} %product.30.refs_1_), channel_id=1, source_target_pairs={{0,2},{1,3},{2,0},{3,1},{4,6},{5,7},{6,4},{7,5},{8,10},{9,11},{10,... | collective-permute-start | bytes 1179656 | tf_op jit(solution)/shard_map/ppermute | solution.py:1072
  517.0 13.4 %collective-permute-start.59 = (bf16[64,1920]{1,0:T(8,128)(2,1)}, bf16[64,1920]{1,0:T(8,128)(2,1)S(1)}, u32[]{:S(2)}, u32[]{:S(2)}) collective-permute-start(bf16[64,1920]{1,0:T(8,128)(2,1)} %get-tuple-element.169), channel_id=1, source_target_pairs={{0,8},{1,9},{2,10},{3,11},{4,12},{5,13},{6,14},{7,15},{8,0},{9,1},... | collective-permute-start | bytes 737288 | tf_op jit(solution)/shard_map/ppermute | solution.py:1072
  530.5 15.3 %collective-permute-start.60 = (bf16[64,1920]{1,0:T(8,128)(2,1)S(1)}, bf16[64,1920]{1,0:T(8,128)(2,1)S(1)}, u32[]{:S(2)}, u32[]{:S(2)}) collective-permute-start(bf16[64,1920]{1,0:T(8,128)(2,1)S(1)} %add_convert_fusion.12), channel_id=1, source_target_pairs={{0,16},{1,17},{2,18},{3,19},{4,20},{5,21},{6,22},{7,23},{8,24},{9,... | collective-permute-start | bytes 737288 | tf_op jit(solution)/shard_map/ppermute | solution.py:1072
  534.5 13.7 %collective-permute-start.51 = (bf16[128,768]{1,0:T(8,128)(2,1)}, bf16[128,768]{1,0:T(8,128)(2,1)}, u32[]{:S(2)}, u32[]{:S(2)}) collective-permute-start(bf16[128,768]{1,0:T(8,128)(2,1)} %get-tuple-element.161.refs_1_), channel_id=1, source_target_pairs={{0,4},{1,5},{2,6},{3,7},{4,0},{5,1},{6,2},{7,3},{8,12},{9,13},{10,... | collective-permute-start | bytes 589832 | tf_op jit(solution)/shard_map/ppermute | solution.py:1072
  544.1 27.3 %collective-permute-start.55 = (bf16[128,3584]{1,0:T(8,128)(2,1)}, bf16[128,3584]{1,0:T(8,128)(2,1)}, u32[]{:S(2)}, u32[]{:S(2)}) collective-permute-start(bf16[128,3584]{1,0:T(8,128)(2,1)} %join.5.refs_1_.own_ref), channel_id=1, source_target_pairs={{0,4},{1,5},{2,6},{3,7},{4,0},{5,1},{6,2},{7,3},{8,12},{9,13},{10,... | collective-permute-start | bytes 2752520 | tf_op jit(solution)/shard_map/ppermute | solution.py:1072
  574.9 13.6 %collective-permute-start.64 = (bf16[128,768]{1,0:T(8,128)(2,1)}, bf16[128,768]{1,0:T(8,128)(2,1)}, u32[]{:S(2)}, u32[]{:S(2)}) collective-permute-start(bf16[128,768]{1,0:T(8,128)(2,1)} %after.88.refs_1_), channel_id=1, source_target_pairs={{0,4},{1,5},{2,6},{3,7},{4,0},{5,1},{6,2},{7,3},{8,12},{9,13},{10,... | collective-permute-start | bytes 589832 | tf_op jit(solution)/shard_map/ppermute | solution.py:1072
  (95 other events, 655.1 us)

commit v5 on v4

--- a/solution.py
+++ b/solution.py
@@ -191,7 +191,7 @@
             mixing.append((couple * jnp.exp(gap)).astype(BF16))
         y = dot_nn(jnp.concatenate(mixing, axis=1), split_pair(weighted.astype(BF16), low))
         state = state_ref[:, tile(j)]
-        sin_ref[0, :, tile(j)] = state
+        sin_ref[0, :, tile(j)] = state.astype(BF16)
         y = y + dot_nn(c_mat, state.astype(BF16)) * spread(into, j, low)
         y_ref[:, tile(j)] = y + skip_ref[0:1, tile(j)] * x
         fresh = dot_nn(b_turned, (weighted * spread(ending, j, low)).astype(BF16))
@@ -241,7 +241,7 @@
         ],
         out_shape=[
             jax.ShapeDtypeStruct((rows, MAMBA_INNER), F32),
-            jax.ShapeDtypeStruct((count, STATE_SIZE, MAMBA_INNER), F32),
+            jax.ShapeDtypeStruct((count, STATE_SIZE, MAMBA_INNER), BF16),
             jax.ShapeDtypeStruct((MESSAGE_ROWS, MAMBA_INNER), BF16),
             jax.ShapeDtypeStruct((MESSAGE_ROWS, MAMBA_INNER), F32),
             jax.ShapeDtypeStruct((rows, LANES), F32),
@@ -290,10 +290,10 @@
         state = state_ref[:, tile(j)]
         y = y_ref[:, tile(j)] + dot_nn(c_mat, state.astype(BF16)) * spread(decay, j, low)
         total_ref[:, tile(j)] = y
-        z = z_ref[:, tile(j)]
+        z = z_ref[:, tile(j)].astype(F32)
         both_ref[:, gated_tile(j)] = (y * (z * jax.nn.sigmoid(z))).astype(BF16)
         true_ref[0, :, tile(j)] = (
-            sin_ref[0, :, tile(j)] + state * spread(before, j, low_row)
+            sin_ref[0, :, tile(j)].astype(F32) + state * spread(before, j, low_row)
         ).astype(BF16)
     for i, vec_ref in enumerate((vec0_ref, vec0_ref, vec1_ref, vec1_ref)):
         both_ref[:, attn_tile(i)] = vec_ref[:, tile(i % 2)]
@@ -344,7 +344,7 @@
     decay = dec_ref[...]
     c_turned = c_ref[...].astype(F32).T.astype(BF16)
     for j in range(PAIRS):
-        z = z_ref[:, tile(j)]
+        z = z_ref[:, tile(j)].astype(F32)
         sig = jax.nn.sigmoid(z)
         silu = z * sig
         grad = both_ref[:, gated_tile(j)].astype(F32)
@@ -1641,7 +1641,7 @@
     )
     attended.append(second)
     second_done = attended[1][0]
-    gate_z = dot_nn(normed, full_z)
+    gate_z = dot_nn(normed, full_z).astype(BF16)
     state_in = scan.finish([second_done])
     y_total, both, state_true = mamba_correct(
         y_local, state_local, c_mat, decay, state_in, gate_z, attended[0][0], attended[1][0]

time: 602 us -> 600 us (level)
  transfers between devices with their start and end apart: 66 -> 66, of which waited for: 21 -> 22; matrix products, arithmetic and copies ran while one was open for 21% -> 21% of each run, Pallas kernels for 35% -> 35%
where the time goes in v5:
time: 600 us; the launch traced here: 592 us
  Pallas kernels  227 us (38%)
  starting transfers between devices  109 us (18%)
  waiting for transfers between devices  84.3 us (14%)
  matrix products  61.5 us (10%)
  other arithmetic  58.9 us (10%)
  local copies, waits for them, and re-layouts  48.8 us (8%)
    ppermute x64, starting transfers between devices, swap(): return lax.ppermute(block, DEVICES, route)  104 us
    ppermute x64, waiting for transfers between devices, swap(): return lax.ppermute(block, DEVICES, route)  84.3 us
    pallas_call x16, Pallas kernels, product(): pl.pallas_call(without(functools.partial(product_kernel, len(which), len(...  74.9 us
    dot_general x6, matrix products, dot_nt(): lax.dot_general(a, b, (((1,), (1,)), ((), ())), preferred_element_type=F32)  32.7 us
    dot_general x7, matrix products, dot_nn(): lax.dot_general(a, b, (((1,), (0,)), ((), ())), precision=precision, pref...  28.8 us
    pallas_call x1, Pallas kernels, mamba_back(): pl.pallas_call(without(mamba_back_kernel, 13, len(tokens)), grid=(count,)...  25.4 us
    unnamed x159, local copies, waits for them, and re-layouts  21 us
    pallas_call x6, Pallas kernels, scan_step(): pl.pallas_call(functools.partial(scan_step_kernel, seen is None, ends), i...  16.7 us
  transfers between devices with their start and end apart: 66, of which 22 were waited for; matrix products, arithmetic and copies ran while one was open for 21% of the time, Pallas kernels for 35%

profile of v5, /device:TPU:0, one launch (start us, length us, event | category | flops | bytes accessed | tf_op | source)
XLA Modules:
  0.0 592.2 jit_solution(9161846086717135672)
XLA Ops:
  1.5 4.1 concatenate.64
  43.0 5.6 collective-permute-done.9
  50.9 6.5 %collective-permute-done.15 = bf16[512,128]{1,0:T(8,128)(2,1)S(1)} collective-permute-done((bf16[512,128]{1,0:T(8,128)(2,1)S(1)}, bf16[512,128]{1,0:T(8,128)(2,1)S(1)}, u32[]{:S(2)}, u32[]{:S(2)}) %collective-permute-start.15) | collective-permute-done | bytes 131104 | tf_op jit(solution)/shard_map/ppermute | solution.py:1072
  60.2 3.8 place.4.refs_1_
  64.0 4.1 fusion.7.refs_2_
  83.1 13.4 %mamba_forward.1 = (f32[512,1536]{1,0:T(8,128)}, bf16[4,128,1536]{2,1,0:T(8,128)(2,1)}, bf16[144,1536]{1,0:T(8,128)(2,1)}, f32[144,1536]{1,0:T(8,128)}, f32[512,128]{1,0:T(8,128)}, /*index=5*/bf16[512,128]{1,0:T(8,128)(2,1)}) custom-call(s32[5]{0:T(128)} %pad_add_fusion.refs_0_, f32[8,1792]{1,0:T(8,128)} %convert_element_type.263.refs_1_, ...), custom_call_target="tpu_custom_call" | custom-call | flops 14949999616 | tf_op jit(solution)/shard_map/mamba_forward/pallas_call | solution.py:220
  102.3 6.5 %collective-permute-done.11.refs_0_ = bf16[144,1536]{1,0:T(8,128)(2,1)} collective-permute-done((bf16[144,1536]{1,0:T(8,128)(2,1)}, bf16[144,1536]{1,0:T(8,128)(2,1)}, u32[]{:S(2)}, u32[]{:S(2)}) %collective-permute-start.11) | collective-permute-done | bytes 442400 | tf_op jit(solution)/shard_map/ppermute | solution.py:1072
  113.3 5.0 attend.2
  123.6 10.7 %collective-permute-start.14 = (bf16[144,1536]{1,0:T(8,128)(2,1)}, bf16[144,1536]{1,0:T(8,128)(2,1)S(1)}, u32[]{:S(2)}, u32[]{:S(2)}) collective-permute-start(bf16[144,1536]{1,0:T(8,128)(2,1)} %get-tuple-element.115.refs_9_), channel_id=1, source_target_pairs={{0,16},{1,17},{2,18},{3,19},{4,20},{5,21},{6,22},{7,23},{8,24},{9,... | collective-permute-start | bytes 1327112 | tf_op jit(solution)/shard_map/ppermute | solution.py:1072
  134.3 8.5 %attend.3 = (bf16[512,256]{1,0:T(8,128)(2,1)}, f32[512,256]{1,0:T(8,128)}, f32[2,8,1024]{2,1,0:T(8,128)}, bf16[1024,1536]{1,0:T(8,128)(2,1)}, bf16[2048,1024]{1,0:T(8,128)(2,1)}) custom-call(s32[13]{0:T(128)} %pad_add_fusion.2.refs_0_, bf16[512,512]{1,0:T(8,128)(2,1)} %get-tuple-element.101.refs_1_, bf16[4096,128]{1,0:T(8,128)(2,1)} %pad_maximum_fusion.4.refs_2_.refs_5_, ...), custom_call_target="tpu_custom_call" | custom-call | flops 20700000256 | tf_op jit(solution)/shard_map/attend/pallas_call | solution.py:867
  142.8 12.0 %collective-permute-done.14.refs_0_ = bf16[144,1536]{1,0:T(8,128)(2,1)S(1)} collective-permute-done((bf16[144,1536]{1,0:T(8,128)(2,1)}, bf16[144,1536]{1,0:T(8,128)(2,1)S(1)}, u32[]{:S(2)}, u32[]{:S(2)}) %collective-permute-start.14) | collective-permute-done | bytes 442400 | tf_op jit(solution)/shard_map/ppermute | solution.py:1072
  161.3 8.1 %mamba_correct.1 = (f32[512,1536]{1,0:T(8,128)}, bf16[512,2048]{1,0:T(8,128)(2,1)}, bf16[4,128,1536]{2,1,0:T(8,128)(2,1)}) custom-call(f32[512,1536]{1,0:T(8,128)} %get-tuple-element.103.y_ref, bf16[4,128,1536]{2,1,0:T(8,128)(2,1)} %get-tuple-element.104.sin_ref, bf16[512,128]{1,0:T(8,128)(2,1)} %get-tuple-element.105.c_ref.refs_3_, ...), custom_call_target="tpu_custom_call" | custom-call | flops 9774999552 | tf_op jit(solution)/shard_map/mamba_correct/pallas_call | solution.py:308
  170.1 5.2 multiply_reduce_fusion.3
  177.3 9.4 %place.5 = (bf16[1024,4096]{1,0:T(8,128)(2,1)}, bf16[2048,1024]{1,0:T(8,128)(2,1)}) custom-call(s32[12]{0:T(128)} %stack.74.refs_4_.at_ref, bf16[256,6144]{1,0:T(8,128)(2,1)} %after.48.refs_0_, bf16[256,6144]{1,0:T(8,128)(2,1)} %collective-permute-done.7.refs_5_.refs_1_, bf16[256,6144]{1,0:T(8,128)(2,1)} %after.57.refs_2_, bf16[256,6144]{1,0:T(8,128)(2,1)} %copy-done.72), custom_call_target="tpu_custom_call" | custom-call | flops 10796899328 | tf_op jit(solution)/shard_map/place/pallas_call | solution.py:1113
  186.7 7.0 %fusion.53 = f32[512,4096]{1,0:T(8,128)S(1)} fusion(bf16[512,1024]{1,0:T(8,128)(2,1)S(1)} %multiply_convert_fusion.1.refs_1_.refs_2_, bf16[1024,4096]{1,0:T(8,128)(2,1)} %get-tuple-element.122), kind=kOutput, calls=%fused_computation.154 | convolution fusion | flops 4294967296 | bytes 17825792 | tf_op jit(solution)/shard_map/dot_general | solution.py:38
  193.8 5.2 fusion.2
  201.4 6.4 %product.16 = bf16[512,4096]{1,0:T(8,128)(2,1)} custom-call(s32[3]{0:T(128)} %add_add_fusion.refs_0_, bf16[512,1024]{1,0:T(8,128)(2,1)} %copy-done.33, bf16[512,1024]{1,0:T(8,128)(2,1)} %copy-done.33, bf16[512,4096]{1,0:T(8,128)(2,1)} %pad_maximum_fusion.refs_3_.refs_2_), custom_call_target="tpu_custom_call" | custom-call | flops 8385174528 | tf_op jit(solution)/shard_map/product/pallas_call | solution.py:1207
  209.7 4.8 product.18
  214.5 7.2 %multiply_reduce_fusion.2 = (f32[512]{0:T(512)S(1)}, f32[512,1024]{1,0:T(8,128)S(1)}) fusion(f32[512,1024]{1,0:T(8,128)S(1)} %get-tuple-element.287, f32[1024]{0:T(1024)S(1)} %bitcast.116, bf16[1024,4096]{1,0:T(8,128)(2,1)} %get-tuple-element.122, bf16[512,2048]{1,0:T(8,128)(2,1)S(1)} %get-tuple-element.258, bf16[512,2048]{1,0:T(8,128)(2,1)S(1)} %get-tuple-element.257), kind=kOutput, calls=%fused_computation.34 | convolution fusion | flops 4304928256 | bytes 16783360 | tf_op jit(solution)/shard_map/dot_general | solution.py:44
  224.1 5.2 product.17.refs_5_.refs_1_
  230.5 5.5 product.19
  236.2 6.3 %convolution_convert_fusion.refs_0_ = bf16[512,2048]{1,0:T(8,128)(2,1)} fusion(bf16[512,1024]{1,0:T(8,128)(2,1)} %after.58.refs_3_, bf16[2048,1024]{1,0:T(8,128)(2,1)} %get-tuple-element.120), kind=kOutput, calls=%fused_computation.19 | convolution fusion | flops 2148532224 | bytes 7340032 | tf_op jit(solution)/shard_map/dot_general | solution.py:44
  242.5 7.4 %mamba_gate_back.1 = (bf16[512,1536]{1,0:T(8,128)(2,1)}, bf16[512,1536]{1,0:T(8,128)(2,1)}, f32[144,1536]{1,0:T(8,128)}, bf16[144,1536]{1,0:T(8,128)(2,1)}, bf16[512,512]{1,0:T(8,128)(2,1)}) custom-call(bf16[512,2048]{1,0:T(8,128)(2,1)} %convolution_convert_fusion.refs_0_, bf16[512,1536]{1,0:T(8,128)(2,1)} %convolution_convert_fusion.1.z_ref.refs_1_, ...), custom_call_target="tpu_custom_call" | custom-call | flops 8625000448 | tf_op jit(solution)/shard_map/mamba_gate_back/pallas_call | solution.py:370
  249.9 4.9 product.21
  256.7 4.4 product.23
  263.0 8.0 %collective-permute-done.24.refs_1_ = bf16[144,1536]{1,0:T(8,128)(2,1)} collective-permute-done((bf16[144,1536]{1,0:T(8,128)(2,1)}, bf16[144,1536]{1,0:T(8,128)(2,1)}, u32[]{:S(2)}, u32[]{:S(2)}) %collective-permute-start.24) | collective-permute-done | bytes 442400 | tf_op jit(solution)/shard_map/ppermute | solution.py:1072
  277.6 6.0 %product.20 = (bf16[128,4096]{1,0:T(8,128)(2,1)}, bf16[128,4096]{1,0:T(8,128)(2,1)}) custom-call(s32[2]{0:T(128)} %pad_add_fusion.4.refs_0_, bf16[512,1024]{1,0:T(8,128)(2,1)} %copy-done.33, bf16[512,4096]{1,0:T(8,128)(2,1)} %pad_maximum_fusion.refs_3_.refs_2_, bf16[512,4096]{1,0:T(8,128)(2,1)} %collective-permute-done.22.refs_3_, ...), custom_call_target="tpu_custom_call" | custom-call | flops 4767587328 | tf_op jit(solution)/shard_map/product/pallas_call | solution.py:1207
  297.0 5.4 product.22
  304.1 5.9 collective-permute-done.28.refs_0_
  314.5 7.5 %attend_back.2 = (f32[512,256]{1,0:T(8,128)}, bf16[4096,128]{1,0:T(8,128)(2,1)}) custom-call(s32[13]{0:T(128)} %pad_add_fusion.2.refs_0_, bf16[512,512]{1,0:T(8,128)(2,1)} %get-tuple-element.101.refs_1_, bf16[512,512]{1,0:T(8,128)(2,1)} %get-tuple-element.126.refs_1_.refs_2_, f32[512,256]{1,0:T(8,128)} %get-tuple-element.140.refs_3_, ...), custom_call_target="tpu_custom_call" | custom-call | flops 29899999232 | tf_op jit(solution)/shard_map/attend_back/pallas_call | solution.py:973
  323.8 4.0 product.25
  343.0 13.0 %collective-permute-start.37 = (bf16[64,6144]{1,0:T(8,128)(2,1)}, bf16[64,6144]{1,0:T(8,128)(2,1)S(1)}, u32[]{:S(2)}, u32[]{:S(2)}) collective-permute-start(bf16[64,6144]{1,0:T(8,128)(2,1)} %add_convert_fusion.4.refs_13_), channel_id=1, source_target_pairs={{0,16},{1,17},{2,18},{3,19},{4,20},{5,21},{6,22},{7,23},{8,24},{9,... | collective-permute-start | bytes 2359304 | tf_op jit(solution)/shard_map/ppermute | solution.py:1072
  356.0 25.4 %mamba_back.1 = (bf16[512,1920]{1,0:T(8,128)(2,1)}, f32[8,1792]{1,0:T(8,128)}, f32[8,1792]{1,0:T(8,128)}, f32[8,1792]{1,0:T(8,128)}, f32[8,128]{1,0:T(8,128)}) custom-call(s32[5]{0:T(128)} %pad_add_fusion.refs_0_, f32[8,1792]{1,0:T(8,128)} %convert_element_type.263.refs_1_, bf16[512,1792]{1,0:T(8,128)(2,1)} %copy-done.71, f32[512,128]{1,0:T(8,128)} %fusion.23.refs_3_, ...), custom_call_target="tpu_custom_call" | custom-call | flops 28750000128 | tf_op jit(solution)/shard_map/mamba_back/pallas_call | solution.py:600
  396.4 5.1 product.26
  401.6 6.6 %collective-permute-start.42 = (bf16[64,6144]{1,0:T(8,128)(2,1)}, bf16[64,6144]{1,0:T(8,128)(2,1)}, u32[]{:S(2)}, u32[]{:S(2)}) collective-permute-start(bf16[64,6144]{1,0:T(8,128)(2,1)} %add_convert_fusion.3.refs_5_.own_ref), channel_id=1, source_target_pairs={{0,8},{1,9},{2,10},{3,11},{4,12},{5,13},{6,14},{7,15},{8,0},{9,1},... | collective-permute-start | bytes 2359304 | tf_op jit(solution)/shard_map/ppermute | solution.py:1072
  408.2 6.1 %fusion.21 = bf16[1,512,1024]{2,1,0:T(8,128)(2,1)} fusion(f32[512,1024]{1,0:T(8,128)S(1)} %get-tuple-element.287, bf16[512,2048]{1,0:T(8,128)(2,1)} %get-tuple-element.259.refs_1_.refs_2_, bf16[2048,1024]{1,0:T(8,128)(2,1)} %get-tuple-element.123), kind=kOutput, calls=%fused_computation.48 | convolution fusion | flops 2148532224 | bytes 9437184 | tf_op jit(solution)/shard_map/dot_general | solution.py:38
  419.0 4.3 product.27.refs_1_.refs_7_
  429.6 7.2 %attend_back.3 = (f32[512,256]{1,0:T(8,128)}, bf16[4096,128]{1,0:T(8,128)(2,1)}) custom-call(s32[13]{0:T(128)} %pad_add_fusion.2.refs_0_, bf16[512,512]{1,0:T(8,128)(2,1)} %get-tuple-element.101.refs_1_, bf16[512,512]{1,0:T(8,128)(2,1)} %get-tuple-element.126.refs_1_.refs_2_, f32[512,256]{1,0:T(8,128)} %get-tuple-element.127.refs_3_, ...), custom_call_target="tpu_custom_call" | custom-call | flops 29899999232 | tf_op jit(solution)/shard_map/attend_back/pallas_call | solution.py:973
  440.4 14.5 %collective-permute-start.45 = (bf16[512,128]{1,0:T(8,128)(2,1)}, bf16[512,128]{1,0:T(8,128)(2,1)S(1)}, u32[]{:S(2)}, u32[]{:S(2)}) collective-permute-start(bf16[512,128]{1,0:T(8,128)(2,1)} %slice.232), channel_id=1, source_target_pairs={{0,16},{1,17},{2,18},{3,19},{4,20},{5,21},{6,22},{7,23},{8,24},{9,... | collective-permute-start | bytes 393224 | tf_op jit(solution)/shard_map/ppermute | solution.py:1072
  459.8 10.6 %collective-permute-done.43 = bf16[2048,128]{1,0:T(8,128)(2,1)S(1)} collective-permute-done((bf16[2048,128]{1,0:T(8,128)(2,1)S(1)}, bf16[2048,128]{1,0:T(8,128)(2,1)S(1)}, u32[]{:S(2)}, u32[]{:S(2)}) %collective-permute-start.43) | collective-permute-done | bytes 524320 | tf_op jit(solution)/shard_map/ppermute | solution.py:1072
  472.2 4.6 product.28
  476.8 5.3 collective-permute-start.47
  482.0 4.2 fusion.54
  490.7 7.4 %collective-permute-done.48 = bf16[512,128]{1,0:T(8,128)(2,1)S(1)} collective-permute-done((bf16[512,128]{1,0:T(8,128)(2,1)S(1)}, bf16[512,128]{1,0:T(8,128)(2,1)S(1)}, u32[]{:S(2)}, u32[]{:S(2)}) %collective-permute-start.48) | collective-permute-done | bytes 131104 | tf_op jit(solution)/shard_map/ppermute | solution.py:1072
  501.8 3.7 product.29.refs_1_
  515.6 4.9 collective-permute-start.59
  520.5 5.1 unpack.7
  533.4 6.4 %fusion.55 = f32[512,1024]{1,0:T(8,128)} fusion(bf16[512,1920]{1,0:T(8,128)(2,1)} %after.78, bf16[1024,1920]{1,0:T(8,128)(2,1)} %place.4.refs_1_), kind=kOutput, calls=%fused_computation.156 | convolution fusion | flops 2013265920 | bytes 7995392 | tf_op jit(solution)/shard_map/dot_general | solution.py:44
  (471 shorter events, 251.9 us)
Async XLA Ops:
  7.5 17.5 %collective-permute-start = (bf16[272,768]{1,0:T(8,128)(2,1)}, bf16[272,768]{1,0:T(8,128)(2,1)}, u32[]{:S(2)}, u32[]{:S(2)}) collective-permute-start(bf16[272,768]{1,0:T(8,128)(2,1)} %pad_maximum_fusion.7.refs_0_), channel_id=1, source_target_pairs={{0,1},{1,0},{2,3},{3,2},{4,5},{5,4},{6,7},{7,6},{8,9},{9,8},{10,11... | collective-permute-start | bytes 1253384 | tf_op jit(solution)/shard_map/ppermute | solution.py:1072
  13.5 46.0 %collective-permute-start.3 = (bf16[256,1920]{1,0:T(8,128)(2,1)}, bf16[256,1920]{1,0:T(8,128)(2,1)}, u32[]{:S(2)}, u32[]{:S(2)}) collective-permute-start(bf16[256,1920]{1,0:T(8,128)(2,1)} %fusion.22.refs_0_), channel_id=1, source_target_pairs={{0,1},{1,0},{2,3},{3,2},{4,5},{5,4},{6,7},{7,6},{8,9},{9,8},{10,11... | collective-permute-start | bytes 2949128 | tf_op jit(solution)/shard_map/ppermute | solution.py:1072
  13.7 28.4 %collective-permute-start.4 = (bf16[256,1920]{1,0:T(8,128)(2,1)}, bf16[256,1920]{1,0:T(8,128)(2,1)}, u32[]{:S(2)}, u32[]{:S(2)}) collective-permute-start(bf16[256,1920]{1,0:T(8,128)(2,1)} %fusion.22.refs_0_), channel_id=1, source_target_pairs={{0,2},{1,3},{2,0},{3,1},{4,6},{5,7},{6,4},{7,5},{8,10},{9,11},{10,... | collective-permute-start | bytes 2949128 | tf_op jit(solution)/shard_map/ppermute | solution.py:1072
  21.3 38.8 %collective-permute-start.7 = (bf16[256,6144]{1,0:T(8,128)(2,1)}, bf16[256,6144]{1,0:T(8,128)(2,1)}, u32[]{:S(2)}, u32[]{:S(2)}) collective-permute-start(bf16[256,6144]{1,0:T(8,128)(2,1)} %after.48.refs_0_), channel_id=1, source_target_pairs={{0,1},{1,0},{2,3},{3,2},{4,5},{5,4},{6,7},{7,6},{8,9},{9,8},{10,11... | collective-permute-start | bytes 9437192 | tf_op jit(solution)/shard_map/ppermute | solution.py:1072
  25.0 35.2 %collective-permute-start.6 = (bf16[256,3584]{1,0:T(8,128)(2,1)}, bf16[256,3584]{1,0:T(8,128)(2,1)}, u32[]{:S(2)}, u32[]{:S(2)}) collective-permute-start(bf16[256,3584]{1,0:T(8,128)(2,1)} %after.47.refs_5_), channel_id=1, source_target_pairs={{0,1},{1,0},{2,3},{3,2},{4,5},{5,4},{6,7},{7,6},{8,9},{9,8},{10,11... | collective-permute-start | bytes 5505032 | tf_op jit(solution)/shard_map/ppermute | solution.py:1072
  42.2 18.0 %collective-permute-start.5 = (bf16[256,1920]{1,0:T(8,128)(2,1)}, bf16[256,1920]{1,0:T(8,128)(2,1)}, u32[]{:S(2)}, u32[]{:S(2)}) collective-permute-start(bf16[256,1920]{1,0:T(8,128)(2,1)} %after.46.refs_2_), channel_id=1, source_target_pairs={{0,1},{1,0},{2,3},{3,2},{4,5},{5,4},{6,7},{7,6},{8,9},{9,8},{10,11... | collective-permute-start | bytes 2949128 | tf_op jit(solution)/shard_map/ppermute | solution.py:1072
  57.4 55.3 %collective-permute-start.18 = (bf16[256,3584]{1,0:T(8,128)(2,1)S(1)}, bf16[256,3584]{1,0:T(8,128)(2,1)}, u32[]{:S(2)}, u32[]{:S(2)}) collective-permute-start(bf16[256,3584]{1,0:T(8,128)(2,1)S(1)} %copy-done.5), channel_id=1, source_target_pairs={{0,2},{1,3},{2,0},{3,1},{4,6},{5,7},{6,4},{7,5},{8,10},{9,11},{10,... | collective-permute-start | bytes 5505032 | tf_op jit(solution)/shard_map/ppermute | solution.py:1072
  59.5 109.9 %collective-permute-start.20 = (bf16[256,6144]{1,0:T(8,128)(2,1)}, bf16[256,6144]{1,0:T(8,128)(2,1)}, u32[]{:S(2)}, u32[]{:S(2)}) collective-permute-start(bf16[256,6144]{1,0:T(8,128)(2,1)} %after.48.refs_0_), channel_id=1, source_target_pairs={{0,2},{1,3},{2,0},{3,1},{4,6},{5,7},{6,4},{7,5},{8,10},{9,11},{10,... | collective-permute-start | bytes 9437192 | tf_op jit(solution)/shard_map/ppermute | solution.py:1072
  75.4 22.5 %collective-permute-start.16 = (bf16[1024,128]{1,0:T(8,128)(2,1)}, bf16[1024,128]{1,0:T(8,128)(2,1)S(1)}, u32[]{:S(2)}, u32[]{:S(2)}) collective-permute-start(bf16[1024,128]{1,0:T(8,128)(2,1)} %after.53), channel_id=1, source_target_pairs={{0,8},{1,9},{2,10},{3,11},{4,12},{5,13},{6,14},{7,15},{8,0},{9,1},... | collective-permute-start | bytes 786440 | tf_op jit(solution)/shard_map/ppermute | solution.py:1072
  82.3 17.8 %collective-permute-start.12 = (bf16[2048,128]{1,0:T(8,128)(2,1)S(1)}, bf16[2048,128]{1,0:T(8,128)(2,1)}, u32[]{:S(2)}, u32[]{:S(2)}) collective-permute-start(bf16[2048,128]{1,0:T(8,128)(2,1)S(1)} %pad_maximum_fusion.5.refs_8_), channel_id=1, source_target_pairs={{0,4},{1,5},{2,6},{3,7},{4,0},{5,1},{6,2},{7,3},{8,12},{9,13},{10,... | collective-permute-start | bytes 1572872 | tf_op jit(solution)/shard_map/ppermute | solution.py:1072
  99.4 18.9 %collective-permute-start.17 = (bf16[2048,128]{1,0:T(8,128)(2,1)}, bf16[2048,128]{1,0:T(8,128)(2,1)}, u32[]{:S(2)}, u32[]{:S(2)}) collective-permute-start(bf16[2048,128]{1,0:T(8,128)(2,1)} %pad_maximum_fusion.6), channel_id=1, source_target_pairs={{0,4},{1,5},{2,6},{3,7},{4,0},{5,1},{6,2},{7,3},{8,12},{9,13},{10,... | collective-permute-start | bytes 1572872 | tf_op jit(solution)/shard_map/ppermute | solution.py:1072
  112.7 21.6 %collective-permute-start.19 = (bf16[256,3584]{1,0:T(8,128)(2,1)}, bf16[256,3584]{1,0:T(8,128)(2,1)}, u32[]{:S(2)}, u32[]{:S(2)}) collective-permute-start(bf16[256,3584]{1,0:T(8,128)(2,1)} %after.55.refs_7_), channel_id=1, source_target_pairs={{0,1},{1,0},{2,3},{3,2},{4,5},{5,4},{6,7},{7,6},{8,9},{9,8},{10,11... | collective-permute-start | bytes 5505032 | tf_op jit(solution)/shard_map/ppermute | solution.py:1072
  123.6 31.3 %collective-permute-start.14 = (bf16[144,1536]{1,0:T(8,128)(2,1)}, bf16[144,1536]{1,0:T(8,128)(2,1)S(1)}, u32[]{:S(2)}, u32[]{:S(2)}) collective-permute-start(bf16[144,1536]{1,0:T(8,128)(2,1)} %get-tuple-element.115.refs_9_), channel_id=1, source_target_pairs={{0,16},{1,17},{2,18},{3,19},{4,20},{5,21},{6,22},{7,23},{8,24},{9,... | collective-permute-start | bytes 1327112 | tf_op jit(solution)/shard_map/ppermute | solution.py:1072
  207.8 16.2 %collective-permute-start.22 = (bf16[512,4096]{1,0:T(8,128)(2,1)}, bf16[512,4096]{1,0:T(8,128)(2,1)}, u32[]{:S(2)}, u32[]{:S(2)}) collective-permute-start(bf16[512,4096]{1,0:T(8,128)(2,1)} %product.16), channel_id=1, source_target_pairs={{0,1},{1,0},{2,3},{3,2},{4,5},{5,4},{6,7},{7,6},{8,9},{9,8},{10,11... | collective-permute-start | bytes 12582920 | tf_op jit(solution)/shard_map/ppermute | solution.py:1072
  214.5 16.0 %collective-permute-start.23 = (bf16[1024,1024]{1,0:T(8,128)(2,1)}, bf16[1024,1024]{1,0:T(8,128)(2,1)}, u32[]{:S(2)}, u32[]{:S(2)}) collective-permute-start(bf16[1024,1024]{1,0:T(8,128)(2,1)} %product.18), channel_id=1, source_target_pairs={{0,1},{1,0},{2,3},{3,2},{4,5},{5,4},{6,7},{7,6},{8,9},{9,8},{10,11... | collective-permute-start | bytes 6291464 | tf_op jit(solution)/shard_map/ppermute | solution.py:1072
  229.3 48.3 %collective-permute-start.26 = (bf16[256,4096]{1,0:T(8,128)(2,1)}, bf16[256,4096]{1,0:T(8,128)(2,1)}, u32[]{:S(2)}, u32[]{:S(2)}) collective-permute-start(bf16[256,4096]{1,0:T(8,128)(2,1)} %product.17.refs_5_.refs_1_), channel_id=1, source_target_pairs={{0,2},{1,3},{2,0},{3,1},{4,6},{5,7},{6,4},{7,5},{8,10},{9,11},{10,... | collective-permute-start | bytes 6291464 | tf_op jit(solution)/shard_map/ppermute | solution.py:1072
  236.0 38.6 %collective-permute-start.29 = (bf16[512,1024]{1,0:T(8,128)(2,1)}, bf16[512,1024]{1,0:T(8,128)(2,1)S(1)}, u32[]{:S(2)}, u32[]{:S(2)}) collective-permute-start(bf16[512,1024]{1,0:T(8,128)(2,1)} %get-tuple-element.124.refs_2_), channel_id=1, source_target_pairs={{0,4},{1,5},{2,6},{3,7},{4,0},{5,1},{6,2},{7,3},{8,12},{9,13},{10,... | collective-permute-start | bytes 3145736 | tf_op jit(solution)/shard_map/ppermute | solution.py:1072
  254.8 16.1 %collective-permute-start.24 = (bf16[144,1536]{1,0:T(8,128)(2,1)}, bf16[144,1536]{1,0:T(8,128)(2,1)}, u32[]{:S(2)}, u32[]{:S(2)}) collective-permute-start(bf16[144,1536]{1,0:T(8,128)(2,1)} %get-tuple-element.132), channel_id=1, source_target_pairs={{0,4},{1,5},{2,6},{3,7},{4,0},{5,1},{6,2},{7,3},{8,12},{9,13},{10,... | collective-permute-start | bytes 1327112 | tf_op jit(solution)/shard_map/ppermute | solution.py:1072
  256.6 40.3 %collective-permute-start.31 = (bf16[1024,1024]{1,0:T(8,128)(2,1)}, bf16[1024,1024]{1,0:T(8,128)(2,1)}, u32[]{:S(2)}, u32[]{:S(2)}) collective-permute-start(bf16[1024,1024]{1,0:T(8,128)(2,1)} %product.21), channel_id=1, source_target_pairs={{0,1},{1,0},{2,3},{3,2},{4,5},{5,4},{6,7},{7,6},{8,9},{9,8},{10,11... | collective-permute-start | bytes 6291464 | tf_op jit(solution)/shard_map/ppermute | solution.py:1072
  261.0 24.8 %collective-permute-start.32 = (bf16[512,1536]{1,0:T(8,128)(2,1)}, bf16[512,1536]{1,0:T(8,128)(2,1)}, u32[]{:S(2)}, u32[]{:S(2)}) collective-permute-start(bf16[512,1536]{1,0:T(8,128)(2,1)} %product.23), channel_id=1, source_target_pairs={{0,1},{1,0},{2,3},{3,2},{4,5},{5,4},{6,7},{7,6},{8,9},{9,8},{10,11... | collective-permute-start | bytes 4718600 | tf_op jit(solution)/shard_map/ppermute | solution.py:1072
  273.8 16.8 %collective-permute-start.25 = (bf16[144,1536]{1,0:T(8,128)(2,1)}, bf16[144,1536]{1,0:T(8,128)(2,1)}, u32[]{:S(2)}, u32[]{:S(2)}) collective-permute-start(bf16[144,1536]{1,0:T(8,128)(2,1)} %get-tuple-element.135.refs_1_), channel_id=1, source_target_pairs={{0,8},{1,9},{2,10},{3,11},{4,12},{5,13},{6,14},{7,15},{8,0},{9,1},... | collective-permute-start | bytes 1327112 | tf_op jit(solution)/shard_map/ppermute | solution.py:1072
  283.6 26.4 %collective-permute-start.28 = (bf16[128,4096]{1,0:T(8,128)(2,1)}, bf16[128,4096]{1,0:T(8,128)(2,1)}, u32[]{:S(2)}, u32[]{:S(2)}) collective-permute-start(bf16[128,4096]{1,0:T(8,128)(2,1)} %get-tuple-element.136.refs_1_.refs_5_), channel_id=1, source_target_pairs={{0,4},{1,5},{2,6},{3,7},{4,0},{5,1},{6,2},{7,3},{8,12},{9,13},{10,... | collective-permute-start | bytes 3145736 | tf_op jit(solution)/shard_map/ppermute | solution.py:1072
  284.9 19.2 %collective-permute-start.30 = (bf16[256,1024]{1,0:T(8,128)(2,1)}, bf16[256,1024]{1,0:T(8,128)(2,1)}, u32[]{:S(2)}, u32[]{:S(2)}) collective-permute-start(bf16[256,1024]{1,0:T(8,128)(2,1)} %get-tuple-element.262), channel_id=1, source_target_pairs={{0,2},{1,3},{2,0},{3,1},{4,6},{5,7},{6,4},{7,5},{8,10},{9,11},{10,... | collective-permute-start | bytes 1572872 | tf_op jit(solution)/shard_map/ppermute | solution.py:1072
  289.5 34.3 %collective-permute-start.34 = (bf16[256,1536]{1,0:T(8,128)(2,1)}, bf16[256,1536]{1,0:T(8,128)(2,1)}, u32[]{:S(2)}, u32[]{:S(2)}) collective-permute-start(bf16[256,1536]{1,0:T(8,128)(2,1)} %product.24.refs_10_), channel_id=1, source_target_pairs={{0,2},{1,3},{2,0},{3,1},{4,6},{5,7},{6,4},{7,5},{8,10},{9,11},{10,... | collective-permute-start | bytes 2359304 | tf_op jit(solution)/shard_map/ppermute | solution.py:1072
  293.7 43.7 %collective-permute-start.27 = (bf16[144,1536]{1,0:T(8,128)(2,1)}, bf16[144,1536]{1,0:T(8,128)(2,1)}, u32[]{:S(2)}, u32[]{:S(2)}) collective-permute-start(bf16[144,1536]{1,0:T(8,128)(2,1)} %get-tuple-element.139.refs_1_.refs_7_), channel_id=1, source_target_pairs={{0,16},{1,17},{2,18},{3,19},{4,20},{5,21},{6,22},{7,23},{8,24},{9,... | collective-permute-start | bytes 1327112 | tf_op jit(solution)/shard_map/ppermute | solution.py:1072
  302.3 30.0 %collective-permute-start.35 = (bf16[512,1024]{1,0:T(8,128)(2,1)}, bf16[512,1024]{1,0:T(8,128)(2,1)S(1)}, u32[]{:S(2)}, u32[]{:S(2)}) collective-permute-start(bf16[512,1024]{1,0:T(8,128)(2,1)} %get-tuple-element.145.refs_9_), channel_id=1, source_target_pairs={{0,4},{1,5},{2,6},{3,7},{4,0},{5,1},{6,2},{7,3},{8,12},{9,13},{10,... | collective-permute-start | bytes 3145736 | tf_op jit(solution)/shard_map/ppermute | solution.py:1072
  313.3 26.4 %collective-permute-start.33 = (bf16[64,6144]{1,0:T(8,128)(2,1)}, bf16[64,6144]{1,0:T(8,128)(2,1)}, u32[]{:S(2)}, u32[]{:S(2)}) collective-permute-start(bf16[64,6144]{1,0:T(8,128)(2,1)} %get-tuple-element.144.refs_8_), channel_id=1, source_target_pairs={{0,8},{1,9},{2,10},{3,11},{4,12},{5,13},{6,14},{7,15},{8,0},{9,1},... | collective-permute-start | bytes 2359304 | tf_op jit(solution)/shard_map/ppermute | solution.py:1072
  327.8 63.0 %collective-permute-start.38 = (bf16[128,1536]{1,0:T(8,128)(2,1)}, bf16[128,1536]{1,0:T(8,128)(2,1)S(1)}, u32[]{:S(2)}, u32[]{:S(2)}) collective-permute-start(bf16[128,1536]{1,0:T(8,128)(2,1)} %get-tuple-element.148.refs_14_), channel_id=1, source_target_pairs={{0,4},{1,5},{2,6},{3,7},{4,0},{5,1},{6,2},{7,3},{8,12},{9,13},{10,... | collective-permute-start | bytes 1179656 | tf_op jit(solution)/shard_map/ppermute | solution.py:1072
  336.3 55.3 %collective-permute-start.39 = (bf16[256,1024]{1,0:T(8,128)(2,1)}, bf16[256,1024]{1,0:T(8,128)(2,1)}, u32[]{:S(2)}, u32[]{:S(2)}) collective-permute-start(bf16[256,1024]{1,0:T(8,128)(2,1)} %get-tuple-element.261.refs_15_), channel_id=1, source_target_pairs={{0,2},{1,3},{2,0},{3,1},{4,6},{5,7},{6,4},{7,5},{8,10},{9,11},{10,... | collective-permute-start | bytes 1572872 | tf_op jit(solution)/shard_map/ppermute | solution.py:1072
  337.4 47.4 %collective-permute-start.40 = (bf16[2048,128]{1,0:T(8,128)(2,1)}, bf16[2048,128]{1,0:T(8,128)(2,1)}, u32[]{:S(2)}, u32[]{:S(2)}) collective-permute-start(bf16[2048,128]{1,0:T(8,128)(2,1)} %slice.188.refs_16_), channel_id=1, source_target_pairs={{0,4},{1,5},{2,6},{3,7},{4,0},{5,1},{6,2},{7,3},{8,12},{9,13},{10,... | collective-permute-start | bytes 1572872 | tf_op jit(solution)/shard_map/ppermute | solution.py:1072
  343.0 50.1 %collective-permute-start.37 = (bf16[64,6144]{1,0:T(8,128)(2,1)}, bf16[64,6144]{1,0:T(8,128)(2,1)S(1)}, u32[]{:S(2)}, u32[]{:S(2)}) collective-permute-start(bf16[64,6144]{1,0:T(8,128)(2,1)} %add_convert_fusion.4.refs_13_), channel_id=1, source_target_pairs={{0,16},{1,17},{2,18},{3,19},{4,20},{5,21},{6,22},{7,23},{8,24},{9,... | collective-permute-start | bytes 2359304 | tf_op jit(solution)/shard_map/ppermute | solution.py:1072
  401.5 17.5 %collective-permute-start.41 = (bf16[512,1920]{1,0:T(8,128)(2,1)}, bf16[512,1920]{1,0:T(8,128)(2,1)}, u32[]{:S(2)}, u32[]{:S(2)}) collective-permute-start(bf16[512,1920]{1,0:T(8,128)(2,1)} %product.26), channel_id=1, source_target_pairs={{0,1},{1,0},{2,3},{3,2},{4,5},{5,4},{6,7},{7,6},{8,9},{9,8},{10,11... | collective-permute-start | bytes 5898248 | tf_op jit(solution)/shard_map/ppermute | solution.py:1072
  401.6 25.3 %collective-permute-start.42 = (bf16[64,6144]{1,0:T(8,128)(2,1)}, bf16[64,6144]{1,0:T(8,128)(2,1)}, u32[]{:S(2)}, u32[]{:S(2)}) collective-permute-start(bf16[64,6144]{1,0:T(8,128)(2,1)} %add_convert_fusion.3.refs_5_.own_ref), channel_id=1, source_target_pairs={{0,8},{1,9},{2,10},{3,11},{4,12},{5,13},{6,14},{7,15},{8,0},{9,1},... | collective-permute-start | bytes 2359304 | tf_op jit(solution)/shard_map/ppermute | solution.py:1072
  414.4 23.6 %collective-permute-start.44 = (bf16[1024,128]{1,0:T(8,128)(2,1)S(1)}, bf16[1024,128]{1,0:T(8,128)(2,1)S(1)}, u32[]{:S(2)}, u32[]{:S(2)}) collective-permute-start(bf16[1024,128]{1,0:T(8,128)(2,1)S(1)} %slice.230), channel_id=1, source_target_pairs={{0,8},{1,9},{2,10},{3,11},{4,12},{5,13},{6,14},{7,15},{8,0},{9,1},... | collective-permute-start | bytes 786440 | tf_op jit(solution)/shard_map/ppermute | solution.py:1072
  417.1 40.6 %collective-permute-start.52 = (bf16[64,3584]{1,0:T(8,128)(2,1)}, bf16[64,3584]{1,0:T(8,128)(2,1)S(1)}, u32[]{:S(2)}, u32[]{:S(2)}) collective-permute-start(bf16[64,3584]{1,0:T(8,128)(2,1)} %get-tuple-element.157.refs_8_), channel_id=1, source_target_pairs={{0,8},{1,9},{2,10},{3,11},{4,12},{5,13},{6,14},{7,15},{8,0},{9,1},... | collective-permute-start | bytes 1376264 | tf_op jit(solution)/shard_map/ppermute | solution.py:1072
  423.3 48.9 %collective-permute-start.46 = (bf16[256,1920]{1,0:T(8,128)(2,1)}, bf16[256,1920]{1,0:T(8,128)(2,1)}, u32[]{:S(2)}, u32[]{:S(2)}) collective-permute-start(bf16[256,1920]{1,0:T(8,128)(2,1)} %product.27.refs_1_.refs_7_), channel_id=1, source_target_pairs={{0,2},{1,3},{2,0},{3,1},{4,6},{5,7},{6,4},{7,5},{8,10},{9,11},{10,... | collective-permute-start | bytes 2949128 | tf_op jit(solution)/shard_map/ppermute | solution.py:1072
  440.4 31.1 %collective-permute-start.45 = (bf16[512,128]{1,0:T(8,128)(2,1)}, bf16[512,128]{1,0:T(8,128)(2,1)S(1)}, u32[]{:S(2)}, u32[]{:S(2)}) collective-permute-start(bf16[512,128]{1,0:T(8,128)(2,1)} %slice.232), channel_id=1, source_target_pairs={{0,16},{1,17},{2,18},{3,19},{4,20},{5,21},{6,22},{7,23},{8,24},{9,... | collective-permute-start | bytes 393224 | tf_op jit(solution)/shard_map/ppermute | solution.py:1072
  455.0 15.5 %collective-permute-start.43 = (bf16[2048,128]{1,0:T(8,128)(2,1)S(1)}, bf16[2048,128]{1,0:T(8,128)(2,1)S(1)}, u32[]{:S(2)}, u32[]{:S(2)}) collective-permute-start(bf16[2048,128]{1,0:T(8,128)(2,1)S(1)} %slice.194.refs_1_), channel_id=1, source_target_pairs={{0,4},{1,5},{2,6},{3,7},{4,0},{5,1},{6,2},{7,3},{8,12},{9,13},{10,... | collective-permute-start | bytes 1572872 | tf_op jit(solution)/shard_map/ppermute | solution.py:1072
  459.6 46.0 %collective-permute-start.53 = (bf16[64,3584]{1,0:T(8,128)(2,1)S(1)}, bf16[64,3584]{1,0:T(8,128)(2,1)}, u32[]{:S(2)}, u32[]{:S(2)}) collective-permute-start(bf16[64,3584]{1,0:T(8,128)(2,1)S(1)} %add_convert_fusion.8), channel_id=1, source_target_pairs={{0,16},{1,17},{2,18},{3,19},{4,20},{5,21},{6,22},{7,23},{8,24},{9,... | collective-permute-start | bytes 1376264 | tf_op jit(solution)/shard_map/ppermute | solution.py:1072
  459.7 60.8 %collective-permute-start.65 = (bf16[128,6144]{1,0:T(8,128)(2,1)}, bf16[128,6144]{1,0:T(8,128)(2,1)}, u32[]{:S(2)}, u32[]{:S(2)}) collective-permute-start(bf16[128,6144]{1,0:T(8,128)(2,1)} %after.90), channel_id=1, source_target_pairs={{0,4},{1,5},{2,6},{3,7},{4,0},{5,1},{6,2},{7,3},{8,12},{9,13},{10,... | collective-permute-start | bytes 4718600 | tf_op jit(solution)/shard_map/ppermute | solution.py:1072
  490.6 22.9 %collective-permute-start.58 = (bf16[128,1920]{1,0:T(8,128)(2,1)S(1)}, bf16[128,1920]{1,0:T(8,128)(2,1)}, u32[]{:S(2)}, u32[]{:S(2)}) collective-permute-start(bf16[128,1920]{1,0:T(8,128)(2,1)S(1)} %copy-done.47), channel_id=1, source_target_pairs={{0,4},{1,5},{2,6},{3,7},{4,0},{5,1},{6,2},{7,3},{8,12},{9,13},{10,... | collective-permute-start | bytes 1474568 | tf_op jit(solution)/shard_map/ppermute | solution.py:1072
  507.5 32.3 %collective-permute-start.54 = (bf16[64,3584]{1,0:T(8,128)(2,1)}, bf16[64,3584]{1,0:T(8,128)(2,1)S(1)}, u32[]{:S(2)}, u32[]{:S(2)}) collective-permute-start(bf16[64,3584]{1,0:T(8,128)(2,1)} %add_convert_fusion.7.own_ref), channel_id=1, source_target_pairs={{0,8},{1,9},{2,10},{3,11},{4,12},{5,13},{6,14},{7,15},{8,0},{9,1},... | collective-permute-start | bytes 1376264 | tf_op jit(solution)/shard_map/ppermute | solution.py:1072
  511.5 18.0 %collective-permute-start.50 = (bf16[256,768]{1,0:T(8,128)(2,1)}, bf16[256,768]{1,0:T(8,128)(2,1)}, u32[]{:S(2)}, u32[]{:S(2)}) collective-permute-start(bf16[256,768]{1,0:T(8,128)(2,1)} %product.30.refs_1_), channel_id=1, source_target_pairs={{0,2},{1,3},{2,0},{3,1},{4,6},{5,7},{6,4},{7,5},{8,10},{9,11},{10,... | collective-permute-start | bytes 1179656 | tf_op jit(solution)/shard_map/ppermute | solution.py:1072
  515.6 13.4 %collective-permute-start.59 = (bf16[64,1920]{1,0:T(8,128)(2,1)}, bf16[64,1920]{1,0:T(8,128)(2,1)S(1)}, u32[]{:S(2)}, u32[]{:S(2)}) collective-permute-start(bf16[64,1920]{1,0:T(8,128)(2,1)} %get-tuple-element.169), channel_id=1, source_target_pairs={{0,8},{1,9},{2,10},{3,11},{4,12},{5,13},{6,14},{7,15},{8,0},{9,1},... | collective-permute-start | bytes 737288 | tf_op jit(solution)/shard_map/ppermute | solution.py:1072
  529.1 15.3 %collective-permute-start.60 = (bf16[64,1920]{1,0:T(8,128)(2,1)S(1)}, bf16[64,1920]{1,0:T(8,128)(2,1)S(1)}, u32[]{:S(2)}, u32[]{:S(2)}) collective-permute-start(bf16[64,1920]{1,0:T(8,128)(2,1)S(1)} %add_convert_fusion.12), channel_id=1, source_target_pairs={{0,16},{1,17},{2,18},{3,19},{4,20},{5,21},{6,22},{7,23},{8,24},{9,... | collective-permute-start | bytes 737288 | tf_op jit(solution)/shard_map/ppermute | solution.py:1072
  533.1 13.7 %collective-permute-start.51 = (bf16[128,768]{1,0:T(8,128)(2,1)}, bf16[128,768]{1,0:T(8,128)(2,1)}, u32[]{:S(2)}, u32[]{:S(2)}) collective-permute-start(bf16[128,768]{1,0:T(8,128)(2,1)} %get-tuple-element.161.refs_1_), channel_id=1, source_target_pairs={{0,4},{1,5},{2,6},{3,7},{4,0},{5,1},{6,2},{7,3},{8,12},{9,13},{10,... | collective-permute-start | bytes 589832 | tf_op jit(solution)/shard_map/ppermute | solution.py:1072
  542.7 27.3 %collective-permute-start.55 = (bf16[128,3584]{1,0:T(8,128)(2,1)}, bf16[128,3584]{1,0:T(8,128)(2,1)}, u32[]{:S(2)}, u32[]{:S(2)}) collective-permute-start(bf16[128,3584]{1,0:T(8,128)(2,1)} %join.5.refs_1_.own_ref), channel_id=1, source_target_pairs={{0,4},{1,5},{2,6},{3,7},{4,0},{5,1},{6,2},{7,3},{8,12},{9,13},{10,... | collective-permute-start | bytes 2752520 | tf_op jit(solution)/shard_map/ppermute | solution.py:1072
  573.5 13.6 %collective-permute-start.64 = (bf16[128,768]{1,0:T(8,128)(2,1)}, bf16[128,768]{1,0:T(8,128)(2,1)}, u32[]{:S(2)}, u32[]{:S(2)}) collective-permute-start(bf16[128,768]{1,0:T(8,128)(2,1)} %after.88.refs_1_), channel_id=1, source_target_pairs={{0,4},{1,5},{2,6},{3,7},{4,0},{5,1},{6,2},{7,3},{8,12},{9,13},{10,... | collective-permute-start | bytes 589832 | tf_op jit(solution)/shard_map/ppermute | solution.py:1072
  (95 other events, 655.5 us)
